TPU v7x, 32 devices: a whole 2x2x4 slice. The times are simulated.
32 devices in a mesh: row: 8 (over z, y), col: 4 (over x, core).
Axes of the slice: x: 2, y: 2, z: 4, core: 2. Of those that a mesh axis runs over, the one named last changes fastest.
Arguments:
- pair: bfloat16 [128, 128, 128], P('row', 'col'), may hold values from -6 to 6
- chain_lengths: int32 [8], replicated, may hold values from 1 to 16, 96 in all
- norm_in_gain: float32 [128], replicated, may hold values from 0.1 to 1.9
- norm_in_bias: float32 [128], replicated, may hold values from -3 to 3
- proj_in: bfloat16 [128, 256], replicated, may hold values from -0.5 to 0.5
- gate_in: bfloat16 [128, 256], replicated, may hold values from -0.5 to 0.5
- norm_out_gain: float32 [128], replicated, may hold values from 0.1 to 1.9
- norm_out_bias: float32 [128], replicated, may hold values from -3 to 3
- proj_out: bfloat16 [128, 128], replicated, may hold values from -0.5 to 0.5
- gate_out: bfloat16 [128, 128], replicated, may hold values from -0.5 to 0.5
Outputs:
- update: bfloat16 [128, 128, 128], P('row', 'col')
Inputs may be any that keep to these rules, and one draw needn't show every extreme that they name: Chain c owns token slots c * 16 to (c + 1) * 16 - 1; its first chain_lengths[c] slots are real tokens and the rest padding; the lengths sum to 96 and one of them is 16.
All inputs are finite; a program needn't handle non-finite values.
Results may differ from a plain program's by a relative error of at most 0.0055.
Values may be sent and summed in bfloat16 or wider, within the bound.
No kernel may reach another device: no remote copies, remote signals or barrier semaphores. Data moves between devices by JAX's collectives and lax.ppermute only.
A program may use at most 64 MiB of HBM per device.

v0:
```python
import jax
import jax.numpy as jnp
from jax import lax
from jax.sharding import PartitionSpec as P


def broadcast(value, axis, source):
    kept = jnp.where(lax.axis_index(axis) == source, value, 0).astype(value.dtype)
    return lax.psum(kept, axis)


def layer_norm(values, gain, bias):
    mean = jnp.mean(values, axis=-1, keepdims=True)
    centered = values - mean
    variance = jnp.mean(centered * centered, axis=-1, keepdims=True)
    return centered * lax.rsqrt(variance + 1e-05) * gain + bias


def token_valid(chain_lengths, tokens_idx, slots):
    chain = tokens_idx // slots
    position = tokens_idx % slots
    chain_ids = jnp.arange(chain_lengths.shape[0], dtype=jnp.int32)
    length_of = jnp.sum(
        jnp.where(chain[:, None] == chain_ids[None, :], chain_lengths[None, :], 0), axis=1
    )
    return (position < length_of).astype(jnp.float32)


def shards(
    pair,
    chain_lengths,
    norm_in_gain,
    norm_in_bias,
    proj_in,
    gate_in,
    norm_out_gain,
    norm_out_bias,
    proj_out,
    gate_out,
):
    row_count = pair.shape[0]
    col_count = pair.shape[1]
    channels = pair.shape[2]
    hidden = proj_out.shape[0]
    row_index = lax.axis_index("row")
    col_index = lax.axis_index("col")
    slots = row_count * lax.axis_size("row") // chain_lengths.shape[0]
    valid_rows = token_valid(
        chain_lengths, row_index * row_count + jnp.arange(row_count, dtype=jnp.int32), slots
    )
    valid_cols = token_valid(
        chain_lengths, col_index * col_count + jnp.arange(col_count, dtype=jnp.int32), slots
    )
    pair_mask = valid_rows[:, None] * valid_cols[None, :]
    normed = layer_norm(pair.astype(jnp.float32), norm_in_gain, norm_in_bias).astype(jnp.bfloat16)
    flat = normed.reshape(-1, channels)
    values = jnp.dot(flat, proj_in, preferred_element_type=jnp.float32)
    gates = jnp.dot(flat, gate_in, preferred_element_type=jnp.float32)
    mixed = (jax.nn.sigmoid(gates) * values).reshape(row_count, col_count, 2 * hidden) * pair_mask[
        :, :, None
    ]
    left_tile = mixed[:, :, :hidden].astype(jnp.bfloat16)
    right_tile = mixed[:, :, hidden:].astype(jnp.bfloat16)
    ratio = lax.axis_size("row") // lax.axis_size("col")
    right_full = lax.all_gather(right_tile, "col", axis=1, tiled=True)
    received = []
    for part in range(ratio):
        received.append(broadcast(right_full, "row", col_index * ratio + part))
    right_mine = jnp.concatenate(received, axis=0)
    triangle = jnp.einsum(
        "ikh,jkh->ijh",
        lax.all_gather(left_tile, "col", axis=1, tiled=True),
        right_mine,
        preferred_element_type=jnp.float32,
    )
    tri_normed = layer_norm(triangle, norm_out_gain, norm_out_bias).astype(jnp.bfloat16)
    projected = jnp.dot(
        tri_normed.reshape(-1, hidden), proj_out, preferred_element_type=jnp.float32
    )
    gate = jax.nn.sigmoid(jnp.dot(flat, gate_out, preferred_element_type=jnp.float32))
    return (gate * projected).astype(jnp.bfloat16).reshape(row_count, col_count, channels)


def solution(mesh):
    return jax.shard_map(
        shards,
        mesh=mesh,
        in_specs=(P("row", "col", None), P(), P(), P(), P(), P(), P(), P(), P(), P()),
        out_specs=P("row", "col", None),
        check_vma=False,
    )
```

profile of v0, /device:TPU:0, one launch (start us, length us, event | category | flops | bytes accessed | tf_op | source)
XLA Modules:
  0.0 113.5 jit_solution(3530703770712773168)
XLA Ops:
  6.5 0.0 copy-start
  6.5 0.0 all-reduce.3.cloned.1.call-start
  6.6 0.8 select_reduce_fusion.1
  7.4 0.7 select_reduce_fusion
  8.1 1.0 convert_reduce_fusion
  9.2 1.2 %fusion.14 = f32[16,32]{1,0:T(8,128)S(1)} fusion(bf16[16,32,128]{2,1,0:T(8,128)(2,1)} %param.10, f32[16,32]{1,0:T(8,128)S(1)} %broadcast_multiply_fusion.2), kind=kLoop, calls=%fused_computation.23 | loop fusion | flops 261632 | bytes 135168 | tf_op jit(solution)/shard_map/reduce_sum | solution.py:15
  10.3 0.1 broadcast_multiply_fusion
  10.4 1.1 fusion.17
  11.6 0.0 copy-done
  11.6 0.0 copy-start.1
  11.6 0.3 fusion.2
  11.9 0.5 copy-done.1
  12.4 0.2 convolution_multiply_fusion
  12.6 0.3 fusion.11
  13.0 8.6 %all_gather.6 = bf16[16,128,128]{2,0,1:T(8,128)(2,1)S(1)} all-gather(bf16[16,32,128]{2,0,1:T(8,128)(2,1)S(1)} %get-tuple-element.9), channel_id=1, replica_groups=mesh['row'=8,'col'=4] {'col'}, dimensions={1}, use_global_device_ids=true | all-gather | bytes 655360 | tf_op jit(solution)/shard_map/all_gather | solution.py:65
  21.6 0.7 copy.25
  22.4 1.1 broadcast_select_fusion.1
  23.5 0.0 all-reduce.3.cloned.1.call-update
  23.5 0.0 copy-start.5
  23.5 7.3 %all_gather.7 = bf16[16,128,128]{2,0,1:T(8,128)(2,1)S(1)} all-gather(bf16[16,32,128]{2,0,1:T(8,128)(2,1)S(1)} %get-tuple-element.10), channel_id=1, replica_groups=mesh['row'=8,'col'=4] {'col'}, dimensions={1}, use_global_device_ids=true | all-gather | bytes 655360 | tf_op jit(solution)/shard_map/all_gather | solution.py:72
  30.8 0.7 copy.27
  31.6 0.0 copy-done.5
  31.6 0.2 fusion.5
  31.8 71.0 %all-reduce.3.cloned.1.call-done = (bf16[16,128,128]{1,0,2:T(8,128)(2,1)}, bf16[16,128,128]{1,0,2:T(8,128)(2,1)}) async-done(((bf16[16,128,128]{1,0,2:T(8,128)(2,1)}, bf16[16,128,128]{1,0,2:T(8,128)(2,1)}), (bf16[16,128,128]{1,0,2:T(8,128)(2,1)}, bf16[16,128,128]{1,0,2:T(8,128)(2,1)})) %all-reduce.3.cloned.1.call-update) | async-done | bytes 1048592 | tf_op jit(solution)/shard_map/psum | solution.py:9
  102.8 1.8 %fusion.7 = f32[128,32,16]{1,2,0:T(8,128)S(1)} fusion(bf16[16,128,128]{1,0,2:T(8,128)(2,1)S(1)} %copy.27, bf16[16,128,128]{1,0,2:T(8,128)(2,1)} %get-tuple-element.5, bf16[16,128,128]{1,0,2:T(8,128)(2,1)} %get-tuple-element.6), kind=kOutput, calls=%fused_computation.11 | convolution fusion | flops 18874368 | bytes 1835008 | tf_op jit(solution)/shard_map/ikh,jkh->ijh/dot_general | solution.py:70
  104.7 0.0 copy-start.3
  104.7 0.0 copy-start.4
  104.7 0.0 copy-start.2
  104.7 0.4 copy.28
  105.1 0.1 bitcast_reduce_fusion
  105.3 0.3 multiply_reduce_fusion
  105.5 0.0 copy-done.3
  105.6 0.0 copy-done.4
  105.6 0.2 add_convert_fusion
  105.8 0.0 copy-done.2
  105.8 0.8 fusion.6
  (9 shorter events, 0.1 us)
Async XLA Ops:
  6.5 5.0 %copy-start = (bf16[128,256]{1,0:T(8,128)(2,1)S(1)}, bf16[128,256]{1,0:T(8,128)(2,1)}, u32[]{:S(2)}) copy-start(bf16[128,256]{1,0:T(8,128)(2,1)} %param.15) | copy-start | bytes 196612
  6.5 96.3 %all-reduce.3.cloned.1.call-start = ((), (), s32[]{:S(2)}) async-start(), calls=%async_computation | async-start | bytes 2097152 | tf_op jit(solution)/shard_map/psum | solution.py:9
  11.6 0.8 copy-start.1
  23.5 8.0 %copy-start.5 = (bf16[128,128]{1,0:T(8,128)(2,1)S(1)}, bf16[128,128]{1,0:T(8,128)(2,1)}, u32[]{:S(2)}) copy-start(bf16[128,128]{1,0:T(8,128)(2,1)} %param.19) | copy-start | bytes 98308
  104.7 0.9 copy-start.3
  104.7 0.9 copy-start.4
  104.7 1.1 copy-start.2
Sparse Core Ops, SparseCore 0:
  23.6 79.1 all-reduce.2
where the time goes:
time: 114 us; the launch traced here: 113 us
  waiting for transfers between devices  71 us (62%)
  blocking collectives  15.9 us (14%)
  between operations  13.6 us (12%)
  other arithmetic  7.01 us (6%)
  matrix products  3.37 us (3%)
  local copies, waits for them, and re-layouts  2.51 us (2%)
    psum x1, waiting for transfers between devices, broadcast(): return lax.psum(kept, axis)  71 us
    all_gather x1, blocking collectives, shards(): right_full = lax.all_gather(right_tile, 'col', axis=1, tiled=True)  8.62 us
    all_gather x1, blocking collectives, shards(): lax.all_gather(left_tile, 'col', axis=1, tiled=True)  7.29 us
  transfers between devices with their start and end apart: 1, of which 1 were waited for; matrix products, arithmetic and copies ran while one was open for 1% of the time, Pallas kernels for 0%

commit v1 on v0

--- a/solution.py
+++ b/solution.py
@@ -1,7 +1,14 @@
+import functools
 import jax
 import jax.numpy as jnp
 from jax import lax
+from jax.experimental import pallas as pl
+from jax.experimental.pallas import tpu as pltpu
 from jax.sharding import PartitionSpec as P
+
+LANES = 128
+F32 = jnp.float32
+BF16 = jnp.bfloat16
 
 
 def broadcast(value, axis, source):
@@ -26,7 +33,7 @@
     return (position < length_of).astype(jnp.float32)
 
 
-def shards(
+def gathered(
     pair,
     chain_lengths,
     norm_in_gain,
@@ -81,7 +88,256 @@
     return (gate * projected).astype(jnp.bfloat16).reshape(row_count, col_count, channels)
 
 
+def iota2(shape):
+    return (
+        lax.broadcasted_iota(jnp.int32, shape, 0),
+        lax.broadcasted_iota(jnp.int32, shape, 1),
+    )
+
+
+def one_hot(condition):
+    return jnp.where(condition, 1.0, 0.0).astype(BF16)
+
+
+def dot(a, b, a_dim=1, b_dim=0):
+    return lax.dot_general(a, b, (((a_dim,), (b_dim,)), ((), ())), preferred_element_type=F32)
+
+
+def mix_kernel(
+    slots, chain_ref, pair_ref, gain_ref, bias_ref, proj_ref, gate_ref, sent_ref, normed_ref
+):
+    rows, cols, channels = pair_ref.shape
+    hidden = proj_ref.shape[1] // 2
+    cells = rows * cols
+    groups = cells // LANES
+    chunks = sent_ref.shape[0]
+    own = hidden // chunks
+    flat = pair_ref[...].reshape(cells, channels).astype(F32)
+    normed = layer_norm(flat, gain_ref[...], bias_ref[...]).astype(BF16)
+    normed_ref[...] = normed
+
+    cell = lax.broadcasted_iota(jnp.int32, (1, cells), 1)
+
+    def valid(token):
+        length = jnp.zeros_like(token)
+        for chain in range(chain_ref.shape[0]):
+            length = jnp.where(token // slots == chain, chain_ref[chain], length)
+        return token % slots < length
+
+    row_ok = valid(lax.axis_index("row") * rows + cell // cols)
+    col_ok = valid(lax.axis_index("col") * cols + cell % cols)
+    mask = jnp.where(row_ok & col_ok, 1.0, 0.0)
+
+    values = dot(proj_ref[...], normed, 0, 1)
+    gates = dot(gate_ref[...], normed, 0, 1)
+    mixed = (jax.nn.sigmoid(gates) * values * mask).astype(BF16)
+
+    block = LANES // groups
+    out, source = iota2((LANES, LANES))
+    order = one_hot((out // groups == source % block) & (out % groups == source // block))
+    for side in range(2):
+        for part in range(hidden // block):
+            first = side * hidden + part * block
+            stack = jnp.concatenate(
+                [
+                    mixed[first : first + block, g * LANES : (g + 1) * LANES]
+                    for g in range(groups)
+                ],
+                axis=0,
+            )
+            moved = dot(order, stack).astype(BF16)
+            count = block // own
+            sent_ref[
+                part * count : (part + 1) * count, side * own * groups : (side + 1) * own * groups
+            ] = moved.reshape(count, own * groups, LANES)
+
+
+def triangle_kernel(grid_rows, grid_cols, rows, cols, got_ref, sent_ref):
+    groups = rows * cols // LANES
+    inner = LANES // cols
+    own = got_ref.shape[1] // (2 * groups)
+    side = own * groups
+    got = got_ref[...].reshape(grid_rows, grid_cols, 2 * side, LANES)
+    high = grid_rows * side
+    ratio = grid_rows // grid_cols
+    quarter = ratio * side
+
+    def block(column, which):
+        return got[:, column, which * side : (which + 1) * side].reshape(high, LANES)
+
+    left = jnp.concatenate([block(c, 0) for c in range(grid_cols)], axis=1)
+    right = jnp.concatenate([block(c, 1) for c in range(grid_cols)], axis=0)
+
+    lane = lax.broadcasted_iota(jnp.int32, (1, grid_cols * LANES), 1)
+    left_by = jnp.concatenate(
+        [left * one_hot(lane % LANES // cols == i) for i in range(inner)], axis=0
+    )
+    source, out = iota2((LANES, inner * LANES))
+    spread = one_hot((source // cols == out // LANES) & (source % cols == out % cols))
+    wide = dot(right, spread).astype(BF16)
+    right_by = jnp.concatenate(
+        [
+            jnp.concatenate(
+                [
+                    wide[
+                        c * high + d * quarter : c * high + (d + 1) * quarter,
+                        j * LANES : (j + 1) * LANES,
+                    ]
+                    for c in range(grid_cols)
+                ],
+                axis=1,
+            )
+            for d in range(grid_cols)
+            for j in range(inner)
+        ],
+        axis=0,
+    )
+    product = dot(left_by, right_by, 1, 1)
+
+    width = inner * quarter
+    a, b = iota2((high, width))
+    same = jnp.where(a // groups % own == b // groups % own, 1.0, 0.0)
+    kept = jnp.concatenate(
+        [
+            jnp.concatenate(
+                [
+                    (product[i * high : (i + 1) * high, d * width : (d + 1) * width] * same).astype(
+                        BF16
+                    )
+                    for i in range(inner)
+                ],
+                axis=1,
+            )
+            for d in range(grid_cols)
+        ],
+        axis=0,
+    )
+    source, out = iota2((inner * width, LANES))
+    at = source % width
+    token = at % quarter // side * rows + at % groups * inner + at // quarter
+    order = one_hot((source // width == out // cols) & (token == out % cols))
+    moved = dot(kept, order).astype(BF16).reshape(grid_cols, grid_rows, side, LANES)
+    for c in range(grid_cols):
+        for r in range(grid_rows):
+            sent_ref[r * grid_cols + c] = moved[c, r]
+
+
+def gate_kernel(normed_ref, gate_ref, out_ref):
+    out_ref[...] = jax.nn.sigmoid(dot(normed_ref[...], gate_ref[...]))
+
+
+def update_kernel(got_ref, open_ref, gain_ref, bias_ref, proj_ref, out_ref):
+    rows, cols, channels = out_ref.shape
+    hidden = proj_ref.shape[0]
+    groups = rows * cols // LANES
+    inner = LANES // cols
+    block = LANES // groups
+    got = got_ref[...].reshape(hidden * groups, LANES)
+    out, source = iota2((LANES, LANES))
+    order = one_hot((source // groups == out % block) & (source % groups == out // block))
+    pieces = [
+        dot(order, got[part * LANES : (part + 1) * LANES]) for part in range(hidden // block)
+    ]
+    a, b = iota2((hidden, hidden))
+    gain = jnp.sum(jnp.where(a == b, gain_ref[...], 0.0), axis=1, keepdims=True)
+    bias = jnp.sum(jnp.where(a == b, bias_ref[...], 0.0), axis=1, keepdims=True)
+    for g in range(groups):
+        values = jnp.concatenate([piece[g * block : (g + 1) * block] for piece in pieces], axis=0)
+        mean = jnp.mean(values, axis=0, keepdims=True)
+        centered = values - mean
+        variance = jnp.mean(centered * centered, axis=0, keepdims=True)
+        tri_normed = (centered * lax.rsqrt(variance + 1e-05) * gain + bias).astype(BF16)
+        projected = dot(tri_normed, proj_ref[...], 0, 0)
+        update = (open_ref[g * LANES : (g + 1) * LANES] * projected).astype(BF16)
+        out_ref[g * inner : (g + 1) * inner] = update.reshape(inner, cols, channels)
+
+
+VMEM = pl.BlockSpec(memory_space=pltpu.VMEM)
+SMEM = pl.BlockSpec(memory_space=pltpu.SMEM)
+PARAMS = pltpu.CompilerParams(vmem_limit_bytes=40 * 1024 * 1024)
+
+
+def exchanged(
+    pair,
+    chain_lengths,
+    norm_in_gain,
+    norm_in_bias,
+    proj_in,
+    gate_in,
+    norm_out_gain,
+    norm_out_bias,
+    proj_out,
+    gate_out,
+):
+    rows, cols, channels = pair.shape
+    hidden = proj_out.shape[0]
+    grid_rows, grid_cols = lax.axis_size("row"), lax.axis_size("col")
+    devices = grid_rows * grid_cols
+    groups = rows * cols // LANES
+    side = hidden // devices * groups
+    slots = rows * grid_rows // chain_lengths.shape[0]
+    sent, normed = pl.pallas_call(
+        functools.partial(mix_kernel, slots),
+        out_shape=(
+            jax.ShapeDtypeStruct((devices, 2 * side, LANES), BF16),
+            jax.ShapeDtypeStruct((rows * cols, channels), BF16),
+        ),
+        in_specs=[SMEM] + [VMEM] * 5,
+        out_specs=(VMEM, VMEM),
+        compiler_params=PARAMS,
+        name="mix",
+    )(
+        chain_lengths,
+        pair,
+        norm_in_gain.reshape(1, channels),
+        norm_in_bias.reshape(1, channels),
+        proj_in,
+        gate_in,
+    )
+    got = lax.all_to_all(sent, ("row", "col"), 0, 0, tiled=True)
+    opened = pl.pallas_call(
+        gate_kernel,
+        out_shape=jax.ShapeDtypeStruct((rows * cols, channels), F32),
+        in_specs=[VMEM] * 2,
+        out_specs=VMEM,
+        compiler_params=PARAMS,
+        name="gate",
+    )(normed, gate_out)
+    sums = pl.pallas_call(
+        functools.partial(triangle_kernel, grid_rows, grid_cols, rows, cols),
+        out_shape=jax.ShapeDtypeStruct((devices, side, LANES), BF16),
+        in_specs=[VMEM],
+        out_specs=VMEM,
+        compiler_params=PARAMS,
+        name="triangle",
+    )(got)
+    mine = lax.all_to_all(sums, ("row", "col"), 0, 0, tiled=True)
+    return pl.pallas_call(
+        update_kernel,
+        out_shape=jax.ShapeDtypeStruct((rows, cols, channels), BF16),
+        in_specs=[VMEM] * 5,
+        out_specs=VMEM,
+        compiler_params=PARAMS,
+        name="update",
+    )(mine, opened, norm_out_gain.reshape(1, hidden), norm_out_bias.reshape(1, hidden), proj_out)
+
+
 def solution(mesh):
+    devices = mesh.shape["row"] * mesh.shape["col"]
+
+    def shards(*arrays):
+        rows, cols, _ = arrays[0].shape
+        hidden = arrays[8].shape[0]
+        fits = (
+            hidden % devices == 0
+            and LANES % cols == 0
+            and rows * cols % LANES == 0
+            and mesh.shape["row"] % mesh.shape["col"] == 0
+            and mesh.shape["row"] // mesh.shape["col"] * rows == cols
+            and hidden // devices * (rows * cols // LANES) % 16 == 0
+        )
+        return exchanged(*arrays) if fits else gathered(*arrays)
+
     return jax.shard_map(
         shards,
         mesh=mesh,

time: 114 us -> 36.9 us (0.32)
  waiting for transfers between devices: 71 us -> 8.02 us
  between operations: 13.6 us -> 0.05 us
  other arithmetic: 7.01 us -> 0 us
  Pallas kernels: 0 us -> 4.15 us
  matrix products: 3.37 us -> 0 us
  starting transfers between devices: 0.01 us -> 2.71 us
  blocking collectives: 15.9 us -> 17.7 us
  local copies, waits for them, and re-layouts: 2.51 us -> 3.94 us
    psum x1 -> x0, waiting for transfers between devices: 71 us -> none  [broadcast(): return lax.psum(kept, axis)]
    all_to_all x0 -> x1, blocking collectives: none -> 17.7 us  [exchanged(): got = lax.all_to_all(sent, ('row', 'col'), 0, 0, tiled=True)]
    all_gather x2 -> x0, blocking collectives: 15.9 us -> none  [the longest x1 8.62 us: shards(): right_full = lax.all_gather(right_tile, 'col', axis=1, tiled=True)]
    all_to_all x0 -> x1, waiting for transfers between devices: none -> 8.02 us  [exchanged(): mine = lax.all_to_all(sums, ('row', 'col'), 0, 0, tiled=True)]
    pallas_call x0 -> x4, Pallas kernels: none -> 4.15 us  [the longest x1 1.66 us: exchanged(): pl.pallas_call(functools.partial(triangle_kernel, grid_rows, grid_cols, r...]
    reduce_sum x6 -> x0, other arithmetic: 4.11 us -> none  [the longest x2 1.51 us: token_valid(): jnp.sum(jnp.where(chain[:, None] == chain_ids[None, :], chain_lengths[Non...]
    dot_general x5 -> x0, matrix products: 3.37 us -> none  [the longest x1 1.84 us: shards(): jnp.einsum('ikh,jkh->ijh', lax.all_gather(left_tile, 'col', axis=1, tiled...]
    unnamed x12 -> x20, local copies, waits for them, and re-layouts: 0.58 us -> 3.94 us
  transfers between devices with their start and end apart: 1 -> 1, of which waited for: 1 -> 1; matrix products, arithmetic and copies ran while one was open for 1% -> 0% of each run, Pallas kernels for 0% -> 0%
where the time goes in v1:
time: 36.9 us; the launch traced here: 36.6 us
  blocking collectives  17.7 us (48%)
  waiting for transfers between devices  8.02 us (22%)
  Pallas kernels  4.15 us (11%)
  local copies, waits for them, and re-layouts  3.94 us (11%)
  starting transfers between devices  2.71 us (7%)
    all_to_all x1, blocking collectives, exchanged(): got = lax.all_to_all(sent, ('row', 'col'), 0, 0, tiled=True)  17.7 us
    all_to_all x1, waiting for transfers between devices, exchanged(): mine = lax.all_to_all(sums, ('row', 'col'), 0, 0, tiled=True)  8.02 us
    unnamed x20, local copies, waits for them, and re-layouts  3.94 us
    all_to_all x1, starting transfers between devices, exchanged(): mine = lax.all_to_all(sums, ('row', 'col'), 0, 0, tiled=True)  2.71 us
    pallas_call x1, Pallas kernels, exchanged(): pl.pallas_call(functools.partial(triangle_kernel, grid_rows, grid_cols, r...  1.66 us
    pallas_call x1, Pallas kernels, exchanged(): pl.pallas_call(functools.partial(mix_kernel, slots), out_shape=(jax.Shape...  1.2 us
    pallas_call x1, Pallas kernels, exchanged(): pl.pallas_call(update_kernel, out_shape=jax.ShapeDtypeStruct((rows, cols,...  1.11 us
  transfers between devices with their start and end apart: 1, of which 1 were waited for; matrix products, arithmetic and copies ran while one was open for 0% of the time, Pallas kernels for 0%

profile of v1, /device:TPU:0, one launch (start us, length us, event | category | flops | bytes accessed | tf_op | source)
XLA Modules:
  0.0 36.6 jit_solution(3595863557567849200)
XLA Ops:
  0.0 0.0 copy-start.5
  0.0 0.0 copy-start.6
  0.0 0.0 copy-start.7
  0.0 0.6 %copy-done.5 = s32[8]{0:T(128)S(1)} copy-done((s32[8]{0:T(128)S(1)}, s32[8]{0:T(128)}, u32[]{:S(2)}) %copy-start.5) | copy-done | bytes 56
  0.7 0.0 copy-done.6
  0.7 0.0 copy-done.7
  0.7 0.0 copy-start
  0.7 0.9 %copy-done = bf16[16,32,128]{2,1,0:T(8,128)(2,1)S(1)} copy-done((bf16[16,32,128]{2,1,0:T(8,128)(2,1)S(1)}, bf16[16,32,128]{2,1,0:T(8,128)(2,1)}, u32[]{:S(2)}) %copy-start) | copy-done | bytes 131096
  1.6 0.0 copy-start.1
  1.6 0.8 %copy-done.1 = bf16[128,256]{1,0:T(8,128)(2,1)S(1)} copy-done((bf16[128,256]{1,0:T(8,128)(2,1)S(1)}, bf16[128,256]{1,0:T(8,128)(2,1)}, u32[]{:S(2)}) %copy-start.1) | copy-done | bytes 65560
  2.4 0.0 copy-start.2
  2.4 0.8 %copy-done.2 = bf16[128,256]{1,0:T(8,128)(2,1)S(1)} copy-done((bf16[128,256]{1,0:T(8,128)(2,1)S(1)}, bf16[128,256]{1,0:T(8,128)(2,1)}, u32[]{:S(2)}) %copy-start.2) | copy-done | bytes 65560
  3.3 1.2 %mix.1 = (bf16[32,32,128]{2,1,0:T(8,128)(2,1)S(1)}, bf16[512,128]{1,0:T(8,128)(2,1)S(1)}) custom-call(s32[8]{0:T(128)S(1)} %copy-done.5, bf16[16,32,128]{2,1,0:T(8,128)(2,1)S(1)} %copy-done, f32[1,128]{1,0:T(1,128)S(1)} %bitcast.4, f32[1,128]{1,0:T(1,128)S(1)} %bitcast.5, bf16[128,256]{1,0:T(8,128)(2,1)S(1)} %copy-done.1, bf16[128,256]{1,0:T(8,128)(2,1)S(1)} %copy-done.2), custom_call_target="tpu_custom_call" | custom-call | tf_op jit(solution)/shard_map/mix/pallas_call | solution.py:279
  4.5 17.7 %all_to_all.10.got_ref = bf16[32,32,128]{2,1,0:T(8,128)(2,1)S(1)} all-to-all(bf16[32,32,128]{2,1,0:T(8,128)(2,1)S(1)} %get-tuple-element.7), channel_id=1, replica_groups=mesh['row'=8,'col'=4] {'row','col'}, dimensions={0} | all-to-all | bytes 524288 | tf_op jit(solution)/shard_map/all_to_all | solution.py:297
  22.2 1.7 %triangle.1 = bf16[32,16,128]{2,1,0:T(8,128)(2,1)} custom-call(bf16[32,32,128]{2,1,0:T(8,128)(2,1)S(1)} %all_to_all.10.got_ref), custom_call_target="tpu_custom_call" | custom-call | tf_op jit(solution)/shard_map/triangle/pallas_call | solution.py:306
  23.8 0.0 copy-start.4
  23.8 2.7 %all-to-all-start.1 = ((bf16[32,16,128]{2,1,0:T(8,128)(2,1)}), bf16[32,16,128]{2,1,0:T(8,128)(2,1)S(1)}, u32[]{:S(2)}, u32[]{:S(2)}) async-start(bf16[32,16,128]{2,1,0:T(8,128)(2,1)} %triangle.1), calls=%async_computation.1 | async-start | bytes 262144 | tf_op jit(solution)/shard_map/all_to_all | solution.py:314
  26.6 0.0 copy-done.4
  26.6 0.0 copy-start.3
  26.6 0.2 gate.1.open_ref
  26.8 8.0 %all-to-all-done.1.got_ref = bf16[32,16,128]{2,1,0:T(8,128)(2,1)S(1)} async-done(((bf16[32,16,128]{2,1,0:T(8,128)(2,1)}), bf16[32,16,128]{2,1,0:T(8,128)(2,1)S(1)}, u32[]{:S(2)}, u32[]{:S(2)}) %all-to-all-start.1) | async-done | bytes 131104 | tf_op jit(solution)/shard_map/all_to_all | solution.py:314
  34.8 0.0 copy-start.8
  34.8 0.0 copy-start.9
  34.8 0.0 copy-done.3
  34.8 0.6 %copy-done.8 = f32[128]{0:T(128)S(1)} copy-done((f32[128]{0:T(128)S(1)}, f32[128]{0:T(128)}, u32[]{:S(2)}) %copy-start.8) | copy-done | bytes 536
  35.4 0.0 copy-done.9
  35.5 1.1 %update.1 = bf16[16,32,128]{2,1,0:T(8,128)(2,1)} custom-call(bf16[32,16,128]{2,1,0:T(8,128)(2,1)S(1)} %all-to-all-done.1.got_ref, f32[512,128]{1,0:T(8,128)S(1)} %gate.1.open_ref, f32[1,128]{1,0:T(1,128)S(1)} %bitcast.6, f32[1,128]{1,0:T(1,128)S(1)} %bitcast.7, bf16[128,128]{1,0:T(8,128)(2,1)S(1)} %copy-done.3), custom_call_target="tpu_custom_call" | custom-call | tf_op jit(solution)/shard_map/update/pallas_call | solution.py:315
Async XLA Ops:
  0.0 0.7 %copy-start.5 = (s32[8]{0:T(128)S(1)}, s32[8]{0:T(128)}, u32[]{:S(2)}) copy-start(s32[8]{0:T(128)} %chain_ref.1) | copy-start | bytes 100
  0.0 0.7 %copy-start.6 = (f32[128]{0:T(128)S(1)}, f32[128]{0:T(128)}, u32[]{:S(2)}) copy-start(f32[128]{0:T(128)} %param.12) | copy-start | bytes 1540
  0.0 0.7 %copy-start.7 = (f32[128]{0:T(128)S(1)}, f32[128]{0:T(128)}, u32[]{:S(2)}) copy-start(f32[128]{0:T(128)} %param.13) | copy-start | bytes 1540
  0.7 0.9 %copy-start = (bf16[16,32,128]{2,1,0:T(8,128)(2,1)S(1)}, bf16[16,32,128]{2,1,0:T(8,128)(2,1)}, u32[]{:S(2)}) copy-start(bf16[16,32,128]{2,1,0:T(8,128)(2,1)} %pair_ref.1) | copy-start | bytes 393220
  1.6 0.8 %copy-start.1 = (bf16[128,256]{1,0:T(8,128)(2,1)S(1)}, bf16[128,256]{1,0:T(8,128)(2,1)}, u32[]{:S(2)}) copy-start(bf16[128,256]{1,0:T(8,128)(2,1)} %proj_ref.2) | copy-start | bytes 196612
  2.4 0.8 %copy-start.2 = (bf16[128,256]{1,0:T(8,128)(2,1)S(1)}, bf16[128,256]{1,0:T(8,128)(2,1)}, u32[]{:S(2)}) copy-start(bf16[128,256]{1,0:T(8,128)(2,1)} %gate_ref.2) | copy-start | bytes 196612
  23.8 2.7 %copy-start.4 = (bf16[128,128]{1,0:T(8,128)(2,1)S(1)}, bf16[128,128]{1,0:T(8,128)(2,1)}, u32[]{:S(2)}) copy-start(bf16[128,128]{1,0:T(8,128)(2,1)} %gate_ref.3) | copy-start | bytes 98308
  23.8 10.9 %all-to-all-start.1 = ((bf16[32,16,128]{2,1,0:T(8,128)(2,1)}), bf16[32,16,128]{2,1,0:T(8,128)(2,1)S(1)}, u32[]{:S(2)}, u32[]{:S(2)}) async-start(bf16[32,16,128]{2,1,0:T(8,128)(2,1)} %triangle.1), calls=%async_computation.1 | async-start | bytes 262144 | tf_op jit(solution)/shard_map/all_to_all | solution.py:314
  26.6 8.2 %copy-start.3 = (bf16[128,128]{1,0:T(8,128)(2,1)S(1)}, bf16[128,128]{1,0:T(8,128)(2,1)}, u32[]{:S(2)}) copy-start(bf16[128,128]{1,0:T(8,128)(2,1)} %proj_ref.3) | copy-start | bytes 98308
  34.8 0.7 %copy-start.8 = (f32[128]{0:T(128)S(1)}, f32[128]{0:T(128)}, u32[]{:S(2)}) copy-start(f32[128]{0:T(128)} %param.16) | copy-start | bytes 1540
  34.8 0.7 %copy-start.9 = (f32[128]{0:T(128)S(1)}, f32[128]{0:T(128)}, u32[]{:S(2)}) copy-start(f32[128]{0:T(128)} %param.17) | copy-start | bytes 1540

commit v2 on v1

--- a/solution.py
+++ b/solution.py
@@ -103,15 +103,47 @@
     return lax.dot_general(a, b, (((a_dim,), (b_dim,)), ((), ())), preferred_element_type=F32)
 
 
+def fetch(sources, targets, sems):
+    copies = [
+        pltpu.make_async_copy(source, target, sems.at[n])
+        for n, (source, target) in enumerate(zip(sources, targets))
+    ]
+    for copy in copies:
+        copy.start()
+    return copies
+
+
 def mix_kernel(
-    slots, chain_ref, pair_ref, gain_ref, bias_ref, proj_ref, gate_ref, sent_ref, normed_ref
+    slots,
+    chain_hbm,
+    pair_hbm,
+    gain_hbm,
+    bias_hbm,
+    proj_hbm,
+    gate_hbm,
+    sent_ref,
+    normed_ref,
+    chain_ref,
+    pair_ref,
+    gain_ref,
+    bias_ref,
+    proj_ref,
+    gate_ref,
+    sems,
 ):
+    copies = fetch(
+        (pair_hbm, gain_hbm, bias_hbm, chain_hbm, proj_hbm, gate_hbm),
+        (pair_ref, gain_ref, bias_ref, chain_ref, proj_ref, gate_ref),
+        sems,
+    )
     rows, cols, channels = pair_ref.shape
     hidden = proj_ref.shape[1] // 2
     cells = rows * cols
     groups = cells // LANES
     chunks = sent_ref.shape[0]
     own = hidden // chunks
+    for copy in copies:
+        copy.wait()
     flat = pair_ref[...].reshape(cells, channels).astype(F32)
     normed = layer_norm(flat, gain_ref[...], bias_ref[...]).astype(BF16)
     normed_ref[...] = normed
@@ -124,7 +156,7 @@
             length = jnp.where(token // slots == chain, chain_ref[chain], length)
         return token % slots < length
 
-    row_ok = valid(lax.axis_index("row") * rows + cell // cols)
+    row_ok = valid(lax.axis_index(("high", "low")) * rows + cell // cols)
     col_ok = valid(lax.axis_index("col") * cols + cell % cols)
     mask = jnp.where(row_ok & col_ok, 1.0, 0.0)
 
@@ -152,18 +184,22 @@
             ] = moved.reshape(count, own * groups, LANES)
 
 
-def triangle_kernel(grid_rows, grid_cols, rows, cols, got_ref, sent_ref):
+def triangle_kernel(split, grid_cols, rows, cols, got_ref, sent_ref):
+    grid_rows = split[0] * split[1]
     groups = rows * cols // LANES
     inner = LANES // cols
     own = got_ref.shape[1] // (2 * groups)
     side = own * groups
-    got = got_ref[...].reshape(grid_rows, grid_cols, 2 * side, LANES)
+    got = got_ref[...].reshape(grid_cols, split[1], split[0], 2 * side, LANES)
     high = grid_rows * side
     ratio = grid_rows // grid_cols
     quarter = ratio * side
 
     def block(column, which):
-        return got[:, column, which * side : (which + 1) * side].reshape(high, LANES)
+        part = got[column, :, :, which * side : (which + 1) * side]
+        return jnp.concatenate(
+            [part[y, z] for z in range(split[0]) for y in range(split[1])], axis=0
+        )
 
     left = jnp.concatenate([block(c, 0) for c in range(grid_cols)], axis=1)
     right = jnp.concatenate([block(c, 1) for c in range(grid_cols)], axis=0)
@@ -219,11 +255,35 @@
     moved = dot(kept, order).astype(BF16).reshape(grid_cols, grid_rows, side, LANES)
     for c in range(grid_cols):
         for r in range(grid_rows):
-            sent_ref[r * grid_cols + c] = moved[c, r]
-
-
-def gate_kernel(normed_ref, gate_ref, out_ref):
-    out_ref[...] = jax.nn.sigmoid(dot(normed_ref[...], gate_ref[...]))
+            z, y = r // split[1], r % split[1]
+            sent_ref[(c * split[1] + y) * split[0] + z] = moved[c, r]
+
+
+def gate_kernel(
+    normed_ref,
+    gate_hbm,
+    gain_hbm,
+    bias_hbm,
+    proj_hbm,
+    open_ref,
+    gain_out,
+    bias_out,
+    proj_out,
+    gate_ref,
+    gain_ref,
+    bias_ref,
+    sems,
+):
+    copies = fetch(
+        (gate_hbm, gain_hbm, bias_hbm, proj_hbm), (gate_ref, gain_ref, bias_ref, proj_out), sems
+    )
+    for copy in copies:
+        copy.wait()
+    open_ref[...] = jax.nn.sigmoid(dot(normed_ref[...], gate_ref[...]))
+    a, b = iota2(gain_out.shape)
+    for source, target in ((gain_ref, gain_out), (bias_ref, bias_out)):
+        column = jnp.sum(jnp.where(a == b, source[...], 0.0), axis=1, keepdims=True)
+        target[...] = jnp.broadcast_to(column, target.shape)
 
 
 def update_kernel(got_ref, open_ref, gain_ref, bias_ref, proj_ref, out_ref):
@@ -238,9 +298,7 @@
     pieces = [
         dot(order, got[part * LANES : (part + 1) * LANES]) for part in range(hidden // block)
     ]
-    a, b = iota2((hidden, hidden))
-    gain = jnp.sum(jnp.where(a == b, gain_ref[...], 0.0), axis=1, keepdims=True)
-    bias = jnp.sum(jnp.where(a == b, bias_ref[...], 0.0), axis=1, keepdims=True)
+    gain, bias = gain_ref[...], bias_ref[...]
     for g in range(groups):
         values = jnp.concatenate([piece[g * block : (g + 1) * block] for piece in pieces], axis=0)
         mean = jnp.mean(values, axis=0, keepdims=True)
@@ -253,11 +311,13 @@
 
 
 VMEM = pl.BlockSpec(memory_space=pltpu.VMEM)
-SMEM = pl.BlockSpec(memory_space=pltpu.SMEM)
+ANY = pl.BlockSpec(memory_space=pl.ANY)
 PARAMS = pltpu.CompilerParams(vmem_limit_bytes=40 * 1024 * 1024)
 
 
 def exchanged(
+    split,
+    grid_cols,
     pair,
     chain_lengths,
     norm_in_gain,
@@ -271,7 +331,7 @@
 ):
     rows, cols, channels = pair.shape
     hidden = proj_out.shape[0]
-    grid_rows, grid_cols = lax.axis_size("row"), lax.axis_size("col")
+    grid_rows = split[0] * split[1]
     devices = grid_rows * grid_cols
     groups = rows * cols // LANES
     side = hidden // devices * groups
@@ -282,8 +342,17 @@
             jax.ShapeDtypeStruct((devices, 2 * side, LANES), BF16),
             jax.ShapeDtypeStruct((rows * cols, channels), BF16),
         ),
-        in_specs=[SMEM] + [VMEM] * 5,
+        in_specs=[ANY] * 6,
         out_specs=(VMEM, VMEM),
+        scratch_shapes=[
+            pltpu.SMEM(chain_lengths.shape, jnp.int32),
+            pltpu.VMEM(pair.shape, BF16),
+            pltpu.VMEM((1, channels), F32),
+            pltpu.VMEM((1, channels), F32),
+            pltpu.VMEM(proj_in.shape, BF16),
+            pltpu.VMEM(gate_in.shape, BF16),
+            pltpu.SemaphoreType.DMA((6,)),
+        ],
         compiler_params=PARAMS,
         name="mix",
     )(
@@ -294,24 +363,36 @@
         proj_in,
         gate_in,
     )
-    got = lax.all_to_all(sent, ("row", "col"), 0, 0, tiled=True)
-    opened = pl.pallas_call(
+    order = ("col", "low", "high")
+    got = lax.all_to_all(sent, order, 0, 0, tiled=True)
+    opened, gain, bias, proj = pl.pallas_call(
         gate_kernel,
-        out_shape=jax.ShapeDtypeStruct((rows * cols, channels), F32),
-        in_specs=[VMEM] * 2,
-        out_specs=VMEM,
+        out_shape=(
+            jax.ShapeDtypeStruct((rows * cols, channels), F32),
+            jax.ShapeDtypeStruct((hidden, LANES), F32),
+            jax.ShapeDtypeStruct((hidden, LANES), F32),
+            jax.ShapeDtypeStruct(proj_out.shape, BF16),
+        ),
+        in_specs=[VMEM] + [ANY] * 4,
+        out_specs=[VMEM] * 4,
+        scratch_shapes=[
+            pltpu.VMEM(gate_out.shape, BF16),
+            pltpu.VMEM((1, hidden), F32),
+            pltpu.VMEM((1, hidden), F32),
+            pltpu.SemaphoreType.DMA((4,)),
+        ],
         compiler_params=PARAMS,
         name="gate",
-    )(normed, gate_out)
+    )(normed, gate_out, norm_out_gain.reshape(1, hidden), norm_out_bias.reshape(1, hidden), proj_out)
     sums = pl.pallas_call(
-        functools.partial(triangle_kernel, grid_rows, grid_cols, rows, cols),
+        functools.partial(triangle_kernel, split, grid_cols, rows, cols),
         out_shape=jax.ShapeDtypeStruct((devices, side, LANES), BF16),
         in_specs=[VMEM],
         out_specs=VMEM,
         compiler_params=PARAMS,
         name="triangle",
     )(got)
-    mine = lax.all_to_all(sums, ("row", "col"), 0, 0, tiled=True)
+    mine = lax.all_to_all(sums, order, 0, 0, tiled=True)
     return pl.pallas_call(
         update_kernel,
         out_shape=jax.ShapeDtypeStruct((rows, cols, channels), BF16),
@@ -319,29 +400,45 @@
         out_specs=VMEM,
         compiler_params=PARAMS,
         name="update",
-    )(mine, opened, norm_out_gain.reshape(1, hidden), norm_out_bias.reshape(1, hidden), proj_out)
+    )(mine, opened, gain, bias, proj)
 
 
 def solution(mesh):
-    devices = mesh.shape["row"] * mesh.shape["col"]
-
-    def shards(*arrays):
-        rows, cols, _ = arrays[0].shape
-        hidden = arrays[8].shape[0]
-        fits = (
+    grid_rows, grid_cols = mesh.shape["row"], mesh.shape["col"]
+    split = (grid_rows // 2, 2)
+    fine = jax.sharding.Mesh(
+        mesh.devices.reshape(split + (grid_cols,)), ("high", "low", "col")
+    )
+
+    def fits(rows, cols, hidden):
+        devices = grid_rows * grid_cols
+        return (
             hidden % devices == 0
+            and hidden == LANES
             and LANES % cols == 0
             and rows * cols % LANES == 0
-            and mesh.shape["row"] % mesh.shape["col"] == 0
-            and mesh.shape["row"] // mesh.shape["col"] * rows == cols
+            and grid_rows % grid_cols == 0
+            and grid_rows // grid_cols * rows == cols
             and hidden // devices * (rows * cols // LANES) % 16 == 0
         )
-        return exchanged(*arrays) if fits else gathered(*arrays)
-
-    return jax.shard_map(
-        shards,
-        mesh=mesh,
-        in_specs=(P("row", "col", None), P(), P(), P(), P(), P(), P(), P(), P(), P()),
-        out_specs=P("row", "col", None),
-        check_vma=False,
-    )
+
+    def call(*arrays):
+        tokens, _, _ = arrays[0].shape
+        hidden = arrays[8].shape[0]
+        if fits(tokens // grid_rows, tokens // grid_cols, hidden):
+            return jax.shard_map(
+                functools.partial(exchanged, split, grid_cols),
+                mesh=fine,
+                in_specs=(P(("high", "low"), "col", None),) + (P(),) * 9,
+                out_specs=P(("high", "low"), "col", None),
+                check_vma=False,
+            )(*arrays)
+        return jax.shard_map(
+            gathered,
+            mesh=mesh,
+            in_specs=(P("row", "col", None),) + (P(),) * 9,
+            out_specs=P("row", "col", None),
+            check_vma=False,
+        )(*arrays)
+
+    return call

time: 36.9 us -> 36.1 us (0.978)
  waiting for transfers between devices: 8.02 us -> 6.78 us
    all_to_all x1, waiting for transfers between devices: 8.02 us -> 6.78 us  [exchanged(): mine = lax.all_to_all(sums, order, 0, 0, tiled=True)]
  transfers between devices with their start and end apart: 1 -> 1, of which waited for: 1 -> 1; matrix products, arithmetic and copies ran while one was open for 0% -> 0% of each run, Pallas kernels for 0% -> 1%
where the time goes in v2:
time: 36.1 us; the launch traced here: 35.8 us
  blocking collectives  17.9 us (50%)
  waiting for transfers between devices  6.78 us (19%)
  Pallas kernels  4.43 us (12%)
  local copies, waits for them, and re-layouts  3.91 us (11%)
  starting transfers between devices  2.71 us (8%)
    all_to_all x1, blocking collectives, exchanged(): got = lax.all_to_all(sent, order, 0, 0, tiled=True)  17.9 us
    all_to_all x1, waiting for transfers between devices, exchanged(): mine = lax.all_to_all(sums, order, 0, 0, tiled=True)  6.78 us
    unnamed x20, local copies, waits for them, and re-layouts  3.91 us
    all_to_all x1, starting transfers between devices, exchanged(): mine = lax.all_to_all(sums, order, 0, 0, tiled=True)  2.71 us
    pallas_call x1, Pallas kernels, exchanged(): pl.pallas_call(functools.partial(triangle_kernel, split, grid_cols, rows,...  1.66 us
    pallas_call x1, Pallas kernels, exchanged(): pl.pallas_call(functools.partial(mix_kernel, slots), out_shape=(jax.Shape...  1.4 us
    pallas_call x1, Pallas kernels, exchanged(): pl.pallas_call(update_kernel, out_shape=jax.ShapeDtypeStruct((rows, cols,...  1.1 us
  transfers between devices with their start and end apart: 1, of which 1 were waited for; matrix products, arithmetic and copies ran while one was open for 0% of the time, Pallas kernels for 1%

profile of v2, /device:TPU:0, one launch (start us, length us, event | category | flops | bytes accessed | tf_op | source)
XLA Modules:
  0.0 35.8 jit_solution(3604612028039709454)
XLA Ops:
  0.0 0.0 copy-start.5
  0.0 0.0 copy-start.6
  0.0 0.0 copy-start.7
  0.0 0.6 %copy-done.5 = s32[8]{0:T(128)S(1)} copy-done((s32[8]{0:T(128)S(1)}, s32[8]{0:T(128)}, u32[]{:S(2)}) %copy-start.5) | copy-done | bytes 56
  0.7 0.0 copy-done.6
  0.7 0.0 copy-done.7
  0.7 0.0 copy-start
  0.7 0.9 %copy-done = bf16[16,32,128]{2,1,0:T(8,128)(2,1)S(1)} copy-done((bf16[16,32,128]{2,1,0:T(8,128)(2,1)S(1)}, bf16[16,32,128]{2,1,0:T(8,128)(2,1)}, u32[]{:S(2)}) %copy-start) | copy-done | bytes 131096
  1.6 0.0 copy-start.1
  1.6 0.8 %copy-done.1 = bf16[128,256]{1,0:T(8,128)(2,1)S(1)} copy-done((bf16[128,256]{1,0:T(8,128)(2,1)S(1)}, bf16[128,256]{1,0:T(8,128)(2,1)}, u32[]{:S(2)}) %copy-start.1) | copy-done | bytes 65560
  2.4 0.0 copy-start.2
  2.4 0.8 %copy-done.2 = bf16[128,256]{1,0:T(8,128)(2,1)S(1)} copy-done((bf16[128,256]{1,0:T(8,128)(2,1)S(1)}, bf16[128,256]{1,0:T(8,128)(2,1)}, u32[]{:S(2)}) %copy-start.2) | copy-done | bytes 65560
  3.3 1.4 %mix.1 = (bf16[32,32,128]{2,1,0:T(8,128)(2,1)S(1)}, bf16[512,128]{1,0:T(8,128)(2,1)S(1)}) custom-call(s32[8]{0:T(128)S(1)} %copy-done.5, bf16[16,32,128]{2,1,0:T(8,128)(2,1)S(1)} %copy-done, f32[1,128]{1,0:T(1,128)S(1)} %bitcast.4, f32[1,128]{1,0:T(1,128)S(1)} %bitcast.5, bf16[128,256]{1,0:T(8,128)(2,1)S(1)} %copy-done.1, bf16[128,256]{1,0:T(8,128)(2,1)S(1)} %copy-done.2), custom_call_target="tpu_custom_call" | custom-call | tf_op jit(solution)/shard_map/mix/pallas_call | solution.py:339
  4.7 17.9 %all_to_all.10.got_ref = bf16[32,32,128]{2,1,0:T(8,128)(2,1)S(1)} all-to-all(bf16[32,32,128]{2,1,0:T(8,128)(2,1)S(1)} %get-tuple-element.11), channel_id=1, replica_groups=mesh['high'=4,'low'=2,'col'=4] {'col','low','high'}, dimensions={0} | all-to-all | bytes 524288 | tf_op jit(solution)/shard_map/all_to_all | solution.py:367
  22.6 1.7 %triangle.1 = bf16[32,16,128]{2,1,0:T(8,128)(2,1)} custom-call(bf16[32,32,128]{2,1,0:T(8,128)(2,1)S(1)} %all_to_all.10.got_ref), custom_call_target="tpu_custom_call" | custom-call | tf_op jit(solution)/shard_map/triangle/pallas_call | solution.py:387
  24.2 0.0 copy-start.3
  24.2 0.0 copy-start.4
  24.2 2.7 %all-to-all-start.1 = ((bf16[32,16,128]{2,1,0:T(8,128)(2,1)}), bf16[32,16,128]{2,1,0:T(8,128)(2,1)S(1)}, u32[]{:S(2)}, u32[]{:S(2)}) async-start(bf16[32,16,128]{2,1,0:T(8,128)(2,1)} %triangle.1), calls=%async_computation.1 | async-start | bytes 262144 | tf_op jit(solution)/shard_map/all_to_all | solution.py:395
  26.9 0.0 copy-start.8
  26.9 0.0 copy-start.9
  27.0 0.0 copy-done.3
  27.0 0.0 copy-done.4
  27.0 0.6 %copy-done.8 = f32[128]{0:T(128)S(1)} copy-done((f32[128]{0:T(128)S(1)}, f32[128]{0:T(128)}, u32[]{:S(2)}) %copy-start.8) | copy-done | bytes 536
  27.6 0.0 copy-done.9
  27.6 0.3 gate.1
  27.9 6.8 %all-to-all-done.1.got_ref = bf16[32,16,128]{2,1,0:T(8,128)(2,1)S(1)} async-done(((bf16[32,16,128]{2,1,0:T(8,128)(2,1)}), bf16[32,16,128]{2,1,0:T(8,128)(2,1)S(1)}, u32[]{:S(2)}, u32[]{:S(2)}) %all-to-all-start.1) | async-done | bytes 131104 | tf_op jit(solution)/shard_map/all_to_all | solution.py:395
  34.7 1.1 %update.1 = bf16[16,32,128]{2,1,0:T(8,128)(2,1)} custom-call(bf16[32,16,128]{2,1,0:T(8,128)(2,1)S(1)} %all-to-all-done.1.got_ref, f32[512,128]{1,0:T(8,128)S(1)} %get-tuple-element.13.open_ref, f32[128,128]{1,0:T(8,128)S(1)} %get-tuple-element.14.gain_ref, f32[128,128]{1,0:T(8,128)S(1)} %get-tuple-element.15.bias_ref, ...), custom_call_target="tpu_custom_call" | custom-call | tf_op jit(solution)/shard_map/update/pallas_call | solution.py:396
Async XLA Ops:
  0.0 0.7 %copy-start.5 = (s32[8]{0:T(128)S(1)}, s32[8]{0:T(128)}, u32[]{:S(2)}) copy-start(s32[8]{0:T(128)} %chain_hbm.1) | copy-start | bytes 100
  0.0 0.7 %copy-start.6 = (f32[128]{0:T(128)S(1)}, f32[128]{0:T(128)}, u32[]{:S(2)}) copy-start(f32[128]{0:T(128)} %param.12) | copy-start | bytes 1540
  0.0 0.7 %copy-start.7 = (f32[128]{0:T(128)S(1)}, f32[128]{0:T(128)}, u32[]{:S(2)}) copy-start(f32[128]{0:T(128)} %param.13) | copy-start | bytes 1540
  0.7 0.9 %copy-start = (bf16[16,32,128]{2,1,0:T(8,128)(2,1)S(1)}, bf16[16,32,128]{2,1,0:T(8,128)(2,1)}, u32[]{:S(2)}) copy-start(bf16[16,32,128]{2,1,0:T(8,128)(2,1)} %pair_hbm.1) | copy-start | bytes 393220
  1.6 0.8 %copy-start.1 = (bf16[128,256]{1,0:T(8,128)(2,1)S(1)}, bf16[128,256]{1,0:T(8,128)(2,1)}, u32[]{:S(2)}) copy-start(bf16[128,256]{1,0:T(8,128)(2,1)} %proj_hbm.2) | copy-start | bytes 196612
  2.4 0.8 %copy-start.2 = (bf16[128,256]{1,0:T(8,128)(2,1)S(1)}, bf16[128,256]{1,0:T(8,128)(2,1)}, u32[]{:S(2)}) copy-start(bf16[128,256]{1,0:T(8,128)(2,1)} %gate_hbm.2) | copy-start | bytes 196612
  24.2 2.7 %copy-start.3 = (bf16[128,128]{1,0:T(8,128)(2,1)S(1)}, bf16[128,128]{1,0:T(8,128)(2,1)}, u32[]{:S(2)}) copy-start(bf16[128,128]{1,0:T(8,128)(2,1)} %gate_hbm.3) | copy-start | bytes 98308
  24.2 2.8 %copy-start.4 = (bf16[128,128]{1,0:T(8,128)(2,1)S(1)}, bf16[128,128]{1,0:T(8,128)(2,1)}, u32[]{:S(2)}) copy-start(bf16[128,128]{1,0:T(8,128)(2,1)} %proj_hbm.3) | copy-start | bytes 98308
  24.2 10.5 %all-to-all-start.1 = ((bf16[32,16,128]{2,1,0:T(8,128)(2,1)}), bf16[32,16,128]{2,1,0:T(8,128)(2,1)S(1)}, u32[]{:S(2)}, u32[]{:S(2)}) async-start(bf16[32,16,128]{2,1,0:T(8,128)(2,1)} %triangle.1), calls=%async_computation.1 | async-start | bytes 262144 | tf_op jit(solution)/shard_map/all_to_all | solution.py:395
  26.9 0.7 %copy-start.8 = (f32[128]{0:T(128)S(1)}, f32[128]{0:T(128)}, u32[]{:S(2)}) copy-start(f32[128]{0:T(128)} %param.16) | copy-start | bytes 1540
  26.9 0.7 %copy-start.9 = (f32[128]{0:T(128)S(1)}, f32[128]{0:T(128)}, u32[]{:S(2)}) copy-start(f32[128]{0:T(128)} %param.17) | copy-start | bytes 1540

commit v3 on v2

--- a/solution.py
+++ b/solution.py
@@ -184,79 +184,108 @@
             ] = moved.reshape(count, own * groups, LANES)
 
 
-def triangle_kernel(split, grid_cols, rows, cols, got_ref, sent_ref):
-    grid_rows = split[0] * split[1]
+def pick_kernel(grid_cols, got_ref, right_ref):
+    side = got_ref.shape[1] // 2
+    blocks = side // 16
+    lows = got_ref.shape[0] // grid_cols
+    for q in range(blocks):
+        for y in range(lows):
+            for c in range(grid_cols):
+                right_ref[(q * lows + y) * 16 : (q * lows + y + 1) * 16, c * LANES : (c + 1) * LANES] = (
+                    got_ref[y * grid_cols + c, side + q * 16 : side + (q + 1) * 16]
+                )
+
+
+def triangle_kernel(planes, grid_cols, rows, cols, got_ref, *refs):
+    own_ref, below, above = refs[0], refs[1:planes], refs[planes : 2 * planes - 1]
+    sent_ref, right_ref = refs[2 * planes - 1 :]
+    height = own_ref.shape[0]
+    place = lax.axis_index("high")
+    for p in range(planes):
+        for here in range(planes):
+            source = own_ref if here == p else below[here - p - 1] if here > p else above[p - here - 1]
+
+            @pl.when(place == here)
+            def _(p=p, source=source):
+                right_ref[p * height : (p + 1) * height] = source[...]
+
     groups = rows * cols // LANES
     inner = LANES // cols
-    own = got_ref.shape[1] // (2 * groups)
-    side = own * groups
-    got = got_ref[...].reshape(grid_cols, split[1], split[0], 2 * side, LANES)
-    high = grid_rows * side
-    ratio = grid_rows // grid_cols
-    quarter = ratio * side
-
-    def block(column, which):
-        part = got[column, :, :, which * side : (which + 1) * side]
-        return jnp.concatenate(
-            [part[y, z] for z in range(split[0]) for y in range(split[1])], axis=0
+    side = got_ref.shape[1] // 2
+    blocks = side // 16
+    some = 16 // groups
+    lows = got_ref.shape[0] // grid_cols
+    here = lows * 16
+    high = planes * here
+    lane = lax.broadcasted_iota(jnp.int32, (1, grid_cols * LANES), 1)
+    own = [one_hot(lane % LANES // cols == i) for i in range(inner)]
+    a, b = iota2((here, high))
+    same = jnp.where(a // groups % some == b // groups % some, 1.0, 0.0)
+    kept = []
+    for q in range(blocks):
+        left = jnp.concatenate(
+            [
+                jnp.concatenate(
+                    [
+                        got_ref[y * grid_cols + c, q * 16 : (q + 1) * 16]
+                        for c in range(grid_cols)
+                    ],
+                    axis=1,
+                )
+                for y in range(lows)
+            ],
+            axis=0,
         )
-
-    left = jnp.concatenate([block(c, 0) for c in range(grid_cols)], axis=1)
-    right = jnp.concatenate([block(c, 1) for c in range(grid_cols)], axis=0)
-
-    lane = lax.broadcasted_iota(jnp.int32, (1, grid_cols * LANES), 1)
-    left_by = jnp.concatenate(
-        [left * one_hot(lane % LANES // cols == i) for i in range(inner)], axis=0
-    )
-    source, out = iota2((LANES, inner * LANES))
-    spread = one_hot((source // cols == out // LANES) & (source % cols == out % cols))
-    wide = dot(right, spread).astype(BF16)
-    right_by = jnp.concatenate(
-        [
-            jnp.concatenate(
-                [
-                    wide[
-                        c * high + d * quarter : c * high + (d + 1) * quarter,
-                        j * LANES : (j + 1) * LANES,
-                    ]
-                    for c in range(grid_cols)
-                ],
-                axis=1,
+        left_by = jnp.concatenate([left * mask for mask in own], axis=0)
+        right = jnp.concatenate(
+            [
+                right_ref[(p * blocks + q) * here : (p * blocks + q + 1) * here]
+                for p in range(planes)
+            ],
+            axis=0,
+        ).astype(F32)
+        turned = []
+        for turn in range(inner):
+            turned.append(
+                jnp.concatenate(
+                    [
+                        pltpu.roll(right[:, c * LANES : (c + 1) * LANES], turn * cols, 1)
+                        if turn
+                        else right[:, c * LANES : (c + 1) * LANES]
+                        for c in range(grid_cols)
+                    ],
+                    axis=1,
+                ).astype(BF16)
             )
-            for d in range(grid_cols)
-            for j in range(inner)
-        ],
-        axis=0,
-    )
-    product = dot(left_by, right_by, 1, 1)
-
-    width = inner * quarter
-    a, b = iota2((high, width))
-    same = jnp.where(a // groups % own == b // groups % own, 1.0, 0.0)
-    kept = jnp.concatenate(
-        [
-            jnp.concatenate(
-                [
-                    (product[i * high : (i + 1) * high, d * width : (d + 1) * width] * same).astype(
-                        BF16
-                    )
-                    for i in range(inner)
-                ],
-                axis=1,
+        product = dot(left_by, jnp.concatenate(turned, axis=0), 1, 1)
+        for d in range(grid_cols):
+            kept.append(
+                jnp.concatenate(
+                    [
+                        (
+                            product[
+                                i * here : (i + 1) * here,
+                                t * high + d * here : t * high + (d + 1) * here,
+                            ]
+                            * same[:, :here]
+                        ).astype(BF16)
+                        for i in range(inner)
+                        for t in range(inner)
+                    ],
+                    axis=1,
+                )
             )
-            for d in range(grid_cols)
-        ],
-        axis=0,
-    )
-    source, out = iota2((inner * width, LANES))
-    at = source % width
-    token = at % quarter // side * rows + at % groups * inner + at // quarter
-    order = one_hot((source // width == out // cols) & (token == out % cols))
-    moved = dot(kept, order).astype(BF16).reshape(grid_cols, grid_rows, side, LANES)
-    for c in range(grid_cols):
-        for r in range(grid_rows):
-            z, y = r // split[1], r % split[1]
-            sent_ref[(c * split[1] + y) * split[0] + z] = moved[c, r]
+    source, out = iota2((inner * inner * here, LANES))
+    at = source % here
+    i, turn = source // (inner * here), source // here % inner
+    token = at // 16 * rows + at % groups * inner + (i + inner - turn) % inner
+    order = one_hot((i == out // cols) & (token == out % cols))
+    moved = dot(jnp.concatenate(kept, axis=0), order).astype(BF16)
+    for q in range(blocks):
+        for d in range(grid_cols):
+            for y in range(lows):
+                at = (q * grid_cols + d) * here + y * 16
+                sent_ref[y * grid_cols + d, q * 16 : (q + 1) * 16] = moved[at : at + 16]
 
 
 def gate_kernel(
@@ -311,8 +340,9 @@
 
 
 VMEM = pl.BlockSpec(memory_space=pltpu.VMEM)
-ANY = pl.BlockSpec(memory_space=pl.ANY)
-PARAMS = pltpu.CompilerParams(vmem_limit_bytes=40 * 1024 * 1024)
+HBM = pl.BlockSpec(memory_space=pltpu.HBM)
+PARAMS = pltpu.CompilerParams(vmem_limit_bytes=32 * 1024 * 1024)
+FETCHING = pltpu.CompilerParams(vmem_limit_bytes=60 * 1024 * 1024)
 
 
 def exchanged(
@@ -332,7 +362,8 @@
     rows, cols, channels = pair.shape
     hidden = proj_out.shape[0]
     grid_rows = split[0] * split[1]
-    devices = grid_rows * grid_cols
+    planes, lows = split
+    devices = lows * grid_cols
     groups = rows * cols // LANES
     side = hidden // devices * groups
     slots = rows * grid_rows // chain_lengths.shape[0]
@@ -342,7 +373,7 @@
             jax.ShapeDtypeStruct((devices, 2 * side, LANES), BF16),
             jax.ShapeDtypeStruct((rows * cols, channels), BF16),
         ),
-        in_specs=[ANY] * 6,
+        in_specs=[HBM] * 6,
         out_specs=(VMEM, VMEM),
         scratch_shapes=[
             pltpu.SMEM(chain_lengths.shape, jnp.int32),
@@ -353,7 +384,7 @@
             pltpu.VMEM(gate_in.shape, BF16),
             pltpu.SemaphoreType.DMA((6,)),
         ],
-        compiler_params=PARAMS,
+        compiler_params=FETCHING,
         name="mix",
     )(
         chain_lengths,
@@ -363,8 +394,24 @@
         proj_in,
         gate_in,
     )
-    order = ("col", "low", "high")
+    order = ("low", "col")
     got = lax.all_to_all(sent, order, 0, 0, tiled=True)
+    right = pl.pallas_call(
+        functools.partial(pick_kernel, grid_cols),
+        out_shape=jax.ShapeDtypeStruct((side * lows, grid_cols * LANES), BF16),
+        in_specs=[VMEM],
+        out_specs=VMEM,
+        compiler_params=PARAMS,
+        name="pick",
+    )(got)
+    below, above = [right], [right]
+    for step in range(1, planes):
+        below.append(
+            lax.ppermute(below[-1], "high", [(p, p + 1) for p in range(step - 1, planes - 1)])
+        )
+        above.append(
+            lax.ppermute(above[-1], "high", [(p, p - 1) for p in range(1, planes - step + 1)])
+        )
     opened, gain, bias, proj = pl.pallas_call(
         gate_kernel,
         out_shape=(
@@ -373,7 +420,7 @@
             jax.ShapeDtypeStruct((hidden, LANES), F32),
             jax.ShapeDtypeStruct(proj_out.shape, BF16),
         ),
-        in_specs=[VMEM] + [ANY] * 4,
+        in_specs=[VMEM] + [HBM] * 4,
         out_specs=[VMEM] * 4,
         scratch_shapes=[
             pltpu.VMEM(gate_out.shape, BF16),
@@ -381,17 +428,18 @@
             pltpu.VMEM((1, hidden), F32),
             pltpu.SemaphoreType.DMA((4,)),
         ],
-        compiler_params=PARAMS,
+        compiler_params=FETCHING,
         name="gate",
     )(normed, gate_out, norm_out_gain.reshape(1, hidden), norm_out_bias.reshape(1, hidden), proj_out)
     sums = pl.pallas_call(
-        functools.partial(triangle_kernel, split, grid_cols, rows, cols),
+        functools.partial(triangle_kernel, planes, grid_cols, rows, cols),
         out_shape=jax.ShapeDtypeStruct((devices, side, LANES), BF16),
-        in_specs=[VMEM],
+        in_specs=[VMEM] * (2 * planes),
         out_specs=VMEM,
+        scratch_shapes=[pltpu.VMEM((planes * side * lows, grid_cols * LANES), BF16)],
         compiler_params=PARAMS,
         name="triangle",
-    )(got)
+    )(got, *below, *above[1:])
     mine = lax.all_to_all(sums, order, 0, 0, tiled=True)
     return pl.pallas_call(
         update_kernel,
@@ -411,14 +459,15 @@
     )
 
     def fits(rows, cols, hidden):
-        devices = grid_rows * grid_cols
+        devices = split[1] * grid_cols
         return (
             hidden % devices == 0
             and hidden == LANES
             and LANES % cols == 0
             and rows * cols % LANES == 0
-            and grid_rows % grid_cols == 0
-            and grid_rows // grid_cols * rows == cols
+            and split[0] == grid_cols
+            and split[1] * rows == cols
+            and 16 % (rows * cols // LANES) == 0
             and hidden // devices * (rows * cols // LANES) % 16 == 0
         )
 

time: 36.1 us -> 52.3 us (1.45)
  the two profiles are of different devices: /device:TPU:0 before, /device:TPU:24 now
where the time goes in v3:
time: 52.3 us; the launch traced here: 51.6 us
  waiting for transfers between devices  18.2 us (35%)
  starting transfers between devices  10.9 us (21%)
  blocking collectives  10.7 us (20%)
  Pallas kernels  8.43 us (16%)
  local copies, waits for them, and re-layouts  3.39 us (6%)
    ppermute x3, waiting for transfers between devices, exchanged(): lax.ppermute(below[-1], 'high', [(p, p + 1) for p in range(step - 1, plan...  14.1 us
    all_to_all x1, blocking collectives, exchanged(): got = lax.all_to_all(sent, order, 0, 0, tiled=True)  10.7 us
    ppermute x3, starting transfers between devices, exchanged(): lax.ppermute(below[-1], 'high', [(p, p + 1) for p in range(step - 1, plan...  3.85 us
    ppermute x3, starting transfers between devices, exchanged(): lax.ppermute(above[-1], 'high', [(p, p - 1) for p in range(1, planes - st...  3.68 us
    unnamed x8, local copies, waits for them, and re-layouts  3.39 us
    all_to_all x1, starting transfers between devices, exchanged(): mine = lax.all_to_all(sums, order, 0, 0, tiled=True)  3.37 us
    all_to_all x1, waiting for transfers between devices, exchanged(): mine = lax.all_to_all(sums, order, 0, 0, tiled=True)  2.83 us
    pallas_call x1, Pallas kernels, exchanged(): pl.pallas_call(gate_kernel, out_shape=(jax.ShapeDtypeStruct((rows * cols,...  2.63 us
  transfers between devices with their start and end apart: 7, of which 5 were waited for; matrix products, arithmetic and copies ran while one was open for 0% of the time, Pallas kernels for 5%

profile of v3, /device:TPU:24, one launch (start us, length us, event | category | flops | bytes accessed | tf_op | source)
XLA Modules:
  0.0 51.6 jit_solution(4478454080631878104)
XLA Ops:
  0.0 2.4 %mix.1 = (bf16[8,128,128]{2,1,0:T(8,128)(2,1)}, bf16[512,128]{1,0:T(8,128)(2,1)}) custom-call(s32[8]{0:T(128)} %chain_hbm.1, bf16[16,32,128]{2,1,0:T(8,128)(2,1)} %pair_hbm.1, f32[1,128]{1,0:T(1,128)} %bitcast.4, f32[1,128]{1,0:T(1,128)} %bitcast.5, bf16[128,256]{1,0:T(8,128)(2,1)} %proj_hbm.2, bf16[128,256]{1,0:T(8,128)(2,1)} %gate_hbm.2), custom_call_target="tpu_custom_call" | custom-call | tf_op jit(solution)/shard_map/mix/pallas_call | solution.py:370
  2.4 10.7 %all_to_all.10.got_ref = bf16[8,128,128]{2,1,0:T(8,128)(2,1)S(1)} all-to-all(bf16[8,128,128]{2,1,0:T(8,128)(2,1)} %get-tuple-element.11), channel_id=1, replica_groups=mesh['high'=4,'low'=2,'col'=4] {'low','col'}, dimensions={0} | all-to-all | bytes 524288 | tf_op jit(solution)/shard_map/all_to_all | solution.py:398
  13.1 2.4 %collective-permute-start.3 = (bf16[128,512]{1,0:T(8,128)(2,1)S(1)}, bf16[128,512]{1,0:T(8,128)(2,1)S(1)}, u32[]{:S(2)}, u32[]{:S(2)}) collective-permute-start(bf16[128,512]{1,0:T(8,128)(2,1)S(1)} %pick.1.refs_0_), channel_id=1, source_target_pairs={{8,0},{16,8},{24,16},{9,1},{17,9},{25,17},{10,2},{18,10},{26,18},{... | collective-permute-start | bytes 393224 | tf_op jit(solution)/shard_map/ppermute | solution.py:413
  15.5 1.3 %collective-permute-start = (bf16[128,512]{1,0:T(8,128)(2,1)S(1)}, bf16[128,512]{1,0:T(8,128)(2,1)S(1)}, u32[]{:S(2)}, u32[]{:S(2)}) collective-permute-start(bf16[128,512]{1,0:T(8,128)(2,1)S(1)} %pick.1.refs_0_), channel_id=1, source_target_pairs={{0,8},{8,16},{16,24},{1,9},{9,17},{17,25},{2,10},{10,18},{18,26},{... | collective-permute-start | bytes 393224 | tf_op jit(solution)/shard_map/ppermute | solution.py:410
  16.8 1.2 %collective-permute-done.3.refs_4_ = bf16[128,512]{1,0:T(8,128)(2,1)S(1)} collective-permute-done((bf16[128,512]{1,0:T(8,128)(2,1)S(1)}, bf16[128,512]{1,0:T(8,128)(2,1)S(1)}, u32[]{:S(2)}, u32[]{:S(2)}) %collective-permute-start.3) | collective-permute-done | bytes 131104 | tf_op jit(solution)/shard_map/ppermute | solution.py:413
  17.9 0.7 %collective-permute-start.4 = (bf16[128,512]{1,0:T(8,128)(2,1)S(1)}, bf16[128,512]{1,0:T(8,128)(2,1)S(1)}, u32[]{:S(2)}, u32[]{:S(2)}) collective-permute-start(bf16[128,512]{1,0:T(8,128)(2,1)S(1)} %collective-permute-done.3.refs_4_), channel_id=1, source_target_pairs={{8,0},{16,8},{9,1},{17,9},{10,2},{18,10},{11,3},{19,11},{12,4},{20... | collective-permute-start | bytes 393224 | tf_op jit(solution)/shard_map/ppermute | solution.py:413
  18.6 3.7 %collective-permute-done.refs_1_ = bf16[128,512]{1,0:T(8,128)(2,1)S(1)} collective-permute-done((bf16[128,512]{1,0:T(8,128)(2,1)S(1)}, bf16[128,512]{1,0:T(8,128)(2,1)S(1)}, u32[]{:S(2)}, u32[]{:S(2)}) %collective-permute-start) | collective-permute-done | bytes 131104 | tf_op jit(solution)/shard_map/ppermute | solution.py:410
  22.3 1.3 %collective-permute-start.1 = (bf16[128,512]{1,0:T(8,128)(2,1)S(1)}, bf16[128,512]{1,0:T(8,128)(2,1)S(1)}, u32[]{:S(2)}, u32[]{:S(2)}) collective-permute-start(bf16[128,512]{1,0:T(8,128)(2,1)S(1)} %collective-permute-done.refs_1_), channel_id=1, source_target_pairs={{8,16},{16,24},{9,17},{17,25},{10,18},{18,26},{11,19},{19,27},{12,... | collective-permute-start | bytes 393224 | tf_op jit(solution)/shard_map/ppermute | solution.py:410
  23.6 0.0 collective-permute-done.4.refs_5_
  23.6 0.7 %collective-permute-start.5 = (bf16[128,512]{1,0:T(8,128)(2,1)S(1)}, bf16[128,512]{1,0:T(8,128)(2,1)S(1)}, u32[]{:S(2)}, u32[]{:S(2)}) collective-permute-start(bf16[128,512]{1,0:T(8,128)(2,1)S(1)} %collective-permute-done.4.refs_5_), channel_id=1, source_target_pairs={{8,0},{9,1},{10,2},{11,3},{12,4},{13,5},{14,6},{15,7}} | collective-permute-start | bytes 393224 | tf_op jit(solution)/shard_map/ppermute | solution.py:413
  24.3 4.9 %collective-permute-done.1.refs_2_ = bf16[128,512]{1,0:T(8,128)(2,1)S(1)} collective-permute-done((bf16[128,512]{1,0:T(8,128)(2,1)S(1)}, bf16[128,512]{1,0:T(8,128)(2,1)S(1)}, u32[]{:S(2)}, u32[]{:S(2)}) %collective-permute-start.1) | collective-permute-done | bytes 131104 | tf_op jit(solution)/shard_map/ppermute | solution.py:410
  29.2 1.3 %collective-permute-start.2 = (bf16[128,512]{1,0:T(8,128)(2,1)S(1)}, bf16[128,512]{1,0:T(8,128)(2,1)S(1)}, u32[]{:S(2)}, u32[]{:S(2)}) collective-permute-start(bf16[128,512]{1,0:T(8,128)(2,1)S(1)} %collective-permute-done.1.refs_2_), channel_id=1, source_target_pairs={{16,24},{17,25},{18,26},{19,27},{20,28},{21,29},{22,30},{23,31}} | collective-permute-start | bytes 393224 | tf_op jit(solution)/shard_map/ppermute | solution.py:410
  30.5 0.0 collective-permute-done.5.refs_6_
  30.5 5.6 %collective-permute-done.2.refs_3_ = bf16[128,512]{1,0:T(8,128)(2,1)S(1)} collective-permute-done((bf16[128,512]{1,0:T(8,128)(2,1)S(1)}, bf16[128,512]{1,0:T(8,128)(2,1)S(1)}, u32[]{:S(2)}, u32[]{:S(2)}) %collective-permute-start.2) | collective-permute-done | bytes 131104 | tf_op jit(solution)/shard_map/ppermute | solution.py:410
  36.0 2.3 %triangle.1 = bf16[8,64,128]{2,1,0:T(8,128)(2,1)} custom-call(bf16[8,128,128]{2,1,0:T(8,128)(2,1)S(1)} %all_to_all.10.got_ref, bf16[128,512]{1,0:T(8,128)(2,1)S(1)} %pick.1.refs_0_, bf16[128,512]{1,0:T(8,128)(2,1)S(1)} %collective-permute-done.refs_1_, bf16[128,512]{1,0:T(8,128)(2,1)S(1)} %collective-permute-done.1.refs_2_, ...), custom_call_target="tpu_custom_call" | custom-call | tf_op jit(solution)/shard_map/triangle/pallas_call | solution.py:434
  38.3 3.4 %all-to-all-start.1 = ((bf16[8,64,128]{2,1,0:T(8,128)(2,1)}), bf16[8,64,128]{2,1,0:T(8,128)(2,1)S(1)}, u32[]{:S(2)}, u32[]{:S(2)}) async-start(bf16[8,64,128]{2,1,0:T(8,128)(2,1)} %triangle.1), calls=%async_computation.1 | async-start | bytes 262144 | tf_op jit(solution)/shard_map/all_to_all | solution.py:443
  41.7 2.6 %gate.1 = (f32[512,128]{1,0:T(8,128)}, f32[128,128]{1,0:T(8,128)}, f32[128,128]{1,0:T(8,128)}, bf16[128,128]{1,0:T(8,128)(2,1)}) custom-call(bf16[512,128]{1,0:T(8,128)(2,1)} %get-tuple-element.12.normed_ref, bf16[128,128]{1,0:T(8,128)(2,1)} %gate_hbm.3, f32[1,128]{1,0:T(1,128)} %bitcast.6, f32[1,128]{1,0:T(1,128)} %bitcast.7, bf16[128,128]{1,0:T(8,128)(2,1)} %proj_hbm.3), custom_call_target="tpu_custom_call" | custom-call | tf_op jit(solution)/shard_map/gate/pallas_call | solution.py:415
  44.3 2.8 %all-to-all-done.1.got_ref = bf16[8,64,128]{2,1,0:T(8,128)(2,1)S(1)} async-done(((bf16[8,64,128]{2,1,0:T(8,128)(2,1)}), bf16[8,64,128]{2,1,0:T(8,128)(2,1)S(1)}, u32[]{:S(2)}, u32[]{:S(2)}) %all-to-all-start.1) | async-done | bytes 131104 | tf_op jit(solution)/shard_map/all_to_all | solution.py:443
  47.2 0.0 copy-start
  47.2 0.9 %copy-done = f32[512,128]{1,0:T(8,128)S(1)} copy-done((f32[512,128]{1,0:T(8,128)S(1)}, f32[512,128]{1,0:T(8,128)}, u32[]{:S(2)}) %copy-start) | copy-done | bytes 262168
  48.1 0.0 copy-start.1
  48.1 0.8 %copy-done.1 = f32[128,128]{1,0:T(8,128)S(1)} copy-done((f32[128,128]{1,0:T(8,128)S(1)}, f32[128,128]{1,0:T(8,128)}, u32[]{:S(2)}) %copy-start.1) | copy-done | bytes 65560
  48.9 0.0 copy-start.2
  48.9 0.8 %copy-done.2 = f32[128,128]{1,0:T(8,128)S(1)} copy-done((f32[128,128]{1,0:T(8,128)S(1)}, f32[128,128]{1,0:T(8,128)}, u32[]{:S(2)}) %copy-start.2) | copy-done | bytes 65560
  49.8 0.0 copy-start.3
  49.8 0.8 %copy-done.3 = bf16[128,128]{1,0:T(8,128)(2,1)S(1)} copy-done((bf16[128,128]{1,0:T(8,128)(2,1)S(1)}, bf16[128,128]{1,0:T(8,128)(2,1)}, u32[]{:S(2)}) %copy-start.3) | copy-done | bytes 32792
  50.5 1.1 %update.1 = bf16[16,32,128]{2,1,0:T(8,128)(2,1)} custom-call(bf16[8,64,128]{2,1,0:T(8,128)(2,1)S(1)} %all-to-all-done.1.got_ref, f32[512,128]{1,0:T(8,128)S(1)} %copy-done, f32[128,128]{1,0:T(8,128)S(1)} %copy-done.1, f32[128,128]{1,0:T(8,128)S(1)} %copy-done.2, bf16[128,128]{1,0:T(8,128)(2,1)S(1)} %copy-done.3), custom_call_target="tpu_custom_call" | custom-call | tf_op jit(solution)/shard_map/update/pallas_call | solution.py:444
  (1 shorter events, 0.0 us)
Async XLA Ops:
  13.1 4.9 %collective-permute-start.3 = (bf16[128,512]{1,0:T(8,128)(2,1)S(1)}, bf16[128,512]{1,0:T(8,128)(2,1)S(1)}, u32[]{:S(2)}, u32[]{:S(2)}) collective-permute-start(bf16[128,512]{1,0:T(8,128)(2,1)S(1)} %pick.1.refs_0_), channel_id=1, source_target_pairs={{8,0},{16,8},{24,16},{9,1},{17,9},{25,17},{10,2},{18,10},{26,18},{... | collective-permute-start | bytes 393224 | tf_op jit(solution)/shard_map/ppermute | solution.py:413
  15.5 6.9 %collective-permute-start = (bf16[128,512]{1,0:T(8,128)(2,1)S(1)}, bf16[128,512]{1,0:T(8,128)(2,1)S(1)}, u32[]{:S(2)}, u32[]{:S(2)}) collective-permute-start(bf16[128,512]{1,0:T(8,128)(2,1)S(1)} %pick.1.refs_0_), channel_id=1, source_target_pairs={{0,8},{8,16},{16,24},{1,9},{9,17},{17,25},{2,10},{10,18},{18,26},{... | collective-permute-start | bytes 393224 | tf_op jit(solution)/shard_map/ppermute | solution.py:410
  17.9 5.7 %collective-permute-start.4 = (bf16[128,512]{1,0:T(8,128)(2,1)S(1)}, bf16[128,512]{1,0:T(8,128)(2,1)S(1)}, u32[]{:S(2)}, u32[]{:S(2)}) collective-permute-start(bf16[128,512]{1,0:T(8,128)(2,1)S(1)} %collective-permute-done.3.refs_4_), channel_id=1, source_target_pairs={{8,0},{16,8},{9,1},{17,9},{10,2},{18,10},{11,3},{19,11},{12,4},{20... | collective-permute-start | bytes 393224 | tf_op jit(solution)/shard_map/ppermute | solution.py:413
  22.3 6.8 %collective-permute-start.1 = (bf16[128,512]{1,0:T(8,128)(2,1)S(1)}, bf16[128,512]{1,0:T(8,128)(2,1)S(1)}, u32[]{:S(2)}, u32[]{:S(2)}) collective-permute-start(bf16[128,512]{1,0:T(8,128)(2,1)S(1)} %collective-permute-done.refs_1_), channel_id=1, source_target_pairs={{8,16},{16,24},{9,17},{17,25},{10,18},{18,26},{11,19},{19,27},{12,... | collective-permute-start | bytes 393224 | tf_op jit(solution)/shard_map/ppermute | solution.py:410
  23.6 6.8 %collective-permute-start.5 = (bf16[128,512]{1,0:T(8,128)(2,1)S(1)}, bf16[128,512]{1,0:T(8,128)(2,1)S(1)}, u32[]{:S(2)}, u32[]{:S(2)}) collective-permute-start(bf16[128,512]{1,0:T(8,128)(2,1)S(1)} %collective-permute-done.4.refs_5_), channel_id=1, source_target_pairs={{8,0},{9,1},{10,2},{11,3},{12,4},{13,5},{14,6},{15,7}} | collective-permute-start | bytes 393224 | tf_op jit(solution)/shard_map/ppermute | solution.py:413
  29.2 6.8 %collective-permute-start.2 = (bf16[128,512]{1,0:T(8,128)(2,1)S(1)}, bf16[128,512]{1,0:T(8,128)(2,1)S(1)}, u32[]{:S(2)}, u32[]{:S(2)}) collective-permute-start(bf16[128,512]{1,0:T(8,128)(2,1)S(1)} %collective-permute-done.1.refs_2_), channel_id=1, source_target_pairs={{16,24},{17,25},{18,26},{19,27},{20,28},{21,29},{22,30},{23,31}} | collective-permute-start | bytes 393224 | tf_op jit(solution)/shard_map/ppermute | solution.py:410
  38.3 8.8 %all-to-all-start.1 = ((bf16[8,64,128]{2,1,0:T(8,128)(2,1)}), bf16[8,64,128]{2,1,0:T(8,128)(2,1)S(1)}, u32[]{:S(2)}, u32[]{:S(2)}) async-start(bf16[8,64,128]{2,1,0:T(8,128)(2,1)} %triangle.1), calls=%async_computation.1 | async-start | bytes 262144 | tf_op jit(solution)/shard_map/all_to_all | solution.py:443
  47.2 1.0 %copy-start = (f32[512,128]{1,0:T(8,128)S(1)}, f32[512,128]{1,0:T(8,128)}, u32[]{:S(2)}) copy-start(f32[512,128]{1,0:T(8,128)} %get-tuple-element.13.open_ref) | copy-start | bytes 786436
  48.1 0.8 %copy-start.1 = (f32[128,128]{1,0:T(8,128)S(1)}, f32[128,128]{1,0:T(8,128)}, u32[]{:S(2)}) copy-start(f32[128,128]{1,0:T(8,128)} %get-tuple-element.14.gain_ref) | copy-start | bytes 196612
  48.9 0.8 %copy-start.2 = (f32[128,128]{1,0:T(8,128)S(1)}, f32[128,128]{1,0:T(8,128)}, u32[]{:S(2)}) copy-start(f32[128,128]{1,0:T(8,128)} %get-tuple-element.15.bias_ref) | copy-start | bytes 196612
  49.8 0.8 %copy-start.3 = (bf16[128,128]{1,0:T(8,128)(2,1)S(1)}, bf16[128,128]{1,0:T(8,128)(2,1)}, u32[]{:S(2)}) copy-start(bf16[128,128]{1,0:T(8,128)(2,1)} %get-tuple-element.16.proj_ref) | copy-start | bytes 98308

commit v4 on v2

--- a/solution.py
+++ b/solution.py
@@ -208,23 +208,21 @@
     left_by = jnp.concatenate(
         [left * one_hot(lane % LANES // cols == i) for i in range(inner)], axis=0
     )
-    source, out = iota2((LANES, inner * LANES))
-    spread = one_hot((source // cols == out // LANES) & (source % cols == out % cols))
-    wide = dot(right, spread).astype(BF16)
+    right = right.astype(F32)
+    turned = [right.astype(BF16)] + [
+        pltpu.roll(right, turn * cols, 1).astype(BF16) for turn in range(1, inner)
+    ]
     right_by = jnp.concatenate(
         [
             jnp.concatenate(
                 [
-                    wide[
-                        c * high + d * quarter : c * high + (d + 1) * quarter,
-                        j * LANES : (j + 1) * LANES,
-                    ]
+                    turned[turn][c * high + d * quarter : c * high + (d + 1) * quarter]
                     for c in range(grid_cols)
                 ],
                 axis=1,
             )
             for d in range(grid_cols)
-            for j in range(inner)
+            for turn in range(inner)
         ],
         axis=0,
     )
@@ -249,9 +247,10 @@
         axis=0,
     )
     source, out = iota2((inner * width, LANES))
-    at = source % width
-    token = at % quarter // side * rows + at % groups * inner + at // quarter
-    order = one_hot((source // width == out // cols) & (token == out % cols))
+    i, at = source // width, source % width
+    j = (i + inner - at // quarter) % inner
+    token = at % quarter // side * rows + at % groups * inner + j
+    order = one_hot((i == out // cols) & (token == out % cols))
     moved = dot(kept, order).astype(BF16).reshape(grid_cols, grid_rows, side, LANES)
     for c in range(grid_cols):
         for r in range(grid_rows):
@@ -311,8 +310,9 @@
 
 
 VMEM = pl.BlockSpec(memory_space=pltpu.VMEM)
-ANY = pl.BlockSpec(memory_space=pl.ANY)
-PARAMS = pltpu.CompilerParams(vmem_limit_bytes=40 * 1024 * 1024)
+HBM = pl.BlockSpec(memory_space=pltpu.HBM)
+PARAMS = pltpu.CompilerParams(vmem_limit_bytes=32 * 1024 * 1024)
+FETCHING = pltpu.CompilerParams(vmem_limit_bytes=60 * 1024 * 1024)
 
 
 def exchanged(
@@ -342,7 +342,7 @@
             jax.ShapeDtypeStruct((devices, 2 * side, LANES), BF16),
             jax.ShapeDtypeStruct((rows * cols, channels), BF16),
         ),
-        in_specs=[ANY] * 6,
+        in_specs=[HBM] * 6,
         out_specs=(VMEM, VMEM),
         scratch_shapes=[
             pltpu.SMEM(chain_lengths.shape, jnp.int32),
@@ -353,7 +353,7 @@
             pltpu.VMEM(gate_in.shape, BF16),
             pltpu.SemaphoreType.DMA((6,)),
         ],
-        compiler_params=PARAMS,
+        compiler_params=FETCHING,
         name="mix",
     )(
         chain_lengths,
@@ -373,7 +373,7 @@
             jax.ShapeDtypeStruct((hidden, LANES), F32),
             jax.ShapeDtypeStruct(proj_out.shape, BF16),
         ),
-        in_specs=[VMEM] + [ANY] * 4,
+        in_specs=[VMEM] + [HBM] * 4,
         out_specs=[VMEM] * 4,
         scratch_shapes=[
             pltpu.VMEM(gate_out.shape, BF16),

time: 36.1 us -> 33.8 us (0.936)
  local copies, waits for them, and re-layouts: 3.91 us -> 0.64 us
  Pallas kernels: 4.43 us -> 5.31 us
    unnamed x20 -> x10, local copies, waits for them, and re-layouts: 3.91 us -> 0.64 us
    pallas_call x1, Pallas kernels: 1.4 us -> 2.38 us  [exchanged(): pl.pallas_call(functools.partial(mix_kernel, slots), out_shape=(jax.Shape...]
where the time goes in v4:
time: 33.8 us; the launch traced here: 33.6 us
  blocking collectives  18.1 us (54%)
  waiting for transfers between devices  6.78 us (20%)
  Pallas kernels  5.31 us (16%)
  starting transfers between devices  2.7 us (8%)
  local copies, waits for them, and re-layouts  0.64 us (2%)
    all_to_all x1, blocking collectives, exchanged(): got = lax.all_to_all(sent, order, 0, 0, tiled=True)  18.1 us
    all_to_all x1, waiting for transfers between devices, exchanged(): mine = lax.all_to_all(sums, order, 0, 0, tiled=True)  6.78 us
    all_to_all x1, starting transfers between devices, exchanged(): mine = lax.all_to_all(sums, order, 0, 0, tiled=True)  2.7 us
    pallas_call x1, Pallas kernels, exchanged(): pl.pallas_call(functools.partial(mix_kernel, slots), out_shape=(jax.Shape...  2.38 us
    pallas_call x1, Pallas kernels, exchanged(): pl.pallas_call(functools.partial(triangle_kernel, split, grid_cols, rows,...  1.55 us
    pallas_call x1, Pallas kernels, exchanged(): pl.pallas_call(update_kernel, out_shape=jax.ShapeDtypeStruct((rows, cols,...  1.1 us
  transfers between devices with their start and end apart: 1, of which 1 were waited for; matrix products, arithmetic and copies ran while one was open for 0% of the time, Pallas kernels for 1%

profile of v4, /device:TPU:0, one launch (start us, length us, event | category | flops | bytes accessed | tf_op | source)
XLA Modules:
  0.0 33.6 jit_solution(1455905718022580648)
XLA Ops:
  0.0 2.4 %mix.1 = (bf16[32,32,128]{2,1,0:T(8,128)(2,1)}, bf16[512,128]{1,0:T(8,128)(2,1)}) custom-call(s32[8]{0:T(128)} %chain_hbm.1, bf16[16,32,128]{2,1,0:T(8,128)(2,1)} %pair_hbm.1, f32[1,128]{1,0:T(1,128)} %bitcast.6, f32[1,128]{1,0:T(1,128)} %bitcast.7, bf16[128,256]{1,0:T(8,128)(2,1)} %proj_hbm.2, bf16[128,256]{1,0:T(8,128)(2,1)} %gate_hbm.2), custom_call_target="tpu_custom_call" | custom-call | tf_op jit(solution)/shard_map/mix/pallas_call | solution.py:339
  2.4 18.1 %all_to_all.10.got_ref = bf16[32,32,128]{2,1,0:T(8,128)(2,1)S(1)} all-to-all(bf16[32,32,128]{2,1,0:T(8,128)(2,1)} %get-tuple-element.11), channel_id=1, replica_groups=mesh['high'=4,'low'=2,'col'=4] {'col','low','high'}, dimensions={0} | all-to-all | bytes 524288 | tf_op jit(solution)/shard_map/all_to_all | solution.py:367
  20.5 1.6 %triangle.1 = bf16[32,16,128]{2,1,0:T(8,128)(2,1)} custom-call(bf16[32,32,128]{2,1,0:T(8,128)(2,1)S(1)} %all_to_all.10.got_ref), custom_call_target="tpu_custom_call" | custom-call | tf_op jit(solution)/shard_map/triangle/pallas_call | solution.py:387
  22.0 0.0 copy-start
  22.0 0.0 copy-start.1
  22.0 0.0 copy-start.2
  22.0 2.7 %all-to-all-start.1 = ((bf16[32,16,128]{2,1,0:T(8,128)(2,1)}), bf16[32,16,128]{2,1,0:T(8,128)(2,1)S(1)}, u32[]{:S(2)}, u32[]{:S(2)}) async-start(bf16[32,16,128]{2,1,0:T(8,128)(2,1)} %triangle.1), calls=%async_computation.1 | async-start | bytes 262144 | tf_op jit(solution)/shard_map/all_to_all | solution.py:395
  24.7 0.0 copy-start.3
  24.8 0.0 copy-start.4
  24.8 0.0 copy-done
  24.8 0.0 copy-done.1
  24.8 0.0 copy-done.2
  24.8 0.6 %copy-done.3 = f32[128]{0:T(128)S(1)} copy-done((f32[128]{0:T(128)S(1)}, f32[128]{0:T(128)}, u32[]{:S(2)}) %copy-start.3) | copy-done | bytes 536
  25.4 0.0 copy-done.4
  25.4 0.3 gate.1
  25.7 6.8 %all-to-all-done.1.got_ref = bf16[32,16,128]{2,1,0:T(8,128)(2,1)S(1)} async-done(((bf16[32,16,128]{2,1,0:T(8,128)(2,1)}), bf16[32,16,128]{2,1,0:T(8,128)(2,1)S(1)}, u32[]{:S(2)}, u32[]{:S(2)}) %all-to-all-start.1) | async-done | bytes 131104 | tf_op jit(solution)/shard_map/all_to_all | solution.py:395
  32.5 1.1 %update.1 = bf16[16,32,128]{2,1,0:T(8,128)(2,1)} custom-call(bf16[32,16,128]{2,1,0:T(8,128)(2,1)S(1)} %all-to-all-done.1.got_ref, f32[512,128]{1,0:T(8,128)S(1)} %get-tuple-element.13.open_ref, f32[128,128]{1,0:T(8,128)S(1)} %get-tuple-element.14.gain_ref, f32[128,128]{1,0:T(8,128)S(1)} %get-tuple-element.15.bias_ref, ...), custom_call_target="tpu_custom_call" | custom-call | tf_op jit(solution)/shard_map/update/pallas_call | solution.py:396
Async XLA Ops:
  22.0 2.7 %copy-start = (bf16[512,128]{1,0:T(8,128)(2,1)S(1)}, bf16[512,128]{1,0:T(8,128)(2,1)}, u32[]{:S(2)}) copy-start(bf16[512,128]{1,0:T(8,128)(2,1)} %get-tuple-element.12.normed_ref) | copy-start | bytes 393220
  22.0 2.8 %copy-start.1 = (bf16[128,128]{1,0:T(8,128)(2,1)S(1)}, bf16[128,128]{1,0:T(8,128)(2,1)}, u32[]{:S(2)}) copy-start(bf16[128,128]{1,0:T(8,128)(2,1)} %gate_hbm.3) | copy-start | bytes 98308
  22.0 2.8 %copy-start.2 = (bf16[128,128]{1,0:T(8,128)(2,1)S(1)}, bf16[128,128]{1,0:T(8,128)(2,1)}, u32[]{:S(2)}) copy-start(bf16[128,128]{1,0:T(8,128)(2,1)} %proj_hbm.3) | copy-start | bytes 98308
  22.0 10.4 %all-to-all-start.1 = ((bf16[32,16,128]{2,1,0:T(8,128)(2,1)}), bf16[32,16,128]{2,1,0:T(8,128)(2,1)S(1)}, u32[]{:S(2)}, u32[]{:S(2)}) async-start(bf16[32,16,128]{2,1,0:T(8,128)(2,1)} %triangle.1), calls=%async_computation.1 | async-start | bytes 262144 | tf_op jit(solution)/shard_map/all_to_all | solution.py:395
  24.7 0.7 %copy-start.3 = (f32[128]{0:T(128)S(1)}, f32[128]{0:T(128)}, u32[]{:S(2)}) copy-start(f32[128]{0:T(128)} %param.16) | copy-start | bytes 1540
  24.8 0.7 %copy-start.4 = (f32[128]{0:T(128)S(1)}, f32[128]{0:T(128)}, u32[]{:S(2)}) copy-start(f32[128]{0:T(128)} %param.17) | copy-start | bytes 1540

commit v5 on v4

--- a/solution.py
+++ b/solution.py
@@ -113,6 +113,20 @@
     return copies
 
 
+def exchange_blocks(arrays, cols):
+    lane = lax.broadcasted_iota(jnp.int32, (1, LANES), 1) // cols
+    arrays, step = list(arrays), 1
+    while step < len(arrays):
+        upper = lane // step % 2 == 1
+        for n in range(len(arrays)):
+            if n // step % 2 == 0:
+                a, b = arrays[n], arrays[n + step]
+                arrays[n] = jnp.where(upper, pltpu.roll(b, step * cols, 1), a)
+                arrays[n + step] = jnp.where(upper, b, pltpu.roll(a, LANES - step * cols, 1))
+        step *= 2
+    return arrays
+
+
 def mix_kernel(
     slots,
     chain_hbm,
@@ -121,15 +135,18 @@
     bias_hbm,
     proj_hbm,
     gate_hbm,
-    sent_ref,
-    normed_ref,
+    sent_hbm,
+    normed_hbm,
     chain_ref,
     pair_ref,
     gain_ref,
     bias_ref,
     proj_ref,
     gate_ref,
+    sent_ref,
+    normed_ref,
     sems,
+    out_sems,
 ):
     copies = fetch(
         (pair_hbm, gain_hbm, bias_hbm, chain_hbm, proj_hbm, gate_hbm),
@@ -139,16 +156,20 @@
     rows, cols, channels = pair_ref.shape
     hidden = proj_ref.shape[1] // 2
     cells = rows * cols
-    groups = cells // LANES
+    inner = LANES // cols
+    groups = rows // inner
     chunks = sent_ref.shape[0]
-    own = hidden // chunks
+    some = LANES // rows
+    out, source = iota2((LANES, LANES))
+    order = one_hot((out // rows == source % some) & (out % rows == source // some))
+    cell = lax.broadcasted_iota(jnp.int32, (1, cells), 1)
     for copy in copies:
         copy.wait()
     flat = pair_ref[...].reshape(cells, channels).astype(F32)
     normed = layer_norm(flat, gain_ref[...], bias_ref[...]).astype(BF16)
     normed_ref[...] = normed
-
-    cell = lax.broadcasted_iota(jnp.int32, (1, cells), 1)
+    results = [pltpu.make_async_copy(normed_ref, normed_hbm, out_sems.at[0])]
+    results[0].start()
 
     def valid(token):
         length = jnp.zeros_like(token)
@@ -162,100 +183,76 @@
 
     values = dot(proj_ref[...], normed, 0, 1)
     gates = dot(gate_ref[...], normed, 0, 1)
-    mixed = (jax.nn.sigmoid(gates) * values * mask).astype(BF16)
-
-    block = LANES // groups
-    out, source = iota2((LANES, LANES))
-    order = one_hot((out // groups == source % block) & (out % groups == source // block))
+    mixed = jax.nn.sigmoid(gates) * values * mask
+
+    by_row = []
     for side in range(2):
-        for part in range(hidden // block):
-            first = side * hidden + part * block
+        lines = []
+        for g in range(groups):
+            lines += exchange_blocks(
+                [
+                    mixed[
+                        side * hidden + n * chunks : side * hidden + (n + 1) * chunks,
+                        g * LANES : (g + 1) * LANES,
+                    ]
+                    for n in range(inner)
+                ],
+                cols,
+            )
+        by_row.append(lines)
+    for part in range(chunks // some):
+        here = pl.ds(part * some, some)
+        for side in range(2):
             stack = jnp.concatenate(
-                [
-                    mixed[first : first + block, g * LANES : (g + 1) * LANES]
-                    for g in range(groups)
-                ],
-                axis=0,
-            )
+                [line[part * some : (part + 1) * some] for line in by_row[side]], axis=0
+            ).astype(BF16)
             moved = dot(order, stack).astype(BF16)
-            count = block // own
-            sent_ref[
-                part * count : (part + 1) * count, side * own * groups : (side + 1) * own * groups
-            ] = moved.reshape(count, own * groups, LANES)
+            sent_ref[here, side * rows : (side + 1) * rows] = moved.reshape(some, rows, LANES)
+        results.append(
+            pltpu.make_async_copy(sent_ref.at[here], sent_hbm.at[here], out_sems.at[part + 1])
+        )
+        results[-1].start()
+    for copy in results:
+        copy.wait()
 
 
 def triangle_kernel(split, grid_cols, rows, cols, got_ref, sent_ref):
-    grid_rows = split[0] * split[1]
-    groups = rows * cols // LANES
     inner = LANES // cols
-    own = got_ref.shape[1] // (2 * groups)
-    side = own * groups
-    got = got_ref[...].reshape(grid_cols, split[1], split[0], 2 * side, LANES)
-    high = grid_rows * side
-    ratio = grid_rows // grid_cols
-    quarter = ratio * side
-
-    def block(column, which):
-        part = got[column, :, :, which * side : (which + 1) * side]
+
+    def place(r, c):
+        z, y = r // split[1], r % split[1]
+        return (c * split[1] + y) * split[0] + z
+
+    def side(which):
         return jnp.concatenate(
-            [part[y, z] for z in range(split[0]) for y in range(split[1])], axis=0
+            [
+                jnp.concatenate(
+                    [
+                        got_ref[place(r, c), which * rows : (which + 1) * rows]
+                        for r in range(split[0] * split[1])
+                    ],
+                    axis=0,
+                )
+                for c in range(grid_cols)
+            ],
+            axis=1,
         )
 
-    left = jnp.concatenate([block(c, 0) for c in range(grid_cols)], axis=1)
-    right = jnp.concatenate([block(c, 1) for c in range(grid_cols)], axis=0)
-
+    left, right = side(0), side(1)
     lane = lax.broadcasted_iota(jnp.int32, (1, grid_cols * LANES), 1)
-    left_by = jnp.concatenate(
-        [left * one_hot(lane % LANES // cols == i) for i in range(inner)], axis=0
-    )
-    right = right.astype(F32)
-    turned = [right.astype(BF16)] + [
-        pltpu.roll(right, turn * cols, 1).astype(BF16) for turn in range(1, inner)
-    ]
+    by_channel = [right * one_hot(lane % LANES // cols == n) for n in range(inner)]
     right_by = jnp.concatenate(
         [
-            jnp.concatenate(
-                [
-                    turned[turn][c * high + d * quarter : c * high + (d + 1) * quarter]
-                    for c in range(grid_cols)
-                ],
-                axis=1,
-            )
-            for d in range(grid_cols)
-            for turn in range(inner)
+            by_channel[n][c * cols : (c + 1) * cols]
+            for c in range(grid_cols)
+            for n in range(inner)
         ],
         axis=0,
     )
-    product = dot(left_by, right_by, 1, 1)
-
-    width = inner * quarter
-    a, b = iota2((high, width))
-    same = jnp.where(a // groups % own == b // groups % own, 1.0, 0.0)
-    kept = jnp.concatenate(
-        [
-            jnp.concatenate(
-                [
-                    (product[i * high : (i + 1) * high, d * width : (d + 1) * width] * same).astype(
-                        BF16
-                    )
-                    for i in range(inner)
-                ],
-                axis=1,
-            )
-            for d in range(grid_cols)
-        ],
-        axis=0,
-    )
-    source, out = iota2((inner * width, LANES))
-    i, at = source // width, source % width
-    j = (i + inner - at // quarter) % inner
-    token = at % quarter // side * rows + at % groups * inner + j
-    order = one_hot((i == out // cols) & (token == out % cols))
-    moved = dot(kept, order).astype(BF16).reshape(grid_cols, grid_rows, side, LANES)
+    sums = dot(left, right_by, 1, 1).astype(BF16)
     for c in range(grid_cols):
-        for r in range(grid_rows):
-            z, y = r // split[1], r % split[1]
-            sent_ref[(c * split[1] + y) * split[0] + z] = moved[c, r]
+        for r in range(split[0] * split[1]):
+            sent_ref[place(r, c)] = sums[r * rows : (r + 1) * rows, c * LANES : (c + 1) * LANES]
 
 
 def gate_kernel(
@@ -285,28 +282,42 @@
         target[...] = jnp.broadcast_to(column, target.shape)
 
 
-def update_kernel(got_ref, open_ref, gain_ref, bias_ref, proj_ref, out_ref):
+def update_kernel(
+    got_ref, open_ref, gain_ref, bias_ref, proj_ref, out_hbm, out_ref, out_sems
+):
     rows, cols, channels = out_ref.shape
-    hidden = proj_ref.shape[0]
-    groups = rows * cols // LANES
+    chunks = got_ref.shape[0]
     inner = LANES // cols
-    block = LANES // groups
-    got = got_ref[...].reshape(hidden * groups, LANES)
+    groups = rows // inner
+    some = LANES // rows
     out, source = iota2((LANES, LANES))
-    order = one_hot((source // groups == out % block) & (source % groups == out // block))
-    pieces = [
-        dot(order, got[part * LANES : (part + 1) * LANES]) for part in range(hidden // block)
+    order = one_hot((out // some == source % rows) & (out % some == source // rows))
+    parts = [
+        dot(order, got_ref[part * some : (part + 1) * some].reshape(LANES, LANES))
+        for part in range(chunks // some)
+    ]
+    lines = [
+        jnp.concatenate([part[row * some : (row + 1) * some] for part in parts], axis=0)
+        for row in range(rows)
     ]
     gain, bias = gain_ref[...], bias_ref[...]
+    results = []
     for g in range(groups):
-        values = jnp.concatenate([piece[g * block : (g + 1) * block] for piece in pieces], axis=0)
+        values = jnp.concatenate(
+            exchange_blocks(lines[g * inner : (g + 1) * inner], cols), axis=0
+        )
         mean = jnp.mean(values, axis=0, keepdims=True)
         centered = values - mean
         variance = jnp.mean(centered * centered, axis=0, keepdims=True)
         tri_normed = (centered * lax.rsqrt(variance + 1e-05) * gain + bias).astype(BF16)
         projected = dot(tri_normed, proj_ref[...], 0, 0)
         update = (open_ref[g * LANES : (g + 1) * LANES] * projected).astype(BF16)
-        out_ref[g * inner : (g + 1) * inner] = update.reshape(inner, cols, channels)
+        here = pl.ds(g * inner, inner)
+        out_ref[here] = update.reshape(inner, cols, channels)
+        results.append(pltpu.make_async_copy(out_ref.at[here], out_hbm.at[here], out_sems.at[g]))
+        results[-1].start()
+    for copy in results:
+        copy.wait()
 
 
 VMEM = pl.BlockSpec(memory_space=pltpu.VMEM)
@@ -333,17 +344,15 @@
     hidden = proj_out.shape[0]
     grid_rows = split[0] * split[1]
     devices = grid_rows * grid_cols
-    groups = rows * cols // LANES
-    side = hidden // devices * groups
     slots = rows * grid_rows // chain_lengths.shape[0]
     sent, normed = pl.pallas_call(
         functools.partial(mix_kernel, slots),
         out_shape=(
-            jax.ShapeDtypeStruct((devices, 2 * side, LANES), BF16),
+            jax.ShapeDtypeStruct((devices, 2 * rows, LANES), BF16),
             jax.ShapeDtypeStruct((rows * cols, channels), BF16),
         ),
         in_specs=[HBM] * 6,
-        out_specs=(VMEM, VMEM),
+        out_specs=(HBM, HBM),
         scratch_shapes=[
             pltpu.SMEM(chain_lengths.shape, jnp.int32),
             pltpu.VMEM(pair.shape, BF16),
@@ -351,7 +360,10 @@
             pltpu.VMEM((1, channels), F32),
             pltpu.VMEM(proj_in.shape, BF16),
             pltpu.VMEM(gate_in.shape, BF16),
+            pltpu.VMEM((devices, 2 * rows, LANES), BF16),
+            pltpu.VMEM((rows * cols, channels), BF16),
             pltpu.SemaphoreType.DMA((6,)),
+            pltpu.SemaphoreType.DMA((1 + devices * rows // LANES,)),
         ],
         compiler_params=FETCHING,
         name="mix",
@@ -386,7 +398,7 @@
     )(normed, gate_out, norm_out_gain.reshape(1, hidden), norm_out_bias.reshape(1, hidden), proj_out)
     sums = pl.pallas_call(
         functools.partial(triangle_kernel, split, grid_cols, rows, cols),
-        out_shape=jax.ShapeDtypeStruct((devices, side, LANES), BF16),
+        out_shape=jax.ShapeDtypeStruct((devices, rows, LANES), BF16),
         in_specs=[VMEM],
         out_specs=VMEM,
         compiler_params=PARAMS,
@@ -397,7 +409,11 @@
         update_kernel,
         out_shape=jax.ShapeDtypeStruct((rows, cols, channels), BF16),
         in_specs=[VMEM] * 5,
-        out_specs=VMEM,
+        out_specs=HBM,
+        scratch_shapes=[
+            pltpu.VMEM((rows, cols, channels), BF16),
+            pltpu.SemaphoreType.DMA((rows * cols // LANES,)),
+        ],
         compiler_params=PARAMS,
         name="update",
     )(mine, opened, gain, bias, proj)
@@ -410,22 +426,26 @@
         mesh.devices.reshape(split + (grid_cols,)), ("high", "low", "col")
     )
 
-    def fits(rows, cols, hidden):
+    def fits(rows, cols, channels, hidden):
         devices = grid_rows * grid_cols
+        inner = LANES // cols
         return (
-            hidden % devices == 0
+            channels == LANES
             and hidden == LANES
-            and LANES % cols == 0
-            and rows * cols % LANES == 0
-            and grid_rows % grid_cols == 0
-            and grid_rows // grid_cols * rows == cols
-            and hidden // devices * (rows * cols // LANES) % 16 == 0
+            and inner * cols == LANES
+            and inner & (inner - 1) == 0
+            and inner * devices == hidden
+            and rows % 16 == 0
+            and rows % inner == 0
+            and LANES % rows == 0
+            and devices * rows % LANES == 0
+            and LANES // rows % 8 == 0
         )
 
     def call(*arrays):
-        tokens, _, _ = arrays[0].shape
+        tokens, others, channels = arrays[0].shape
         hidden = arrays[8].shape[0]
-        if fits(tokens // grid_rows, tokens // grid_cols, hidden):
+        if fits(tokens // grid_rows, others // grid_cols, channels, hidden):
             return jax.shard_map(
                 functools.partial(exchanged, split, grid_cols),
                 mesh=fine,

time: 33.8 us -> 33.7 us (level)
    pallas_call x1, Pallas kernels: 1.55 us -> 0.96 us  [exchanged(): pl.pallas_call(functools.partial(triangle_kernel, split, grid_cols, rows,...]
where the time goes in v5:
time: 33.7 us; the launch traced here: 33.4 us
  blocking collectives  18.1 us (54%)
  waiting for transfers between devices  6.78 us (20%)
  Pallas kernels  5.09 us (15%)
  starting transfers between devices  2.7 us (8%)
  local copies, waits for them, and re-layouts  0.64 us (2%)
    all_to_all x1, blocking collectives, exchanged(): got = lax.all_to_all(sent, order, 0, 0, tiled=True)  18.1 us
    all_to_all x1, waiting for transfers between devices, exchanged(): mine = lax.all_to_all(sums, order, 0, 0, tiled=True)  6.78 us
    all_to_all x1, starting transfers between devices, exchanged(): mine = lax.all_to_all(sums, order, 0, 0, tiled=True)  2.7 us
    pallas_call x1, Pallas kernels, exchanged(): pl.pallas_call(functools.partial(mix_kernel, slots), out_shape=(jax.Shape...  2.58 us
    pallas_call x1, Pallas kernels, exchanged(): pl.pallas_call(update_kernel, out_shape=jax.ShapeDtypeStruct((rows, cols,...  1.27 us
    pallas_call x1, Pallas kernels, exchanged(): pl.pallas_call(functools.partial(triangle_kernel, split, grid_cols, rows,...  0.96 us
  transfers between devices with their start and end apart: 1, of which 1 were waited for; matrix products, arithmetic and copies ran while one was open for 0% of the time, Pallas kernels for 1%

profile of v5, /device:TPU:0, one launch (start us, length us, event | category | flops | bytes accessed | tf_op | source)
XLA Modules:
  0.0 33.4 jit_solution(2935132351512156864)
XLA Ops:
  0.0 2.6 %mix.1 = (bf16[32,32,128]{2,1,0:T(8,128)(2,1)}, bf16[512,128]{1,0:T(8,128)(2,1)}) custom-call(s32[8]{0:T(128)} %chain_hbm.1, bf16[16,32,128]{2,1,0:T(8,128)(2,1)} %pair_hbm.1, f32[1,128]{1,0:T(1,128)} %bitcast.6, f32[1,128]{1,0:T(1,128)} %bitcast.7, bf16[128,256]{1,0:T(8,128)(2,1)} %proj_hbm.2, bf16[128,256]{1,0:T(8,128)(2,1)} %gate_hbm.2), custom_call_target="tpu_custom_call" | custom-call | tf_op jit(solution)/shard_map/mix/pallas_call | solution.py:348
  2.6 18.1 %all_to_all.10.got_ref = bf16[32,32,128]{2,1,0:T(8,128)(2,1)S(1)} all-to-all(bf16[32,32,128]{2,1,0:T(8,128)(2,1)} %get-tuple-element.11), channel_id=1, replica_groups=mesh['high'=4,'low'=2,'col'=4] {'col','low','high'}, dimensions={0} | all-to-all | bytes 524288 | tf_op jit(solution)/shard_map/all_to_all | solution.py:379
  20.7 1.0 %triangle.1 = bf16[32,16,128]{2,1,0:T(8,128)(2,1)} custom-call(bf16[32,32,128]{2,1,0:T(8,128)(2,1)S(1)} %all_to_all.10.got_ref), custom_call_target="tpu_custom_call" | custom-call | tf_op jit(solution)/shard_map/triangle/pallas_call | solution.py:399
  21.6 0.0 copy-start
  21.6 0.0 copy-start.1
  21.6 0.0 copy-start.2
  21.7 2.7 %all-to-all-start.1 = ((bf16[32,16,128]{2,1,0:T(8,128)(2,1)}), bf16[32,16,128]{2,1,0:T(8,128)(2,1)S(1)}, u32[]{:S(2)}, u32[]{:S(2)}) async-start(bf16[32,16,128]{2,1,0:T(8,128)(2,1)} %triangle.1), calls=%async_computation.1 | async-start | bytes 262144 | tf_op jit(solution)/shard_map/all_to_all | solution.py:407
  24.4 0.0 copy-start.3
  24.4 0.0 copy-start.4
  24.4 0.0 copy-done
  24.4 0.0 copy-done.1
  24.4 0.0 copy-done.2
  24.4 0.6 %copy-done.3 = f32[128]{0:T(128)S(1)} copy-done((f32[128]{0:T(128)S(1)}, f32[128]{0:T(128)}, u32[]{:S(2)}) %copy-start.3) | copy-done | bytes 536
  25.0 0.0 copy-done.4
  25.0 0.3 gate.1
  25.3 6.8 %all-to-all-done.1.got_ref = bf16[32,16,128]{2,1,0:T(8,128)(2,1)S(1)} async-done(((bf16[32,16,128]{2,1,0:T(8,128)(2,1)}), bf16[32,16,128]{2,1,0:T(8,128)(2,1)S(1)}, u32[]{:S(2)}, u32[]{:S(2)}) %all-to-all-start.1) | async-done | bytes 131104 | tf_op jit(solution)/shard_map/all_to_all | solution.py:407
  32.1 1.3 %update.1 = bf16[16,32,128]{2,1,0:T(8,128)(2,1)} custom-call(bf16[32,16,128]{2,1,0:T(8,128)(2,1)S(1)} %all-to-all-done.1.got_ref, f32[512,128]{1,0:T(8,128)S(1)} %get-tuple-element.13.open_ref, f32[128,128]{1,0:T(8,128)S(1)} %get-tuple-element.14.gain_ref, f32[128,128]{1,0:T(8,128)S(1)} %get-tuple-element.15.bias_ref, ...), custom_call_target="tpu_custom_call" | custom-call | tf_op jit(solution)/shard_map/update/pallas_call | solution.py:408
Async XLA Ops:
  21.6 2.7 %copy-start = (bf16[512,128]{1,0:T(8,128)(2,1)S(1)}, bf16[512,128]{1,0:T(8,128)(2,1)}, u32[]{:S(2)}) copy-start(bf16[512,128]{1,0:T(8,128)(2,1)} %get-tuple-element.12.normed_ref) | copy-start | bytes 393220
  21.6 2.8 %copy-start.1 = (bf16[128,128]{1,0:T(8,128)(2,1)S(1)}, bf16[128,128]{1,0:T(8,128)(2,1)}, u32[]{:S(2)}) copy-start(bf16[128,128]{1,0:T(8,128)(2,1)} %gate_hbm.3) | copy-start | bytes 98308
  21.6 2.8 %copy-start.2 = (bf16[128,128]{1,0:T(8,128)(2,1)S(1)}, bf16[128,128]{1,0:T(8,128)(2,1)}, u32[]{:S(2)}) copy-start(bf16[128,128]{1,0:T(8,128)(2,1)} %proj_hbm.3) | copy-start | bytes 98308
  21.7 10.4 %all-to-all-start.1 = ((bf16[32,16,128]{2,1,0:T(8,128)(2,1)}), bf16[32,16,128]{2,1,0:T(8,128)(2,1)S(1)}, u32[]{:S(2)}, u32[]{:S(2)}) async-start(bf16[32,16,128]{2,1,0:T(8,128)(2,1)} %triangle.1), calls=%async_computation.1 | async-start | bytes 262144 | tf_op jit(solution)/shard_map/all_to_all | solution.py:407
  24.4 0.7 %copy-start.3 = (f32[128]{0:T(128)S(1)}, f32[128]{0:T(128)}, u32[]{:S(2)}) copy-start(f32[128]{0:T(128)} %param.16) | copy-start | bytes 1540
  24.4 0.7 %copy-start.4 = (f32[128]{0:T(128)S(1)}, f32[128]{0:T(128)}, u32[]{:S(2)}) copy-start(f32[128]{0:T(128)} %param.17) | copy-start | bytes 1540

commit v6 on v5

--- a/solution.py
+++ b/solution.py
@@ -396,6 +396,7 @@
         compiler_params=PARAMS,
         name="gate",
     )(normed, gate_out, norm_out_gain.reshape(1, hidden), norm_out_bias.reshape(1, hidden), proj_out)
+    got, opened, gain, bias, proj = lax.optimization_barrier((got, opened, gain, bias, proj))
     sums = pl.pallas_call(
         functools.partial(triangle_kernel, split, grid_cols, rows, cols),
         out_shape=jax.ShapeDtypeStruct((devices, rows, LANES), BF16),

time: 33.7 us -> 32 us (0.950)
  blocking collectives: 18.1 us -> 9.46 us
  starting transfers between devices: 2.7 us -> 7.3 us
  waiting for transfers between devices: 6.78 us -> 9.81 us
  Pallas kernels: 5.09 us -> 4.43 us
    all_to_all x1, blocking collectives: 18.1 us -> 9.46 us  [exchanged(): mine = lax.all_to_all(sums, order, 0, 0, tiled=True)]
    all_to_all x1, starting transfers between devices: 2.7 us -> 7.3 us  [exchanged(): got = lax.all_to_all(sent, order, 0, 0, tiled=True)]
    all_to_all x1, waiting for transfers between devices: 6.78 us -> 9.81 us  [exchanged(): got = lax.all_to_all(sent, order, 0, 0, tiled=True)]
    pallas_call x1, Pallas kernels: 0.96 us -> 0.3 us  [exchanged(): pl.pallas_call(functools.partial(triangle_kernel, split, grid_cols, rows,...]
where the time goes in v6:
time: 32 us; the launch traced here: 31.8 us
  waiting for transfers between devices  9.81 us (31%)
  blocking collectives  9.46 us (30%)
  starting transfers between devices  7.3 us (23%)
  Pallas kernels  4.43 us (14%)
  local copies, waits for them, and re-layouts  0.65 us (2%)
    all_to_all x1, waiting for transfers between devices, exchanged(): got = lax.all_to_all(sent, order, 0, 0, tiled=True)  9.81 us
    all_to_all x1, blocking collectives, exchanged(): mine = lax.all_to_all(sums, order, 0, 0, tiled=True)  9.46 us
    all_to_all x1, starting transfers between devices, exchanged(): got = lax.all_to_all(sent, order, 0, 0, tiled=True)  7.3 us
    pallas_call x1, Pallas kernels, exchanged(): pl.pallas_call(functools.partial(mix_kernel, slots), out_shape=(jax.Shape...  2.58 us
    pallas_call x1, Pallas kernels, exchanged(): pl.pallas_call(update_kernel, out_shape=jax.ShapeDtypeStruct((rows, cols,...  1.27 us
    unnamed x10, local copies, waits for them, and re-layouts  0.65 us
  transfers between devices with their start and end apart: 1, of which 1 were waited for; matrix products, arithmetic and copies ran while one was open for 0% of the time, Pallas kernels for 1%

profile of v6, /device:TPU:0, one launch (start us, length us, event | category | flops | bytes accessed | tf_op | source)
XLA Modules:
  0.0 31.8 jit_solution(7317969420712381975)
XLA Ops:
  0.0 2.6 %mix.1 = (bf16[32,32,128]{2,1,0:T(8,128)(2,1)}, bf16[512,128]{1,0:T(8,128)(2,1)}) custom-call(s32[8]{0:T(128)} %chain_hbm.1, bf16[16,32,128]{2,1,0:T(8,128)(2,1)} %pair_hbm.1, f32[1,128]{1,0:T(1,128)} %bitcast.6, f32[1,128]{1,0:T(1,128)} %bitcast.7, bf16[128,256]{1,0:T(8,128)(2,1)} %proj_hbm.2, bf16[128,256]{1,0:T(8,128)(2,1)} %gate_hbm.2), custom_call_target="tpu_custom_call" | custom-call | tf_op jit(solution)/shard_map/mix/pallas_call | solution.py:348
  2.6 0.0 copy-start
  2.6 0.0 copy-start.1
  2.6 0.0 copy-start.2
  2.6 7.3 %all-to-all-start = ((bf16[32,32,128]{2,1,0:T(8,128)(2,1)}), bf16[32,32,128]{2,1,0:T(8,128)(2,1)S(1)}, u32[]{:S(2)}, u32[]{:S(2)}) async-start(bf16[32,32,128]{2,1,0:T(8,128)(2,1)} %get-tuple-element.16), calls=%async_computation | async-start | bytes 524288 | tf_op jit(solution)/shard_map/all_to_all | solution.py:379
  9.9 0.0 copy-start.3
  10.0 0.0 copy-start.4
  10.0 0.0 copy-done
  10.0 0.0 copy-done.1
  10.0 0.0 copy-done.2
  10.0 0.6 %copy-done.3 = f32[128]{0:T(128)S(1)} copy-done((f32[128]{0:T(128)S(1)}, f32[128]{0:T(128)}, u32[]{:S(2)}) %copy-start.3) | copy-done | bytes 536
  10.6 0.0 copy-done.4
  10.6 0.3 gate.1
  10.9 9.8 %all-to-all-done.got_ref = bf16[32,32,128]{2,1,0:T(8,128)(2,1)S(1)} async-done(((bf16[32,32,128]{2,1,0:T(8,128)(2,1)}), bf16[32,32,128]{2,1,0:T(8,128)(2,1)S(1)}, u32[]{:S(2)}, u32[]{:S(2)}) %all-to-all-start) | async-done | bytes 262176 | tf_op jit(solution)/shard_map/all_to_all | solution.py:379
  20.7 0.3 triangle.1
  21.0 9.5 %all_to_all.10.got_ref = bf16[32,16,128]{2,1,0:T(8,128)(2,1)S(1)} all-to-all(bf16[32,16,128]{2,1,0:T(8,128)(2,1)S(1)} %triangle.1), channel_id=1, replica_groups=mesh['high'=4,'low'=2,'col'=4] {'col','low','high'}, dimensions={0} | all-to-all | bytes 262144 | tf_op jit(solution)/shard_map/all_to_all | solution.py:408
  30.5 1.3 %update.1 = bf16[16,32,128]{2,1,0:T(8,128)(2,1)} custom-call(bf16[32,16,128]{2,1,0:T(8,128)(2,1)S(1)} %all_to_all.10.got_ref, f32[512,128]{1,0:T(8,128)S(1)} %get-tuple-element.23.open_ref, f32[128,128]{1,0:T(8,128)S(1)} %get-tuple-element.24.gain_ref, f32[128,128]{1,0:T(8,128)S(1)} %get-tuple-element.25.bias_ref, ...), custom_call_target="tpu_custom_call" | custom-call | tf_op jit(solution)/shard_map/update/pallas_call | solution.py:409
Async XLA Ops:
  2.6 7.4 %copy-start = (bf16[512,128]{1,0:T(8,128)(2,1)S(1)}, bf16[512,128]{1,0:T(8,128)(2,1)}, u32[]{:S(2)}) copy-start(bf16[512,128]{1,0:T(8,128)(2,1)} %get-tuple-element.17.normed_ref) | copy-start | bytes 393220
  2.6 7.4 %copy-start.1 = (bf16[128,128]{1,0:T(8,128)(2,1)S(1)}, bf16[128,128]{1,0:T(8,128)(2,1)}, u32[]{:S(2)}) copy-start(bf16[128,128]{1,0:T(8,128)(2,1)} %gate_hbm.3) | copy-start | bytes 98308
  2.6 7.4 %copy-start.2 = (bf16[128,128]{1,0:T(8,128)(2,1)S(1)}, bf16[128,128]{1,0:T(8,128)(2,1)}, u32[]{:S(2)}) copy-start(bf16[128,128]{1,0:T(8,128)(2,1)} %proj_hbm.3) | copy-start | bytes 98308
  2.6 18.1 %all-to-all-start = ((bf16[32,32,128]{2,1,0:T(8,128)(2,1)}), bf16[32,32,128]{2,1,0:T(8,128)(2,1)S(1)}, u32[]{:S(2)}, u32[]{:S(2)}) async-start(bf16[32,32,128]{2,1,0:T(8,128)(2,1)} %get-tuple-element.16), calls=%async_computation | async-start | bytes 524288 | tf_op jit(solution)/shard_map/all_to_all | solution.py:379
  9.9 0.7 %copy-start.3 = (f32[128]{0:T(128)S(1)}, f32[128]{0:T(128)}, u32[]{:S(2)}) copy-start(f32[128]{0:T(128)} %param.16) | copy-start | bytes 1540
  10.0 0.7 %copy-start.4 = (f32[128]{0:T(128)S(1)}, f32[128]{0:T(128)}, u32[]{:S(2)}) copy-start(f32[128]{0:T(128)} %param.17) | copy-start | bytes 1540

commit v7 on v6

--- a/solution.py
+++ b/solution.py
@@ -111,6 +111,15 @@
     for copy in copies:
         copy.start()
     return copies
+
+
+def sigmoid(halved):
+    return 0.5 + 0.5 * jnp.tanh(halved)
+
+
+def column(row_ref):
+    a, b = iota2((LANES, LANES))
+    return jnp.sum(jnp.where(a == b, row_ref[...], 0.0), axis=1, keepdims=True)
 
 
 def exchange_blocks(arrays, cols):
@@ -159,14 +168,19 @@
     inner = LANES // cols
     groups = rows // inner
     chunks = sent_ref.shape[0]
-    some = LANES // rows
-    out, source = iota2((LANES, LANES))
+    some = 16
+    out, source = iota2((some * rows, some * rows))
     order = one_hot((out // rows == source % some) & (out % rows == source // some))
+    a, b = iota2((channels, channels))
+    eye = one_hot(a == b)
     cell = lax.broadcasted_iota(jnp.int32, (1, cells), 1)
     for copy in copies:
         copy.wait()
-    flat = pair_ref[...].reshape(cells, channels).astype(F32)
-    normed = layer_norm(flat, gain_ref[...], bias_ref[...]).astype(BF16)
+    flat = dot(eye, pair_ref[...].reshape(cells, channels), 1, 1)
+    centered = flat - jnp.mean(flat, axis=0, keepdims=True)
+    variance = jnp.mean(centered * centered, axis=0, keepdims=True)
+    normed = centered * lax.rsqrt(variance + 1e-05) * column(gain_ref) + column(bias_ref)
+    normed = normed.astype(BF16)
     normed_ref[...] = normed
     results = [pltpu.make_async_copy(normed_ref, normed_hbm, out_sems.at[0])]
     results[0].start()
@@ -181,9 +195,9 @@
     col_ok = valid(lax.axis_index("col") * cols + cell % cols)
     mask = jnp.where(row_ok & col_ok, 1.0, 0.0)
 
-    values = dot(proj_ref[...], normed, 0, 1)
-    gates = dot(gate_ref[...], normed, 0, 1)
-    mixed = jax.nn.sigmoid(gates) * values * mask
+    values = dot(proj_ref[...], normed, 0, 0)
+    gates = dot(gate_ref[...] * 0.5, normed, 0, 0)
+    mixed = (sigmoid(gates) * values * mask).astype(BF16)
 
     by_row = []
     for side in range(2):
@@ -205,7 +219,7 @@
         for side in range(2):
             stack = jnp.concatenate(
                 [line[part * some : (part + 1) * some] for line in by_row[side]], axis=0
-            ).astype(BF16)
+            )
             moved = dot(order, stack).astype(BF16)
             sent_ref[here, side * rows : (side + 1) * rows] = moved.reshape(some, rows, LANES)
         results.append(
@@ -275,11 +289,9 @@
     )
     for copy in copies:
         copy.wait()
-    open_ref[...] = jax.nn.sigmoid(dot(normed_ref[...], gate_ref[...]))
-    a, b = iota2(gain_out.shape)
-    for source, target in ((gain_ref, gain_out), (bias_ref, bias_out)):
-        column = jnp.sum(jnp.where(a == b, source[...], 0.0), axis=1, keepdims=True)
-        target[...] = jnp.broadcast_to(column, target.shape)
+    open_ref[...] = sigmoid(dot(normed_ref[...], gate_ref[...] * 0.5, 0, 0))
+    gain_out[...] = jnp.broadcast_to(column(gain_ref), gain_out.shape)
+    bias_out[...] = jnp.broadcast_to(column(bias_ref), bias_out.shape)
 
 
 def update_kernel(
@@ -289,11 +301,11 @@
     chunks = got_ref.shape[0]
     inner = LANES // cols
     groups = rows // inner
-    some = LANES // rows
-    out, source = iota2((LANES, LANES))
+    some = 16
+    out, source = iota2((some * rows, some * rows))
     order = one_hot((out // some == source % rows) & (out % some == source // rows))
     parts = [
-        dot(order, got_ref[part * some : (part + 1) * some].reshape(LANES, LANES))
+        dot(order, got_ref[part * some : (part + 1) * some].reshape(some * rows, LANES)).astype(BF16)
         for part in range(chunks // some)
     ]
     lines = [
@@ -305,7 +317,7 @@
     for g in range(groups):
         values = jnp.concatenate(
             exchange_blocks(lines[g * inner : (g + 1) * inner], cols), axis=0
-        )
+        ).astype(F32)
         mean = jnp.mean(values, axis=0, keepdims=True)
         centered = values - mean
         variance = jnp.mean(centered * centered, axis=0, keepdims=True)
@@ -349,7 +361,7 @@
         functools.partial(mix_kernel, slots),
         out_shape=(
             jax.ShapeDtypeStruct((devices, 2 * rows, LANES), BF16),
-            jax.ShapeDtypeStruct((rows * cols, channels), BF16),
+            jax.ShapeDtypeStruct((channels, rows * cols), BF16),
         ),
         in_specs=[HBM] * 6,
         out_specs=(HBM, HBM),
@@ -361,9 +373,9 @@
             pltpu.VMEM(proj_in.shape, BF16),
             pltpu.VMEM(gate_in.shape, BF16),
             pltpu.VMEM((devices, 2 * rows, LANES), BF16),
-            pltpu.VMEM((rows * cols, channels), BF16),
+            pltpu.VMEM((channels, rows * cols), BF16),
             pltpu.SemaphoreType.DMA((6,)),
-            pltpu.SemaphoreType.DMA((1 + devices * rows // LANES,)),
+            pltpu.SemaphoreType.DMA((1 + devices // 16,)),
         ],
         compiler_params=FETCHING,
         name="mix",
@@ -438,9 +450,7 @@
             and inner * devices == hidden
             and rows % 16 == 0
             and rows % inner == 0
-            and LANES % rows == 0
-            and devices * rows % LANES == 0
-            and LANES // rows % 8 == 0
+            and devices % 16 == 0
         )
 
     def call(*arrays):

time: 32 us -> 32.2 us (level)
  no operation moved by 1% of the time
where the time goes in v7:
time: 32.2 us; the launch traced here: 31.9 us
  waiting for transfers between devices  9.77 us (30%)
  blocking collectives  9.45 us (29%)
  starting transfers between devices  7.3 us (23%)
  Pallas kernels  4.65 us (14%)
  local copies, waits for them, and re-layouts  0.65 us (2%)
    all_to_all x1, waiting for transfers between devices, exchanged(): got = lax.all_to_all(sent, order, 0, 0, tiled=True)  9.77 us
    all_to_all x1, blocking collectives, exchanged(): mine = lax.all_to_all(sums, order, 0, 0, tiled=True)  9.45 us
    all_to_all x1, starting transfers between devices, exchanged(): got = lax.all_to_all(sent, order, 0, 0, tiled=True)  7.3 us
    pallas_call x1, Pallas kernels, exchanged(): pl.pallas_call(functools.partial(mix_kernel, slots), out_shape=(jax.Shape...  2.74 us
    pallas_call x1, Pallas kernels, exchanged(): pl.pallas_call(update_kernel, out_shape=jax.ShapeDtypeStruct((rows, cols,...  1.28 us
    unnamed x10, local copies, waits for them, and re-layouts  0.65 us
  transfers between devices with their start and end apart: 1, of which 1 were waited for; matrix products, arithmetic and copies ran while one was open for 0% of the time, Pallas kernels for 1%

profile of v7, /device:TPU:0, one launch (start us, length us, event | category | flops | bytes accessed | tf_op | source)
XLA Modules:
  0.0 31.9 jit_solution(2888538741628275883)
XLA Ops:
  0.0 2.7 %mix.1 = (bf16[32,32,128]{2,1,0:T(8,128)(2,1)}, bf16[128,512]{1,0:T(8,128)(2,1)}) custom-call(s32[8]{0:T(128)} %chain_hbm.1, bf16[16,32,128]{2,1,0:T(8,128)(2,1)} %pair_hbm.1, f32[1,128]{1,0:T(1,128)} %bitcast.6, f32[1,128]{1,0:T(1,128)} %bitcast.7, bf16[128,256]{1,0:T(8,128)(2,1)} %proj_hbm.2, bf16[128,256]{1,0:T(8,128)(2,1)} %gate_hbm.2), custom_call_target="tpu_custom_call" | custom-call | tf_op jit(solution)/shard_map/mix/pallas_call | solution.py:360
  2.7 0.0 copy-start
  2.8 0.0 copy-start.1
  2.8 0.0 copy-start.2
  2.8 7.3 %all-to-all-start = ((bf16[32,32,128]{2,1,0:T(8,128)(2,1)}), bf16[32,32,128]{2,1,0:T(8,128)(2,1)S(1)}, u32[]{:S(2)}, u32[]{:S(2)}) async-start(bf16[32,32,128]{2,1,0:T(8,128)(2,1)} %get-tuple-element.16), calls=%async_computation | async-start | bytes 524288 | tf_op jit(solution)/shard_map/all_to_all | solution.py:391
  10.1 0.0 copy-start.3
  10.1 0.0 copy-start.4
  10.1 0.0 copy-done
  10.1 0.0 copy-done.1
  10.1 0.0 copy-done.2
  10.2 0.6 %copy-done.3 = f32[128]{0:T(128)S(1)} copy-done((f32[128]{0:T(128)S(1)}, f32[128]{0:T(128)}, u32[]{:S(2)}) %copy-start.3) | copy-done | bytes 536
  10.8 0.0 copy-done.4
  10.8 0.3 gate.1
  11.1 9.8 %all-to-all-done.got_ref = bf16[32,32,128]{2,1,0:T(8,128)(2,1)S(1)} async-done(((bf16[32,32,128]{2,1,0:T(8,128)(2,1)}), bf16[32,32,128]{2,1,0:T(8,128)(2,1)S(1)}, u32[]{:S(2)}, u32[]{:S(2)}) %all-to-all-start) | async-done | bytes 262176 | tf_op jit(solution)/shard_map/all_to_all | solution.py:391
  20.9 0.3 triangle.1
  21.2 9.5 %all_to_all.10.got_ref = bf16[32,16,128]{2,1,0:T(8,128)(2,1)S(1)} all-to-all(bf16[32,16,128]{2,1,0:T(8,128)(2,1)S(1)} %triangle.1), channel_id=1, replica_groups=mesh['high'=4,'low'=2,'col'=4] {'col','low','high'}, dimensions={0} | all-to-all | bytes 262144 | tf_op jit(solution)/shard_map/all_to_all | solution.py:420
  30.6 1.3 %update.1 = bf16[16,32,128]{2,1,0:T(8,128)(2,1)} custom-call(bf16[32,16,128]{2,1,0:T(8,128)(2,1)S(1)} %all_to_all.10.got_ref, f32[512,128]{1,0:T(8,128)S(1)} %get-tuple-element.23.open_ref, f32[128,128]{1,0:T(8,128)S(1)} %get-tuple-element.24.gain_ref, f32[128,128]{1,0:T(8,128)S(1)} %get-tuple-element.25.bias_ref, ...), custom_call_target="tpu_custom_call" | custom-call | tf_op jit(solution)/shard_map/update/pallas_call | solution.py:421
Async XLA Ops:
  2.7 7.4 %copy-start = (bf16[128,512]{1,0:T(8,128)(2,1)S(1)}, bf16[128,512]{1,0:T(8,128)(2,1)}, u32[]{:S(2)}) copy-start(bf16[128,512]{1,0:T(8,128)(2,1)} %get-tuple-element.17.normed_ref) | copy-start | bytes 393220
  2.8 7.4 %copy-start.1 = (bf16[128,128]{1,0:T(8,128)(2,1)S(1)}, bf16[128,128]{1,0:T(8,128)(2,1)}, u32[]{:S(2)}) copy-start(bf16[128,128]{1,0:T(8,128)(2,1)} %gate_hbm.3) | copy-start | bytes 98308
  2.8 7.4 %copy-start.2 = (bf16[128,128]{1,0:T(8,128)(2,1)S(1)}, bf16[128,128]{1,0:T(8,128)(2,1)}, u32[]{:S(2)}) copy-start(bf16[128,128]{1,0:T(8,128)(2,1)} %proj_hbm.3) | copy-start | bytes 98308
  2.8 18.1 %all-to-all-start = ((bf16[32,32,128]{2,1,0:T(8,128)(2,1)}), bf16[32,32,128]{2,1,0:T(8,128)(2,1)S(1)}, u32[]{:S(2)}, u32[]{:S(2)}) async-start(bf16[32,32,128]{2,1,0:T(8,128)(2,1)} %get-tuple-element.16), calls=%async_computation | async-start | bytes 524288 | tf_op jit(solution)/shard_map/all_to_all | solution.py:391
  10.1 0.7 %copy-start.3 = (f32[128]{0:T(128)S(1)}, f32[128]{0:T(128)}, u32[]{:S(2)}) copy-start(f32[128]{0:T(128)} %param.16) | copy-start | bytes 1540
  10.1 0.7 %copy-start.4 = (f32[128]{0:T(128)S(1)}, f32[128]{0:T(128)}, u32[]{:S(2)}) copy-start(f32[128]{0:T(128)} %param.17) | copy-start | bytes 1540

commit v8 on v7

--- a/solution.py
+++ b/solution.py
@@ -191,7 +191,7 @@
             length = jnp.where(token // slots == chain, chain_ref[chain], length)
         return token % slots < length
 
-    row_ok = valid(lax.axis_index(("high", "low")) * rows + cell // cols)
+    row_ok = valid(lax.axis_index("row") * rows + cell // cols)
     col_ok = valid(lax.axis_index("col") * cols + cell % cols)
     mask = jnp.where(row_ok & col_ok, 1.0, 0.0)
 
@@ -230,12 +230,11 @@
         copy.wait()
 
 
-def triangle_kernel(split, grid_cols, rows, cols, got_ref, sent_ref):
+def triangle_kernel(order, grid_rows, grid_cols, rows, cols, got_ref, sent_ref):
     inner = LANES // cols
 
     def place(r, c):
-        z, y = r // split[1], r % split[1]
-        return (c * split[1] + y) * split[0] + z
+        return order.index(r * grid_cols + c)
 
     def side(which):
         return jnp.concatenate(
@@ -243,7 +242,7 @@
                 jnp.concatenate(
                     [
                         got_ref[place(r, c), which * rows : (which + 1) * rows]
-                        for r in range(split[0] * split[1])
+                        for r in range(grid_rows)
                     ],
                     axis=0,
                 )
@@ -265,7 +264,7 @@
     )
     sums = dot(left, right_by, 1, 1).astype(BF16)
     for c in range(grid_cols):
-        for r in range(split[0] * split[1]):
+        for r in range(grid_rows):
             sent_ref[place(r, c)] = sums[r * rows : (r + 1) * rows, c * LANES : (c + 1) * LANES]
 
 
@@ -339,7 +338,7 @@
 
 
 def exchanged(
-    split,
+    grid_rows,
     grid_cols,
     pair,
     chain_lengths,
@@ -354,7 +353,6 @@
 ):
     rows, cols, channels = pair.shape
     hidden = proj_out.shape[0]
-    grid_rows = split[0] * split[1]
     devices = grid_rows * grid_cols
     slots = rows * grid_rows // chain_lengths.shape[0]
     sent, normed = pl.pallas_call(
@@ -387,8 +385,14 @@
         proj_in,
         gate_in,
     )
-    order = ("col", "low", "high")
-    got = lax.all_to_all(sent, order, 0, 0, tiled=True)
+    order = list(range(devices - 1, -1, -1))
+
+    def exchange(chunks):
+        return lax.all_to_all(
+            chunks, ("row", "col"), 0, 0, tiled=True, axis_index_groups=[order]
+        )
+
+    got = exchange(sent)
     opened, gain, bias, proj = pl.pallas_call(
         gate_kernel,
         out_shape=(
@@ -410,14 +414,14 @@
     )(normed, gate_out, norm_out_gain.reshape(1, hidden), norm_out_bias.reshape(1, hidden), proj_out)
     got, opened, gain, bias, proj = lax.optimization_barrier((got, opened, gain, bias, proj))
     sums = pl.pallas_call(
-        functools.partial(triangle_kernel, split, grid_cols, rows, cols),
+        functools.partial(triangle_kernel, order, grid_rows, grid_cols, rows, cols),
         out_shape=jax.ShapeDtypeStruct((devices, rows, LANES), BF16),
         in_specs=[VMEM],
         out_specs=VMEM,
         compiler_params=PARAMS,
         name="triangle",
     )(got)
-    mine = lax.all_to_all(sums, order, 0, 0, tiled=True)
+    mine = exchange(sums)
     return pl.pallas_call(
         update_kernel,
         out_shape=jax.ShapeDtypeStruct((rows, cols, channels), BF16),
@@ -434,11 +438,6 @@
 
 def solution(mesh):
     grid_rows, grid_cols = mesh.shape["row"], mesh.shape["col"]
-    split = (grid_rows // 2, 2)
-    fine = jax.sharding.Mesh(
-        mesh.devices.reshape(split + (grid_cols,)), ("high", "low", "col")
-    )
-
     def fits(rows, cols, channels, hidden):
         devices = grid_rows * grid_cols
         inner = LANES // cols
@@ -458,10 +457,10 @@
         hidden = arrays[8].shape[0]
         if fits(tokens // grid_rows, others // grid_cols, channels, hidden):
             return jax.shard_map(
-                functools.partial(exchanged, split, grid_cols),
-                mesh=fine,
-                in_specs=(P(("high", "low"), "col", None),) + (P(),) * 9,
-                out_specs=P(("high", "low"), "col", None),
+                functools.partial(exchanged, grid_rows, grid_cols),
+                mesh=mesh,
+                in_specs=(P("row", "col", None),) + (P(),) * 9,
+                out_specs=P("row", "col", None),
                 check_vma=False,
             )(*arrays)
         return jax.shard_map(

time: 32.2 us -> 32.6 us (1.012)
  blocking collectives: 9.45 us -> 10.8 us
  waiting for transfers between devices: 9.77 us -> 8.93 us
    all_to_all x1, blocking collectives: 9.45 us -> 10.8 us  [exchange(): lax.all_to_all(chunks, ('row', 'col'), 0, 0, tiled=True, axis_index_group...]
    all_to_all x1, waiting for transfers between devices: 9.77 us -> 8.93 us  [exchange(): lax.all_to_all(chunks, ('row', 'col'), 0, 0, tiled=True, axis_index_group...]
where the time goes in v8:
time: 32.6 us; the launch traced here: 32.4 us
  blocking collectives  10.8 us (33%)
  waiting for transfers between devices  8.93 us (27%)
  starting transfers between devices  7.3 us (22%)
  Pallas kernels  4.65 us (14%)
  local copies, waits for them, and re-layouts  0.65 us (2%)
    all_to_all x1, blocking collectives, exchange(): lax.all_to_all(chunks, ('row', 'col'), 0, 0, tiled=True, axis_index_group...  10.8 us
    all_to_all x1, waiting for transfers between devices, exchange(): lax.all_to_all(chunks, ('row', 'col'), 0, 0, tiled=True, axis_index_group...  8.93 us
    all_to_all x1, starting transfers between devices, exchange(): lax.all_to_all(chunks, ('row', 'col'), 0, 0, tiled=True, axis_index_group...  7.3 us
    pallas_call x1, Pallas kernels, exchanged(): pl.pallas_call(functools.partial(mix_kernel, slots), out_shape=(jax.Shape...  2.74 us
    pallas_call x1, Pallas kernels, exchanged(): pl.pallas_call(update_kernel, out_shape=jax.ShapeDtypeStruct((rows, cols,...  1.28 us
  transfers between devices with their start and end apart: 1, of which 1 were waited for; matrix products, arithmetic and copies ran while one was open for 0% of the time, Pallas kernels for 1%

profile of v8, /device:TPU:0, one launch (start us, length us, event | category | flops | bytes accessed | tf_op | source)
XLA Modules:
  0.0 32.4 jit_solution(12297166842951944434)
XLA Ops:
  0.0 2.7 %mix.1 = (bf16[32,32,128]{2,1,0:T(8,128)(2,1)}, bf16[128,512]{1,0:T(8,128)(2,1)}) custom-call(s32[8]{0:T(128)} %chain_hbm.1, bf16[16,32,128]{2,1,0:T(8,128)(2,1)} %pair_hbm.1, f32[1,128]{1,0:T(1,128)} %bitcast.6, f32[1,128]{1,0:T(1,128)} %bitcast.7, bf16[128,256]{1,0:T(8,128)(2,1)} %proj_hbm.2, bf16[128,256]{1,0:T(8,128)(2,1)} %gate_hbm.2), custom_call_target="tpu_custom_call" | custom-call | tf_op jit(solution)/shard_map/mix/pallas_call | solution.py:358
  2.7 0.0 copy-start
  2.8 0.0 copy-start.1
  2.8 0.0 copy-start.2
  2.8 7.3 %all-to-all-start = ((bf16[32,32,128]{2,1,0:T(8,128)(2,1)}), bf16[32,32,128]{2,1,0:T(8,128)(2,1)S(1)}, u32[]{:S(2)}, u32[]{:S(2)}) async-start(bf16[32,32,128]{2,1,0:T(8,128)(2,1)} %get-tuple-element.16), calls=%async_computation | async-start | bytes 524288 | tf_op jit(solution)/shard_map/all_to_all | solution.py:391
  10.1 0.0 copy-start.3
  10.1 0.0 copy-start.4
  10.1 0.0 copy-done
  10.1 0.0 copy-done.1
  10.1 0.0 copy-done.2
  10.2 0.6 %copy-done.3 = f32[128]{0:T(128)S(1)} copy-done((f32[128]{0:T(128)S(1)}, f32[128]{0:T(128)}, u32[]{:S(2)}) %copy-start.3) | copy-done | bytes 536
  10.8 0.0 copy-done.4
  10.8 0.3 gate.1
  11.1 8.9 %all-to-all-done.got_ref = bf16[32,32,128]{2,1,0:T(8,128)(2,1)S(1)} async-done(((bf16[32,32,128]{2,1,0:T(8,128)(2,1)}), bf16[32,32,128]{2,1,0:T(8,128)(2,1)S(1)}, u32[]{:S(2)}, u32[]{:S(2)}) %all-to-all-start) | async-done | bytes 262176 | tf_op jit(solution)/shard_map/all_to_all | solution.py:391
  20.0 0.3 triangle.1
  20.4 10.8 %all_to_all.10.got_ref = bf16[32,16,128]{2,1,0:T(8,128)(2,1)S(1)} all-to-all(bf16[32,16,128]{2,1,0:T(8,128)(2,1)S(1)} %triangle.1), channel_id=1, replica_groups={{31,30,29,28,27,26,25,24,23,22,21,20,19,18,17,16,15,14,13,12,11,10,9,8,..., dimensions={0} | all-to-all | bytes 262144 | tf_op jit(solution)/shard_map/all_to_all | solution.py:391
  31.1 1.3 %update.1 = bf16[16,32,128]{2,1,0:T(8,128)(2,1)} custom-call(bf16[32,16,128]{2,1,0:T(8,128)(2,1)S(1)} %all_to_all.10.got_ref, f32[512,128]{1,0:T(8,128)S(1)} %get-tuple-element.23.open_ref, f32[128,128]{1,0:T(8,128)S(1)} %get-tuple-element.24.gain_ref, f32[128,128]{1,0:T(8,128)S(1)} %get-tuple-element.25.bias_ref, ...), custom_call_target="tpu_custom_call" | custom-call | tf_op jit(solution)/shard_map/update/pallas_call | solution.py:425
Async XLA Ops:
  2.7 7.4 %copy-start = (bf16[128,512]{1,0:T(8,128)(2,1)S(1)}, bf16[128,512]{1,0:T(8,128)(2,1)}, u32[]{:S(2)}) copy-start(bf16[128,512]{1,0:T(8,128)(2,1)} %get-tuple-element.17.normed_ref) | copy-start | bytes 393220
  2.8 7.4 %copy-start.1 = (bf16[128,128]{1,0:T(8,128)(2,1)S(1)}, bf16[128,128]{1,0:T(8,128)(2,1)}, u32[]{:S(2)}) copy-start(bf16[128,128]{1,0:T(8,128)(2,1)} %gate_hbm.3) | copy-start | bytes 98308
  2.8 7.4 %copy-start.2 = (bf16[128,128]{1,0:T(8,128)(2,1)S(1)}, bf16[128,128]{1,0:T(8,128)(2,1)}, u32[]{:S(2)}) copy-start(bf16[128,128]{1,0:T(8,128)(2,1)} %proj_hbm.3) | copy-start | bytes 98308
  2.8 17.2 %all-to-all-start = ((bf16[32,32,128]{2,1,0:T(8,128)(2,1)}), bf16[32,32,128]{2,1,0:T(8,128)(2,1)S(1)}, u32[]{:S(2)}, u32[]{:S(2)}) async-start(bf16[32,32,128]{2,1,0:T(8,128)(2,1)} %get-tuple-element.16), calls=%async_computation | async-start | bytes 524288 | tf_op jit(solution)/shard_map/all_to_all | solution.py:391
  10.1 0.7 %copy-start.3 = (f32[128]{0:T(128)S(1)}, f32[128]{0:T(128)}, u32[]{:S(2)}) copy-start(f32[128]{0:T(128)} %param.16) | copy-start | bytes 1540
  10.1 0.7 %copy-start.4 = (f32[128]{0:T(128)S(1)}, f32[128]{0:T(128)}, u32[]{:S(2)}) copy-start(f32[128]{0:T(128)} %param.17) | copy-start | bytes 1540

commit v9 on v8

--- a/solution.py
+++ b/solution.py
@@ -7,6 +7,7 @@
 from jax.sharding import PartitionSpec as P
 
 LANES = 128
+SOME = 16
 F32 = jnp.float32
 BF16 = jnp.bfloat16
 
@@ -136,8 +137,48 @@
     return arrays
 
 
-def mix_kernel(
+def cell_mask(chain_ref, slots, rows, cols):
+    cell = lax.broadcasted_iota(jnp.int32, (1, rows * cols), 1)
+
+    def valid(token):
+        length = jnp.zeros_like(token)
+        for chain in range(chain_ref.shape[0]):
+            length = jnp.where(token // slots == chain, chain_ref[chain], length)
+        return token % slots < length
+
+    row_ok = valid(lax.axis_index("row") * rows + cell // cols)
+    col_ok = valid(lax.axis_index("col") * cols + cell % cols)
+    return jnp.where(row_ok & col_ok, 1.0, 0.0)
+
+
+def chunks_of(normed, proj, gate, mask, rows, cols):
+    hidden = proj.shape[1]
+    inner = LANES // cols
+    chunks = hidden // inner
+    out, source = iota2((SOME * rows, SOME * rows))
+    order = one_hot((out // rows == source % SOME) & (out % rows == source // SOME))
+    values = dot(proj, normed, 0, 0)
+    gates = dot(gate * 0.5, normed, 0, 0)
+    mixed = (sigmoid(gates) * values * mask).astype(BF16)
+    lines = []
+    for g in range(rows // inner):
+        lines += exchange_blocks(
+            [
+                mixed[n * chunks : (n + 1) * chunks, g * LANES : (g + 1) * LANES]
+                for n in range(inner)
+            ],
+            cols,
+        )
+    for part in range(chunks // SOME):
+        stack = jnp.concatenate(
+            [line[part * SOME : (part + 1) * SOME] for line in lines], axis=0
+        )
+        yield dot(order, stack).astype(BF16).reshape(SOME, rows, LANES)
+
+
+def right_kernel(
     slots,
+    halves,
     chain_hbm,
     pair_hbm,
     gain_hbm,
@@ -157,26 +198,27 @@
     sems,
     out_sems,
 ):
+    rows, cols, channels = pair_ref.shape
+    hidden = proj_ref.shape[1]
+    members = sent_ref.shape[0]
+    second = pl.ds(hidden, hidden)
     copies = fetch(
-        (pair_hbm, gain_hbm, bias_hbm, chain_hbm, proj_hbm, gate_hbm),
+        (
+            pair_hbm,
+            gain_hbm,
+            bias_hbm,
+            chain_hbm,
+            proj_hbm.at[:, second],
+            gate_hbm.at[:, second],
+        ),
         (pair_ref, gain_ref, bias_ref, chain_ref, proj_ref, gate_ref),
         sems,
     )
-    rows, cols, channels = pair_ref.shape
-    hidden = proj_ref.shape[1] // 2
-    cells = rows * cols
-    inner = LANES // cols
-    groups = rows // inner
-    chunks = sent_ref.shape[0]
-    some = 16
-    out, source = iota2((some * rows, some * rows))
-    order = one_hot((out // rows == source % some) & (out % rows == source // some))
     a, b = iota2((channels, channels))
     eye = one_hot(a == b)
-    cell = lax.broadcasted_iota(jnp.int32, (1, cells), 1)
     for copy in copies:
         copy.wait()
-    flat = dot(eye, pair_ref[...].reshape(cells, channels), 1, 1)
+    flat = dot(eye, pair_ref[...].reshape(rows * cols, channels), 1, 1)
     centered = flat - jnp.mean(flat, axis=0, keepdims=True)
     variance = jnp.mean(centered * centered, axis=0, keepdims=True)
     normed = centered * lax.rsqrt(variance + 1e-05) * column(gain_ref) + column(bias_ref)
@@ -184,65 +226,65 @@
     normed_ref[...] = normed
     results = [pltpu.make_async_copy(normed_ref, normed_hbm, out_sems.at[0])]
     results[0].start()
-
-    def valid(token):
-        length = jnp.zeros_like(token)
-        for chain in range(chain_ref.shape[0]):
-            length = jnp.where(token // slots == chain, chain_ref[chain], length)
-        return token % slots < length
-
-    row_ok = valid(lax.axis_index("row") * rows + cell // cols)
-    col_ok = valid(lax.axis_index("col") * cols + cell % cols)
-    mask = jnp.where(row_ok & col_ok, 1.0, 0.0)
-
-    values = dot(proj_ref[...], normed, 0, 0)
-    gates = dot(gate_ref[...] * 0.5, normed, 0, 0)
-    mixed = (sigmoid(gates) * values * mask).astype(BF16)
-
-    by_row = []
-    for side in range(2):
-        lines = []
-        for g in range(groups):
-            lines += exchange_blocks(
-                [
-                    mixed[
-                        side * hidden + n * chunks : side * hidden + (n + 1) * chunks,
-                        g * LANES : (g + 1) * LANES,
-                    ]
-                    for n in range(inner)
-                ],
-                cols,
+    mask = cell_mask(chain_ref, slots, rows, cols)
+    blocks = chunks_of(normed, proj_ref[...], gate_ref[...], mask, rows, cols)
+    for part, block in enumerate(blocks):
+        first, sub = part * SOME % members, part * SOME // members
+        here = (pl.ds(first, SOME), pl.ds(sub * rows, rows))
+        sent_ref[here] = block
+        for half in range(halves):
+            there = (pl.ds(half * members + first, SOME), here[1])
+            results.append(
+                pltpu.make_async_copy(
+                    sent_ref.at[here], sent_hbm.at[there], out_sems.at[len(results)]
+                )
             )
-        by_row.append(lines)
-    for part in range(chunks // some):
-        here = pl.ds(part * some, some)
-        for side in range(2):
-            stack = jnp.concatenate(
-                [line[part * some : (part + 1) * some] for line in by_row[side]], axis=0
-            )
-            moved = dot(order, stack).astype(BF16)
-            sent_ref[here, side * rows : (side + 1) * rows] = moved.reshape(some, rows, LANES)
-        results.append(
-            pltpu.make_async_copy(sent_ref.at[here], sent_hbm.at[here], out_sems.at[part + 1])
-        )
-        results[-1].start()
+            results[-1].start()
     for copy in results:
         copy.wait()
 
 
-def triangle_kernel(order, grid_rows, grid_cols, rows, cols, got_ref, sent_ref):
+def left_kernel(
+    slots,
+    rows,
+    cols,
+    chain_ref,
+    normed_ref,
+    proj_ref,
+    gate_ref,
+    open_weight_ref,
+    gain_ref,
+    bias_ref,
+    sent_ref,
+    open_ref,
+    gain_out,
+    bias_out,
+):
+    hidden = proj_ref.shape[1] // 2
+    members = sent_ref.shape[0]
+    normed = normed_ref[...]
+    mask = cell_mask(chain_ref, slots, rows, cols)
+    blocks = chunks_of(normed, proj_ref[:, :hidden], gate_ref[:, :hidden], mask, rows, cols)
+    for part, block in enumerate(blocks):
+        first, sub = part * SOME % members, part * SOME // members
+        sent_ref[first : first + SOME, sub * rows : (sub + 1) * rows] = block
+    open_ref[...] = sigmoid(dot(normed, open_weight_ref[...] * 0.5, 0, 0))
+    gain_out[...] = jnp.broadcast_to(column(gain_ref), gain_out.shape)
+    bias_out[...] = jnp.broadcast_to(column(bias_ref), bias_out.shape)
+
+
+def triangle_kernel(grid_cols, rows, cols, left_ref, right_ref, sent_ref):
     inner = LANES // cols
-
-    def place(r, c):
-        return order.index(r * grid_cols + c)
-
-    def side(which):
+    lane = lax.broadcasted_iota(jnp.int32, (1, grid_cols * LANES), 1)
+    own = [one_hot(lane % LANES // cols == n) for n in range(inner)]
+
+    def whole(ref, sub):
         return jnp.concatenate(
             [
                 jnp.concatenate(
                     [
-                        got_ref[place(r, c), which * rows : (which + 1) * rows]
-                        for r in range(grid_rows)
+                        ref[r * grid_cols + c, sub * rows : (sub + 1) * rows]
+                        for r in range(ref.shape[0] // grid_cols)
                     ],
                     axis=0,
                 )
@@ -251,64 +293,44 @@
             axis=1,
         )
 
-    left, right = side(0), side(1)
-    lane = lax.broadcasted_iota(jnp.int32, (1, grid_cols * LANES), 1)
-    by_channel = [right * one_hot(lane % LANES // cols == n) for n in range(inner)]
-    right_by = jnp.concatenate(
-        [
-            by_channel[n][c * cols : (c + 1) * cols]
-            for c in range(grid_cols)
-            for n in range(inner)
-        ],
-        axis=0,
-    )
-    sums = dot(left, right_by, 1, 1).astype(BF16)
-    for c in range(grid_cols):
-        for r in range(grid_rows):
-            sent_ref[place(r, c)] = sums[r * rows : (r + 1) * rows, c * LANES : (c + 1) * LANES]
-
-
-def gate_kernel(
-    normed_ref,
-    gate_hbm,
-    gain_hbm,
-    bias_hbm,
-    proj_hbm,
-    open_ref,
-    gain_out,
-    bias_out,
-    proj_out,
-    gate_ref,
-    gain_ref,
-    bias_ref,
-    sems,
-):
-    copies = fetch(
-        (gate_hbm, gain_hbm, bias_hbm, proj_hbm), (gate_ref, gain_ref, bias_ref, proj_out), sems
-    )
-    for copy in copies:
-        copy.wait()
-    open_ref[...] = sigmoid(dot(normed_ref[...], gate_ref[...] * 0.5, 0, 0))
-    gain_out[...] = jnp.broadcast_to(column(gain_ref), gain_out.shape)
-    bias_out[...] = jnp.broadcast_to(column(bias_ref), bias_out.shape)
+    for sub in range(left_ref.shape[1] // rows):
+        right = whole(right_ref, sub)
+        by_channel = [right * mask for mask in own]
+        right_by = jnp.concatenate(
+            [
+                by_channel[n][c * cols : (c + 1) * cols]
+                for c in range(grid_cols)
+                for n in range(inner)
+            ],
+            axis=0,
+        )
+        sums = dot(whole(left_ref, sub), right_by, 1, 1).astype(BF16)
+        for r in range(left_ref.shape[0] // grid_cols):
+            for c in range(grid_cols):
+                sent_ref[r * grid_cols + c, sub * rows : (sub + 1) * rows] = sums[
+                    r * rows : (r + 1) * rows, c * LANES : (c + 1) * LANES
+                ]
 
 
 def update_kernel(
     got_ref, open_ref, gain_ref, bias_ref, proj_ref, out_hbm, out_ref, out_sems
 ):
     rows, cols, channels = out_ref.shape
-    chunks = got_ref.shape[0]
+    members = got_ref.shape[0]
     inner = LANES // cols
     groups = rows // inner
-    some = 16
-    out, source = iota2((some * rows, some * rows))
-    order = one_hot((out // some == source % rows) & (out % some == source // rows))
+    out, source = iota2((SOME * rows, SOME * rows))
+    order = one_hot((out // SOME == source % rows) & (out % SOME == source // rows))
     parts = [
-        dot(order, got_ref[part * some : (part + 1) * some].reshape(some * rows, LANES)).astype(BF16)
-        for part in range(chunks // some)
+        dot(
+            order,
+            got_ref[first : first + SOME, sub * rows : (sub + 1) * rows].reshape(-1, LANES),
+        ).astype(BF16)
+        for sub in range(got_ref.shape[1] // rows)
+        for first in range(0, members, SOME)
     ]
     lines = [
-        jnp.concatenate([part[row * some : (row + 1) * some] for part in parts], axis=0)
+        jnp.concatenate([part[row * SOME : (row + 1) * SOME] for part in parts], axis=0)
         for row in range(rows)
     ]
     gain, bias = gain_ref[...], bias_ref[...]
@@ -332,6 +354,7 @@
 
 
 VMEM = pl.BlockSpec(memory_space=pltpu.VMEM)
+SMEM = pl.BlockSpec(memory_space=pltpu.SMEM)
 HBM = pl.BlockSpec(memory_space=pltpu.HBM)
 PARAMS = pltpu.CompilerParams(vmem_limit_bytes=32 * 1024 * 1024)
 FETCHING = pltpu.CompilerParams(vmem_limit_bytes=60 * 1024 * 1024)
@@ -340,6 +363,7 @@
 def exchanged(
     grid_rows,
     grid_cols,
+    halves,
     pair,
     chain_lengths,
     norm_in_gain,
@@ -354,11 +378,20 @@
     rows, cols, channels = pair.shape
     hidden = proj_out.shape[0]
     devices = grid_rows * grid_cols
+    members = devices // halves
     slots = rows * grid_rows // chain_lengths.shape[0]
-    sent, normed = pl.pallas_call(
-        functools.partial(mix_kernel, slots),
+    chunk = (halves * rows, LANES)
+
+    def exchange(chunks, groups):
+        return lax.all_to_all(
+            chunks, ("row", "col"), 0, 0, tiled=True, axis_index_groups=groups
+        )
+
+    by_half = [list(range(h * members, (h + 1) * members)) for h in range(halves)]
+    right, normed = pl.pallas_call(
+        functools.partial(right_kernel, slots, halves),
         out_shape=(
-            jax.ShapeDtypeStruct((devices, 2 * rows, LANES), BF16),
+            jax.ShapeDtypeStruct((devices,) + chunk, BF16),
             jax.ShapeDtypeStruct((channels, rows * cols), BF16),
         ),
         in_specs=[HBM] * 6,
@@ -368,15 +401,15 @@
             pltpu.VMEM(pair.shape, BF16),
             pltpu.VMEM((1, channels), F32),
             pltpu.VMEM((1, channels), F32),
-            pltpu.VMEM(proj_in.shape, BF16),
-            pltpu.VMEM(gate_in.shape, BF16),
-            pltpu.VMEM((devices, 2 * rows, LANES), BF16),
+            pltpu.VMEM((channels, hidden), BF16),
+            pltpu.VMEM((channels, hidden), BF16),
+            pltpu.VMEM((members,) + chunk, BF16),
             pltpu.VMEM((channels, rows * cols), BF16),
             pltpu.SemaphoreType.DMA((6,)),
-            pltpu.SemaphoreType.DMA((1 + devices // 16,)),
+            pltpu.SemaphoreType.DMA((1 + devices // SOME * halves,)),
         ],
         compiler_params=FETCHING,
-        name="mix",
+        name="right",
     )(
         chain_lengths,
         pair,
@@ -385,43 +418,38 @@
         proj_in,
         gate_in,
     )
-    order = list(range(devices - 1, -1, -1))
-
-    def exchange(chunks):
-        return lax.all_to_all(
-            chunks, ("row", "col"), 0, 0, tiled=True, axis_index_groups=[order]
-        )
-
-    got = exchange(sent)
-    opened, gain, bias, proj = pl.pallas_call(
-        gate_kernel,
+    got_right = exchange(right, None)
+    left, opened, gain, bias = pl.pallas_call(
+        functools.partial(left_kernel, slots, rows, cols),
         out_shape=(
+            jax.ShapeDtypeStruct((members,) + chunk, BF16),
             jax.ShapeDtypeStruct((rows * cols, channels), F32),
             jax.ShapeDtypeStruct((hidden, LANES), F32),
             jax.ShapeDtypeStruct((hidden, LANES), F32),
-            jax.ShapeDtypeStruct(proj_out.shape, BF16),
         ),
-        in_specs=[VMEM] + [HBM] * 4,
+        in_specs=[SMEM] + [VMEM] * 6,
         out_specs=[VMEM] * 4,
-        scratch_shapes=[
-            pltpu.VMEM(gate_out.shape, BF16),
-            pltpu.VMEM((1, hidden), F32),
-            pltpu.VMEM((1, hidden), F32),
-            pltpu.SemaphoreType.DMA((4,)),
-        ],
         compiler_params=PARAMS,
-        name="gate",
-    )(normed, gate_out, norm_out_gain.reshape(1, hidden), norm_out_bias.reshape(1, hidden), proj_out)
-    got, opened, gain, bias, proj = lax.optimization_barrier((got, opened, gain, bias, proj))
+        name="left",
+    )(
+        chain_lengths,
+        normed,
+        proj_in,
+        gate_in,
+        gate_out,
+        norm_out_gain.reshape(1, hidden),
+        norm_out_bias.reshape(1, hidden),
+    )
+    got_left = exchange(left, by_half)
     sums = pl.pallas_call(
-        functools.partial(triangle_kernel, order, grid_rows, grid_cols, rows, cols),
-        out_shape=jax.ShapeDtypeStruct((devices, rows, LANES), BF16),
-        in_specs=[VMEM],
+        functools.partial(triangle_kernel, grid_cols, rows, cols),
+        out_shape=jax.ShapeDtypeStruct((members,) + chunk, BF16),
+        in_specs=[VMEM] * 2,
         out_specs=VMEM,
         compiler_params=PARAMS,
         name="triangle",
-    )(got)
-    mine = exchange(sums)
+    )(got_left, got_right)
+    mine = exchange(sums, by_half)
     return pl.pallas_call(
         update_kernel,
         out_shape=jax.ShapeDtypeStruct((rows, cols, channels), BF16),
@@ -433,11 +461,13 @@
         ],
         compiler_params=PARAMS,
         name="update",
-    )(mine, opened, gain, bias, proj)
+    )(mine, opened, gain, bias, proj_out)
 
 
 def solution(mesh):
     grid_rows, grid_cols = mesh.shape["row"], mesh.shape["col"]
+    halves = 2
+
     def fits(rows, cols, channels, hidden):
         devices = grid_rows * grid_cols
         inner = LANES // cols
@@ -449,7 +479,8 @@
             and inner * devices == hidden
             and rows % 16 == 0
             and rows % inner == 0
-            and devices % 16 == 0
+            and grid_rows % halves == 0
+            and devices // halves % SOME == 0
         )
 
     def call(*arrays):
@@ -457,7 +488,7 @@
         hidden = arrays[8].shape[0]
         if fits(tokens // grid_rows, others // grid_cols, channels, hidden):
             return jax.shard_map(
-                functools.partial(exchanged, grid_rows, grid_cols),
+                functools.partial(exchanged, grid_rows, grid_cols, halves),
                 mesh=mesh,
                 in_specs=(P("row", "col", None),) + (P(),) * 9,
                 out_specs=P("row", "col", None),

time: 32.6 us -> 42.2 us (1.29)
  blocking collectives: 10.8 us -> 34.7 us
  waiting for transfers between devices: 8.93 us -> 0 us
  starting transfers between devices: 7.3 us -> 0 us
  Pallas kernels: 4.65 us -> 5.6 us
  local copies, waits for them, and re-layouts: 0.65 us -> 1.56 us
    all_to_all x1 -> x3, blocking collectives: 10.8 us -> 34.7 us  [exchange(): lax.all_to_all(chunks, ('row', 'col'), 0, 0, tiled=True, axis_index_group...]
    all_to_all x1 -> x0, waiting for transfers between devices: 8.93 us -> none  [exchange(): lax.all_to_all(chunks, ('row', 'col'), 0, 0, tiled=True, axis_index_group...]
    all_to_all x1 -> x0, starting transfers between devices: 7.3 us -> none  [exchange(): lax.all_to_all(chunks, ('row', 'col'), 0, 0, tiled=True, axis_index_group...]
    pallas_call x3, Pallas kernels: 3.37 us -> 4.32 us  [the longest x1 2.59 us: exchanged(): pl.pallas_call(functools.partial(right_kernel, slots, halves), out_shape=...]
    unnamed x10 -> x18, local copies, waits for them, and re-layouts: 0.65 us -> 1.56 us
  transfers between devices with their start and end apart: 1 -> 0, of which waited for: 1 -> 0; matrix products, arithmetic and copies ran while one was open for 0% -> 0% of each run, Pallas kernels for 1% -> 0%
where the time goes in v9:
time: 42.2 us; the launch traced here: 41.9 us
  blocking collectives  34.7 us (82%)
  Pallas kernels  5.6 us (13%)
  local copies, waits for them, and re-layouts  1.56 us (4%)
    all_to_all x3, blocking collectives, exchange(): lax.all_to_all(chunks, ('row', 'col'), 0, 0, tiled=True, axis_index_group...  34.7 us
    pallas_call x1, Pallas kernels, exchanged(): pl.pallas_call(functools.partial(right_kernel, slots, halves), out_shape=...  2.59 us
    unnamed x18, local copies, waits for them, and re-layouts  1.56 us
    pallas_call x1, Pallas kernels, exchanged(): pl.pallas_call(functools.partial(left_kernel, slots, rows, cols), out_sha...  1.29 us
    pallas_call x1, Pallas kernels, exchanged(): pl.pallas_call(update_kernel, out_shape=jax.ShapeDtypeStruct((rows, cols,...  1.28 us

profile of v9, /device:TPU:0, one launch (start us, length us, event | category | flops | bytes accessed | tf_op | source)
XLA Modules:
  0.0 41.9 jit_solution(5489006545529804979)
XLA Ops:
  0.0 0.0 copy-start
  0.0 0.0 copy-start.1
  0.0 0.0 copy-start.3
  0.0 2.6 %right.1 = (bf16[32,32,128]{2,1,0:T(8,128)(2,1)}, bf16[128,512]{1,0:T(8,128)(2,1)}) custom-call(s32[8]{0:T(128)} %chain_ref.1, bf16[16,32,128]{2,1,0:T(8,128)(2,1)} %pair_hbm.1, f32[1,128]{1,0:T(1,128)} %bitcast.6, f32[1,128]{1,0:T(1,128)} %bitcast.7, bf16[128,256]{1,0:T(8,128)(2,1)} %proj_ref.2, bf16[128,256]{1,0:T(8,128)(2,1)} %gate_ref.1), custom_call_target="tpu_custom_call" | custom-call | tf_op jit(solution)/shard_map/right/pallas_call | solution.py:391
  2.6 0.0 copy-start.5
  2.6 0.0 copy-start.6
  2.6 0.0 copy-start.7
  2.6 0.0 copy-done
  2.7 0.0 copy-done.1
  2.7 0.0 copy-done.3
  2.7 0.6 %copy-done.5 = s32[8]{0:T(128)S(1)} copy-done((s32[8]{0:T(128)S(1)}, s32[8]{0:T(128)}, u32[]{:S(2)}) %copy-start.5) | copy-done | bytes 56
  3.3 0.0 copy-done.6
  3.3 0.0 copy-done.7
  3.3 0.0 copy-start.2
  3.3 0.9 %copy-done.2 = bf16[128,512]{1,0:T(8,128)(2,1)S(1)} copy-done((bf16[128,512]{1,0:T(8,128)(2,1)S(1)}, bf16[128,512]{1,0:T(8,128)(2,1)}, u32[]{:S(2)}) %copy-start.2) | copy-done | bytes 131096
  4.2 0.0 copy-start.8
  4.2 1.3 %left.1 = (bf16[16,32,128]{2,1,0:T(8,128)(2,1)S(1)}, f32[512,128]{1,0:T(8,128)S(1)}, f32[128,128]{1,0:T(8,128)S(1)}, f32[128,128]{1,0:T(8,128)S(1)}) custom-call(s32[8]{0:T(128)S(1)} %copy-done.5, bf16[128,512]{1,0:T(8,128)(2,1)S(1)} %copy-done.2, bf16[128,256]{1,0:T(8,128)(2,1)S(1)} %copy-done, bf16[128,256]{1,0:T(8,128)(2,1)S(1)} %copy-done.1, ...), custom_call_target="tpu_custom_call" | custom-call | tf_op jit(solution)/shard_map/left/pallas_call | solution.py:422
  5.5 12.4 %all_to_all.15.left_ref = bf16[16,32,128]{2,1,0:T(8,128)(2,1)S(1)} all-to-all(bf16[16,32,128]{2,1,0:T(8,128)(2,1)S(1)} %get-tuple-element.12), channel_id=1, replica_groups={{0,1,2,3,4,5,6,7,8,9,10,11,12,13,14,15},{16,17,18,19,20,21,22,23,24,25,..., dimensions={0} | all-to-all | bytes 262144 | tf_op jit(solution)/shard_map/all_to_all | solution.py:386
  17.9 0.0 copy-done.8
  17.9 13.4 %all_to_all.16.right_ref = bf16[32,32,128]{2,1,0:T(8,128)(2,1)S(1)} all-to-all(bf16[32,32,128]{2,1,0:T(8,128)(2,1)S(1)} %copy-done.8), channel_id=1, replica_groups=mesh['row'=8,'col'=4] {'row','col'}, dimensions={0} | all-to-all | bytes 524288 | tf_op jit(solution)/shard_map/all_to_all | solution.py:386
  31.3 0.4 %triangle.1 = bf16[16,32,128]{2,1,0:T(8,128)(2,1)S(1)} custom-call(bf16[16,32,128]{2,1,0:T(8,128)(2,1)S(1)} %all_to_all.15.left_ref, bf16[32,32,128]{2,1,0:T(8,128)(2,1)S(1)} %all_to_all.16.right_ref), custom_call_target="tpu_custom_call" | custom-call | tf_op jit(solution)/shard_map/triangle/pallas_call | solution.py:444
  31.7 0.0 copy-start.4
  31.7 8.9 %all_to_all.17.got_ref = bf16[16,32,128]{2,1,0:T(8,128)(2,1)S(1)} all-to-all(bf16[16,32,128]{2,1,0:T(8,128)(2,1)S(1)} %triangle.1), channel_id=1, replica_groups={{0,1,2,3,4,5,6,7,8,9,10,11,12,13,14,15},{16,17,18,19,20,21,22,23,24,25,..., dimensions={0} | all-to-all | bytes 262144 | tf_op jit(solution)/shard_map/all_to_all | solution.py:386
  40.7 0.0 copy-done.4
  40.7 1.3 %update.1 = bf16[16,32,128]{2,1,0:T(8,128)(2,1)} custom-call(bf16[16,32,128]{2,1,0:T(8,128)(2,1)S(1)} %all_to_all.17.got_ref, f32[512,128]{1,0:T(8,128)S(1)} %get-tuple-element.14.open_ref, f32[128,128]{1,0:T(8,128)S(1)} %get-tuple-element.15.gain_ref, f32[128,128]{1,0:T(8,128)S(1)} %get-tuple-element.16.bias_ref, bf16[128,128]{1,0:T(8,128)(2,1)S(1)} %copy-done.4), custom_call_target="tpu_custom_call" | custom-call | tf_op jit(solution)/shard_map/update/pallas_call | solution.py:453
Async XLA Ops:
  0.0 2.6 %copy-start = (bf16[128,256]{1,0:T(8,128)(2,1)S(1)}, bf16[128,256]{1,0:T(8,128)(2,1)}, u32[]{:S(2)}) copy-start(bf16[128,256]{1,0:T(8,128)(2,1)} %proj_ref.2) | copy-start | bytes 196612
  0.0 2.6 %copy-start.1 = (bf16[128,256]{1,0:T(8,128)(2,1)S(1)}, bf16[128,256]{1,0:T(8,128)(2,1)}, u32[]{:S(2)}) copy-start(bf16[128,256]{1,0:T(8,128)(2,1)} %gate_ref.1) | copy-start | bytes 196612
  0.0 2.7 %copy-start.3 = (bf16[128,128]{1,0:T(8,128)(2,1)S(1)}, bf16[128,128]{1,0:T(8,128)(2,1)}, u32[]{:S(2)}) copy-start(bf16[128,128]{1,0:T(8,128)(2,1)} %open_weight_ref.1) | copy-start | bytes 98308
  2.6 0.7 %copy-start.5 = (s32[8]{0:T(128)S(1)}, s32[8]{0:T(128)}, u32[]{:S(2)}) copy-start(s32[8]{0:T(128)} %chain_ref.1) | copy-start | bytes 100
  2.6 0.7 %copy-start.6 = (f32[128]{0:T(128)S(1)}, f32[128]{0:T(128)}, u32[]{:S(2)}) copy-start(f32[128]{0:T(128)} %param.16) | copy-start | bytes 1540
  2.6 0.7 %copy-start.7 = (f32[128]{0:T(128)S(1)}, f32[128]{0:T(128)}, u32[]{:S(2)}) copy-start(f32[128]{0:T(128)} %param.17) | copy-start | bytes 1540
  3.3 0.9 %copy-start.2 = (bf16[128,512]{1,0:T(8,128)(2,1)S(1)}, bf16[128,512]{1,0:T(8,128)(2,1)}, u32[]{:S(2)}) copy-start(bf16[128,512]{1,0:T(8,128)(2,1)} %get-tuple-element.11.normed_ref) | copy-start | bytes 393220
  4.2 13.7 %copy-start.8 = (bf16[32,32,128]{2,1,0:T(8,128)(2,1)S(1)}, bf16[32,32,128]{2,1,0:T(8,128)(2,1)}, u32[]{:S(2)}) copy-start(bf16[32,32,128]{2,1,0:T(8,128)(2,1)} %get-tuple-element.13) | copy-start | bytes 786436
  31.7 8.9 %copy-start.4 = (bf16[128,128]{1,0:T(8,128)(2,1)S(1)}, bf16[128,128]{1,0:T(8,128)(2,1)}, u32[]{:S(2)}) copy-start(bf16[128,128]{1,0:T(8,128)(2,1)} %proj_ref.3) | copy-start | bytes 98308

commit v10 on v7

--- a/solution.py
+++ b/solution.py
@@ -103,6 +103,16 @@
     return lax.dot_general(a, b, (((a_dim,), (b_dim,)), ((), ())), preferred_element_type=F32)
 
 
+def over(value, size):
+    if size & (size - 1):
+        return value // size
+    return lax.shift_right_logical(value, jnp.full_like(value, size.bit_length() - 1))
+
+
+def rest(value, size):
+    return value % size if size & (size - 1) else value & (size - 1)
+
+
 def fetch(sources, targets, sems):
     copies = [
         pltpu.make_async_copy(source, target, sems.at[n])
@@ -123,10 +133,10 @@
 
 
 def exchange_blocks(arrays, cols):
-    lane = lax.broadcasted_iota(jnp.int32, (1, LANES), 1) // cols
+    lane = over(lax.broadcasted_iota(jnp.int32, (1, LANES), 1), cols)
     arrays, step = list(arrays), 1
     while step < len(arrays):
-        upper = lane // step % 2 == 1
+        upper = lane & step != 0
         for n in range(len(arrays)):
             if n // step % 2 == 0:
                 a, b = arrays[n], arrays[n + step]
@@ -170,7 +180,9 @@
     chunks = sent_ref.shape[0]
     some = 16
     out, source = iota2((some * rows, some * rows))
-    order = one_hot((out // rows == source % some) & (out % rows == source // some))
+    order = one_hot(
+        (over(out, rows) == rest(source, some)) & (rest(out, rows) == over(source, some))
+    )
     a, b = iota2((channels, channels))
     eye = one_hot(a == b)
     cell = lax.broadcasted_iota(jnp.int32, (1, cells), 1)
@@ -188,11 +200,11 @@
     def valid(token):
         length = jnp.zeros_like(token)
         for chain in range(chain_ref.shape[0]):
-            length = jnp.where(token // slots == chain, chain_ref[chain], length)
-        return token % slots < length
-
-    row_ok = valid(lax.axis_index(("high", "low")) * rows + cell // cols)
-    col_ok = valid(lax.axis_index("col") * cols + cell % cols)
+            length = jnp.where(over(token, slots) == chain, chain_ref[chain], length)
+        return rest(token, slots) < length
+
+    row_ok = valid(lax.axis_index(("high", "low")) * rows + over(cell, cols))
+    col_ok = valid(lax.axis_index("col") * cols + rest(cell, cols))
     mask = jnp.where(row_ok & col_ok, 1.0, 0.0)
 
     values = dot(proj_ref[...], normed, 0, 0)
@@ -254,7 +266,7 @@
 
     left, right = side(0), side(1)
     lane = lax.broadcasted_iota(jnp.int32, (1, grid_cols * LANES), 1)
-    by_channel = [right * one_hot(lane % LANES // cols == n) for n in range(inner)]
+    by_channel = [right * one_hot(over(rest(lane, LANES), cols) == n) for n in range(inner)]
     right_by = jnp.concatenate(
         [
             by_channel[n][c * cols : (c + 1) * cols]
@@ -303,7 +315,9 @@
     groups = rows // inner
     some = 16
     out, source = iota2((some * rows, some * rows))
-    order = one_hot((out // some == source % rows) & (out % some == source // rows))
+    order = one_hot(
+        (over(out, some) == rest(source, rows)) & (rest(out, some) == over(source, rows))
+    )
     parts = [
         dot(order, got_ref[part * some : (part + 1) * some].reshape(some * rows, LANES)).astype(BF16)
         for part in range(chunks // some)

time: 32.2 us -> 32.2 us (level)
  no operation moved by 1% of the time
where the time goes in v10:
time: 32.2 us; the launch traced here: 31.9 us
  waiting for transfers between devices  9.77 us (30%)
  blocking collectives  9.45 us (29%)
  starting transfers between devices  7.3 us (23%)
  Pallas kernels  4.65 us (14%)
  local copies, waits for them, and re-layouts  0.65 us (2%)
    all_to_all x1, waiting for transfers between devices, exchanged(): got = lax.all_to_all(sent, order, 0, 0, tiled=True)  9.77 us
    all_to_all x1, blocking collectives, exchanged(): mine = lax.all_to_all(sums, order, 0, 0, tiled=True)  9.45 us
    all_to_all x1, starting transfers between devices, exchanged(): got = lax.all_to_all(sent, order, 0, 0, tiled=True)  7.3 us
    pallas_call x1, Pallas kernels, exchanged(): pl.pallas_call(functools.partial(mix_kernel, slots), out_shape=(jax.Shape...  2.74 us
    pallas_call x1, Pallas kernels, exchanged(): pl.pallas_call(update_kernel, out_shape=jax.ShapeDtypeStruct((rows, cols,...  1.28 us
    unnamed x10, local copies, waits for them, and re-layouts  0.65 us
  transfers between devices with their start and end apart: 1, of which 1 were waited for; matrix products, arithmetic and copies ran while one was open for 0% of the time, Pallas kernels for 1%

profile of v10, /device:TPU:0, one launch (start us, length us, event | category | flops | bytes accessed | tf_op | source)
XLA Modules:
  0.0 31.9 jit_solution(3143605848471902921)
XLA Ops:
  0.0 2.7 %mix.1 = (bf16[32,32,128]{2,1,0:T(8,128)(2,1)}, bf16[128,512]{1,0:T(8,128)(2,1)}) custom-call(s32[8]{0:T(128)} %chain_hbm.1, bf16[16,32,128]{2,1,0:T(8,128)(2,1)} %pair_hbm.1, f32[1,128]{1,0:T(1,128)} %bitcast.6, f32[1,128]{1,0:T(1,128)} %bitcast.7, bf16[128,256]{1,0:T(8,128)(2,1)} %proj_hbm.2, bf16[128,256]{1,0:T(8,128)(2,1)} %gate_hbm.2), custom_call_target="tpu_custom_call" | custom-call | tf_op jit(solution)/shard_map/mix/pallas_call | solution.py:374
  2.7 0.0 copy-start
  2.8 0.0 copy-start.1
  2.8 0.0 copy-start.2
  2.8 7.3 %all-to-all-start = ((bf16[32,32,128]{2,1,0:T(8,128)(2,1)}), bf16[32,32,128]{2,1,0:T(8,128)(2,1)S(1)}, u32[]{:S(2)}, u32[]{:S(2)}) async-start(bf16[32,32,128]{2,1,0:T(8,128)(2,1)} %get-tuple-element.16), calls=%async_computation | async-start | bytes 524288 | tf_op jit(solution)/shard_map/all_to_all | solution.py:405
  10.1 0.0 copy-start.3
  10.1 0.0 copy-start.4
  10.1 0.0 copy-done
  10.1 0.0 copy-done.1
  10.1 0.0 copy-done.2
  10.2 0.6 %copy-done.3 = f32[128]{0:T(128)S(1)} copy-done((f32[128]{0:T(128)S(1)}, f32[128]{0:T(128)}, u32[]{:S(2)}) %copy-start.3) | copy-done | bytes 536
  10.8 0.0 copy-done.4
  10.8 0.3 gate.1
  11.1 9.8 %all-to-all-done.got_ref = bf16[32,32,128]{2,1,0:T(8,128)(2,1)S(1)} async-done(((bf16[32,32,128]{2,1,0:T(8,128)(2,1)}), bf16[32,32,128]{2,1,0:T(8,128)(2,1)S(1)}, u32[]{:S(2)}, u32[]{:S(2)}) %all-to-all-start) | async-done | bytes 262176 | tf_op jit(solution)/shard_map/all_to_all | solution.py:405
  20.9 0.3 triangle.1
  21.2 9.5 %all_to_all.10.got_ref = bf16[32,16,128]{2,1,0:T(8,128)(2,1)S(1)} all-to-all(bf16[32,16,128]{2,1,0:T(8,128)(2,1)S(1)} %triangle.1), channel_id=1, replica_groups=mesh['high'=4,'low'=2,'col'=4] {'col','low','high'}, dimensions={0} | all-to-all | bytes 262144 | tf_op jit(solution)/shard_map/all_to_all | solution.py:434
  30.6 1.3 %update.1 = bf16[16,32,128]{2,1,0:T(8,128)(2,1)} custom-call(bf16[32,16,128]{2,1,0:T(8,128)(2,1)S(1)} %all_to_all.10.got_ref, f32[512,128]{1,0:T(8,128)S(1)} %get-tuple-element.23.open_ref, f32[128,128]{1,0:T(8,128)S(1)} %get-tuple-element.24.gain_ref, f32[128,128]{1,0:T(8,128)S(1)} %get-tuple-element.25.bias_ref, ...), custom_call_target="tpu_custom_call" | custom-call | tf_op jit(solution)/shard_map/update/pallas_call | solution.py:435
Async XLA Ops:
  2.7 7.4 %copy-start = (bf16[128,512]{1,0:T(8,128)(2,1)S(1)}, bf16[128,512]{1,0:T(8,128)(2,1)}, u32[]{:S(2)}) copy-start(bf16[128,512]{1,0:T(8,128)(2,1)} %get-tuple-element.17.normed_ref) | copy-start | bytes 393220
  2.8 7.4 %copy-start.1 = (bf16[128,128]{1,0:T(8,128)(2,1)S(1)}, bf16[128,128]{1,0:T(8,128)(2,1)}, u32[]{:S(2)}) copy-start(bf16[128,128]{1,0:T(8,128)(2,1)} %gate_hbm.3) | copy-start | bytes 98308
  2.8 7.4 %copy-start.2 = (bf16[128,128]{1,0:T(8,128)(2,1)S(1)}, bf16[128,128]{1,0:T(8,128)(2,1)}, u32[]{:S(2)}) copy-start(bf16[128,128]{1,0:T(8,128)(2,1)} %proj_hbm.3) | copy-start | bytes 98308
  2.8 18.1 %all-to-all-start = ((bf16[32,32,128]{2,1,0:T(8,128)(2,1)}), bf16[32,32,128]{2,1,0:T(8,128)(2,1)S(1)}, u32[]{:S(2)}, u32[]{:S(2)}) async-start(bf16[32,32,128]{2,1,0:T(8,128)(2,1)} %get-tuple-element.16), calls=%async_computation | async-start | bytes 524288 | tf_op jit(solution)/shard_map/all_to_all | solution.py:405
  10.1 0.7 %copy-start.3 = (f32[128]{0:T(128)S(1)}, f32[128]{0:T(128)}, u32[]{:S(2)}) copy-start(f32[128]{0:T(128)} %param.16) | copy-start | bytes 1540
  10.1 0.7 %copy-start.4 = (f32[128]{0:T(128)S(1)}, f32[128]{0:T(128)}, u32[]{:S(2)}) copy-start(f32[128]{0:T(128)} %param.17) | copy-start | bytes 1540

commit v11 on v10

--- a/solution.py
+++ b/solution.py
@@ -7,6 +7,7 @@
 from jax.sharding import PartitionSpec as P
 
 LANES = 128
+SOME = 16
 F32 = jnp.float32
 BF16 = jnp.bfloat16
 
@@ -113,6 +114,16 @@
     return value % size if size & (size - 1) else value & (size - 1)
 
 
+def over(value, size):
+    if size & (size - 1):
+        return value // size
+    return lax.shift_right_logical(value, jnp.full_like(value, size.bit_length() - 1))
+
+
+def rest(value, size):
+    return value % size if size & (size - 1) else value & (size - 1)
+
+
 def fetch(sources, targets, sems):
     copies = [
         pltpu.make_async_copy(source, target, sems.at[n])
@@ -125,11 +136,6 @@
 
 def sigmoid(halved):
     return 0.5 + 0.5 * jnp.tanh(halved)
-
-
-def column(row_ref):
-    a, b = iota2((LANES, LANES))
-    return jnp.sum(jnp.where(a == b, row_ref[...], 0.0), axis=1, keepdims=True)
 
 
 def exchange_blocks(arrays, cols):
@@ -146,17 +152,39 @@
     return arrays
 
 
+def orders_kernel(order_ref, eye_ref):
+    out, source = iota2(order_ref.shape)
+    order_ref[...] = one_hot(
+        (over(out, SOME) == rest(source, SOME)) & (rest(out, SOME) == over(source, SOME))
+    )
+    a, b = iota2(eye_ref.shape)
+    eye_ref[...] = one_hot(a == b)
+
+
+def prepare_kernel(slots, cols, chain_ref, *refs):
+    *rows_in, mask_ref = refs[:5]
+    cell = lax.broadcasted_iota(jnp.int32, mask_ref.shape, 1)
+
+    def valid(token):
+        length = jnp.zeros_like(token)
+        for chain in range(chain_ref.shape[0]):
+            length = jnp.where(over(token, slots) == chain, chain_ref[chain], length)
+        return rest(token, slots) < length
+
+    rows = mask_ref.shape[1] // cols
+    row_ok = valid(lax.axis_index(("high", "low")) * rows + over(cell, cols))
+    col_ok = valid(lax.axis_index("col") * cols + rest(cell, cols))
+    mask_ref[...] = jnp.where(row_ok & col_ok, 1.0, 0.0)
+    a, b = iota2((LANES, LANES))
+    for source, target in zip(rows_in, refs[5:]):
+        column = jnp.sum(jnp.where(a == b, source[...], 0.0), axis=1, keepdims=True)
+        target[...] = jnp.broadcast_to(column, target.shape)
+
+
 def mix_kernel(
-    slots,
-    chain_hbm,
-    pair_hbm,
-    gain_hbm,
-    bias_hbm,
-    proj_hbm,
-    gate_hbm,
-    sent_hbm,
-    normed_hbm,
-    chain_ref,
+    order_ref,
+    eye_ref,
+    mask_ref,
     pair_ref,
     gain_ref,
     bias_ref,
@@ -164,52 +192,30 @@
     gate_ref,
     sent_ref,
     normed_ref,
-    sems,
-    out_sems,
 ):
-    copies = fetch(
-        (pair_hbm, gain_hbm, bias_hbm, chain_hbm, proj_hbm, gate_hbm),
-        (pair_ref, gain_ref, bias_ref, chain_ref, proj_ref, gate_ref),
-        sems,
-    )
     rows, cols, channels = pair_ref.shape
     hidden = proj_ref.shape[1] // 2
     cells = rows * cols
     inner = LANES // cols
     groups = rows // inner
     chunks = sent_ref.shape[0]
-    some = 16
-    out, source = iota2((some * rows, some * rows))
-    order = one_hot(
-        (over(out, rows) == rest(source, some)) & (rest(out, rows) == over(source, some))
-    )
-    a, b = iota2((channels, channels))
-    eye = one_hot(a == b)
-    cell = lax.broadcasted_iota(jnp.int32, (1, cells), 1)
-    for copy in copies:
-        copy.wait()
-    flat = dot(eye, pair_ref[...].reshape(cells, channels), 1, 1)
+    flat = dot(eye_ref[...], pair_ref[...].reshape(cells, channels), 1, 1)
     centered = flat - jnp.mean(flat, axis=0, keepdims=True)
     variance = jnp.mean(centered * centered, axis=0, keepdims=True)
-    normed = centered * lax.rsqrt(variance + 1e-05) * column(gain_ref) + column(bias_ref)
-    normed = normed.astype(BF16)
+    scaled = centered * lax.rsqrt(variance + 1e-05)
+    gain, bias = gain_ref[...], bias_ref[...]
+    normed = jnp.concatenate(
+        [
+            (scaled[:, g * LANES : (g + 1) * LANES] * gain + bias).astype(BF16)
+            for g in range(groups)
+        ],
+        axis=1,
+    )
     normed_ref[...] = normed
-    results = [pltpu.make_async_copy(normed_ref, normed_hbm, out_sems.at[0])]
-    results[0].start()
-
-    def valid(token):
-        length = jnp.zeros_like(token)
-        for chain in range(chain_ref.shape[0]):
-            length = jnp.where(over(token, slots) == chain, chain_ref[chain], length)
-        return rest(token, slots) < length
-
-    row_ok = valid(lax.axis_index(("high", "low")) * rows + over(cell, cols))
-    col_ok = valid(lax.axis_index("col") * cols + rest(cell, cols))
-    mask = jnp.where(row_ok & col_ok, 1.0, 0.0)
 
     values = dot(proj_ref[...], normed, 0, 0)
     gates = dot(gate_ref[...] * 0.5, normed, 0, 0)
-    mixed = (sigmoid(gates) * values * mask).astype(BF16)
+    mixed = (sigmoid(gates) * values * mask_ref[...]).astype(BF16)
 
     by_row = []
     for side in range(2):
@@ -226,20 +232,15 @@
                 cols,
             )
         by_row.append(lines)
-    for part in range(chunks // some):
-        here = pl.ds(part * some, some)
+    order = order_ref[...]
+    for part in range(chunks // SOME):
         for side in range(2):
             stack = jnp.concatenate(
-                [line[part * some : (part + 1) * some] for line in by_row[side]], axis=0
+                [line[part * SOME : (part + 1) * SOME] for line in by_row[side]], axis=0
             )
-            moved = dot(order, stack).astype(BF16)
-            sent_ref[here, side * rows : (side + 1) * rows] = moved.reshape(some, rows, LANES)
-        results.append(
-            pltpu.make_async_copy(sent_ref.at[here], sent_hbm.at[here], out_sems.at[part + 1])
-        )
-        results[-1].start()
-    for copy in results:
-        copy.wait()
+            sent_ref[part * SOME : (part + 1) * SOME, side * rows : (side + 1) * rows] = (
+                dot(order, stack).astype(BF16).reshape(SOME, rows, LANES)
+            )
 
 
 def triangle_kernel(split, grid_cols, rows, cols, got_ref, sent_ref):
@@ -281,52 +282,33 @@
             sent_ref[place(r, c)] = sums[r * rows : (r + 1) * rows, c * LANES : (c + 1) * LANES]
 
 
-def gate_kernel(
+def update_kernel(
+    got_ref,
+    order_ref,
     normed_ref,
-    gate_hbm,
-    gain_hbm,
-    bias_hbm,
-    proj_hbm,
-    open_ref,
-    gain_out,
-    bias_out,
-    proj_out,
-    gate_ref,
     gain_ref,
     bias_ref,
-    sems,
-):
-    copies = fetch(
-        (gate_hbm, gain_hbm, bias_hbm, proj_hbm), (gate_ref, gain_ref, bias_ref, proj_out), sems
-    )
-    for copy in copies:
-        copy.wait()
-    open_ref[...] = sigmoid(dot(normed_ref[...], gate_ref[...] * 0.5, 0, 0))
-    gain_out[...] = jnp.broadcast_to(column(gain_ref), gain_out.shape)
-    bias_out[...] = jnp.broadcast_to(column(bias_ref), bias_out.shape)
-
-
-def update_kernel(
-    got_ref, open_ref, gain_ref, bias_ref, proj_ref, out_hbm, out_ref, out_sems
+    proj_ref,
+    gate_ref,
+    out_hbm,
+    out_ref,
+    out_sems,
 ):
     rows, cols, channels = out_ref.shape
     chunks = got_ref.shape[0]
     inner = LANES // cols
     groups = rows // inner
-    some = 16
-    out, source = iota2((some * rows, some * rows))
-    order = one_hot(
-        (over(out, some) == rest(source, rows)) & (rest(out, some) == over(source, rows))
-    )
+    order = order_ref[...]
     parts = [
-        dot(order, got_ref[part * some : (part + 1) * some].reshape(some * rows, LANES)).astype(BF16)
-        for part in range(chunks // some)
+        dot(order, got_ref[part * SOME : (part + 1) * SOME].reshape(SOME * rows, LANES)).astype(BF16)
+        for part in range(chunks // SOME)
     ]
     lines = [
-        jnp.concatenate([part[row * some : (row + 1) * some] for part in parts], axis=0)
+        jnp.concatenate([part[row * SOME : (row + 1) * SOME] for part in parts], axis=0)
         for row in range(rows)
     ]
     gain, bias = gain_ref[...], bias_ref[...]
+    opened = sigmoid(dot(normed_ref[...], gate_ref[...] * 0.5, 0, 0))
     results = []
     for g in range(groups):
         values = jnp.concatenate(
@@ -337,7 +319,7 @@
         variance = jnp.mean(centered * centered, axis=0, keepdims=True)
         tri_normed = (centered * lax.rsqrt(variance + 1e-05) * gain + bias).astype(BF16)
         projected = dot(tri_normed, proj_ref[...], 0, 0)
-        update = (open_ref[g * LANES : (g + 1) * LANES] * projected).astype(BF16)
+        update = (opened[g * LANES : (g + 1) * LANES] * projected).astype(BF16)
         here = pl.ds(g * inner, inner)
         out_ref[here] = update.reshape(inner, cols, channels)
         results.append(pltpu.make_async_copy(out_ref.at[here], out_hbm.at[here], out_sems.at[g]))
@@ -347,9 +329,9 @@
 
 
 VMEM = pl.BlockSpec(memory_space=pltpu.VMEM)
+SMEM = pl.BlockSpec(memory_space=pltpu.SMEM)
 HBM = pl.BlockSpec(memory_space=pltpu.HBM)
 PARAMS = pltpu.CompilerParams(vmem_limit_bytes=32 * 1024 * 1024)
-FETCHING = pltpu.CompilerParams(vmem_limit_bytes=60 * 1024 * 1024)
 
 
 def exchanged(
@@ -371,58 +353,45 @@
     grid_rows = split[0] * split[1]
     devices = grid_rows * grid_cols
     slots = rows * grid_rows // chain_lengths.shape[0]
+    order, eye = pl.pallas_call(
+        orders_kernel,
+        out_shape=(
+            jax.ShapeDtypeStruct((SOME * SOME, SOME * SOME), BF16),
+            jax.ShapeDtypeStruct((LANES, LANES), BF16),
+        ),
+        out_specs=[VMEM] * 2,
+        compiler_params=PARAMS,
+        cost_estimate=pl.CostEstimate(flops=10**9, bytes_accessed=10**6, transcendentals=0),
+        name="orders",
+    )()
+    square = jax.ShapeDtypeStruct((LANES, LANES), F32)
+    mask, *columns = pl.pallas_call(
+        functools.partial(prepare_kernel, slots, cols),
+        out_shape=(jax.ShapeDtypeStruct((1, rows * cols), F32),) + (square,) * 4,
+        in_specs=[SMEM] + [VMEM] * 4,
+        out_specs=[VMEM] * 5,
+        compiler_params=PARAMS,
+        name="prepare",
+    )(
+        chain_lengths,
+        *(
+            row.reshape(1, LANES)
+            for row in (norm_in_gain, norm_in_bias, norm_out_gain, norm_out_bias)
+        ),
+    )
     sent, normed = pl.pallas_call(
-        functools.partial(mix_kernel, slots),
+        mix_kernel,
         out_shape=(
             jax.ShapeDtypeStruct((devices, 2 * rows, LANES), BF16),
             jax.ShapeDtypeStruct((channels, rows * cols), BF16),
         ),
-        in_specs=[HBM] * 6,
-        out_specs=(HBM, HBM),
-        scratch_shapes=[
-            pltpu.SMEM(chain_lengths.shape, jnp.int32),
-            pltpu.VMEM(pair.shape, BF16),
-            pltpu.VMEM((1, channels), F32),
-            pltpu.VMEM((1, channels), F32),
-            pltpu.VMEM(proj_in.shape, BF16),
-            pltpu.VMEM(gate_in.shape, BF16),
-            pltpu.VMEM((devices, 2 * rows, LANES), BF16),
-            pltpu.VMEM((channels, rows * cols), BF16),
-            pltpu.SemaphoreType.DMA((6,)),
-            pltpu.SemaphoreType.DMA((1 + devices // 16,)),
-        ],
-        compiler_params=FETCHING,
+        in_specs=[VMEM] * 8,
+        out_specs=(VMEM, VMEM),
+        compiler_params=PARAMS,
         name="mix",
-    )(
-        chain_lengths,
-        pair,
-        norm_in_gain.reshape(1, channels),
-        norm_in_bias.reshape(1, channels),
-        proj_in,
-        gate_in,
-    )
-    order = ("col", "low", "high")
-    got = lax.all_to_all(sent, order, 0, 0, tiled=True)
-    opened, gain, bias, proj = pl.pallas_call(
-        gate_kernel,
-        out_shape=(
-            jax.ShapeDtypeStruct((rows * cols, channels), F32),
-            jax.ShapeDtypeStruct((hidden, LANES), F32),
-            jax.ShapeDtypeStruct((hidden, LANES), F32),
-            jax.ShapeDtypeStruct(proj_out.shape, BF16),
-        ),
-        in_specs=[VMEM] + [HBM] * 4,
-        out_specs=[VMEM] * 4,
-        scratch_shapes=[
-            pltpu.VMEM(gate_out.shape, BF16),
-            pltpu.VMEM((1, hidden), F32),
-            pltpu.VMEM((1, hidden), F32),
-            pltpu.SemaphoreType.DMA((4,)),
-        ],
-        compiler_params=PARAMS,
-        name="gate",
-    )(normed, gate_out, norm_out_gain.reshape(1, hidden), norm_out_bias.reshape(1, hidden), proj_out)
-    got, opened, gain, bias, proj = lax.optimization_barrier((got, opened, gain, bias, proj))
+    )(order, eye, mask, pair, *columns[:2], proj_in, gate_in)
+    axes = ("col", "low", "high")
+    got = lax.all_to_all(sent, axes, 0, 0, tiled=True)
     sums = pl.pallas_call(
         functools.partial(triangle_kernel, split, grid_cols, rows, cols),
         out_shape=jax.ShapeDtypeStruct((devices, rows, LANES), BF16),
@@ -431,11 +400,11 @@
         compiler_params=PARAMS,
         name="triangle",
     )(got)
-    mine = lax.all_to_all(sums, order, 0, 0, tiled=True)
+    mine = lax.all_to_all(sums, axes, 0, 0, tiled=True)
     return pl.pallas_call(
         update_kernel,
         out_shape=jax.ShapeDtypeStruct((rows, cols, channels), BF16),
-        in_specs=[VMEM] * 5,
+        in_specs=[VMEM] * 7,
         out_specs=HBM,
         scratch_shapes=[
             pltpu.VMEM((rows, cols, channels), BF16),
@@ -443,7 +412,7 @@
         ],
         compiler_params=PARAMS,
         name="update",
-    )(mine, opened, gain, bias, proj)
+    )(mine, order, normed, *columns[2:], proj_out, gate_out)
 
 
 def solution(mesh):
@@ -462,9 +431,9 @@
             and inner * cols == LANES
             and inner & (inner - 1) == 0
             and inner * devices == hidden
-            and rows % 16 == 0
+            and rows == SOME
             and rows % inner == 0
-            and devices % 16 == 0
+            and devices % SOME == 0
         )
 
     def call(*arrays):

time: 32.2 us -> 31.8 us (0.988)
  blocking collectives: 9.45 us -> 27.3 us
  waiting for transfers between devices: 9.77 us -> 0 us
  starting transfers between devices: 7.3 us -> 0 us
  Pallas kernels: 4.65 us -> 3.33 us
    all_to_all x1 -> x2, blocking collectives: 9.45 us -> 27.3 us  [the longest x1 17.9 us: exchanged(): got = lax.all_to_all(sent, axes, 0, 0, tiled=True)]
    all_to_all x1 -> x0, waiting for transfers between devices: 9.77 us -> none  [exchanged(): got = lax.all_to_all(sent, order, 0, 0, tiled=True)]
    all_to_all x1 -> x0, starting transfers between devices: 7.3 us -> none  [exchanged(): got = lax.all_to_all(sent, order, 0, 0, tiled=True)]
    pallas_call x2 -> x3, Pallas kernels: 3.06 us -> 1.76 us  [the longest x1 1.04 us: exchanged(): pl.pallas_call(mix_kernel, out_shape=(jax.ShapeDtypeStruct((devices, 2 *...]
    unnamed x10 -> x20, local copies, waits for them, and re-layouts: 0.65 us -> 0.78 us
  transfers between devices with their start and end apart: 1 -> 0, of which waited for: 1 -> 0; matrix products, arithmetic and copies ran while one was open for 0% -> 0% of each run, Pallas kernels for 1% -> 0%
where the time goes in v11:
time: 31.8 us; the launch traced here: 31.6 us
  blocking collectives  27.3 us (86%)
  Pallas kernels  3.33 us (10%)
  local copies, waits for them, and re-layouts  0.78 us (2%)
    all_to_all x1, blocking collectives, exchanged(): got = lax.all_to_all(sent, axes, 0, 0, tiled=True)  17.9 us
    all_to_all x1, blocking collectives, exchanged(): mine = lax.all_to_all(sums, axes, 0, 0, tiled=True)  9.46 us
    pallas_call x1, Pallas kernels, exchanged(): pl.pallas_call(update_kernel, out_shape=jax.ShapeDtypeStruct((rows, cols,...  1.27 us
    pallas_call x1, Pallas kernels, exchanged(): pl.pallas_call(mix_kernel, out_shape=(jax.ShapeDtypeStruct((devices, 2 *...  1.04 us
    unnamed x20, local copies, waits for them, and re-layouts  0.78 us
    pallas_call x1, Pallas kernels, exchanged(): pl.pallas_call(functools.partial(prepare_kernel, slots, cols), out_shape=...  0.68 us

profile of v11, /device:TPU:0, one launch (start us, length us, event | category | flops | bytes accessed | tf_op | source)
XLA Modules:
  0.0 31.6 jit_solution(10913762508823593709)
XLA Ops:
  0.0 0.0 copy-start.2
  0.0 0.0 copy-start.1
  0.0 0.0 copy-start
  0.0 0.0 copy-start.8
  0.0 0.0 copy-start.9
  0.1 0.0 copy-start.5
  0.1 0.0 copy-start.6
  0.1 0.0 copy-start.7
  0.1 0.6 %copy-done.8 = f32[128]{0:T(128)S(1)} copy-done((f32[128]{0:T(128)S(1)}, f32[128]{0:T(128)}, u32[]{:S(2)}) %copy-start.8) | copy-done | bytes 536
  0.7 0.0 copy-done.9
  0.7 0.1 copy-done.5
  0.8 0.0 copy-done.6
  0.8 0.0 copy-done.7
  0.8 0.7 %prepare.1 = (f32[1,512]{1,0:T(1,128)S(1)}, f32[128,128]{1,0:T(8,128)S(1)}, f32[128,128]{1,0:T(8,128)S(1)}, f32[128,128]{1,0:T(8,128)S(1)}, f32[128,128]{1,0:T(8,128)S(1)}) custom-call(s32[8]{0:T(128)S(1)} %copy-done.5, f32[1,128]{1,0:T(1,128)S(1)} %bitcast.4, f32[1,128]{1,0:T(1,128)S(1)} %bitcast.5, f32[1,128]{1,0:T(1,128)S(1)} %bitcast.6, f32[1,128]{1,0:T(1,128)S(1)} %bitcast.7), custom_call_target="tpu_custom_call" | custom-call | tf_op jit(solution)/shard_map/prepare/pallas_call | solution.py:368
  1.5 0.0 copy-done.2
  1.5 0.0 copy-done.1
  1.6 0.0 copy-done
  1.6 1.0 %mix.1 = (bf16[32,32,128]{2,1,0:T(8,128)(2,1)S(1)}, bf16[128,512]{1,0:T(8,128)(2,1)S(1)}) custom-call(bf16[256,256]{1,0:T(8,128)(2,1)S(1)} %get-tuple-element.14.order_ref, bf16[128,128]{1,0:T(8,128)(2,1)S(1)} %get-tuple-element.15.eye_ref, f32[1,512]{1,0:T(1,128)S(1)} %get-tuple-element.16.mask_ref, bf16[16,32,128]{2,1,0:T(8,128)(2,1)S(1)} %copy-done, ...), custom_call_target="tpu_custom_call" | custom-call | tf_op jit(solution)/shard_map/mix/pallas_call | solution.py:382
  2.6 17.9 %all_to_all.10.got_ref = bf16[32,32,128]{2,1,0:T(8,128)(2,1)S(1)} all-to-all(bf16[32,32,128]{2,1,0:T(8,128)(2,1)S(1)} %get-tuple-element.19), channel_id=1, replica_groups=mesh['high'=4,'low'=2,'col'=4] {'col','low','high'}, dimensions={0} | all-to-all | bytes 524288 | tf_op jit(solution)/shard_map/all_to_all | solution.py:394
  20.5 0.3 triangle.1
  20.8 0.0 copy-start.3
  20.8 0.0 copy-start.4
  20.8 9.5 %all_to_all.11.got_ref = bf16[32,16,128]{2,1,0:T(8,128)(2,1)S(1)} all-to-all(bf16[32,16,128]{2,1,0:T(8,128)(2,1)S(1)} %triangle.1), channel_id=1, replica_groups=mesh['high'=4,'low'=2,'col'=4] {'col','low','high'}, dimensions={0} | all-to-all | bytes 262144 | tf_op jit(solution)/shard_map/all_to_all | solution.py:403
  30.3 0.0 copy-done.3
  30.3 0.0 copy-done.4
  30.3 1.3 %update.1 = bf16[16,32,128]{2,1,0:T(8,128)(2,1)} custom-call(bf16[32,16,128]{2,1,0:T(8,128)(2,1)S(1)} %all_to_all.11.got_ref, bf16[256,256]{1,0:T(8,128)(2,1)S(1)} %get-tuple-element.14.order_ref, bf16[128,512]{1,0:T(8,128)(2,1)S(1)} %get-tuple-element.20.normed_ref, f32[128,128]{1,0:T(8,128)S(1)} %get-tuple-element.21.gain_ref, ...), custom_call_target="tpu_custom_call" | custom-call | tf_op jit(solution)/shard_map/update/pallas_call | solution.py:404
  (1 shorter events, 0.0 us)
Async XLA Ops:
  0.0 1.5 %copy-start.2 = (bf16[128,256]{1,0:T(8,128)(2,1)S(1)}, bf16[128,256]{1,0:T(8,128)(2,1)}, u32[]{:S(2)}) copy-start(bf16[128,256]{1,0:T(8,128)(2,1)} %gate_ref.2) | copy-start | bytes 196612
  0.0 1.5 %copy-start.1 = (bf16[128,256]{1,0:T(8,128)(2,1)S(1)}, bf16[128,256]{1,0:T(8,128)(2,1)}, u32[]{:S(2)}) copy-start(bf16[128,256]{1,0:T(8,128)(2,1)} %proj_ref.2) | copy-start | bytes 196612
  0.0 1.6 %copy-start = (bf16[16,32,128]{2,1,0:T(8,128)(2,1)S(1)}, bf16[16,32,128]{2,1,0:T(8,128)(2,1)}, u32[]{:S(2)}) copy-start(bf16[16,32,128]{2,1,0:T(8,128)(2,1)} %pair_ref.1) | copy-start | bytes 393220
  0.0 0.7 %copy-start.8 = (f32[128]{0:T(128)S(1)}, f32[128]{0:T(128)}, u32[]{:S(2)}) copy-start(f32[128]{0:T(128)} %param.16) | copy-start | bytes 1540
  0.0 0.7 %copy-start.9 = (f32[128]{0:T(128)S(1)}, f32[128]{0:T(128)}, u32[]{:S(2)}) copy-start(f32[128]{0:T(128)} %param.17) | copy-start | bytes 1540
  0.1 0.7 %copy-start.5 = (s32[8]{0:T(128)S(1)}, s32[8]{0:T(128)}, u32[]{:S(2)}) copy-start(s32[8]{0:T(128)} %chain_ref.1) | copy-start | bytes 100
  0.1 0.8 %copy-start.6 = (f32[128]{0:T(128)S(1)}, f32[128]{0:T(128)}, u32[]{:S(2)}) copy-start(f32[128]{0:T(128)} %param.12) | copy-start | bytes 1540
  0.1 0.8 %copy-start.7 = (f32[128]{0:T(128)S(1)}, f32[128]{0:T(128)}, u32[]{:S(2)}) copy-start(f32[128]{0:T(128)} %param.13) | copy-start | bytes 1540
  20.8 9.5 %copy-start.3 = (bf16[128,128]{1,0:T(8,128)(2,1)S(1)}, bf16[128,128]{1,0:T(8,128)(2,1)}, u32[]{:S(2)}) copy-start(bf16[128,128]{1,0:T(8,128)(2,1)} %proj_ref.3) | copy-start | bytes 98308
  20.8 9.5 %copy-start.4 = (bf16[128,128]{1,0:T(8,128)(2,1)S(1)}, bf16[128,128]{1,0:T(8,128)(2,1)}, u32[]{:S(2)}) copy-start(bf16[128,128]{1,0:T(8,128)(2,1)} %gate_ref.3) | copy-start | bytes 98308

commit v12 on v11

--- a/solution.py
+++ b/solution.py
@@ -161,37 +161,43 @@
     eye_ref[...] = one_hot(a == b)
 
 
-def prepare_kernel(slots, cols, chain_ref, *refs):
-    *rows_in, mask_ref = refs[:5]
-    cell = lax.broadcasted_iota(jnp.int32, mask_ref.shape, 1)
+def column(row):
+    a, b = iota2((LANES, LANES))
+    return jnp.sum(jnp.where(a == b, row, 0.0), axis=1, keepdims=True)
+
+
+def cell_mask(lengths, slots, rows, cols):
+    cell = lax.broadcasted_iota(jnp.int32, (1, rows * cols), 1)
 
     def valid(token):
         length = jnp.zeros_like(token)
-        for chain in range(chain_ref.shape[0]):
-            length = jnp.where(over(token, slots) == chain, chain_ref[chain], length)
+        for chain in range(lengths.shape[1]):
+            length = jnp.where(
+                over(token, slots) == chain, lengths[:, chain : chain + 1], length
+            )
         return rest(token, slots) < length
 
-    rows = mask_ref.shape[1] // cols
     row_ok = valid(lax.axis_index(("high", "low")) * rows + over(cell, cols))
     col_ok = valid(lax.axis_index("col") * cols + rest(cell, cols))
-    mask_ref[...] = jnp.where(row_ok & col_ok, 1.0, 0.0)
-    a, b = iota2((LANES, LANES))
-    for source, target in zip(rows_in, refs[5:]):
-        column = jnp.sum(jnp.where(a == b, source[...], 0.0), axis=1, keepdims=True)
-        target[...] = jnp.broadcast_to(column, target.shape)
+    return jnp.where(row_ok & col_ok, 1.0, 0.0)
 
 
 def mix_kernel(
+    slots,
     order_ref,
     eye_ref,
-    mask_ref,
+    chain_ref,
     pair_ref,
     gain_ref,
     bias_ref,
     proj_ref,
     gate_ref,
+    last_gain_ref,
+    last_bias_ref,
     sent_ref,
     normed_ref,
+    last_gain_out,
+    last_bias_out,
 ):
     rows, cols, channels = pair_ref.shape
     hidden = proj_ref.shape[1] // 2
@@ -202,20 +208,16 @@
     flat = dot(eye_ref[...], pair_ref[...].reshape(cells, channels), 1, 1)
     centered = flat - jnp.mean(flat, axis=0, keepdims=True)
     variance = jnp.mean(centered * centered, axis=0, keepdims=True)
-    scaled = centered * lax.rsqrt(variance + 1e-05)
-    gain, bias = gain_ref[...], bias_ref[...]
-    normed = jnp.concatenate(
-        [
-            (scaled[:, g * LANES : (g + 1) * LANES] * gain + bias).astype(BF16)
-            for g in range(groups)
-        ],
-        axis=1,
-    )
+    gain, bias = column(gain_ref[...]), column(bias_ref[...])
+    normed = (centered * lax.rsqrt(variance + 1e-05) * gain + bias).astype(BF16)
     normed_ref[...] = normed
+    for source, target in ((last_gain_ref, last_gain_out), (last_bias_ref, last_bias_out)):
+        target[...] = jnp.broadcast_to(column(source[...]), target.shape)
 
     values = dot(proj_ref[...], normed, 0, 0)
     gates = dot(gate_ref[...] * 0.5, normed, 0, 0)
-    mixed = (sigmoid(gates) * values * mask_ref[...]).astype(BF16)
+    mask = cell_mask(chain_ref[...], slots, rows, cols)
+    mixed = (sigmoid(gates) * values * mask).astype(BF16)
 
     by_row = []
     for side in range(2):
@@ -329,7 +331,6 @@
 
 
 VMEM = pl.BlockSpec(memory_space=pltpu.VMEM)
-SMEM = pl.BlockSpec(memory_space=pltpu.SMEM)
 HBM = pl.BlockSpec(memory_space=pltpu.HBM)
 PARAMS = pltpu.CompilerParams(vmem_limit_bytes=32 * 1024 * 1024)
 
@@ -365,31 +366,30 @@
         name="orders",
     )()
     square = jax.ShapeDtypeStruct((LANES, LANES), F32)
-    mask, *columns = pl.pallas_call(
-        functools.partial(prepare_kernel, slots, cols),
-        out_shape=(jax.ShapeDtypeStruct((1, rows * cols), F32),) + (square,) * 4,
-        in_specs=[SMEM] + [VMEM] * 4,
-        out_specs=[VMEM] * 5,
-        compiler_params=PARAMS,
-        name="prepare",
-    )(
-        chain_lengths,
-        *(
-            row.reshape(1, LANES)
-            for row in (norm_in_gain, norm_in_bias, norm_out_gain, norm_out_bias)
-        ),
-    )
-    sent, normed = pl.pallas_call(
-        mix_kernel,
+    sent, normed, last_gain, last_bias = pl.pallas_call(
+        functools.partial(mix_kernel, slots),
         out_shape=(
             jax.ShapeDtypeStruct((devices, 2 * rows, LANES), BF16),
             jax.ShapeDtypeStruct((channels, rows * cols), BF16),
+            square,
+            square,
         ),
-        in_specs=[VMEM] * 8,
-        out_specs=(VMEM, VMEM),
+        in_specs=[VMEM] * 10,
+        out_specs=[VMEM] * 4,
         compiler_params=PARAMS,
         name="mix",
-    )(order, eye, mask, pair, *columns[:2], proj_in, gate_in)
+    )(
+        order,
+        eye,
+        chain_lengths.reshape(1, -1),
+        pair,
+        norm_in_gain.reshape(1, LANES),
+        norm_in_bias.reshape(1, LANES),
+        proj_in,
+        gate_in,
+        norm_out_gain.reshape(1, LANES),
+        norm_out_bias.reshape(1, LANES),
+    )
     axes = ("col", "low", "high")
     got = lax.all_to_all(sent, axes, 0, 0, tiled=True)
     sums = pl.pallas_call(
@@ -412,7 +412,7 @@
         ],
         compiler_params=PARAMS,
         name="update",
-    )(mine, order, normed, *columns[2:], proj_out, gate_out)
+    )(mine, order, normed, last_gain, last_bias, proj_out, gate_out)
 
 
 def solution(mesh):

time: 31.8 us -> 31.2 us (0.981)
  Pallas kernels: 3.33 us -> 2.67 us
    pallas_call x2 -> x1, Pallas kernels: 1.72 us -> 1.05 us  [exchanged(): pl.pallas_call(functools.partial(mix_kernel, slots), out_shape=(jax.Shape...]
where the time goes in v12:
time: 31.2 us; the launch traced here: 31 us
  blocking collectives  27.3 us (88%)
  Pallas kernels  2.67 us (9%)
  local copies, waits for them, and re-layouts  0.92 us (3%)
    all_to_all x1, blocking collectives, exchanged(): got = lax.all_to_all(sent, axes, 0, 0, tiled=True)  17.9 us
    all_to_all x1, blocking collectives, exchanged(): mine = lax.all_to_all(sums, axes, 0, 0, tiled=True)  9.45 us
    pallas_call x1, Pallas kernels, exchanged(): pl.pallas_call(update_kernel, out_shape=jax.ShapeDtypeStruct((rows, cols,...  1.27 us
    pallas_call x1, Pallas kernels, exchanged(): pl.pallas_call(functools.partial(mix_kernel, slots), out_shape=(jax.Shape...  1.05 us
    unnamed x20, local copies, waits for them, and re-layouts  0.92 us

profile of v12, /device:TPU:0, one launch (start us, length us, event | category | flops | bytes accessed | tf_op | source)
XLA Modules:
  0.0 31.0 jit_solution(991230443654503765)
XLA Ops:
  0.0 0.0 copy-start.2
  0.0 0.0 copy-start.1
  0.0 0.0 copy-start
  0.0 0.0 copy-start.8
  0.0 0.0 copy-start.9
  0.1 0.0 copy-start.5
  0.1 0.0 copy-start.6
  0.1 0.0 copy-start.7
  0.1 0.7 %copy-done.2 = bf16[128,256]{1,0:T(8,128)(2,1)S(1)} copy-done((bf16[128,256]{1,0:T(8,128)(2,1)S(1)}, bf16[128,256]{1,0:T(8,128)(2,1)}, u32[]{:S(2)}) %copy-start.2) | copy-done | bytes 65560
  0.8 0.0 copy-done.1
  0.9 0.1 copy-done
  1.0 0.0 copy-done.8
  1.0 0.0 copy-done.9
  1.0 0.0 copy-done.5
  1.0 0.0 copy-done.6
  1.0 0.0 copy-done.7
  1.0 1.0 %mix.1 = (bf16[32,32,128]{2,1,0:T(8,128)(2,1)S(1)}, bf16[128,512]{1,0:T(8,128)(2,1)S(1)}, f32[128,128]{1,0:T(8,128)S(1)}, f32[128,128]{1,0:T(8,128)S(1)}) custom-call(bf16[256,256]{1,0:T(8,128)(2,1)S(1)} %get-tuple-element.11.order_ref, bf16[128,128]{1,0:T(8,128)(2,1)S(1)} %get-tuple-element.12.eye_ref, s32[1,8]{1,0:T(1,128)S(1)} %bitcast.5, ...), custom_call_target="tpu_custom_call" | custom-call | tf_op jit(solution)/shard_map/mix/pallas_call | solution.py:369
  2.1 17.9 %all_to_all.10.got_ref = bf16[32,32,128]{2,1,0:T(8,128)(2,1)S(1)} all-to-all(bf16[32,32,128]{2,1,0:T(8,128)(2,1)S(1)} %get-tuple-element.13), channel_id=1, replica_groups=mesh['high'=4,'low'=2,'col'=4] {'col','low','high'}, dimensions={0} | all-to-all | bytes 524288 | tf_op jit(solution)/shard_map/all_to_all | solution.py:394
  19.9 0.3 triangle.1
  20.2 0.0 copy-start.3
  20.3 0.0 copy-start.4
  20.3 9.5 %all_to_all.11.got_ref = bf16[32,16,128]{2,1,0:T(8,128)(2,1)S(1)} all-to-all(bf16[32,16,128]{2,1,0:T(8,128)(2,1)S(1)} %triangle.1), channel_id=1, replica_groups=mesh['high'=4,'low'=2,'col'=4] {'col','low','high'}, dimensions={0} | all-to-all | bytes 262144 | tf_op jit(solution)/shard_map/all_to_all | solution.py:403
  29.7 0.0 copy-done.3
  29.7 0.0 copy-done.4
  29.7 1.3 %update.1 = bf16[16,32,128]{2,1,0:T(8,128)(2,1)} custom-call(bf16[32,16,128]{2,1,0:T(8,128)(2,1)S(1)} %all_to_all.11.got_ref, bf16[256,256]{1,0:T(8,128)(2,1)S(1)} %get-tuple-element.11.order_ref, bf16[128,512]{1,0:T(8,128)(2,1)S(1)} %get-tuple-element.14.normed_ref, f32[128,128]{1,0:T(8,128)S(1)} %get-tuple-element.15.gain_ref, ...), custom_call_target="tpu_custom_call" | custom-call | tf_op jit(solution)/shard_map/update/pallas_call | solution.py:404
  (1 shorter events, 0.0 us)
Async XLA Ops:
  0.0 0.8 %copy-start.2 = (bf16[128,256]{1,0:T(8,128)(2,1)S(1)}, bf16[128,256]{1,0:T(8,128)(2,1)}, u32[]{:S(2)}) copy-start(bf16[128,256]{1,0:T(8,128)(2,1)} %gate_ref.2) | copy-start | bytes 196612
  0.0 0.9 %copy-start.1 = (bf16[128,256]{1,0:T(8,128)(2,1)S(1)}, bf16[128,256]{1,0:T(8,128)(2,1)}, u32[]{:S(2)}) copy-start(bf16[128,256]{1,0:T(8,128)(2,1)} %proj_ref.2) | copy-start | bytes 196612
  0.0 1.0 %copy-start = (bf16[16,32,128]{2,1,0:T(8,128)(2,1)S(1)}, bf16[16,32,128]{2,1,0:T(8,128)(2,1)}, u32[]{:S(2)}) copy-start(bf16[16,32,128]{2,1,0:T(8,128)(2,1)} %pair_ref.1) | copy-start | bytes 393220
  0.0 1.0 %copy-start.8 = (f32[128]{0:T(128)S(1)}, f32[128]{0:T(128)}, u32[]{:S(2)}) copy-start(f32[128]{0:T(128)} %param.16) | copy-start | bytes 1540
  0.0 1.0 %copy-start.9 = (f32[128]{0:T(128)S(1)}, f32[128]{0:T(128)}, u32[]{:S(2)}) copy-start(f32[128]{0:T(128)} %param.17) | copy-start | bytes 1540
  0.1 0.9 %copy-start.5 = (s32[8]{0:T(128)S(1)}, s32[8]{0:T(128)}, u32[]{:S(2)}) copy-start(s32[8]{0:T(128)} %param.11) | copy-start | bytes 100
  0.1 0.9 %copy-start.6 = (f32[128]{0:T(128)S(1)}, f32[128]{0:T(128)}, u32[]{:S(2)}) copy-start(f32[128]{0:T(128)} %param.12) | copy-start | bytes 1540
  0.1 0.9 %copy-start.7 = (f32[128]{0:T(128)S(1)}, f32[128]{0:T(128)}, u32[]{:S(2)}) copy-start(f32[128]{0:T(128)} %param.13) | copy-start | bytes 1540
  20.2 9.5 %copy-start.3 = (bf16[128,128]{1,0:T(8,128)(2,1)S(1)}, bf16[128,128]{1,0:T(8,128)(2,1)}, u32[]{:S(2)}) copy-start(bf16[128,128]{1,0:T(8,128)(2,1)} %proj_ref.3) | copy-start | bytes 98308
  20.3 9.5 %copy-start.4 = (bf16[128,128]{1,0:T(8,128)(2,1)S(1)}, bf16[128,128]{1,0:T(8,128)(2,1)}, u32[]{:S(2)}) copy-start(bf16[128,128]{1,0:T(8,128)(2,1)} %gate_ref.3) | copy-start | bytes 98308

commit v13 on v12

--- a/solution.py
+++ b/solution.py
@@ -152,13 +152,11 @@
     return arrays
 
 
-def orders_kernel(order_ref, eye_ref):
+def order_kernel(order_ref):
     out, source = iota2(order_ref.shape)
     order_ref[...] = one_hot(
         (over(out, SOME) == rest(source, SOME)) & (rest(out, SOME) == over(source, SOME))
     )
-    a, b = iota2(eye_ref.shape)
-    eye_ref[...] = one_hot(a == b)
 
 
 def column(row):
@@ -185,7 +183,6 @@
 def mix_kernel(
     slots,
     order_ref,
-    eye_ref,
     chain_ref,
     pair_ref,
     gain_ref,
@@ -205,17 +202,14 @@
     inner = LANES // cols
     groups = rows // inner
     chunks = sent_ref.shape[0]
-    flat = dot(eye_ref[...], pair_ref[...].reshape(cells, channels), 1, 1)
-    centered = flat - jnp.mean(flat, axis=0, keepdims=True)
-    variance = jnp.mean(centered * centered, axis=0, keepdims=True)
-    gain, bias = column(gain_ref[...]), column(bias_ref[...])
-    normed = (centered * lax.rsqrt(variance + 1e-05) * gain + bias).astype(BF16)
+    flat = pair_ref[...].reshape(cells, channels).astype(F32)
+    normed = layer_norm(flat, gain_ref[...], bias_ref[...]).astype(BF16)
     normed_ref[...] = normed
     for source, target in ((last_gain_ref, last_gain_out), (last_bias_ref, last_bias_out)):
         target[...] = jnp.broadcast_to(column(source[...]), target.shape)
 
-    values = dot(proj_ref[...], normed, 0, 0)
-    gates = dot(gate_ref[...] * 0.5, normed, 0, 0)
+    values = dot(proj_ref[...], normed, 0, 1)
+    gates = dot(gate_ref[...] * 0.5, normed, 0, 1)
     mask = cell_mask(chain_ref[...], slots, rows, cols)
     mixed = (sigmoid(gates) * values * mask).astype(BF16)
 
@@ -310,7 +304,7 @@
         for row in range(rows)
     ]
     gain, bias = gain_ref[...], bias_ref[...]
-    opened = sigmoid(dot(normed_ref[...], gate_ref[...] * 0.5, 0, 0))
+    opened = sigmoid(dot(normed_ref[...], gate_ref[...] * 0.5))
     results = []
     for g in range(groups):
         values = jnp.concatenate(
@@ -354,33 +348,29 @@
     grid_rows = split[0] * split[1]
     devices = grid_rows * grid_cols
     slots = rows * grid_rows // chain_lengths.shape[0]
-    order, eye = pl.pallas_call(
-        orders_kernel,
-        out_shape=(
-            jax.ShapeDtypeStruct((SOME * SOME, SOME * SOME), BF16),
-            jax.ShapeDtypeStruct((LANES, LANES), BF16),
-        ),
-        out_specs=[VMEM] * 2,
+    order = pl.pallas_call(
+        order_kernel,
+        out_shape=jax.ShapeDtypeStruct((SOME * SOME, SOME * SOME), BF16),
+        out_specs=VMEM,
         compiler_params=PARAMS,
         cost_estimate=pl.CostEstimate(flops=10**9, bytes_accessed=10**6, transcendentals=0),
-        name="orders",
+        name="order",
     )()
     square = jax.ShapeDtypeStruct((LANES, LANES), F32)
     sent, normed, last_gain, last_bias = pl.pallas_call(
         functools.partial(mix_kernel, slots),
         out_shape=(
             jax.ShapeDtypeStruct((devices, 2 * rows, LANES), BF16),
-            jax.ShapeDtypeStruct((channels, rows * cols), BF16),
+            jax.ShapeDtypeStruct((rows * cols, channels), BF16),
             square,
             square,
         ),
-        in_specs=[VMEM] * 10,
+        in_specs=[VMEM] * 9,
         out_specs=[VMEM] * 4,
         compiler_params=PARAMS,
         name="mix",
     )(
         order,
-        eye,
         chain_lengths.reshape(1, -1),
         pair,
         norm_in_gain.reshape(1, LANES),

time: 31.2 us -> 31.2 us (level)
  no operation moved by 1% of the time
where the time goes in v13:
time: 31.2 us; the launch traced here: 30.9 us
  blocking collectives  27.3 us (88%)
  Pallas kernels  2.61 us (8%)
  local copies, waits for them, and re-layouts  0.92 us (3%)
    all_to_all x1, blocking collectives, exchanged(): got = lax.all_to_all(sent, axes, 0, 0, tiled=True)  17.9 us
    all_to_all x1, blocking collectives, exchanged(): mine = lax.all_to_all(sums, axes, 0, 0, tiled=True)  9.45 us
    pallas_call x1, Pallas kernels, exchanged(): pl.pallas_call(update_kernel, out_shape=jax.ShapeDtypeStruct((rows, cols,...  1.27 us
    pallas_call x1, Pallas kernels, exchanged(): pl.pallas_call(functools.partial(mix_kernel, slots), out_shape=(jax.Shape...  1 us
    unnamed x20, local copies, waits for them, and re-layouts  0.92 us

profile of v13, /device:TPU:0, one launch (start us, length us, event | category | flops | bytes accessed | tf_op | source)
XLA Modules:
  0.0 30.9 jit_solution(5080294166147327412)
XLA Ops:
  0.0 0.0 copy-start.2
  0.0 0.0 copy-start.1
  0.0 0.0 copy-start
  0.0 0.0 copy-start.8
  0.0 0.0 copy-start.9
  0.1 0.0 copy-start.5
  0.1 0.0 copy-start.6
  0.1 0.0 copy-start.7
  0.1 0.7 %copy-done.2 = bf16[128,256]{1,0:T(8,128)(2,1)S(1)} copy-done((bf16[128,256]{1,0:T(8,128)(2,1)S(1)}, bf16[128,256]{1,0:T(8,128)(2,1)}, u32[]{:S(2)}) %copy-start.2) | copy-done | bytes 65560
  0.8 0.0 copy-done.1
  0.9 0.1 copy-done
  1.0 0.0 copy-done.8
  1.0 0.0 copy-done.9
  1.0 0.0 copy-done.5
  1.0 0.0 copy-done.6
  1.0 0.0 copy-done.7
  1.0 1.0 %mix.1 = (bf16[32,32,128]{2,1,0:T(8,128)(2,1)S(1)}, bf16[512,128]{1,0:T(8,128)(2,1)S(1)}, f32[128,128]{1,0:T(8,128)S(1)}, f32[128,128]{1,0:T(8,128)S(1)}) custom-call(bf16[256,256]{1,0:T(8,128)(2,1)S(1)} %order.1.order_ref, s32[1,8]{1,0:T(1,128)S(1)} %bitcast.5, bf16[16,32,128]{2,1,0:T(8,128)(2,1)S(1)} %copy-done, f32[1,128]{1,0:T(1,128)S(1)} %bitcast.6, ...), custom_call_target="tpu_custom_call" | custom-call | tf_op jit(solution)/shard_map/mix/pallas_call | solution.py:360
  2.0 17.9 %all_to_all.10.got_ref = bf16[32,32,128]{2,1,0:T(8,128)(2,1)S(1)} all-to-all(bf16[32,32,128]{2,1,0:T(8,128)(2,1)S(1)} %get-tuple-element.9), channel_id=1, replica_groups=mesh['high'=4,'low'=2,'col'=4] {'col','low','high'}, dimensions={0} | all-to-all | bytes 524288 | tf_op jit(solution)/shard_map/all_to_all | solution.py:384
  19.9 0.3 triangle.1
  20.2 0.0 copy-start.3
  20.2 0.0 copy-start.4
  20.2 9.5 %all_to_all.11.got_ref = bf16[32,16,128]{2,1,0:T(8,128)(2,1)S(1)} all-to-all(bf16[32,16,128]{2,1,0:T(8,128)(2,1)S(1)} %triangle.1), channel_id=1, replica_groups=mesh['high'=4,'low'=2,'col'=4] {'col','low','high'}, dimensions={0} | all-to-all | bytes 262144 | tf_op jit(solution)/shard_map/all_to_all | solution.py:393
  29.7 0.0 copy-done.3
  29.7 0.0 copy-done.4
  29.7 1.3 %update.1 = bf16[16,32,128]{2,1,0:T(8,128)(2,1)} custom-call(bf16[32,16,128]{2,1,0:T(8,128)(2,1)S(1)} %all_to_all.11.got_ref, bf16[256,256]{1,0:T(8,128)(2,1)S(1)} %order.1.order_ref, bf16[512,128]{1,0:T(8,128)(2,1)S(1)} %get-tuple-element.10.normed_ref, f32[128,128]{1,0:T(8,128)S(1)} %get-tuple-element.11.gain_ref, ...), custom_call_target="tpu_custom_call" | custom-call | tf_op jit(solution)/shard_map/update/pallas_call | solution.py:394
  (1 shorter events, 0.0 us)
Async XLA Ops:
  0.0 0.8 %copy-start.2 = (bf16[128,256]{1,0:T(8,128)(2,1)S(1)}, bf16[128,256]{1,0:T(8,128)(2,1)}, u32[]{:S(2)}) copy-start(bf16[128,256]{1,0:T(8,128)(2,1)} %gate_ref.2) | copy-start | bytes 196612
  0.0 0.9 %copy-start.1 = (bf16[128,256]{1,0:T(8,128)(2,1)S(1)}, bf16[128,256]{1,0:T(8,128)(2,1)}, u32[]{:S(2)}) copy-start(bf16[128,256]{1,0:T(8,128)(2,1)} %proj_ref.2) | copy-start | bytes 196612
  0.0 1.0 %copy-start = (bf16[16,32,128]{2,1,0:T(8,128)(2,1)S(1)}, bf16[16,32,128]{2,1,0:T(8,128)(2,1)}, u32[]{:S(2)}) copy-start(bf16[16,32,128]{2,1,0:T(8,128)(2,1)} %pair_ref.1) | copy-start | bytes 393220
  0.0 1.0 %copy-start.8 = (f32[128]{0:T(128)S(1)}, f32[128]{0:T(128)}, u32[]{:S(2)}) copy-start(f32[128]{0:T(128)} %param.16) | copy-start | bytes 1540
  0.0 1.0 %copy-start.9 = (f32[128]{0:T(128)S(1)}, f32[128]{0:T(128)}, u32[]{:S(2)}) copy-start(f32[128]{0:T(128)} %param.17) | copy-start | bytes 1540
  0.1 0.9 %copy-start.5 = (s32[8]{0:T(128)S(1)}, s32[8]{0:T(128)}, u32[]{:S(2)}) copy-start(s32[8]{0:T(128)} %param.11) | copy-start | bytes 100
  0.1 0.9 %copy-start.6 = (f32[128]{0:T(128)S(1)}, f32[128]{0:T(128)}, u32[]{:S(2)}) copy-start(f32[128]{0:T(128)} %param.12) | copy-start | bytes 1540
  0.1 0.9 %copy-start.7 = (f32[128]{0:T(128)S(1)}, f32[128]{0:T(128)}, u32[]{:S(2)}) copy-start(f32[128]{0:T(128)} %param.13) | copy-start | bytes 1540
  20.2 9.5 %copy-start.3 = (bf16[128,128]{1,0:T(8,128)(2,1)S(1)}, bf16[128,128]{1,0:T(8,128)(2,1)}, u32[]{:S(2)}) copy-start(bf16[128,128]{1,0:T(8,128)(2,1)} %proj_ref.3) | copy-start | bytes 98308
  20.2 9.5 %copy-start.4 = (bf16[128,128]{1,0:T(8,128)(2,1)S(1)}, bf16[128,128]{1,0:T(8,128)(2,1)}, u32[]{:S(2)}) copy-start(bf16[128,128]{1,0:T(8,128)(2,1)} %gate_ref.3) | copy-start | bytes 98308

commit v14 on v13

--- a/solution.py
+++ b/solution.py
@@ -175,7 +175,7 @@
             )
         return rest(token, slots) < length
 
-    row_ok = valid(lax.axis_index(("high", "low")) * rows + over(cell, cols))
+    row_ok = valid(lax.axis_index("row") * rows + over(cell, cols))
     col_ok = valid(lax.axis_index("col") * cols + rest(cell, cols))
     return jnp.where(row_ok & col_ok, 1.0, 0.0)
 
@@ -239,12 +239,11 @@
             )
 
 
-def triangle_kernel(split, grid_cols, rows, cols, got_ref, sent_ref):
+def triangle_kernel(grid_rows, grid_cols, rows, cols, got_ref, sent_ref):
     inner = LANES // cols
 
     def place(r, c):
-        z, y = r // split[1], r % split[1]
-        return (c * split[1] + y) * split[0] + z
+        return r * grid_cols + c
 
     def side(which):
         return jnp.concatenate(
@@ -252,7 +251,7 @@
                 jnp.concatenate(
                     [
                         got_ref[place(r, c), which * rows : (which + 1) * rows]
-                        for r in range(split[0] * split[1])
+                        for r in range(grid_rows)
                     ],
                     axis=0,
                 )
@@ -274,7 +273,7 @@
     )
     sums = dot(left, right_by, 1, 1).astype(BF16)
     for c in range(grid_cols):
-        for r in range(split[0] * split[1]):
+        for r in range(grid_rows):
             sent_ref[place(r, c)] = sums[r * rows : (r + 1) * rows, c * LANES : (c + 1) * LANES]
 
 
@@ -330,7 +329,7 @@
 
 
 def exchanged(
-    split,
+    grid_rows,
     grid_cols,
     pair,
     chain_lengths,
@@ -345,7 +344,6 @@
 ):
     rows, cols, channels = pair.shape
     hidden = proj_out.shape[0]
-    grid_rows = split[0] * split[1]
     devices = grid_rows * grid_cols
     slots = rows * grid_rows // chain_lengths.shape[0]
     order = pl.pallas_call(
@@ -380,10 +378,10 @@
         norm_out_gain.reshape(1, LANES),
         norm_out_bias.reshape(1, LANES),
     )
-    axes = ("col", "low", "high")
+    axes = ("row", "col")
     got = lax.all_to_all(sent, axes, 0, 0, tiled=True)
     sums = pl.pallas_call(
-        functools.partial(triangle_kernel, split, grid_cols, rows, cols),
+        functools.partial(triangle_kernel, grid_rows, grid_cols, rows, cols),
         out_shape=jax.ShapeDtypeStruct((devices, rows, LANES), BF16),
         in_specs=[VMEM],
         out_specs=VMEM,
@@ -407,11 +405,6 @@
 
 def solution(mesh):
     grid_rows, grid_cols = mesh.shape["row"], mesh.shape["col"]
-    split = (grid_rows // 2, 2)
-    fine = jax.sharding.Mesh(
-        mesh.devices.reshape(split + (grid_cols,)), ("high", "low", "col")
-    )
-
     def fits(rows, cols, channels, hidden):
         devices = grid_rows * grid_cols
         inner = LANES // cols
@@ -431,10 +424,10 @@
         hidden = arrays[8].shape[0]
         if fits(tokens // grid_rows, others // grid_cols, channels, hidden):
             return jax.shard_map(
-                functools.partial(exchanged, split, grid_cols),
-                mesh=fine,
-                in_specs=(P(("high", "low"), "col", None),) + (P(),) * 9,
-                out_specs=P(("high", "low"), "col", None),
+                functools.partial(exchanged, grid_rows, grid_cols),
+                mesh=mesh,
+                in_specs=(P("row", "col", None),) + (P(),) * 9,
+                out_specs=P("row", "col", None),
                 check_vma=False,
             )(*arrays)
         return jax.shard_map(

time: 31.2 us -> 32 us (1.026)
  blocking collectives: 27.3 us -> 28.1 us
    all_to_all x1, blocking collectives: 9.45 us -> 10.4 us  [exchanged(): mine = lax.all_to_all(sums, axes, 0, 0, tiled=True)]
where the time goes in v14:
time: 32 us; the launch traced here: 31.8 us
  blocking collectives  28.1 us (88%)
  Pallas kernels  2.61 us (8%)
  local copies, waits for them, and re-layouts  0.92 us (3%)
    all_to_all x1, blocking collectives, exchanged(): got = lax.all_to_all(sent, axes, 0, 0, tiled=True)  17.7 us
    all_to_all x1, blocking collectives, exchanged(): mine = lax.all_to_all(sums, axes, 0, 0, tiled=True)  10.4 us
    pallas_call x1, Pallas kernels, exchanged(): pl.pallas_call(update_kernel, out_shape=jax.ShapeDtypeStruct((rows, cols,...  1.26 us
    pallas_call x1, Pallas kernels, exchanged(): pl.pallas_call(functools.partial(mix_kernel, slots), out_shape=(jax.Shape...  1 us
    unnamed x20, local copies, waits for them, and re-layouts  0.92 us

profile of v14, /device:TPU:0, one launch (start us, length us, event | category | flops | bytes accessed | tf_op | source)
XLA Modules:
  0.0 31.8 jit_solution(17441033631139635258)
XLA Ops:
  0.0 0.0 copy-start.2
  0.0 0.0 copy-start.1
  0.0 0.0 copy-start
  0.0 0.0 copy-start.8
  0.0 0.0 copy-start.9
  0.1 0.0 copy-start.5
  0.1 0.0 copy-start.6
  0.1 0.0 copy-start.7
  0.1 0.7 %copy-done.2 = bf16[128,256]{1,0:T(8,128)(2,1)S(1)} copy-done((bf16[128,256]{1,0:T(8,128)(2,1)S(1)}, bf16[128,256]{1,0:T(8,128)(2,1)}, u32[]{:S(2)}) %copy-start.2) | copy-done | bytes 65560
  0.8 0.0 copy-done.1
  0.9 0.1 copy-done
  1.0 0.0 copy-done.8
  1.0 0.0 copy-done.9
  1.0 0.0 copy-done.5
  1.0 0.0 copy-done.6
  1.0 0.0 copy-done.7
  1.0 1.0 %mix.1 = (bf16[32,32,128]{2,1,0:T(8,128)(2,1)S(1)}, bf16[512,128]{1,0:T(8,128)(2,1)S(1)}, f32[128,128]{1,0:T(8,128)S(1)}, f32[128,128]{1,0:T(8,128)S(1)}) custom-call(bf16[256,256]{1,0:T(8,128)(2,1)S(1)} %order.1.order_ref, s32[1,8]{1,0:T(1,128)S(1)} %bitcast.5, bf16[16,32,128]{2,1,0:T(8,128)(2,1)S(1)} %copy-done, f32[1,128]{1,0:T(1,128)S(1)} %bitcast.6, ...), custom_call_target="tpu_custom_call" | custom-call | tf_op jit(solution)/shard_map/mix/pallas_call | solution.py:358
  2.0 17.7 %all_to_all.10.got_ref = bf16[32,32,128]{2,1,0:T(8,128)(2,1)S(1)} all-to-all(bf16[32,32,128]{2,1,0:T(8,128)(2,1)S(1)} %get-tuple-element.9), channel_id=1, replica_groups=mesh['row'=8,'col'=4] {'row','col'}, dimensions={0} | all-to-all | bytes 524288 | tf_op jit(solution)/shard_map/all_to_all | solution.py:382
  19.7 0.3 triangle.1
  20.0 0.0 copy-start.3
  20.0 0.0 copy-start.4
  20.0 10.4 %all_to_all.11.got_ref = bf16[32,16,128]{2,1,0:T(8,128)(2,1)S(1)} all-to-all(bf16[32,16,128]{2,1,0:T(8,128)(2,1)S(1)} %triangle.1), channel_id=1, replica_groups=mesh['row'=8,'col'=4] {'row','col'}, dimensions={0} | all-to-all | bytes 262144 | tf_op jit(solution)/shard_map/all_to_all | solution.py:391
  30.5 0.0 copy-done.3
  30.5 0.0 copy-done.4
  30.5 1.3 %update.1 = bf16[16,32,128]{2,1,0:T(8,128)(2,1)} custom-call(bf16[32,16,128]{2,1,0:T(8,128)(2,1)S(1)} %all_to_all.11.got_ref, bf16[256,256]{1,0:T(8,128)(2,1)S(1)} %order.1.order_ref, bf16[512,128]{1,0:T(8,128)(2,1)S(1)} %get-tuple-element.10.normed_ref, f32[128,128]{1,0:T(8,128)S(1)} %get-tuple-element.11.gain_ref, ...), custom_call_target="tpu_custom_call" | custom-call | tf_op jit(solution)/shard_map/update/pallas_call | solution.py:392
  (1 shorter events, 0.0 us)
Async XLA Ops:
  0.0 0.8 %copy-start.2 = (bf16[128,256]{1,0:T(8,128)(2,1)S(1)}, bf16[128,256]{1,0:T(8,128)(2,1)}, u32[]{:S(2)}) copy-start(bf16[128,256]{1,0:T(8,128)(2,1)} %gate_ref.2) | copy-start | bytes 196612
  0.0 0.9 %copy-start.1 = (bf16[128,256]{1,0:T(8,128)(2,1)S(1)}, bf16[128,256]{1,0:T(8,128)(2,1)}, u32[]{:S(2)}) copy-start(bf16[128,256]{1,0:T(8,128)(2,1)} %proj_ref.2) | copy-start | bytes 196612
  0.0 1.0 %copy-start = (bf16[16,32,128]{2,1,0:T(8,128)(2,1)S(1)}, bf16[16,32,128]{2,1,0:T(8,128)(2,1)}, u32[]{:S(2)}) copy-start(bf16[16,32,128]{2,1,0:T(8,128)(2,1)} %pair_ref.1) | copy-start | bytes 393220
  0.0 1.0 %copy-start.8 = (f32[128]{0:T(128)S(1)}, f32[128]{0:T(128)}, u32[]{:S(2)}) copy-start(f32[128]{0:T(128)} %param.16) | copy-start | bytes 1540
  0.0 1.0 %copy-start.9 = (f32[128]{0:T(128)S(1)}, f32[128]{0:T(128)}, u32[]{:S(2)}) copy-start(f32[128]{0:T(128)} %param.17) | copy-start | bytes 1540
  0.1 0.9 %copy-start.5 = (s32[8]{0:T(128)S(1)}, s32[8]{0:T(128)}, u32[]{:S(2)}) copy-start(s32[8]{0:T(128)} %param.11) | copy-start | bytes 100
  0.1 0.9 %copy-start.6 = (f32[128]{0:T(128)S(1)}, f32[128]{0:T(128)}, u32[]{:S(2)}) copy-start(f32[128]{0:T(128)} %param.12) | copy-start | bytes 1540
  0.1 0.9 %copy-start.7 = (f32[128]{0:T(128)S(1)}, f32[128]{0:T(128)}, u32[]{:S(2)}) copy-start(f32[128]{0:T(128)} %param.13) | copy-start | bytes 1540
  20.0 10.5 %copy-start.3 = (bf16[128,128]{1,0:T(8,128)(2,1)S(1)}, bf16[128,128]{1,0:T(8,128)(2,1)}, u32[]{:S(2)}) copy-start(bf16[128,128]{1,0:T(8,128)(2,1)} %proj_ref.3) | copy-start | bytes 98308
  20.0 10.5 %copy-start.4 = (bf16[128,128]{1,0:T(8,128)(2,1)S(1)}, bf16[128,128]{1,0:T(8,128)(2,1)}, u32[]{:S(2)}) copy-start(bf16[128,128]{1,0:T(8,128)(2,1)} %gate_ref.3) | copy-start | bytes 98308

commit v15 on v13

--- a/solution.py
+++ b/solution.py
@@ -303,21 +303,26 @@
         jnp.concatenate([part[row * SOME : (row + 1) * SOME] for part in parts], axis=0)
         for row in range(rows)
     ]
-    gain, bias = gain_ref[...], bias_ref[...]
     opened = sigmoid(dot(normed_ref[...], gate_ref[...] * 0.5))
+    values = jnp.concatenate(
+        [
+            jnp.concatenate(
+                exchange_blocks(lines[g * inner : (g + 1) * inner], cols), axis=0
+            )
+            for g in range(groups)
+        ],
+        axis=1,
+    ).astype(F32)
+    mean = jnp.mean(values, axis=0, keepdims=True)
+    centered = values - mean
+    variance = jnp.mean(centered * centered, axis=0, keepdims=True)
+    scaled = centered * lax.rsqrt(variance + 1e-05)
+    tri_normed = (scaled * gain_ref[:, :1] + bias_ref[:, :1]).astype(BF16)
+    update = (opened * dot(tri_normed, proj_ref[...], 0, 0)).astype(BF16)
     results = []
     for g in range(groups):
-        values = jnp.concatenate(
-            exchange_blocks(lines[g * inner : (g + 1) * inner], cols), axis=0
-        ).astype(F32)
-        mean = jnp.mean(values, axis=0, keepdims=True)
-        centered = values - mean
-        variance = jnp.mean(centered * centered, axis=0, keepdims=True)
-        tri_normed = (centered * lax.rsqrt(variance + 1e-05) * gain + bias).astype(BF16)
-        projected = dot(tri_normed, proj_ref[...], 0, 0)
-        update = (opened[g * LANES : (g + 1) * LANES] * projected).astype(BF16)
         here = pl.ds(g * inner, inner)
-        out_ref[here] = update.reshape(inner, cols, channels)
+        out_ref[here] = update[g * LANES : (g + 1) * LANES].reshape(inner, cols, channels)
         results.append(pltpu.make_async_copy(out_ref.at[here], out_hbm.at[here], out_sems.at[g]))
         results[-1].start()
     for copy in results:

time: 31.2 us -> 31.2 us (level)
  no operation moved by 1% of the time
where the time goes in v15:
time: 31.2 us; the launch traced here: 31 us
  blocking collectives  27.3 us (88%)
  Pallas kernels  2.63 us (8%)
  local copies, waits for them, and re-layouts  0.92 us (3%)
    all_to_all x1, blocking collectives, exchanged(): got = lax.all_to_all(sent, axes, 0, 0, tiled=True)  17.9 us
    all_to_all x1, blocking collectives, exchanged(): mine = lax.all_to_all(sums, axes, 0, 0, tiled=True)  9.45 us
    pallas_call x1, Pallas kernels, exchanged(): pl.pallas_call(update_kernel, out_shape=jax.ShapeDtypeStruct((rows, cols,...  1.29 us
    pallas_call x1, Pallas kernels, exchanged(): pl.pallas_call(functools.partial(mix_kernel, slots), out_shape=(jax.Shape...  1 us
    unnamed x20, local copies, waits for them, and re-layouts  0.92 us

profile of v15, /device:TPU:0, one launch (start us, length us, event | category | flops | bytes accessed | tf_op | source)
XLA Modules:
  0.0 31.0 jit_solution(1266566076672005316)
XLA Ops:
  0.0 0.0 copy-start.2
  0.0 0.0 copy-start.1
  0.0 0.0 copy-start
  0.0 0.0 copy-start.8
  0.0 0.0 copy-start.9
  0.1 0.0 copy-start.5
  0.1 0.0 copy-start.6
  0.1 0.0 copy-start.7
  0.1 0.7 %copy-done.2 = bf16[128,256]{1,0:T(8,128)(2,1)S(1)} copy-done((bf16[128,256]{1,0:T(8,128)(2,1)S(1)}, bf16[128,256]{1,0:T(8,128)(2,1)}, u32[]{:S(2)}) %copy-start.2) | copy-done | bytes 65560
  0.8 0.0 copy-done.1
  0.9 0.1 copy-done
  1.0 0.0 copy-done.8
  1.0 0.0 copy-done.9
  1.0 0.0 copy-done.5
  1.0 0.0 copy-done.6
  1.0 0.0 copy-done.7
  1.0 1.0 %mix.1 = (bf16[32,32,128]{2,1,0:T(8,128)(2,1)S(1)}, bf16[512,128]{1,0:T(8,128)(2,1)S(1)}, f32[128,128]{1,0:T(8,128)S(1)}, f32[128,128]{1,0:T(8,128)S(1)}) custom-call(bf16[256,256]{1,0:T(8,128)(2,1)S(1)} %order.1.order_ref, s32[1,8]{1,0:T(1,128)S(1)} %bitcast.5, bf16[16,32,128]{2,1,0:T(8,128)(2,1)S(1)} %copy-done, f32[1,128]{1,0:T(1,128)S(1)} %bitcast.6, ...), custom_call_target="tpu_custom_call" | custom-call | tf_op jit(solution)/shard_map/mix/pallas_call | solution.py:365
  2.0 17.9 %all_to_all.10.got_ref = bf16[32,32,128]{2,1,0:T(8,128)(2,1)S(1)} all-to-all(bf16[32,32,128]{2,1,0:T(8,128)(2,1)S(1)} %get-tuple-element.9), channel_id=1, replica_groups=mesh['high'=4,'low'=2,'col'=4] {'col','low','high'}, dimensions={0} | all-to-all | bytes 524288 | tf_op jit(solution)/shard_map/all_to_all | solution.py:389
  19.9 0.3 triangle.1
  20.2 0.0 copy-start.3
  20.2 0.0 copy-start.4
  20.2 9.5 %all_to_all.11.got_ref = bf16[32,16,128]{2,1,0:T(8,128)(2,1)S(1)} all-to-all(bf16[32,16,128]{2,1,0:T(8,128)(2,1)S(1)} %triangle.1), channel_id=1, replica_groups=mesh['high'=4,'low'=2,'col'=4] {'col','low','high'}, dimensions={0} | all-to-all | bytes 262144 | tf_op jit(solution)/shard_map/all_to_all | solution.py:398
  29.7 0.0 copy-done.3
  29.7 0.0 copy-done.4
  29.7 1.3 %update.1 = bf16[16,32,128]{2,1,0:T(8,128)(2,1)} custom-call(bf16[32,16,128]{2,1,0:T(8,128)(2,1)S(1)} %all_to_all.11.got_ref, bf16[256,256]{1,0:T(8,128)(2,1)S(1)} %order.1.order_ref, bf16[512,128]{1,0:T(8,128)(2,1)S(1)} %get-tuple-element.10.normed_ref, f32[128,128]{1,0:T(8,128)S(1)} %get-tuple-element.11.gain_ref, ...), custom_call_target="tpu_custom_call" | custom-call | tf_op jit(solution)/shard_map/update/pallas_call | solution.py:399
  (1 shorter events, 0.0 us)
Async XLA Ops:
  0.0 0.8 %copy-start.2 = (bf16[128,256]{1,0:T(8,128)(2,1)S(1)}, bf16[128,256]{1,0:T(8,128)(2,1)}, u32[]{:S(2)}) copy-start(bf16[128,256]{1,0:T(8,128)(2,1)} %gate_ref.2) | copy-start | bytes 196612
  0.0 0.9 %copy-start.1 = (bf16[128,256]{1,0:T(8,128)(2,1)S(1)}, bf16[128,256]{1,0:T(8,128)(2,1)}, u32[]{:S(2)}) copy-start(bf16[128,256]{1,0:T(8,128)(2,1)} %proj_ref.2) | copy-start | bytes 196612
  0.0 1.0 %copy-start = (bf16[16,32,128]{2,1,0:T(8,128)(2,1)S(1)}, bf16[16,32,128]{2,1,0:T(8,128)(2,1)}, u32[]{:S(2)}) copy-start(bf16[16,32,128]{2,1,0:T(8,128)(2,1)} %pair_ref.1) | copy-start | bytes 393220
  0.0 1.0 %copy-start.8 = (f32[128]{0:T(128)S(1)}, f32[128]{0:T(128)}, u32[]{:S(2)}) copy-start(f32[128]{0:T(128)} %param.16) | copy-start | bytes 1540
  0.0 1.0 %copy-start.9 = (f32[128]{0:T(128)S(1)}, f32[128]{0:T(128)}, u32[]{:S(2)}) copy-start(f32[128]{0:T(128)} %param.17) | copy-start | bytes 1540
  0.1 0.9 %copy-start.5 = (s32[8]{0:T(128)S(1)}, s32[8]{0:T(128)}, u32[]{:S(2)}) copy-start(s32[8]{0:T(128)} %param.11) | copy-start | bytes 100
  0.1 0.9 %copy-start.6 = (f32[128]{0:T(128)S(1)}, f32[128]{0:T(128)}, u32[]{:S(2)}) copy-start(f32[128]{0:T(128)} %param.12) | copy-start | bytes 1540
  0.1 0.9 %copy-start.7 = (f32[128]{0:T(128)S(1)}, f32[128]{0:T(128)}, u32[]{:S(2)}) copy-start(f32[128]{0:T(128)} %param.13) | copy-start | bytes 1540
  20.2 9.5 %copy-start.3 = (bf16[128,128]{1,0:T(8,128)(2,1)S(1)}, bf16[128,128]{1,0:T(8,128)(2,1)}, u32[]{:S(2)}) copy-start(bf16[128,128]{1,0:T(8,128)(2,1)} %proj_ref.3) | copy-start | bytes 98308
  20.2 9.5 %copy-start.4 = (bf16[128,128]{1,0:T(8,128)(2,1)S(1)}, bf16[128,128]{1,0:T(8,128)(2,1)}, u32[]{:S(2)}) copy-start(bf16[128,128]{1,0:T(8,128)(2,1)} %gate_ref.3) | copy-start | bytes 98308

commit v16 on v14

--- a/solution.py
+++ b/solution.py
@@ -239,11 +239,11 @@
             )
 
 
-def triangle_kernel(grid_rows, grid_cols, rows, cols, got_ref, sent_ref):
+def triangle_kernel(ring, grid_rows, grid_cols, rows, cols, got_ref, sent_ref):
     inner = LANES // cols
 
     def place(r, c):
-        return r * grid_cols + c
+        return ring.index(r * grid_cols + c)
 
     def side(which):
         return jnp.concatenate(
@@ -326,6 +326,16 @@
 VMEM = pl.BlockSpec(memory_space=pltpu.VMEM)
 HBM = pl.BlockSpec(memory_space=pltpu.HBM)
 PARAMS = pltpu.CompilerParams(vmem_limit_bytes=32 * 1024 * 1024)
+
+
+def ring_of(grid_rows, grid_cols):
+    return [
+        (z * 2 + y) * grid_cols + x * 2 + core
+        for x in range(grid_cols // 2)
+        for y in range(2)
+        for z in range(grid_rows // 2)
+        for core in range(2)
+    ]
 
 
 def exchanged(
@@ -378,17 +388,23 @@
         norm_out_gain.reshape(1, LANES),
         norm_out_bias.reshape(1, LANES),
     )
-    axes = ("row", "col")
-    got = lax.all_to_all(sent, axes, 0, 0, tiled=True)
+    ring = ring_of(grid_rows, grid_cols)
+
+    def exchange(chunks):
+        return lax.all_to_all(
+            chunks, ("row", "col"), 0, 0, tiled=True, axis_index_groups=[ring]
+        )
+
+    got = exchange(sent)
     sums = pl.pallas_call(
-        functools.partial(triangle_kernel, grid_rows, grid_cols, rows, cols),
+        functools.partial(triangle_kernel, ring, grid_rows, grid_cols, rows, cols),
         out_shape=jax.ShapeDtypeStruct((devices, rows, LANES), BF16),
         in_specs=[VMEM],
         out_specs=VMEM,
         compiler_params=PARAMS,
         name="triangle",
     )(got)
-    mine = lax.all_to_all(sums, axes, 0, 0, tiled=True)
+    mine = exchange(sums)
     return pl.pallas_call(
         update_kernel,
         out_shape=jax.ShapeDtypeStruct((rows, cols, channels), BF16),
@@ -417,6 +433,8 @@
             and rows == SOME
             and rows % inner == 0
             and devices % SOME == 0
+            and grid_rows % 2 == 0
+            and grid_cols % 2 == 0
         )
 
     def call(*arrays):

time: 32 us -> 31.8 us (level)
  no operation moved by 1% of the time
where the time goes in v16:
time: 31.8 us; the launch traced here: 31.6 us
  blocking collectives  28 us (88%)
  Pallas kernels  2.61 us (8%)
  local copies, waits for them, and re-layouts  0.92 us (3%)
    all_to_all x2, blocking collectives, exchange(): lax.all_to_all(chunks, ('row', 'col'), 0, 0, tiled=True, axis_index_group...  28 us
    pallas_call x1, Pallas kernels, exchanged(): pl.pallas_call(update_kernel, out_shape=jax.ShapeDtypeStruct((rows, cols,...  1.27 us
    pallas_call x1, Pallas kernels, exchanged(): pl.pallas_call(functools.partial(mix_kernel, slots), out_shape=(jax.Shape...  1 us
    unnamed x20, local copies, waits for them, and re-layouts  0.92 us

profile of v16, /device:TPU:0, one launch (start us, length us, event | category | flops | bytes accessed | tf_op | source)
XLA Modules:
  0.0 31.6 jit_solution(16451441406721828128)
XLA Ops:
  0.0 0.0 copy-start.2
  0.0 0.0 copy-start.1
  0.0 0.0 copy-start
  0.0 0.0 copy-start.8
  0.0 0.0 copy-start.9
  0.1 0.0 copy-start.5
  0.1 0.0 copy-start.6
  0.1 0.0 copy-start.7
  0.1 0.7 %copy-done.2 = bf16[128,256]{1,0:T(8,128)(2,1)S(1)} copy-done((bf16[128,256]{1,0:T(8,128)(2,1)S(1)}, bf16[128,256]{1,0:T(8,128)(2,1)}, u32[]{:S(2)}) %copy-start.2) | copy-done | bytes 65560
  0.8 0.0 copy-done.1
  0.9 0.1 copy-done
  1.0 0.0 copy-done.8
  1.0 0.0 copy-done.9
  1.0 0.0 copy-done.5
  1.0 0.0 copy-done.6
  1.0 0.0 copy-done.7
  1.0 1.0 %mix.1 = (bf16[32,32,128]{2,1,0:T(8,128)(2,1)S(1)}, bf16[512,128]{1,0:T(8,128)(2,1)S(1)}, f32[128,128]{1,0:T(8,128)S(1)}, f32[128,128]{1,0:T(8,128)S(1)}) custom-call(bf16[256,256]{1,0:T(8,128)(2,1)S(1)} %order.1.order_ref, s32[1,8]{1,0:T(1,128)S(1)} %bitcast.5, bf16[16,32,128]{2,1,0:T(8,128)(2,1)S(1)} %copy-done, f32[1,128]{1,0:T(1,128)S(1)} %bitcast.6, ...), custom_call_target="tpu_custom_call" | custom-call | tf_op jit(solution)/shard_map/mix/pallas_call | solution.py:368
  2.0 17.5 %all_to_all.10.got_ref = bf16[32,32,128]{2,1,0:T(8,128)(2,1)S(1)} all-to-all(bf16[32,32,128]{2,1,0:T(8,128)(2,1)S(1)} %get-tuple-element.9), channel_id=1, replica_groups={{0,1,8,9,16,17,24,25,4,5,12,13,20,21,28,29,2,3,10,11,18,19,26,27,6,7,14..., dimensions={0} | all-to-all | bytes 524288 | tf_op jit(solution)/shard_map/all_to_all | solution.py:394
  19.5 0.3 triangle.1
  19.8 0.0 copy-start.3
  19.8 0.0 copy-start.4
  19.8 10.5 %all_to_all.11.got_ref = bf16[32,16,128]{2,1,0:T(8,128)(2,1)S(1)} all-to-all(bf16[32,16,128]{2,1,0:T(8,128)(2,1)S(1)} %triangle.1), channel_id=1, replica_groups={{0,1,8,9,16,17,24,25,4,5,12,13,20,21,28,29,2,3,10,11,18,19,26,27,6,7,14..., dimensions={0} | all-to-all | bytes 262144 | tf_op jit(solution)/shard_map/all_to_all | solution.py:394
  30.3 0.0 copy-done.3
  30.3 0.0 copy-done.4
  30.3 1.3 %update.1 = bf16[16,32,128]{2,1,0:T(8,128)(2,1)} custom-call(bf16[32,16,128]{2,1,0:T(8,128)(2,1)S(1)} %all_to_all.11.got_ref, bf16[256,256]{1,0:T(8,128)(2,1)S(1)} %order.1.order_ref, bf16[512,128]{1,0:T(8,128)(2,1)S(1)} %get-tuple-element.10.normed_ref, f32[128,128]{1,0:T(8,128)S(1)} %get-tuple-element.11.gain_ref, ...), custom_call_target="tpu_custom_call" | custom-call | tf_op jit(solution)/shard_map/update/pallas_call | solution.py:408
  (1 shorter events, 0.0 us)
Async XLA Ops:
  0.0 0.8 %copy-start.2 = (bf16[128,256]{1,0:T(8,128)(2,1)S(1)}, bf16[128,256]{1,0:T(8,128)(2,1)}, u32[]{:S(2)}) copy-start(bf16[128,256]{1,0:T(8,128)(2,1)} %gate_ref.2) | copy-start | bytes 196612
  0.0 0.9 %copy-start.1 = (bf16[128,256]{1,0:T(8,128)(2,1)S(1)}, bf16[128,256]{1,0:T(8,128)(2,1)}, u32[]{:S(2)}) copy-start(bf16[128,256]{1,0:T(8,128)(2,1)} %proj_ref.2) | copy-start | bytes 196612
  0.0 1.0 %copy-start = (bf16[16,32,128]{2,1,0:T(8,128)(2,1)S(1)}, bf16[16,32,128]{2,1,0:T(8,128)(2,1)}, u32[]{:S(2)}) copy-start(bf16[16,32,128]{2,1,0:T(8,128)(2,1)} %pair_ref.1) | copy-start | bytes 393220
  0.0 1.0 %copy-start.8 = (f32[128]{0:T(128)S(1)}, f32[128]{0:T(128)}, u32[]{:S(2)}) copy-start(f32[128]{0:T(128)} %param.16) | copy-start | bytes 1540
  0.0 1.0 %copy-start.9 = (f32[128]{0:T(128)S(1)}, f32[128]{0:T(128)}, u32[]{:S(2)}) copy-start(f32[128]{0:T(128)} %param.17) | copy-start | bytes 1540
  0.1 0.9 %copy-start.5 = (s32[8]{0:T(128)S(1)}, s32[8]{0:T(128)}, u32[]{:S(2)}) copy-start(s32[8]{0:T(128)} %param.11) | copy-start | bytes 100
  0.1 0.9 %copy-start.6 = (f32[128]{0:T(128)S(1)}, f32[128]{0:T(128)}, u32[]{:S(2)}) copy-start(f32[128]{0:T(128)} %param.12) | copy-start | bytes 1540
  0.1 0.9 %copy-start.7 = (f32[128]{0:T(128)S(1)}, f32[128]{0:T(128)}, u32[]{:S(2)}) copy-start(f32[128]{0:T(128)} %param.13) | copy-start | bytes 1540
  19.8 10.5 %copy-start.3 = (bf16[128,128]{1,0:T(8,128)(2,1)S(1)}, bf16[128,128]{1,0:T(8,128)(2,1)}, u32[]{:S(2)}) copy-start(bf16[128,128]{1,0:T(8,128)(2,1)} %proj_ref.3) | copy-start | bytes 98308
  19.8 10.5 %copy-start.4 = (bf16[128,128]{1,0:T(8,128)(2,1)S(1)}, bf16[128,128]{1,0:T(8,128)(2,1)}, u32[]{:S(2)}) copy-start(bf16[128,128]{1,0:T(8,128)(2,1)} %gate_ref.3) | copy-start | bytes 98308

commit v17 on v14

--- a/solution.py
+++ b/solution.py
@@ -239,18 +239,18 @@
             )
 
 
-def triangle_kernel(grid_rows, grid_cols, rows, cols, got_ref, sent_ref):
+def triangle_kernel(ring_in, ring_out, grid_rows, grid_cols, rows, cols, got_ref, sent_ref):
     inner = LANES // cols
 
-    def place(r, c):
-        return r * grid_cols + c
+    def place(ring, r, c):
+        return ring.index(r * grid_cols + c)
 
     def side(which):
         return jnp.concatenate(
             [
                 jnp.concatenate(
                     [
-                        got_ref[place(r, c), which * rows : (which + 1) * rows]
+                        got_ref[place(ring_in, r, c), which * rows : (which + 1) * rows]
                         for r in range(grid_rows)
                     ],
                     axis=0,
@@ -274,10 +274,11 @@
     sums = dot(left, right_by, 1, 1).astype(BF16)
     for c in range(grid_cols):
         for r in range(grid_rows):
-            sent_ref[place(r, c)] = sums[r * rows : (r + 1) * rows, c * LANES : (c + 1) * LANES]
+            sent_ref[place(ring_out, r, c)] = sums[r * rows : (r + 1) * rows, c * LANES : (c + 1) * LANES]
 
 
 def update_kernel(
+    places,
     got_ref,
     order_ref,
     normed_ref,
@@ -295,7 +296,12 @@
     groups = rows // inner
     order = order_ref[...]
     parts = [
-        dot(order, got_ref[part * SOME : (part + 1) * SOME].reshape(SOME * rows, LANES)).astype(BF16)
+        dot(
+            order,
+            jnp.concatenate(
+                [got_ref[place] for place in places[part * SOME : (part + 1) * SOME]], axis=0
+            ),
+        ).astype(BF16)
         for part in range(chunks // SOME)
     ]
     lines = [
@@ -326,6 +332,15 @@
 VMEM = pl.BlockSpec(memory_space=pltpu.VMEM)
 HBM = pl.BlockSpec(memory_space=pltpu.HBM)
 PARAMS = pltpu.CompilerParams(vmem_limit_bytes=32 * 1024 * 1024)
+
+
+def ring_of(axes, grid_rows, grid_cols):
+    sizes = {"z": grid_rows // 2, "y": 2, "x": grid_cols // 2, "c": 2}
+    strides = {"z": 2 * grid_cols, "y": grid_cols, "x": 2, "c": 1}
+    ring = [0]
+    for axis in axes:
+        ring = [device + n * strides[axis] for device in ring for n in range(sizes[axis])]
+    return ring
 
 
 def exchanged(
@@ -378,19 +393,27 @@
         norm_out_gain.reshape(1, LANES),
         norm_out_bias.reshape(1, LANES),
     )
-    axes = ("row", "col")
-    got = lax.all_to_all(sent, axes, 0, 0, tiled=True)
+    ring_in = ring_of("xyzc", grid_rows, grid_cols)
+    ring_out = ring_of("xcyz", grid_rows, grid_cols)
+
+    def exchange(chunks, ring):
+        return lax.all_to_all(
+            chunks, ("row", "col"), 0, 0, tiled=True, axis_index_groups=[ring]
+        )
+
+    got = exchange(sent, ring_in)
     sums = pl.pallas_call(
-        functools.partial(triangle_kernel, grid_rows, grid_cols, rows, cols),
+        functools.partial(triangle_kernel, ring_in, ring_out, grid_rows, grid_cols, rows, cols),
         out_shape=jax.ShapeDtypeStruct((devices, rows, LANES), BF16),
         in_specs=[VMEM],
         out_specs=VMEM,
         compiler_params=PARAMS,
         name="triangle",
     )(got)
-    mine = lax.all_to_all(sums, axes, 0, 0, tiled=True)
+    mine = exchange(sums, ring_out)
+    places = [ring_out.index(device) for device in ring_in]
     return pl.pallas_call(
-        update_kernel,
+        functools.partial(update_kernel, places),
         out_shape=jax.ShapeDtypeStruct((rows, cols, channels), BF16),
         in_specs=[VMEM] * 7,
         out_specs=HBM,
@@ -417,6 +440,8 @@
             and rows == SOME
             and rows % inner == 0
             and devices % SOME == 0
+            and grid_rows % 2 == 0
+            and grid_cols % 2 == 0
         )
 
     def call(*arrays):

time: 32 us -> 31.4 us (0.981)
  blocking collectives: 28.1 us -> 27.6 us
    all_to_all x2, blocking collectives: 28.1 us -> 27.6 us  [exchange(): lax.all_to_all(chunks, ('row', 'col'), 0, 0, tiled=True, axis_index_group...]
where the time goes in v17:
time: 31.4 us; the launch traced here: 31.2 us
  blocking collectives  27.6 us (88%)
  Pallas kernels  2.61 us (8%)
  local copies, waits for them, and re-layouts  0.92 us (3%)
    all_to_all x2, blocking collectives, exchange(): lax.all_to_all(chunks, ('row', 'col'), 0, 0, tiled=True, axis_index_group...  27.6 us
    pallas_call x1, Pallas kernels, exchanged(): pl.pallas_call(functools.partial(update_kernel, places), out_shape=jax.Sh...  1.27 us
    pallas_call x1, Pallas kernels, exchanged(): pl.pallas_call(functools.partial(mix_kernel, slots), out_shape=(jax.Shape...  1 us
    unnamed x20, local copies, waits for them, and re-layouts  0.92 us

profile of v17, /device:TPU:0, one launch (start us, length us, event | category | flops | bytes accessed | tf_op | source)
XLA Modules:
  0.0 31.2 jit_solution(6909686884132714799)
XLA Ops:
  0.0 0.0 copy-start.2
  0.0 0.0 copy-start.1
  0.0 0.0 copy-start
  0.0 0.0 copy-start.8
  0.0 0.0 copy-start.9
  0.1 0.0 copy-start.5
  0.1 0.0 copy-start.6
  0.1 0.0 copy-start.7
  0.1 0.7 %copy-done.2 = bf16[128,256]{1,0:T(8,128)(2,1)S(1)} copy-done((bf16[128,256]{1,0:T(8,128)(2,1)S(1)}, bf16[128,256]{1,0:T(8,128)(2,1)}, u32[]{:S(2)}) %copy-start.2) | copy-done | bytes 65560
  0.8 0.0 copy-done.1
  0.9 0.1 copy-done
  1.0 0.0 copy-done.8
  1.0 0.0 copy-done.9
  1.0 0.0 copy-done.5
  1.0 0.0 copy-done.6
  1.0 0.0 copy-done.7
  1.0 1.0 %mix.1 = (bf16[32,32,128]{2,1,0:T(8,128)(2,1)S(1)}, bf16[512,128]{1,0:T(8,128)(2,1)S(1)}, f32[128,128]{1,0:T(8,128)S(1)}, f32[128,128]{1,0:T(8,128)S(1)}) custom-call(bf16[256,256]{1,0:T(8,128)(2,1)S(1)} %order.1.order_ref, s32[1,8]{1,0:T(1,128)S(1)} %bitcast.5, bf16[16,32,128]{2,1,0:T(8,128)(2,1)S(1)} %copy-done, f32[1,128]{1,0:T(1,128)S(1)} %bitcast.6, ...), custom_call_target="tpu_custom_call" | custom-call | tf_op jit(solution)/shard_map/mix/pallas_call | solution.py:373
  2.0 17.5 %all_to_all.10.got_ref = bf16[32,32,128]{2,1,0:T(8,128)(2,1)S(1)} all-to-all(bf16[32,32,128]{2,1,0:T(8,128)(2,1)S(1)} %get-tuple-element.9), channel_id=1, replica_groups={{0,1,8,9,16,17,24,25,4,5,12,13,20,21,28,29,2,3,10,11,18,19,26,27,6,7,14..., dimensions={0} | all-to-all | bytes 524288 | tf_op jit(solution)/shard_map/all_to_all | solution.py:400
  19.5 0.3 triangle.1
  19.8 0.0 copy-start.3
  19.8 0.0 copy-start.4
  19.8 10.1 %all_to_all.11.got_ref = bf16[32,16,128]{2,1,0:T(8,128)(2,1)S(1)} all-to-all(bf16[32,16,128]{2,1,0:T(8,128)(2,1)S(1)} %triangle.1), channel_id=1, replica_groups={{0,8,16,24,4,12,20,28,1,9,17,25,5,13,21,29,2,10,18,26,6,14,22,30,3,11,1..., dimensions={0} | all-to-all | bytes 262144 | tf_op jit(solution)/shard_map/all_to_all | solution.py:400
  29.9 0.0 copy-done.3
  29.9 0.0 copy-done.4
  29.9 1.3 %update.1 = bf16[16,32,128]{2,1,0:T(8,128)(2,1)} custom-call(bf16[32,16,128]{2,1,0:T(8,128)(2,1)S(1)} %all_to_all.11.got_ref, bf16[256,256]{1,0:T(8,128)(2,1)S(1)} %order.1.order_ref, bf16[512,128]{1,0:T(8,128)(2,1)S(1)} %get-tuple-element.10.normed_ref, f32[128,128]{1,0:T(8,128)S(1)} %get-tuple-element.11.gain_ref, ...), custom_call_target="tpu_custom_call" | custom-call | tf_op jit(solution)/shard_map/update/pallas_call | solution.py:415
  (1 shorter events, 0.0 us)
Async XLA Ops:
  0.0 0.8 %copy-start.2 = (bf16[128,256]{1,0:T(8,128)(2,1)S(1)}, bf16[128,256]{1,0:T(8,128)(2,1)}, u32[]{:S(2)}) copy-start(bf16[128,256]{1,0:T(8,128)(2,1)} %gate_ref.2) | copy-start | bytes 196612
  0.0 0.9 %copy-start.1 = (bf16[128,256]{1,0:T(8,128)(2,1)S(1)}, bf16[128,256]{1,0:T(8,128)(2,1)}, u32[]{:S(2)}) copy-start(bf16[128,256]{1,0:T(8,128)(2,1)} %proj_ref.2) | copy-start | bytes 196612
  0.0 1.0 %copy-start = (bf16[16,32,128]{2,1,0:T(8,128)(2,1)S(1)}, bf16[16,32,128]{2,1,0:T(8,128)(2,1)}, u32[]{:S(2)}) copy-start(bf16[16,32,128]{2,1,0:T(8,128)(2,1)} %pair_ref.1) | copy-start | bytes 393220
  0.0 1.0 %copy-start.8 = (f32[128]{0:T(128)S(1)}, f32[128]{0:T(128)}, u32[]{:S(2)}) copy-start(f32[128]{0:T(128)} %param.16) | copy-start | bytes 1540
  0.0 1.0 %copy-start.9 = (f32[128]{0:T(128)S(1)}, f32[128]{0:T(128)}, u32[]{:S(2)}) copy-start(f32[128]{0:T(128)} %param.17) | copy-start | bytes 1540
  0.1 0.9 %copy-start.5 = (s32[8]{0:T(128)S(1)}, s32[8]{0:T(128)}, u32[]{:S(2)}) copy-start(s32[8]{0:T(128)} %param.11) | copy-start | bytes 100
  0.1 0.9 %copy-start.6 = (f32[128]{0:T(128)S(1)}, f32[128]{0:T(128)}, u32[]{:S(2)}) copy-start(f32[128]{0:T(128)} %param.12) | copy-start | bytes 1540
  0.1 0.9 %copy-start.7 = (f32[128]{0:T(128)S(1)}, f32[128]{0:T(128)}, u32[]{:S(2)}) copy-start(f32[128]{0:T(128)} %param.13) | copy-start | bytes 1540
  19.8 10.1 %copy-start.3 = (bf16[128,128]{1,0:T(8,128)(2,1)S(1)}, bf16[128,128]{1,0:T(8,128)(2,1)}, u32[]{:S(2)}) copy-start(bf16[128,128]{1,0:T(8,128)(2,1)} %proj_ref.3) | copy-start | bytes 98308
  19.8 10.1 %copy-start.4 = (bf16[128,128]{1,0:T(8,128)(2,1)S(1)}, bf16[128,128]{1,0:T(8,128)(2,1)}, u32[]{:S(2)}) copy-start(bf16[128,128]{1,0:T(8,128)(2,1)} %gate_ref.3) | copy-start | bytes 98308

commit v18 on v17

--- a/solution.py
+++ b/solution.py
@@ -175,8 +175,8 @@
             )
         return rest(token, slots) < length
 
-    row_ok = valid(lax.axis_index("row") * rows + over(cell, cols))
-    col_ok = valid(lax.axis_index("col") * cols + rest(cell, cols))
+    row_ok = valid(lax.axis_index(("z", "y")) * rows + over(cell, cols))
+    col_ok = valid(lax.axis_index(("x", "c")) * cols + rest(cell, cols))
     return jnp.where(row_ok & col_ok, 1.0, 0.0)
 
 
@@ -393,15 +393,10 @@
         norm_out_gain.reshape(1, LANES),
         norm_out_bias.reshape(1, LANES),
     )
-    ring_in = ring_of("xyzc", grid_rows, grid_cols)
-    ring_out = ring_of("xcyz", grid_rows, grid_cols)
-
-    def exchange(chunks, ring):
-        return lax.all_to_all(
-            chunks, ("row", "col"), 0, 0, tiled=True, axis_index_groups=[ring]
-        )
-
-    got = exchange(sent, ring_in)
+    axes_in, axes_out = "xyzc", "xcyz"
+    ring_in = ring_of(axes_in, grid_rows, grid_cols)
+    ring_out = ring_of(axes_out, grid_rows, grid_cols)
+    got = lax.all_to_all(sent, tuple(axes_in), 0, 0, tiled=True)
     sums = pl.pallas_call(
         functools.partial(triangle_kernel, ring_in, ring_out, grid_rows, grid_cols, rows, cols),
         out_shape=jax.ShapeDtypeStruct((devices, rows, LANES), BF16),
@@ -410,7 +405,7 @@
         compiler_params=PARAMS,
         name="triangle",
     )(got)
-    mine = exchange(sums, ring_out)
+    mine = lax.all_to_all(sums, tuple(axes_out), 0, 0, tiled=True)
     places = [ring_out.index(device) for device in ring_in]
     return pl.pallas_call(
         functools.partial(update_kernel, places),
@@ -428,6 +423,11 @@
 
 def solution(mesh):
     grid_rows, grid_cols = mesh.shape["row"], mesh.shape["col"]
+    fine = jax.sharding.Mesh(
+        mesh.devices.reshape(max(grid_rows // 2, 1), -1, max(grid_cols // 2, 1), min(grid_cols, 2)),
+        ("z", "y", "x", "c"),
+    )
+
     def fits(rows, cols, channels, hidden):
         devices = grid_rows * grid_cols
         inner = LANES // cols
@@ -450,9 +450,9 @@
         if fits(tokens // grid_rows, others // grid_cols, channels, hidden):
             return jax.shard_map(
                 functools.partial(exchanged, grid_rows, grid_cols),
-                mesh=mesh,
-                in_specs=(P("row", "col", None),) + (P(),) * 9,
-                out_specs=P("row", "col", None),
+                mesh=fine,
+                in_specs=(P(("z", "y"), ("x", "c"), None),) + (P(),) * 9,
+                out_specs=P(("z", "y"), ("x", "c"), None),
                 check_vma=False,
             )(*arrays)
         return jax.shard_map(

time: 31.4 us -> 31.4 us (level)
  no operation moved by 1% of the time
where the time goes in v18:
time: 31.4 us; the launch traced here: 31.2 us
  blocking collectives  27.6 us (88%)
  Pallas kernels  2.61 us (8%)
  local copies, waits for them, and re-layouts  0.92 us (3%)
    all_to_all x1, blocking collectives, exchanged(): got = lax.all_to_all(sent, tuple(axes_in), 0, 0, tiled=True)  17.5 us
    all_to_all x1, blocking collectives, exchanged(): mine = lax.all_to_all(sums, tuple(axes_out), 0, 0, tiled=True)  10.1 us
    pallas_call x1, Pallas kernels, exchanged(): pl.pallas_call(functools.partial(update_kernel, places), out_shape=jax.Sh...  1.27 us
    pallas_call x1, Pallas kernels, exchanged(): pl.pallas_call(functools.partial(mix_kernel, slots), out_shape=(jax.Shape...  1 us
    unnamed x20, local copies, waits for them, and re-layouts  0.92 us

profile of v18, /device:TPU:0, one launch (start us, length us, event | category | flops | bytes accessed | tf_op | source)
XLA Modules:
  0.0 31.2 jit_solution(8308420691345152048)
XLA Ops:
  0.0 0.0 copy-start.2
  0.0 0.0 copy-start.1
  0.0 0.0 copy-start
  0.0 0.0 copy-start.8
  0.0 0.0 copy-start.9
  0.1 0.0 copy-start.5
  0.1 0.0 copy-start.6
  0.1 0.0 copy-start.7
  0.1 0.7 %copy-done.2 = bf16[128,256]{1,0:T(8,128)(2,1)S(1)} copy-done((bf16[128,256]{1,0:T(8,128)(2,1)S(1)}, bf16[128,256]{1,0:T(8,128)(2,1)}, u32[]{:S(2)}) %copy-start.2) | copy-done | bytes 65560
  0.8 0.0 copy-done.1
  0.9 0.1 copy-done
  1.0 0.0 copy-done.8
  1.0 0.0 copy-done.9
  1.0 0.0 copy-done.5
  1.0 0.0 copy-done.6
  1.0 0.0 copy-done.7
  1.0 1.0 %mix.1 = (bf16[32,32,128]{2,1,0:T(8,128)(2,1)S(1)}, bf16[512,128]{1,0:T(8,128)(2,1)S(1)}, f32[128,128]{1,0:T(8,128)S(1)}, f32[128,128]{1,0:T(8,128)S(1)}) custom-call(bf16[256,256]{1,0:T(8,128)(2,1)S(1)} %order.1.order_ref, s32[1,8]{1,0:T(1,128)S(1)} %bitcast.5, bf16[16,32,128]{2,1,0:T(8,128)(2,1)S(1)} %copy-done, f32[1,128]{1,0:T(1,128)S(1)} %bitcast.6, ...), custom_call_target="tpu_custom_call" | custom-call | tf_op jit(solution)/shard_map/mix/pallas_call | solution.py:373
  2.0 17.5 %all_to_all.10.got_ref = bf16[32,32,128]{2,1,0:T(8,128)(2,1)S(1)} all-to-all(bf16[32,32,128]{2,1,0:T(8,128)(2,1)S(1)} %get-tuple-element.9), channel_id=1, replica_groups=mesh['z'=4,'y'=2,'x'=2,'c'=2] {'x','y','z','c'}, dimensions={0} | all-to-all | bytes 524288 | tf_op jit(solution)/shard_map/all_to_all | solution.py:399
  19.5 0.3 triangle.1
  19.8 0.0 copy-start.3
  19.8 0.0 copy-start.4
  19.8 10.1 %all_to_all.11.got_ref = bf16[32,16,128]{2,1,0:T(8,128)(2,1)S(1)} all-to-all(bf16[32,16,128]{2,1,0:T(8,128)(2,1)S(1)} %triangle.1), channel_id=1, replica_groups=mesh['z'=4,'y'=2,'x'=2,'c'=2] {'x','c','y','z'}, dimensions={0} | all-to-all | bytes 262144 | tf_op jit(solution)/shard_map/all_to_all | solution.py:408
  29.9 0.0 copy-done.3
  29.9 0.0 copy-done.4
  29.9 1.3 %update.1 = bf16[16,32,128]{2,1,0:T(8,128)(2,1)} custom-call(bf16[32,16,128]{2,1,0:T(8,128)(2,1)S(1)} %all_to_all.11.got_ref, bf16[256,256]{1,0:T(8,128)(2,1)S(1)} %order.1.order_ref, bf16[512,128]{1,0:T(8,128)(2,1)S(1)} %get-tuple-element.10.normed_ref, f32[128,128]{1,0:T(8,128)S(1)} %get-tuple-element.11.gain_ref, ...), custom_call_target="tpu_custom_call" | custom-call | tf_op jit(solution)/shard_map/update/pallas_call | solution.py:410
  (1 shorter events, 0.0 us)
Async XLA Ops:
  0.0 0.8 %copy-start.2 = (bf16[128,256]{1,0:T(8,128)(2,1)S(1)}, bf16[128,256]{1,0:T(8,128)(2,1)}, u32[]{:S(2)}) copy-start(bf16[128,256]{1,0:T(8,128)(2,1)} %gate_ref.2) | copy-start | bytes 196612
  0.0 0.9 %copy-start.1 = (bf16[128,256]{1,0:T(8,128)(2,1)S(1)}, bf16[128,256]{1,0:T(8,128)(2,1)}, u32[]{:S(2)}) copy-start(bf16[128,256]{1,0:T(8,128)(2,1)} %proj_ref.2) | copy-start | bytes 196612
  0.0 1.0 %copy-start = (bf16[16,32,128]{2,1,0:T(8,128)(2,1)S(1)}, bf16[16,32,128]{2,1,0:T(8,128)(2,1)}, u32[]{:S(2)}) copy-start(bf16[16,32,128]{2,1,0:T(8,128)(2,1)} %pair_ref.1) | copy-start | bytes 393220
  0.0 1.0 %copy-start.8 = (f32[128]{0:T(128)S(1)}, f32[128]{0:T(128)}, u32[]{:S(2)}) copy-start(f32[128]{0:T(128)} %param.16) | copy-start | bytes 1540
  0.0 1.0 %copy-start.9 = (f32[128]{0:T(128)S(1)}, f32[128]{0:T(128)}, u32[]{:S(2)}) copy-start(f32[128]{0:T(128)} %param.17) | copy-start | bytes 1540
  0.1 0.9 %copy-start.5 = (s32[8]{0:T(128)S(1)}, s32[8]{0:T(128)}, u32[]{:S(2)}) copy-start(s32[8]{0:T(128)} %param.11) | copy-start | bytes 100
  0.1 0.9 %copy-start.6 = (f32[128]{0:T(128)S(1)}, f32[128]{0:T(128)}, u32[]{:S(2)}) copy-start(f32[128]{0:T(128)} %param.12) | copy-start | bytes 1540
  0.1 0.9 %copy-start.7 = (f32[128]{0:T(128)S(1)}, f32[128]{0:T(128)}, u32[]{:S(2)}) copy-start(f32[128]{0:T(128)} %param.13) | copy-start | bytes 1540
  19.8 10.1 %copy-start.3 = (bf16[128,128]{1,0:T(8,128)(2,1)S(1)}, bf16[128,128]{1,0:T(8,128)(2,1)}, u32[]{:S(2)}) copy-start(bf16[128,128]{1,0:T(8,128)(2,1)} %proj_ref.3) | copy-start | bytes 98308
  19.8 10.1 %copy-start.4 = (bf16[128,128]{1,0:T(8,128)(2,1)S(1)}, bf16[128,128]{1,0:T(8,128)(2,1)}, u32[]{:S(2)}) copy-start(bf16[128,128]{1,0:T(8,128)(2,1)} %gate_ref.3) | copy-start | bytes 98308

commit v19 on v18

--- a/solution.py
+++ b/solution.py
@@ -393,7 +393,7 @@
         norm_out_gain.reshape(1, LANES),
         norm_out_bias.reshape(1, LANES),
     )
-    axes_in, axes_out = "xyzc", "xcyz"
+    axes_in, axes_out = "cxyz", "cxyz"
     ring_in = ring_of(axes_in, grid_rows, grid_cols)
     ring_out = ring_of(axes_out, grid_rows, grid_cols)
     got = lax.all_to_all(sent, tuple(axes_in), 0, 0, tiled=True)

time: 31.4 us -> 31.6 us (level)
    all_to_all x1, blocking collectives: 17.5 us -> 18.1 us  [exchanged(): got = lax.all_to_all(sent, tuple(axes_in), 0, 0, tiled=True)]
    all_to_all x1, blocking collectives: 10.1 us -> 9.69 us  [exchanged(): mine = lax.all_to_all(sums, tuple(axes_out), 0, 0, tiled=True)]
where the time goes in v19:
time: 31.6 us; the launch traced here: 31.4 us
  blocking collectives  27.7 us (88%)
  Pallas kernels  2.61 us (8%)
  local copies, waits for them, and re-layouts  0.92 us (3%)
    all_to_all x1, blocking collectives, exchanged(): got = lax.all_to_all(sent, tuple(axes_in), 0, 0, tiled=True)  18.1 us
    all_to_all x1, blocking collectives, exchanged(): mine = lax.all_to_all(sums, tuple(axes_out), 0, 0, tiled=True)  9.69 us
    pallas_call x1, Pallas kernels, exchanged(): pl.pallas_call(functools.partial(update_kernel, places), out_shape=jax.Sh...  1.26 us
    pallas_call x1, Pallas kernels, exchanged(): pl.pallas_call(functools.partial(mix_kernel, slots), out_shape=(jax.Shape...  1 us
    unnamed x20, local copies, waits for them, and re-layouts  0.92 us

profile of v19, /device:TPU:0, one launch (start us, length us, event | category | flops | bytes accessed | tf_op | source)
XLA Modules:
  0.0 31.4 jit_solution(16176281396532851627)
XLA Ops:
  0.0 0.0 copy-start.2
  0.0 0.0 copy-start.1
  0.0 0.0 copy-start
  0.0 0.0 copy-start.8
  0.0 0.0 copy-start.9
  0.1 0.0 copy-start.5
  0.1 0.0 copy-start.6
  0.1 0.0 copy-start.7
  0.1 0.7 %copy-done.2 = bf16[128,256]{1,0:T(8,128)(2,1)S(1)} copy-done((bf16[128,256]{1,0:T(8,128)(2,1)S(1)}, bf16[128,256]{1,0:T(8,128)(2,1)}, u32[]{:S(2)}) %copy-start.2) | copy-done | bytes 65560
  0.8 0.0 copy-done.1
  0.9 0.1 copy-done
  1.0 0.0 copy-done.8
  1.0 0.0 copy-done.9
  1.0 0.0 copy-done.5
  1.0 0.0 copy-done.6
  1.0 0.0 copy-done.7
  1.0 1.0 %mix.1 = (bf16[32,32,128]{2,1,0:T(8,128)(2,1)S(1)}, bf16[512,128]{1,0:T(8,128)(2,1)S(1)}, f32[128,128]{1,0:T(8,128)S(1)}, f32[128,128]{1,0:T(8,128)S(1)}) custom-call(bf16[256,256]{1,0:T(8,128)(2,1)S(1)} %order.1.order_ref, s32[1,8]{1,0:T(1,128)S(1)} %bitcast.5, bf16[16,32,128]{2,1,0:T(8,128)(2,1)S(1)} %copy-done, f32[1,128]{1,0:T(1,128)S(1)} %bitcast.6, ...), custom_call_target="tpu_custom_call" | custom-call | tf_op jit(solution)/shard_map/mix/pallas_call | solution.py:373
  2.0 18.1 %all_to_all.10.got_ref = bf16[32,32,128]{2,1,0:T(8,128)(2,1)S(1)} all-to-all(bf16[32,32,128]{2,1,0:T(8,128)(2,1)S(1)} %get-tuple-element.9), channel_id=1, replica_groups=mesh['z'=4,'y'=2,'x'=2,'c'=2] {'c','x','y','z'}, dimensions={0} | all-to-all | bytes 524288 | tf_op jit(solution)/shard_map/all_to_all | solution.py:399
  20.1 0.3 triangle.1
  20.4 0.0 copy-start.3
  20.4 0.0 copy-start.4
  20.4 9.7 %all_to_all.11.got_ref = bf16[32,16,128]{2,1,0:T(8,128)(2,1)S(1)} all-to-all(bf16[32,16,128]{2,1,0:T(8,128)(2,1)S(1)} %triangle.1), channel_id=1, replica_groups=mesh['z'=4,'y'=2,'x'=2,'c'=2] {'c','x','y','z'}, dimensions={0} | all-to-all | bytes 262144 | tf_op jit(solution)/shard_map/all_to_all | solution.py:408
  30.1 0.0 copy-done.3
  30.1 0.0 copy-done.4
  30.1 1.3 %update.1 = bf16[16,32,128]{2,1,0:T(8,128)(2,1)} custom-call(bf16[32,16,128]{2,1,0:T(8,128)(2,1)S(1)} %all_to_all.11.got_ref, bf16[256,256]{1,0:T(8,128)(2,1)S(1)} %order.1.order_ref, bf16[512,128]{1,0:T(8,128)(2,1)S(1)} %get-tuple-element.10.normed_ref, f32[128,128]{1,0:T(8,128)S(1)} %get-tuple-element.11.gain_ref, ...), custom_call_target="tpu_custom_call" | custom-call | tf_op jit(solution)/shard_map/update/pallas_call | solution.py:410
  (1 shorter events, 0.0 us)
Async XLA Ops:
  0.0 0.8 %copy-start.2 = (bf16[128,256]{1,0:T(8,128)(2,1)S(1)}, bf16[128,256]{1,0:T(8,128)(2,1)}, u32[]{:S(2)}) copy-start(bf16[128,256]{1,0:T(8,128)(2,1)} %gate_ref.2) | copy-start | bytes 196612
  0.0 0.9 %copy-start.1 = (bf16[128,256]{1,0:T(8,128)(2,1)S(1)}, bf16[128,256]{1,0:T(8,128)(2,1)}, u32[]{:S(2)}) copy-start(bf16[128,256]{1,0:T(8,128)(2,1)} %proj_ref.2) | copy-start | bytes 196612
  0.0 1.0 %copy-start = (bf16[16,32,128]{2,1,0:T(8,128)(2,1)S(1)}, bf16[16,32,128]{2,1,0:T(8,128)(2,1)}, u32[]{:S(2)}) copy-start(bf16[16,32,128]{2,1,0:T(8,128)(2,1)} %pair_ref.1) | copy-start | bytes 393220
  0.0 1.0 %copy-start.8 = (f32[128]{0:T(128)S(1)}, f32[128]{0:T(128)}, u32[]{:S(2)}) copy-start(f32[128]{0:T(128)} %param.16) | copy-start | bytes 1540
  0.0 1.0 %copy-start.9 = (f32[128]{0:T(128)S(1)}, f32[128]{0:T(128)}, u32[]{:S(2)}) copy-start(f32[128]{0:T(128)} %param.17) | copy-start | bytes 1540
  0.1 0.9 %copy-start.5 = (s32[8]{0:T(128)S(1)}, s32[8]{0:T(128)}, u32[]{:S(2)}) copy-start(s32[8]{0:T(128)} %param.11) | copy-start | bytes 100
  0.1 0.9 %copy-start.6 = (f32[128]{0:T(128)S(1)}, f32[128]{0:T(128)}, u32[]{:S(2)}) copy-start(f32[128]{0:T(128)} %param.12) | copy-start | bytes 1540
  0.1 0.9 %copy-start.7 = (f32[128]{0:T(128)S(1)}, f32[128]{0:T(128)}, u32[]{:S(2)}) copy-start(f32[128]{0:T(128)} %param.13) | copy-start | bytes 1540
  20.4 9.7 %copy-start.3 = (bf16[128,128]{1,0:T(8,128)(2,1)S(1)}, bf16[128,128]{1,0:T(8,128)(2,1)}, u32[]{:S(2)}) copy-start(bf16[128,128]{1,0:T(8,128)(2,1)} %proj_ref.3) | copy-start | bytes 98308
  20.4 9.7 %copy-start.4 = (bf16[128,128]{1,0:T(8,128)(2,1)S(1)}, bf16[128,128]{1,0:T(8,128)(2,1)}, u32[]{:S(2)}) copy-start(bf16[128,128]{1,0:T(8,128)(2,1)} %gate_ref.3) | copy-start | bytes 98308

commit v20 on v19

--- a/solution.py
+++ b/solution.py
@@ -393,7 +393,7 @@
         norm_out_gain.reshape(1, LANES),
         norm_out_bias.reshape(1, LANES),
     )
-    axes_in, axes_out = "cxyz", "cxyz"
+    axes_in, axes_out = "ycxz", "ycxz"
     ring_in = ring_of(axes_in, grid_rows, grid_cols)
     ring_out = ring_of(axes_out, grid_rows, grid_cols)
     got = lax.all_to_all(sent, tuple(axes_in), 0, 0, tiled=True)

time: 31.6 us -> 31.2 us (0.987)
  blocking collectives: 27.7 us -> 27.3 us
where the time goes in v20:
time: 31.2 us; the launch traced here: 30.9 us
  blocking collectives  27.3 us (88%)
  Pallas kernels  2.61 us (8%)
  local copies, waits for them, and re-layouts  0.92 us (3%)
    all_to_all x1, blocking collectives, exchanged(): got = lax.all_to_all(sent, tuple(axes_in), 0, 0, tiled=True)  17.9 us
    all_to_all x1, blocking collectives, exchanged(): mine = lax.all_to_all(sums, tuple(axes_out), 0, 0, tiled=True)  9.46 us
    pallas_call x1, Pallas kernels, exchanged(): pl.pallas_call(functools.partial(update_kernel, places), out_shape=jax.Sh...  1.26 us
    pallas_call x1, Pallas kernels, exchanged(): pl.pallas_call(functools.partial(mix_kernel, slots), out_shape=(jax.Shape...  1 us
    unnamed x20, local copies, waits for them, and re-layouts  0.92 us

profile of v20, /device:TPU:0, one launch (start us, length us, event | category | flops | bytes accessed | tf_op | source)
XLA Modules:
  0.0 30.9 jit_solution(17255814027840084610)
XLA Ops:
  0.0 0.0 copy-start.2
  0.0 0.0 copy-start.1
  0.0 0.0 copy-start
  0.0 0.0 copy-start.8
  0.0 0.0 copy-start.9
  0.1 0.0 copy-start.5
  0.1 0.0 copy-start.6
  0.1 0.0 copy-start.7
  0.1 0.7 %copy-done.2 = bf16[128,256]{1,0:T(8,128)(2,1)S(1)} copy-done((bf16[128,256]{1,0:T(8,128)(2,1)S(1)}, bf16[128,256]{1,0:T(8,128)(2,1)}, u32[]{:S(2)}) %copy-start.2) | copy-done | bytes 65560
  0.8 0.0 copy-done.1
  0.9 0.1 copy-done
  1.0 0.0 copy-done.8
  1.0 0.0 copy-done.9
  1.0 0.0 copy-done.5
  1.0 0.0 copy-done.6
  1.0 0.0 copy-done.7
  1.0 1.0 %mix.1 = (bf16[32,32,128]{2,1,0:T(8,128)(2,1)S(1)}, bf16[512,128]{1,0:T(8,128)(2,1)S(1)}, f32[128,128]{1,0:T(8,128)S(1)}, f32[128,128]{1,0:T(8,128)S(1)}) custom-call(bf16[256,256]{1,0:T(8,128)(2,1)S(1)} %order.1.order_ref, s32[1,8]{1,0:T(1,128)S(1)} %bitcast.5, bf16[16,32,128]{2,1,0:T(8,128)(2,1)S(1)} %copy-done, f32[1,128]{1,0:T(1,128)S(1)} %bitcast.6, ...), custom_call_target="tpu_custom_call" | custom-call | tf_op jit(solution)/shard_map/mix/pallas_call | solution.py:373
  2.0 17.9 %all_to_all.10.got_ref = bf16[32,32,128]{2,1,0:T(8,128)(2,1)S(1)} all-to-all(bf16[32,32,128]{2,1,0:T(8,128)(2,1)S(1)} %get-tuple-element.9), channel_id=1, replica_groups=mesh['z'=4,'y'=2,'x'=2,'c'=2] {'y','c','x','z'}, dimensions={0} | all-to-all | bytes 524288 | tf_op jit(solution)/shard_map/all_to_all | solution.py:399
  19.9 0.3 triangle.1
  20.2 0.0 copy-start.3
  20.2 0.0 copy-start.4
  20.2 9.5 %all_to_all.11.got_ref = bf16[32,16,128]{2,1,0:T(8,128)(2,1)S(1)} all-to-all(bf16[32,16,128]{2,1,0:T(8,128)(2,1)S(1)} %triangle.1), channel_id=1, replica_groups=mesh['z'=4,'y'=2,'x'=2,'c'=2] {'y','c','x','z'}, dimensions={0} | all-to-all | bytes 262144 | tf_op jit(solution)/shard_map/all_to_all | solution.py:408
  29.7 0.0 copy-done.3
  29.7 0.0 copy-done.4
  29.7 1.3 %update.1 = bf16[16,32,128]{2,1,0:T(8,128)(2,1)} custom-call(bf16[32,16,128]{2,1,0:T(8,128)(2,1)S(1)} %all_to_all.11.got_ref, bf16[256,256]{1,0:T(8,128)(2,1)S(1)} %order.1.order_ref, bf16[512,128]{1,0:T(8,128)(2,1)S(1)} %get-tuple-element.10.normed_ref, f32[128,128]{1,0:T(8,128)S(1)} %get-tuple-element.11.gain_ref, ...), custom_call_target="tpu_custom_call" | custom-call | tf_op jit(solution)/shard_map/update/pallas_call | solution.py:410
  (1 shorter events, 0.0 us)
Async XLA Ops:
  0.0 0.8 %copy-start.2 = (bf16[128,256]{1,0:T(8,128)(2,1)S(1)}, bf16[128,256]{1,0:T(8,128)(2,1)}, u32[]{:S(2)}) copy-start(bf16[128,256]{1,0:T(8,128)(2,1)} %gate_ref.2) | copy-start | bytes 196612
  0.0 0.9 %copy-start.1 = (bf16[128,256]{1,0:T(8,128)(2,1)S(1)}, bf16[128,256]{1,0:T(8,128)(2,1)}, u32[]{:S(2)}) copy-start(bf16[128,256]{1,0:T(8,128)(2,1)} %proj_ref.2) | copy-start | bytes 196612
  0.0 1.0 %copy-start = (bf16[16,32,128]{2,1,0:T(8,128)(2,1)S(1)}, bf16[16,32,128]{2,1,0:T(8,128)(2,1)}, u32[]{:S(2)}) copy-start(bf16[16,32,128]{2,1,0:T(8,128)(2,1)} %pair_ref.1) | copy-start | bytes 393220
  0.0 1.0 %copy-start.8 = (f32[128]{0:T(128)S(1)}, f32[128]{0:T(128)}, u32[]{:S(2)}) copy-start(f32[128]{0:T(128)} %param.16) | copy-start | bytes 1540
  0.0 1.0 %copy-start.9 = (f32[128]{0:T(128)S(1)}, f32[128]{0:T(128)}, u32[]{:S(2)}) copy-start(f32[128]{0:T(128)} %param.17) | copy-start | bytes 1540
  0.1 0.9 %copy-start.5 = (s32[8]{0:T(128)S(1)}, s32[8]{0:T(128)}, u32[]{:S(2)}) copy-start(s32[8]{0:T(128)} %param.11) | copy-start | bytes 100
  0.1 0.9 %copy-start.6 = (f32[128]{0:T(128)S(1)}, f32[128]{0:T(128)}, u32[]{:S(2)}) copy-start(f32[128]{0:T(128)} %param.12) | copy-start | bytes 1540
  0.1 0.9 %copy-start.7 = (f32[128]{0:T(128)S(1)}, f32[128]{0:T(128)}, u32[]{:S(2)}) copy-start(f32[128]{0:T(128)} %param.13) | copy-start | bytes 1540
  20.2 9.5 %copy-start.3 = (bf16[128,128]{1,0:T(8,128)(2,1)S(1)}, bf16[128,128]{1,0:T(8,128)(2,1)}, u32[]{:S(2)}) copy-start(bf16[128,128]{1,0:T(8,128)(2,1)} %proj_ref.3) | copy-start | bytes 98308
  20.2 9.5 %copy-start.4 = (bf16[128,128]{1,0:T(8,128)(2,1)S(1)}, bf16[128,128]{1,0:T(8,128)(2,1)}, u32[]{:S(2)}) copy-start(bf16[128,128]{1,0:T(8,128)(2,1)} %gate_ref.3) | copy-start | bytes 98308

commit v21 on v20

--- a/solution.py
+++ b/solution.py
@@ -334,13 +334,15 @@
 PARAMS = pltpu.CompilerParams(vmem_limit_bytes=32 * 1024 * 1024)
 
 
-def ring_of(axes, grid_rows, grid_cols):
-    sizes = {"z": grid_rows // 2, "y": 2, "x": grid_cols // 2, "c": 2}
-    strides = {"z": 2 * grid_cols, "y": grid_cols, "x": 2, "c": 1}
-    ring = [0]
-    for axis in axes:
-        ring = [device + n * strides[axis] for device in ring for n in range(sizes[axis])]
-    return ring
+def ring_of(grid_rows, grid_cols):
+    planes, xs = grid_rows // 2, grid_cols // 2
+    return [
+        ((turn + 2 * x + y) % planes * 2 + y) * grid_cols + 2 * x + core
+        for core in range(2)
+        for turn in range(planes)
+        for x in range(xs)
+        for y in range(2)
+    ]
 
 
 def exchanged(
@@ -393,10 +395,14 @@
         norm_out_gain.reshape(1, LANES),
         norm_out_bias.reshape(1, LANES),
     )
-    axes_in, axes_out = "ycxz", "ycxz"
-    ring_in = ring_of(axes_in, grid_rows, grid_cols)
-    ring_out = ring_of(axes_out, grid_rows, grid_cols)
-    got = lax.all_to_all(sent, tuple(axes_in), 0, 0, tiled=True)
+    ring_in = ring_out = ring_of(grid_rows, grid_cols)
+
+    def exchange(chunks, ring):
+        return lax.all_to_all(
+            chunks, ("z", "y", "x", "c"), 0, 0, tiled=True, axis_index_groups=[ring]
+        )
+
+    got = exchange(sent, ring_in)
     sums = pl.pallas_call(
         functools.partial(triangle_kernel, ring_in, ring_out, grid_rows, grid_cols, rows, cols),
         out_shape=jax.ShapeDtypeStruct((devices, rows, LANES), BF16),
@@ -405,7 +411,7 @@
         compiler_params=PARAMS,
         name="triangle",
     )(got)
-    mine = lax.all_to_all(sums, tuple(axes_out), 0, 0, tiled=True)
+    mine = exchange(sums, ring_out)
     places = [ring_out.index(device) for device in ring_in]
     return pl.pallas_call(
         functools.partial(update_kernel, places),

time: 31.2 us -> 31.7 us (1.016)
  blocking collectives: 27.3 us -> 27.8 us
    all_to_all x2, blocking collectives: 27.3 us -> 27.8 us  [exchange(): lax.all_to_all(chunks, ('z', 'y', 'x', 'c'), 0, 0, tiled=True, axis_index...]
where the time goes in v21:
time: 31.7 us; the launch traced here: 31.5 us
  blocking collectives  27.8 us (88%)
  Pallas kernels  2.61 us (8%)
  local copies, waits for them, and re-layouts  0.92 us (3%)
    all_to_all x2, blocking collectives, exchange(): lax.all_to_all(chunks, ('z', 'y', 'x', 'c'), 0, 0, tiled=True, axis_index...  27.8 us
    pallas_call x1, Pallas kernels, exchanged(): pl.pallas_call(functools.partial(update_kernel, places), out_shape=jax.Sh...  1.27 us
    pallas_call x1, Pallas kernels, exchanged(): pl.pallas_call(functools.partial(mix_kernel, slots), out_shape=(jax.Shape...  1 us
    unnamed x20, local copies, waits for them, and re-layouts  0.92 us

profile of v21, /device:TPU:0, one launch (start us, length us, event | category | flops | bytes accessed | tf_op | source)
XLA Modules:
  0.0 31.5 jit_solution(4442921473017283247)
XLA Ops:
  0.0 0.0 copy-start.2
  0.0 0.0 copy-start.1
  0.0 0.0 copy-start
  0.0 0.0 copy-start.8
  0.0 0.0 copy-start.9
  0.1 0.0 copy-start.5
  0.1 0.0 copy-start.6
  0.1 0.0 copy-start.7
  0.1 0.7 %copy-done.2 = bf16[128,256]{1,0:T(8,128)(2,1)S(1)} copy-done((bf16[128,256]{1,0:T(8,128)(2,1)S(1)}, bf16[128,256]{1,0:T(8,128)(2,1)}, u32[]{:S(2)}) %copy-start.2) | copy-done | bytes 65560
  0.8 0.0 copy-done.1
  0.9 0.1 copy-done
  1.0 0.0 copy-done.8
  1.0 0.0 copy-done.9
  1.0 0.0 copy-done.5
  1.0 0.0 copy-done.6
  1.0 0.0 copy-done.7
  1.0 1.0 %mix.1 = (bf16[32,32,128]{2,1,0:T(8,128)(2,1)S(1)}, bf16[512,128]{1,0:T(8,128)(2,1)S(1)}, f32[128,128]{1,0:T(8,128)S(1)}, f32[128,128]{1,0:T(8,128)S(1)}) custom-call(bf16[256,256]{1,0:T(8,128)(2,1)S(1)} %order.1.order_ref, s32[1,8]{1,0:T(1,128)S(1)} %bitcast.5, bf16[16,32,128]{2,1,0:T(8,128)(2,1)S(1)} %copy-done, f32[1,128]{1,0:T(1,128)S(1)} %bitcast.6, ...), custom_call_target="tpu_custom_call" | custom-call | tf_op jit(solution)/shard_map/mix/pallas_call | solution.py:375
  2.0 17.0 %all_to_all.10.got_ref = bf16[32,32,128]{2,1,0:T(8,128)(2,1)S(1)} all-to-all(bf16[32,32,128]{2,1,0:T(8,128)(2,1)S(1)} %get-tuple-element.9), channel_id=1, replica_groups={{0,12,18,30,8,20,26,6,16,28,2,14,24,4,10,22,1,13,19,31,9,21,27,7,17,29,..., dimensions={0} | all-to-all | bytes 524288 | tf_op jit(solution)/shard_map/all_to_all | solution.py:401
  19.0 0.3 triangle.1
  19.3 0.0 copy-start.3
  19.3 0.0 copy-start.4
  19.4 10.8 %all_to_all.11.got_ref = bf16[32,16,128]{2,1,0:T(8,128)(2,1)S(1)} all-to-all(bf16[32,16,128]{2,1,0:T(8,128)(2,1)S(1)} %triangle.1), channel_id=1, replica_groups={{0,12,18,30,8,20,26,6,16,28,2,14,24,4,10,22,1,13,19,31,9,21,27,7,17,29,..., dimensions={0} | all-to-all | bytes 262144 | tf_op jit(solution)/shard_map/all_to_all | solution.py:401
  30.2 0.0 copy-done.3
  30.2 0.0 copy-done.4
  30.2 1.3 %update.1 = bf16[16,32,128]{2,1,0:T(8,128)(2,1)} custom-call(bf16[32,16,128]{2,1,0:T(8,128)(2,1)S(1)} %all_to_all.11.got_ref, bf16[256,256]{1,0:T(8,128)(2,1)S(1)} %order.1.order_ref, bf16[512,128]{1,0:T(8,128)(2,1)S(1)} %get-tuple-element.10.normed_ref, f32[128,128]{1,0:T(8,128)S(1)} %get-tuple-element.11.gain_ref, ...), custom_call_target="tpu_custom_call" | custom-call | tf_op jit(solution)/shard_map/update/pallas_call | solution.py:416
  (1 shorter events, 0.0 us)
Async XLA Ops:
  0.0 0.8 %copy-start.2 = (bf16[128,256]{1,0:T(8,128)(2,1)S(1)}, bf16[128,256]{1,0:T(8,128)(2,1)}, u32[]{:S(2)}) copy-start(bf16[128,256]{1,0:T(8,128)(2,1)} %gate_ref.2) | copy-start | bytes 196612
  0.0 0.9 %copy-start.1 = (bf16[128,256]{1,0:T(8,128)(2,1)S(1)}, bf16[128,256]{1,0:T(8,128)(2,1)}, u32[]{:S(2)}) copy-start(bf16[128,256]{1,0:T(8,128)(2,1)} %proj_ref.2) | copy-start | bytes 196612
  0.0 1.0 %copy-start = (bf16[16,32,128]{2,1,0:T(8,128)(2,1)S(1)}, bf16[16,32,128]{2,1,0:T(8,128)(2,1)}, u32[]{:S(2)}) copy-start(bf16[16,32,128]{2,1,0:T(8,128)(2,1)} %pair_ref.1) | copy-start | bytes 393220
  0.0 1.0 %copy-start.8 = (f32[128]{0:T(128)S(1)}, f32[128]{0:T(128)}, u32[]{:S(2)}) copy-start(f32[128]{0:T(128)} %param.16) | copy-start | bytes 1540
  0.0 1.0 %copy-start.9 = (f32[128]{0:T(128)S(1)}, f32[128]{0:T(128)}, u32[]{:S(2)}) copy-start(f32[128]{0:T(128)} %param.17) | copy-start | bytes 1540
  0.1 0.9 %copy-start.5 = (s32[8]{0:T(128)S(1)}, s32[8]{0:T(128)}, u32[]{:S(2)}) copy-start(s32[8]{0:T(128)} %param.11) | copy-start | bytes 100
  0.1 0.9 %copy-start.6 = (f32[128]{0:T(128)S(1)}, f32[128]{0:T(128)}, u32[]{:S(2)}) copy-start(f32[128]{0:T(128)} %param.12) | copy-start | bytes 1540
  0.1 0.9 %copy-start.7 = (f32[128]{0:T(128)S(1)}, f32[128]{0:T(128)}, u32[]{:S(2)}) copy-start(f32[128]{0:T(128)} %param.13) | copy-start | bytes 1540
  19.3 10.9 %copy-start.3 = (bf16[128,128]{1,0:T(8,128)(2,1)S(1)}, bf16[128,128]{1,0:T(8,128)(2,1)}, u32[]{:S(2)}) copy-start(bf16[128,128]{1,0:T(8,128)(2,1)} %proj_ref.3) | copy-start | bytes 98308
  19.3 10.8 %copy-start.4 = (bf16[128,128]{1,0:T(8,128)(2,1)S(1)}, bf16[128,128]{1,0:T(8,128)(2,1)}, u32[]{:S(2)}) copy-start(bf16[128,128]{1,0:T(8,128)(2,1)} %gate_ref.3) | copy-start | bytes 98308

commit v22 on v13

--- a/solution.py
+++ b/solution.py
@@ -208,8 +208,9 @@
     for source, target in ((last_gain_ref, last_gain_out), (last_bias_ref, last_bias_out)):
         target[...] = jnp.broadcast_to(column(source[...]), target.shape)
 
-    values = dot(proj_ref[...], normed, 0, 1)
-    gates = dot(gate_ref[...] * 0.5, normed, 0, 1)
+    weights = jnp.concatenate([proj_ref[...], gate_ref[...] * 0.5], axis=1)
+    products = dot(weights, normed, 0, 1)
+    values, gates = products[: 2 * hidden], products[2 * hidden :]
     mask = cell_mask(chain_ref[...], slots, rows, cols)
     mixed = (sigmoid(gates) * values * mask).astype(BF16)
 
@@ -316,10 +317,13 @@
         tri_normed = (centered * lax.rsqrt(variance + 1e-05) * gain + bias).astype(BF16)
         projected = dot(tri_normed, proj_ref[...], 0, 0)
         update = (opened[g * LANES : (g + 1) * LANES] * projected).astype(BF16)
-        here = pl.ds(g * inner, inner)
-        out_ref[here] = update.reshape(inner, cols, channels)
-        results.append(pltpu.make_async_copy(out_ref.at[here], out_hbm.at[here], out_sems.at[g]))
-        results[-1].start()
+        out_ref[g * inner : (g + 1) * inner] = update.reshape(inner, cols, channels)
+        if g % 2:
+            here = pl.ds((g - 1) * inner, 2 * inner)
+            results.append(
+                pltpu.make_async_copy(out_ref.at[here], out_hbm.at[here], out_sems.at[g // 2])
+            )
+            results[-1].start()
     for copy in results:
         copy.wait()
 
@@ -398,7 +402,7 @@
         out_specs=HBM,
         scratch_shapes=[
             pltpu.VMEM((rows, cols, channels), BF16),
-            pltpu.SemaphoreType.DMA((rows * cols // LANES,)),
+            pltpu.SemaphoreType.DMA((rows * cols // LANES // 2,)),
         ],
         compiler_params=PARAMS,
         name="update",
@@ -422,7 +426,7 @@
             and inner & (inner - 1) == 0
             and inner * devices == hidden
             and rows == SOME
-            and rows % inner == 0
+            and rows % (2 * inner) == 0
             and devices % SOME == 0
         )
 

time: 31.2 us -> 31.2 us (level)
  no operation moved by 1% of the time
where the time goes in v22:
time: 31.2 us; the launch traced here: 30.9 us
  blocking collectives  27.3 us (88%)
  Pallas kernels  2.61 us (8%)
  local copies, waits for them, and re-layouts  0.92 us (3%)
    all_to_all x1, blocking collectives, exchanged(): got = lax.all_to_all(sent, axes, 0, 0, tiled=True)  17.9 us
    all_to_all x1, blocking collectives, exchanged(): mine = lax.all_to_all(sums, axes, 0, 0, tiled=True)  9.45 us
    pallas_call x1, Pallas kernels, exchanged(): pl.pallas_call(update_kernel, out_shape=jax.ShapeDtypeStruct((rows, cols,...  1.26 us
    pallas_call x1, Pallas kernels, exchanged(): pl.pallas_call(functools.partial(mix_kernel, slots), out_shape=(jax.Shape...  1 us
    unnamed x20, local copies, waits for them, and re-layouts  0.92 us

profile of v22, /device:TPU:0, one launch (start us, length us, event | category | flops | bytes accessed | tf_op | source)
XLA Modules:
  0.0 30.9 jit_solution(14748333961565285963)
XLA Ops:
  0.0 0.0 copy-start.2
  0.0 0.0 copy-start.1
  0.0 0.0 copy-start
  0.0 0.0 copy-start.8
  0.0 0.0 copy-start.9
  0.1 0.0 copy-start.5
  0.1 0.0 copy-start.6
  0.1 0.0 copy-start.7
  0.1 0.7 %copy-done.2 = bf16[128,256]{1,0:T(8,128)(2,1)S(1)} copy-done((bf16[128,256]{1,0:T(8,128)(2,1)S(1)}, bf16[128,256]{1,0:T(8,128)(2,1)}, u32[]{:S(2)}) %copy-start.2) | copy-done | bytes 65560
  0.8 0.0 copy-done.1
  0.9 0.1 copy-done
  1.0 0.0 copy-done.8
  1.0 0.0 copy-done.9
  1.0 0.0 copy-done.5
  1.0 0.0 copy-done.6
  1.0 0.0 copy-done.7
  1.0 1.0 %mix.1 = (bf16[32,32,128]{2,1,0:T(8,128)(2,1)S(1)}, bf16[512,128]{1,0:T(8,128)(2,1)S(1)}, f32[128,128]{1,0:T(8,128)S(1)}, f32[128,128]{1,0:T(8,128)S(1)}) custom-call(bf16[256,256]{1,0:T(8,128)(2,1)S(1)} %order.1.order_ref, s32[1,8]{1,0:T(1,128)S(1)} %bitcast.5, bf16[16,32,128]{2,1,0:T(8,128)(2,1)S(1)} %copy-done, f32[1,128]{1,0:T(1,128)S(1)} %bitcast.6, ...), custom_call_target="tpu_custom_call" | custom-call | tf_op jit(solution)/shard_map/mix/pallas_call | solution.py:364
  2.0 17.9 %all_to_all.10.got_ref = bf16[32,32,128]{2,1,0:T(8,128)(2,1)S(1)} all-to-all(bf16[32,32,128]{2,1,0:T(8,128)(2,1)S(1)} %get-tuple-element.9), channel_id=1, replica_groups=mesh['high'=4,'low'=2,'col'=4] {'col','low','high'}, dimensions={0} | all-to-all | bytes 524288 | tf_op jit(solution)/shard_map/all_to_all | solution.py:388
  19.9 0.3 triangle.1
  20.2 0.0 copy-start.3
  20.2 0.0 copy-start.4
  20.2 9.5 %all_to_all.11.got_ref = bf16[32,16,128]{2,1,0:T(8,128)(2,1)S(1)} all-to-all(bf16[32,16,128]{2,1,0:T(8,128)(2,1)S(1)} %triangle.1), channel_id=1, replica_groups=mesh['high'=4,'low'=2,'col'=4] {'col','low','high'}, dimensions={0} | all-to-all | bytes 262144 | tf_op jit(solution)/shard_map/all_to_all | solution.py:397
  29.7 0.0 copy-done.3
  29.7 0.0 copy-done.4
  29.7 1.3 %update.1 = bf16[16,32,128]{2,1,0:T(8,128)(2,1)} custom-call(bf16[32,16,128]{2,1,0:T(8,128)(2,1)S(1)} %all_to_all.11.got_ref, bf16[256,256]{1,0:T(8,128)(2,1)S(1)} %order.1.order_ref, bf16[512,128]{1,0:T(8,128)(2,1)S(1)} %get-tuple-element.10.normed_ref, f32[128,128]{1,0:T(8,128)S(1)} %get-tuple-element.11.gain_ref, ...), custom_call_target="tpu_custom_call" | custom-call | tf_op jit(solution)/shard_map/update/pallas_call | solution.py:398
  (1 shorter events, 0.0 us)
Async XLA Ops:
  0.0 0.8 %copy-start.2 = (bf16[128,256]{1,0:T(8,128)(2,1)S(1)}, bf16[128,256]{1,0:T(8,128)(2,1)}, u32[]{:S(2)}) copy-start(bf16[128,256]{1,0:T(8,128)(2,1)} %gate_ref.2) | copy-start | bytes 196612
  0.0 0.9 %copy-start.1 = (bf16[128,256]{1,0:T(8,128)(2,1)S(1)}, bf16[128,256]{1,0:T(8,128)(2,1)}, u32[]{:S(2)}) copy-start(bf16[128,256]{1,0:T(8,128)(2,1)} %proj_ref.2) | copy-start | bytes 196612
  0.0 1.0 %copy-start = (bf16[16,32,128]{2,1,0:T(8,128)(2,1)S(1)}, bf16[16,32,128]{2,1,0:T(8,128)(2,1)}, u32[]{:S(2)}) copy-start(bf16[16,32,128]{2,1,0:T(8,128)(2,1)} %pair_ref.1) | copy-start | bytes 393220
  0.0 1.0 %copy-start.8 = (f32[128]{0:T(128)S(1)}, f32[128]{0:T(128)}, u32[]{:S(2)}) copy-start(f32[128]{0:T(128)} %param.16) | copy-start | bytes 1540
  0.0 1.0 %copy-start.9 = (f32[128]{0:T(128)S(1)}, f32[128]{0:T(128)}, u32[]{:S(2)}) copy-start(f32[128]{0:T(128)} %param.17) | copy-start | bytes 1540
  0.1 0.9 %copy-start.5 = (s32[8]{0:T(128)S(1)}, s32[8]{0:T(128)}, u32[]{:S(2)}) copy-start(s32[8]{0:T(128)} %param.11) | copy-start | bytes 100
  0.1 0.9 %copy-start.6 = (f32[128]{0:T(128)S(1)}, f32[128]{0:T(128)}, u32[]{:S(2)}) copy-start(f32[128]{0:T(128)} %param.12) | copy-start | bytes 1540
  0.1 0.9 %copy-start.7 = (f32[128]{0:T(128)S(1)}, f32[128]{0:T(128)}, u32[]{:S(2)}) copy-start(f32[128]{0:T(128)} %param.13) | copy-start | bytes 1540
  20.2 9.5 %copy-start.3 = (bf16[128,128]{1,0:T(8,128)(2,1)S(1)}, bf16[128,128]{1,0:T(8,128)(2,1)}, u32[]{:S(2)}) copy-start(bf16[128,128]{1,0:T(8,128)(2,1)} %proj_ref.3) | copy-start | bytes 98308
  20.2 9.5 %copy-start.4 = (bf16[128,128]{1,0:T(8,128)(2,1)S(1)}, bf16[128,128]{1,0:T(8,128)(2,1)}, u32[]{:S(2)}) copy-start(bf16[128,128]{1,0:T(8,128)(2,1)} %gate_ref.3) | copy-start | bytes 98308

commit v23 on v16

--- a/solution.py
+++ b/solution.py
@@ -208,8 +208,9 @@
     for source, target in ((last_gain_ref, last_gain_out), (last_bias_ref, last_bias_out)):
         target[...] = jnp.broadcast_to(column(source[...]), target.shape)
 
-    values = dot(proj_ref[...], normed, 0, 1)
-    gates = dot(gate_ref[...] * 0.5, normed, 0, 1)
+    weights = jnp.concatenate([proj_ref[...], gate_ref[...] * 0.5], axis=1)
+    products = dot(weights, normed, 0, 1)
+    values, gates = products[: 2 * hidden], products[2 * hidden :]
     mask = cell_mask(chain_ref[...], slots, rows, cols)
     mixed = (sigmoid(gates) * values * mask).astype(BF16)
 
@@ -315,10 +316,13 @@
         tri_normed = (centered * lax.rsqrt(variance + 1e-05) * gain + bias).astype(BF16)
         projected = dot(tri_normed, proj_ref[...], 0, 0)
         update = (opened[g * LANES : (g + 1) * LANES] * projected).astype(BF16)
-        here = pl.ds(g * inner, inner)
-        out_ref[here] = update.reshape(inner, cols, channels)
-        results.append(pltpu.make_async_copy(out_ref.at[here], out_hbm.at[here], out_sems.at[g]))
-        results[-1].start()
+        out_ref[g * inner : (g + 1) * inner] = update.reshape(inner, cols, channels)
+        if g % 2:
+            here = pl.ds((g - 1) * inner, 2 * inner)
+            results.append(
+                pltpu.make_async_copy(out_ref.at[here], out_hbm.at[here], out_sems.at[g // 2])
+            )
+            results[-1].start()
     for copy in results:
         copy.wait()
 
@@ -329,13 +333,13 @@
 
 
 def ring_of(grid_rows, grid_cols):
-    return [
-        (z * 2 + y) * grid_cols + x * 2 + core
-        for x in range(grid_cols // 2)
+    ring = [
+        (z * 2 + y) * grid_cols + c
+        for c in range(grid_cols)
         for y in range(2)
         for z in range(grid_rows // 2)
-        for core in range(2)
     ]
+    return ring[::-1]
 
 
 def exchanged(
@@ -412,7 +416,7 @@
         out_specs=HBM,
         scratch_shapes=[
             pltpu.VMEM((rows, cols, channels), BF16),
-            pltpu.SemaphoreType.DMA((rows * cols // LANES,)),
+            pltpu.SemaphoreType.DMA((rows * cols // LANES // 2,)),
         ],
         compiler_params=PARAMS,
         name="update",
@@ -431,10 +435,9 @@
             and inner & (inner - 1) == 0
             and inner * devices == hidden
             and rows == SOME
-            and rows % inner == 0
+            and rows % (2 * inner) == 0
             and devices % SOME == 0
             and grid_rows % 2 == 0
-            and grid_cols % 2 == 0
         )
 
     def call(*arrays):

time: 31.8 us -> 32 us (level)
  no operation moved by 1% of the time
where the time goes in v23:
time: 32 us; the launch traced here: 31.8 us
  blocking collectives  28.2 us (88%)
  Pallas kernels  2.61 us (8%)
  local copies, waits for them, and re-layouts  0.92 us (3%)
    all_to_all x2, blocking collectives, exchange(): lax.all_to_all(chunks, ('row', 'col'), 0, 0, tiled=True, axis_index_group...  28.2 us
    pallas_call x1, Pallas kernels, exchanged(): pl.pallas_call(update_kernel, out_shape=jax.ShapeDtypeStruct((rows, cols,...  1.27 us
    pallas_call x1, Pallas kernels, exchanged(): pl.pallas_call(functools.partial(mix_kernel, slots), out_shape=(jax.Shape...  1 us
    unnamed x20, local copies, waits for them, and re-layouts  0.92 us

profile of v23, /device:TPU:0, one launch (start us, length us, event | category | flops | bytes accessed | tf_op | source)
XLA Modules:
  0.0 31.8 jit_solution(9364718143461758888)
XLA Ops:
  0.0 0.0 copy-start.2
  0.0 0.0 copy-start.1
  0.0 0.0 copy-start
  0.0 0.0 copy-start.8
  0.0 0.0 copy-start.9
  0.1 0.0 copy-start.5
  0.1 0.0 copy-start.6
  0.1 0.0 copy-start.7
  0.1 0.7 %copy-done.2 = bf16[128,256]{1,0:T(8,128)(2,1)S(1)} copy-done((bf16[128,256]{1,0:T(8,128)(2,1)S(1)}, bf16[128,256]{1,0:T(8,128)(2,1)}, u32[]{:S(2)}) %copy-start.2) | copy-done | bytes 65560
  0.8 0.0 copy-done.1
  0.9 0.1 copy-done
  1.0 0.0 copy-done.8
  1.0 0.0 copy-done.9
  1.0 0.0 copy-done.5
  1.0 0.0 copy-done.6
  1.0 0.0 copy-done.7
  1.0 1.0 %mix.1 = (bf16[32,32,128]{2,1,0:T(8,128)(2,1)S(1)}, bf16[512,128]{1,0:T(8,128)(2,1)S(1)}, f32[128,128]{1,0:T(8,128)S(1)}, f32[128,128]{1,0:T(8,128)S(1)}) custom-call(bf16[256,256]{1,0:T(8,128)(2,1)S(1)} %order.1.order_ref, s32[1,8]{1,0:T(1,128)S(1)} %bitcast.5, bf16[16,32,128]{2,1,0:T(8,128)(2,1)S(1)} %copy-done, f32[1,128]{1,0:T(1,128)S(1)} %bitcast.6, ...), custom_call_target="tpu_custom_call" | custom-call | tf_op jit(solution)/shard_map/mix/pallas_call | solution.py:372
  2.0 17.1 %all_to_all.10.got_ref = bf16[32,32,128]{2,1,0:T(8,128)(2,1)S(1)} all-to-all(bf16[32,32,128]{2,1,0:T(8,128)(2,1)S(1)} %get-tuple-element.9), channel_id=1, replica_groups={{31,23,15,7,27,19,11,3,30,22,14,6,26,18,10,2,29,21,13,5,25,17,9,1,28,20..., dimensions={0} | all-to-all | bytes 524288 | tf_op jit(solution)/shard_map/all_to_all | solution.py:398
  19.1 0.3 triangle.1
  19.4 0.0 copy-start.3
  19.5 0.0 copy-start.4
  19.5 11.1 %all_to_all.11.got_ref = bf16[32,16,128]{2,1,0:T(8,128)(2,1)S(1)} all-to-all(bf16[32,16,128]{2,1,0:T(8,128)(2,1)S(1)} %triangle.1), channel_id=1, replica_groups={{31,23,15,7,27,19,11,3,30,22,14,6,26,18,10,2,29,21,13,5,25,17,9,1,28,20..., dimensions={0} | all-to-all | bytes 262144 | tf_op jit(solution)/shard_map/all_to_all | solution.py:398
  30.5 0.0 copy-done.3
  30.5 0.0 copy-done.4
  30.5 1.3 %update.1 = bf16[16,32,128]{2,1,0:T(8,128)(2,1)} custom-call(bf16[32,16,128]{2,1,0:T(8,128)(2,1)S(1)} %all_to_all.11.got_ref, bf16[256,256]{1,0:T(8,128)(2,1)S(1)} %order.1.order_ref, bf16[512,128]{1,0:T(8,128)(2,1)S(1)} %get-tuple-element.10.normed_ref, f32[128,128]{1,0:T(8,128)S(1)} %get-tuple-element.11.gain_ref, ...), custom_call_target="tpu_custom_call" | custom-call | tf_op jit(solution)/shard_map/update/pallas_call | solution.py:412
  (1 shorter events, 0.0 us)
Async XLA Ops:
  0.0 0.8 %copy-start.2 = (bf16[128,256]{1,0:T(8,128)(2,1)S(1)}, bf16[128,256]{1,0:T(8,128)(2,1)}, u32[]{:S(2)}) copy-start(bf16[128,256]{1,0:T(8,128)(2,1)} %gate_ref.2) | copy-start | bytes 196612
  0.0 0.9 %copy-start.1 = (bf16[128,256]{1,0:T(8,128)(2,1)S(1)}, bf16[128,256]{1,0:T(8,128)(2,1)}, u32[]{:S(2)}) copy-start(bf16[128,256]{1,0:T(8,128)(2,1)} %proj_ref.2) | copy-start | bytes 196612
  0.0 1.0 %copy-start = (bf16[16,32,128]{2,1,0:T(8,128)(2,1)S(1)}, bf16[16,32,128]{2,1,0:T(8,128)(2,1)}, u32[]{:S(2)}) copy-start(bf16[16,32,128]{2,1,0:T(8,128)(2,1)} %pair_ref.1) | copy-start | bytes 393220
  0.0 1.0 %copy-start.8 = (f32[128]{0:T(128)S(1)}, f32[128]{0:T(128)}, u32[]{:S(2)}) copy-start(f32[128]{0:T(128)} %param.16) | copy-start | bytes 1540
  0.0 1.0 %copy-start.9 = (f32[128]{0:T(128)S(1)}, f32[128]{0:T(128)}, u32[]{:S(2)}) copy-start(f32[128]{0:T(128)} %param.17) | copy-start | bytes 1540
  0.1 0.9 %copy-start.5 = (s32[8]{0:T(128)S(1)}, s32[8]{0:T(128)}, u32[]{:S(2)}) copy-start(s32[8]{0:T(128)} %param.11) | copy-start | bytes 100
  0.1 0.9 %copy-start.6 = (f32[128]{0:T(128)S(1)}, f32[128]{0:T(128)}, u32[]{:S(2)}) copy-start(f32[128]{0:T(128)} %param.12) | copy-start | bytes 1540
  0.1 0.9 %copy-start.7 = (f32[128]{0:T(128)S(1)}, f32[128]{0:T(128)}, u32[]{:S(2)}) copy-start(f32[128]{0:T(128)} %param.13) | copy-start | bytes 1540
  19.4 11.1 %copy-start.3 = (bf16[128,128]{1,0:T(8,128)(2,1)S(1)}, bf16[128,128]{1,0:T(8,128)(2,1)}, u32[]{:S(2)}) copy-start(bf16[128,128]{1,0:T(8,128)(2,1)} %proj_ref.3) | copy-start | bytes 98308
  19.5 11.1 %copy-start.4 = (bf16[128,128]{1,0:T(8,128)(2,1)S(1)}, bf16[128,128]{1,0:T(8,128)(2,1)}, u32[]{:S(2)}) copy-start(bf16[128,128]{1,0:T(8,128)(2,1)} %gate_ref.3) | copy-start | bytes 98308

commit v24 on v23

--- a/solution.py
+++ b/solution.py
@@ -333,13 +333,9 @@
 
 
 def ring_of(grid_rows, grid_cols):
-    ring = [
-        (z * 2 + y) * grid_cols + c
-        for c in range(grid_cols)
-        for y in range(2)
-        for z in range(grid_rows // 2)
-    ]
-    return ring[::-1]
+    line = [(c, y) for c in range(grid_cols) for y in range(2)]
+    places = [(at + z, z, at) for at in range(len(line)) for z in range(grid_rows // 2)]
+    return [(z * 2 + line[at][1]) * grid_cols + line[at][0] for _, z, at in sorted(places)]
 
 
 def exchanged(

time: 32 us -> 31.8 us (level)
  no operation moved by 1% of the time
where the time goes in v24:
time: 31.8 us; the launch traced here: 31.5 us
  blocking collectives  27.9 us (88%)
  Pallas kernels  2.61 us (8%)
  local copies, waits for them, and re-layouts  0.92 us (3%)
    all_to_all x2, blocking collectives, exchange(): lax.all_to_all(chunks, ('row', 'col'), 0, 0, tiled=True, axis_index_group...  27.9 us
    pallas_call x1, Pallas kernels, exchanged(): pl.pallas_call(update_kernel, out_shape=jax.ShapeDtypeStruct((rows, cols,...  1.26 us
    pallas_call x1, Pallas kernels, exchanged(): pl.pallas_call(functools.partial(mix_kernel, slots), out_shape=(jax.Shape...  1 us
    unnamed x20, local copies, waits for them, and re-layouts  0.92 us

profile of v24, /device:TPU:0, one launch (start us, length us, event | category | flops | bytes accessed | tf_op | source)
XLA Modules:
  0.0 31.5 jit_solution(6031913737969537773)
XLA Ops:
  0.0 0.0 copy-start.2
  0.0 0.0 copy-start.1
  0.0 0.0 copy-start
  0.0 0.0 copy-start.8
  0.0 0.0 copy-start.9
  0.1 0.0 copy-start.5
  0.1 0.0 copy-start.6
  0.1 0.0 copy-start.7
  0.1 0.7 %copy-done.2 = bf16[128,256]{1,0:T(8,128)(2,1)S(1)} copy-done((bf16[128,256]{1,0:T(8,128)(2,1)S(1)}, bf16[128,256]{1,0:T(8,128)(2,1)}, u32[]{:S(2)}) %copy-start.2) | copy-done | bytes 65560
  0.8 0.0 copy-done.1
  0.9 0.1 copy-done
  1.0 0.0 copy-done.8
  1.0 0.0 copy-done.9
  1.0 0.0 copy-done.5
  1.0 0.0 copy-done.6
  1.0 0.0 copy-done.7
  1.0 1.0 %mix.1 = (bf16[32,32,128]{2,1,0:T(8,128)(2,1)S(1)}, bf16[512,128]{1,0:T(8,128)(2,1)S(1)}, f32[128,128]{1,0:T(8,128)S(1)}, f32[128,128]{1,0:T(8,128)S(1)}) custom-call(bf16[256,256]{1,0:T(8,128)(2,1)S(1)} %order.1.order_ref, s32[1,8]{1,0:T(1,128)S(1)} %bitcast.5, bf16[16,32,128]{2,1,0:T(8,128)(2,1)S(1)} %copy-done, f32[1,128]{1,0:T(1,128)S(1)} %bitcast.6, ...), custom_call_target="tpu_custom_call" | custom-call | tf_op jit(solution)/shard_map/mix/pallas_call | solution.py:368
  2.0 18.3 %all_to_all.10.got_ref = bf16[32,32,128]{2,1,0:T(8,128)(2,1)S(1)} all-to-all(bf16[32,32,128]{2,1,0:T(8,128)(2,1)S(1)} %get-tuple-element.9), channel_id=1, replica_groups={{0,4,8,1,12,16,5,9,20,24,2,13,17,28,6,10,21,25,3,14,18,29,7,11,22,26,15..., dimensions={0} | all-to-all | bytes 524288 | tf_op jit(solution)/shard_map/all_to_all | solution.py:394
  20.3 0.3 triangle.1
  20.6 0.0 copy-start.3
  20.6 0.0 copy-start.4
  20.7 9.6 %all_to_all.11.got_ref = bf16[32,16,128]{2,1,0:T(8,128)(2,1)S(1)} all-to-all(bf16[32,16,128]{2,1,0:T(8,128)(2,1)S(1)} %triangle.1), channel_id=1, replica_groups={{0,4,8,1,12,16,5,9,20,24,2,13,17,28,6,10,21,25,3,14,18,29,7,11,22,26,15..., dimensions={0} | all-to-all | bytes 262144 | tf_op jit(solution)/shard_map/all_to_all | solution.py:394
  30.3 0.0 copy-done.3
  30.3 0.0 copy-done.4
  30.3 1.3 %update.1 = bf16[16,32,128]{2,1,0:T(8,128)(2,1)} custom-call(bf16[32,16,128]{2,1,0:T(8,128)(2,1)S(1)} %all_to_all.11.got_ref, bf16[256,256]{1,0:T(8,128)(2,1)S(1)} %order.1.order_ref, bf16[512,128]{1,0:T(8,128)(2,1)S(1)} %get-tuple-element.10.normed_ref, f32[128,128]{1,0:T(8,128)S(1)} %get-tuple-element.11.gain_ref, ...), custom_call_target="tpu_custom_call" | custom-call | tf_op jit(solution)/shard_map/update/pallas_call | solution.py:408
  (1 shorter events, 0.0 us)
Async XLA Ops:
  0.0 0.8 %copy-start.2 = (bf16[128,256]{1,0:T(8,128)(2,1)S(1)}, bf16[128,256]{1,0:T(8,128)(2,1)}, u32[]{:S(2)}) copy-start(bf16[128,256]{1,0:T(8,128)(2,1)} %gate_ref.2) | copy-start | bytes 196612
  0.0 0.9 %copy-start.1 = (bf16[128,256]{1,0:T(8,128)(2,1)S(1)}, bf16[128,256]{1,0:T(8,128)(2,1)}, u32[]{:S(2)}) copy-start(bf16[128,256]{1,0:T(8,128)(2,1)} %proj_ref.2) | copy-start | bytes 196612
  0.0 1.0 %copy-start = (bf16[16,32,128]{2,1,0:T(8,128)(2,1)S(1)}, bf16[16,32,128]{2,1,0:T(8,128)(2,1)}, u32[]{:S(2)}) copy-start(bf16[16,32,128]{2,1,0:T(8,128)(2,1)} %pair_ref.1) | copy-start | bytes 393220
  0.0 1.0 %copy-start.8 = (f32[128]{0:T(128)S(1)}, f32[128]{0:T(128)}, u32[]{:S(2)}) copy-start(f32[128]{0:T(128)} %param.16) | copy-start | bytes 1540
  0.0 1.0 %copy-start.9 = (f32[128]{0:T(128)S(1)}, f32[128]{0:T(128)}, u32[]{:S(2)}) copy-start(f32[128]{0:T(128)} %param.17) | copy-start | bytes 1540
  0.1 0.9 %copy-start.5 = (s32[8]{0:T(128)S(1)}, s32[8]{0:T(128)}, u32[]{:S(2)}) copy-start(s32[8]{0:T(128)} %param.11) | copy-start | bytes 100
  0.1 0.9 %copy-start.6 = (f32[128]{0:T(128)S(1)}, f32[128]{0:T(128)}, u32[]{:S(2)}) copy-start(f32[128]{0:T(128)} %param.12) | copy-start | bytes 1540
  0.1 0.9 %copy-start.7 = (f32[128]{0:T(128)S(1)}, f32[128]{0:T(128)}, u32[]{:S(2)}) copy-start(f32[128]{0:T(128)} %param.13) | copy-start | bytes 1540
  20.6 9.6 %copy-start.3 = (bf16[128,128]{1,0:T(8,128)(2,1)S(1)}, bf16[128,128]{1,0:T(8,128)(2,1)}, u32[]{:S(2)}) copy-start(bf16[128,128]{1,0:T(8,128)(2,1)} %proj_ref.3) | copy-start | bytes 98308
  20.6 9.6 %copy-start.4 = (bf16[128,128]{1,0:T(8,128)(2,1)S(1)}, bf16[128,128]{1,0:T(8,128)(2,1)}, u32[]{:S(2)}) copy-start(bf16[128,128]{1,0:T(8,128)(2,1)} %gate_ref.3) | copy-start | bytes 98308

commit v25 on v24

--- a/solution.py
+++ b/solution.py
@@ -335,7 +335,8 @@
 def ring_of(grid_rows, grid_cols):
     line = [(c, y) for c in range(grid_cols) for y in range(2)]
     places = [(at + z, z, at) for at in range(len(line)) for z in range(grid_rows // 2)]
-    return [(z * 2 + line[at][1]) * grid_cols + line[at][0] for _, z, at in sorted(places)]
+    ring = [(z * 2 + line[at][1]) * grid_cols + line[at][0] for _, z, at in sorted(places)]
+    return [device for device in ring if device > 1] + [1, 0]
 
 
 def exchanged(

time: 31.8 us -> 32.1 us (level)
  blocking collectives: 27.9 us -> 28.3 us
    all_to_all x2, blocking collectives: 27.9 us -> 28.3 us  [exchange(): lax.all_to_all(chunks, ('row', 'col'), 0, 0, tiled=True, axis_index_group...]
where the time goes in v25:
time: 32.1 us; the launch traced here: 31.9 us
  blocking collectives  28.3 us (88%)
  Pallas kernels  2.61 us (8%)
  local copies, waits for them, and re-layouts  0.92 us (3%)
    all_to_all x2, blocking collectives, exchange(): lax.all_to_all(chunks, ('row', 'col'), 0, 0, tiled=True, axis_index_group...  28.3 us
    pallas_call x1, Pallas kernels, exchanged(): pl.pallas_call(update_kernel, out_shape=jax.ShapeDtypeStruct((rows, cols,...  1.27 us
    pallas_call x1, Pallas kernels, exchanged(): pl.pallas_call(functools.partial(mix_kernel, slots), out_shape=(jax.Shape...  1 us
    unnamed x20, local copies, waits for them, and re-layouts  0.92 us

profile of v25, /device:TPU:0, one launch (start us, length us, event | category | flops | bytes accessed | tf_op | source)
XLA Modules:
  0.0 31.9 jit_solution(7380682877097343024)
XLA Ops:
  0.0 0.0 copy-start.2
  0.0 0.0 copy-start.1
  0.0 0.0 copy-start
  0.0 0.0 copy-start.8
  0.0 0.0 copy-start.9
  0.1 0.0 copy-start.5
  0.1 0.0 copy-start.6
  0.1 0.0 copy-start.7
  0.1 0.7 %copy-done.2 = bf16[128,256]{1,0:T(8,128)(2,1)S(1)} copy-done((bf16[128,256]{1,0:T(8,128)(2,1)S(1)}, bf16[128,256]{1,0:T(8,128)(2,1)}, u32[]{:S(2)}) %copy-start.2) | copy-done | bytes 65560
  0.8 0.0 copy-done.1
  0.9 0.1 copy-done
  1.0 0.0 copy-done.8
  1.0 0.0 copy-done.9
  1.0 0.0 copy-done.5
  1.0 0.0 copy-done.6
  1.0 0.0 copy-done.7
  1.0 1.0 %mix.1 = (bf16[32,32,128]{2,1,0:T(8,128)(2,1)S(1)}, bf16[512,128]{1,0:T(8,128)(2,1)S(1)}, f32[128,128]{1,0:T(8,128)S(1)}, f32[128,128]{1,0:T(8,128)S(1)}) custom-call(bf16[256,256]{1,0:T(8,128)(2,1)S(1)} %order.1.order_ref, s32[1,8]{1,0:T(1,128)S(1)} %bitcast.5, bf16[16,32,128]{2,1,0:T(8,128)(2,1)S(1)} %copy-done, f32[1,128]{1,0:T(1,128)S(1)} %bitcast.6, ...), custom_call_target="tpu_custom_call" | custom-call | tf_op jit(solution)/shard_map/mix/pallas_call | solution.py:369
  2.0 17.4 %all_to_all.10.got_ref = bf16[32,32,128]{2,1,0:T(8,128)(2,1)S(1)} all-to-all(bf16[32,32,128]{2,1,0:T(8,128)(2,1)S(1)} %get-tuple-element.9), channel_id=1, replica_groups={{4,8,12,16,5,9,20,24,2,13,17,28,6,10,21,25,3,14,18,29,7,11,22,26,15,19,..., dimensions={0} | all-to-all | bytes 524288 | tf_op jit(solution)/shard_map/all_to_all | solution.py:395
  19.4 0.3 triangle.1
  19.8 0.0 copy-start.3
  19.8 0.0 copy-start.4
  19.8 10.8 %all_to_all.11.got_ref = bf16[32,16,128]{2,1,0:T(8,128)(2,1)S(1)} all-to-all(bf16[32,16,128]{2,1,0:T(8,128)(2,1)S(1)} %triangle.1), channel_id=1, replica_groups={{4,8,12,16,5,9,20,24,2,13,17,28,6,10,21,25,3,14,18,29,7,11,22,26,15,19,..., dimensions={0} | all-to-all | bytes 262144 | tf_op jit(solution)/shard_map/all_to_all | solution.py:395
  30.6 0.0 copy-done.3
  30.6 0.0 copy-done.4
  30.6 1.3 %update.1 = bf16[16,32,128]{2,1,0:T(8,128)(2,1)} custom-call(bf16[32,16,128]{2,1,0:T(8,128)(2,1)S(1)} %all_to_all.11.got_ref, bf16[256,256]{1,0:T(8,128)(2,1)S(1)} %order.1.order_ref, bf16[512,128]{1,0:T(8,128)(2,1)S(1)} %get-tuple-element.10.normed_ref, f32[128,128]{1,0:T(8,128)S(1)} %get-tuple-element.11.gain_ref, ...), custom_call_target="tpu_custom_call" | custom-call | tf_op jit(solution)/shard_map/update/pallas_call | solution.py:409
  (1 shorter events, 0.0 us)
Async XLA Ops:
  0.0 0.8 %copy-start.2 = (bf16[128,256]{1,0:T(8,128)(2,1)S(1)}, bf16[128,256]{1,0:T(8,128)(2,1)}, u32[]{:S(2)}) copy-start(bf16[128,256]{1,0:T(8,128)(2,1)} %gate_ref.2) | copy-start | bytes 196612
  0.0 0.9 %copy-start.1 = (bf16[128,256]{1,0:T(8,128)(2,1)S(1)}, bf16[128,256]{1,0:T(8,128)(2,1)}, u32[]{:S(2)}) copy-start(bf16[128,256]{1,0:T(8,128)(2,1)} %proj_ref.2) | copy-start | bytes 196612
  0.0 1.0 %copy-start = (bf16[16,32,128]{2,1,0:T(8,128)(2,1)S(1)}, bf16[16,32,128]{2,1,0:T(8,128)(2,1)}, u32[]{:S(2)}) copy-start(bf16[16,32,128]{2,1,0:T(8,128)(2,1)} %pair_ref.1) | copy-start | bytes 393220
  0.0 1.0 %copy-start.8 = (f32[128]{0:T(128)S(1)}, f32[128]{0:T(128)}, u32[]{:S(2)}) copy-start(f32[128]{0:T(128)} %param.16) | copy-start | bytes 1540
  0.0 1.0 %copy-start.9 = (f32[128]{0:T(128)S(1)}, f32[128]{0:T(128)}, u32[]{:S(2)}) copy-start(f32[128]{0:T(128)} %param.17) | copy-start | bytes 1540
  0.1 0.9 %copy-start.5 = (s32[8]{0:T(128)S(1)}, s32[8]{0:T(128)}, u32[]{:S(2)}) copy-start(s32[8]{0:T(128)} %param.11) | copy-start | bytes 100
  0.1 0.9 %copy-start.6 = (f32[128]{0:T(128)S(1)}, f32[128]{0:T(128)}, u32[]{:S(2)}) copy-start(f32[128]{0:T(128)} %param.12) | copy-start | bytes 1540
  0.1 0.9 %copy-start.7 = (f32[128]{0:T(128)S(1)}, f32[128]{0:T(128)}, u32[]{:S(2)}) copy-start(f32[128]{0:T(128)} %param.13) | copy-start | bytes 1540
  19.8 10.9 %copy-start.3 = (bf16[128,128]{1,0:T(8,128)(2,1)S(1)}, bf16[128,128]{1,0:T(8,128)(2,1)}, u32[]{:S(2)}) copy-start(bf16[128,128]{1,0:T(8,128)(2,1)} %proj_ref.3) | copy-start | bytes 98308
  19.8 10.9 %copy-start.4 = (bf16[128,128]{1,0:T(8,128)(2,1)S(1)}, bf16[128,128]{1,0:T(8,128)(2,1)}, u32[]{:S(2)}) copy-start(bf16[128,128]{1,0:T(8,128)(2,1)} %gate_ref.3) | copy-start | bytes 98308

commit v26 on v25

--- a/solution.py
+++ b/solution.py
@@ -336,7 +336,9 @@
     line = [(c, y) for c in range(grid_cols) for y in range(2)]
     places = [(at + z, z, at) for at in range(len(line)) for z in range(grid_rows // 2)]
     ring = [(z * 2 + line[at][1]) * grid_cols + line[at][0] for _, z, at in sorted(places)]
-    return [device for device in ring if device > 1] + [1, 0]
+    other = ring.index(2 * grid_cols + 1)
+    ring[0], ring[other] = ring[other], ring[0]
+    return ring
 
 
 def exchanged(

time: 32.1 us -> 31.6 us (0.984)
  blocking collectives: 28.3 us -> 27.7 us
    all_to_all x2, blocking collectives: 28.3 us -> 27.7 us  [exchange(): lax.all_to_all(chunks, ('row', 'col'), 0, 0, tiled=True, axis_index_group...]
where the time goes in v26:
time: 31.6 us; the launch traced here: 31.4 us
  blocking collectives  27.7 us (88%)
  Pallas kernels  2.61 us (8%)
  local copies, waits for them, and re-layouts  0.92 us (3%)
    all_to_all x2, blocking collectives, exchange(): lax.all_to_all(chunks, ('row', 'col'), 0, 0, tiled=True, axis_index_group...  27.7 us
    pallas_call x1, Pallas kernels, exchanged(): pl.pallas_call(update_kernel, out_shape=jax.ShapeDtypeStruct((rows, cols,...  1.26 us
    pallas_call x1, Pallas kernels, exchanged(): pl.pallas_call(functools.partial(mix_kernel, slots), out_shape=(jax.Shape...  1 us
    unnamed x20, local copies, waits for them, and re-layouts  0.92 us

profile of v26, /device:TPU:0, one launch (start us, length us, event | category | flops | bytes accessed | tf_op | source)
XLA Modules:
  0.0 31.4 jit_solution(13471624831999677308)
XLA Ops:
  0.0 0.0 copy-start.2
  0.0 0.0 copy-start.1
  0.0 0.0 copy-start
  0.0 0.0 copy-start.8
  0.0 0.0 copy-start.9
  0.1 0.0 copy-start.5
  0.1 0.0 copy-start.6
  0.1 0.0 copy-start.7
  0.1 0.7 %copy-done.2 = bf16[128,256]{1,0:T(8,128)(2,1)S(1)} copy-done((bf16[128,256]{1,0:T(8,128)(2,1)S(1)}, bf16[128,256]{1,0:T(8,128)(2,1)}, u32[]{:S(2)}) %copy-start.2) | copy-done | bytes 65560
  0.8 0.0 copy-done.1
  0.9 0.1 copy-done
  1.0 0.0 copy-done.8
  1.0 0.0 copy-done.9
  1.0 0.0 copy-done.5
  1.0 0.0 copy-done.6
  1.0 0.0 copy-done.7
  1.0 1.0 %mix.1 = (bf16[32,32,128]{2,1,0:T(8,128)(2,1)S(1)}, bf16[512,128]{1,0:T(8,128)(2,1)S(1)}, f32[128,128]{1,0:T(8,128)S(1)}, f32[128,128]{1,0:T(8,128)S(1)}) custom-call(bf16[256,256]{1,0:T(8,128)(2,1)S(1)} %order.1.order_ref, s32[1,8]{1,0:T(1,128)S(1)} %bitcast.5, bf16[16,32,128]{2,1,0:T(8,128)(2,1)S(1)} %copy-done, f32[1,128]{1,0:T(1,128)S(1)} %bitcast.6, ...), custom_call_target="tpu_custom_call" | custom-call | tf_op jit(solution)/shard_map/mix/pallas_call | solution.py:371
  2.0 17.6 %all_to_all.10.got_ref = bf16[32,32,128]{2,1,0:T(8,128)(2,1)S(1)} all-to-all(bf16[32,32,128]{2,1,0:T(8,128)(2,1)S(1)} %get-tuple-element.9), channel_id=1, replica_groups={{9,4,8,1,12,16,5,0,20,24,2,13,17,28,6,10,21,25,3,14,18,29,7,11,22,26,15..., dimensions={0} | all-to-all | bytes 524288 | tf_op jit(solution)/shard_map/all_to_all | solution.py:397
  19.6 0.3 triangle.1
  19.9 0.0 copy-start.3
  19.9 0.0 copy-start.4
  19.9 10.2 %all_to_all.11.got_ref = bf16[32,16,128]{2,1,0:T(8,128)(2,1)S(1)} all-to-all(bf16[32,16,128]{2,1,0:T(8,128)(2,1)S(1)} %triangle.1), channel_id=1, replica_groups={{9,4,8,1,12,16,5,0,20,24,2,13,17,28,6,10,21,25,3,14,18,29,7,11,22,26,15..., dimensions={0} | all-to-all | bytes 262144 | tf_op jit(solution)/shard_map/all_to_all | solution.py:397
  30.1 0.0 copy-done.3
  30.1 0.0 copy-done.4
  30.1 1.3 %update.1 = bf16[16,32,128]{2,1,0:T(8,128)(2,1)} custom-call(bf16[32,16,128]{2,1,0:T(8,128)(2,1)S(1)} %all_to_all.11.got_ref, bf16[256,256]{1,0:T(8,128)(2,1)S(1)} %order.1.order_ref, bf16[512,128]{1,0:T(8,128)(2,1)S(1)} %get-tuple-element.10.normed_ref, f32[128,128]{1,0:T(8,128)S(1)} %get-tuple-element.11.gain_ref, ...), custom_call_target="tpu_custom_call" | custom-call | tf_op jit(solution)/shard_map/update/pallas_call | solution.py:411
  (1 shorter events, 0.0 us)
Async XLA Ops:
  0.0 0.8 %copy-start.2 = (bf16[128,256]{1,0:T(8,128)(2,1)S(1)}, bf16[128,256]{1,0:T(8,128)(2,1)}, u32[]{:S(2)}) copy-start(bf16[128,256]{1,0:T(8,128)(2,1)} %gate_ref.2) | copy-start | bytes 196612
  0.0 0.9 %copy-start.1 = (bf16[128,256]{1,0:T(8,128)(2,1)S(1)}, bf16[128,256]{1,0:T(8,128)(2,1)}, u32[]{:S(2)}) copy-start(bf16[128,256]{1,0:T(8,128)(2,1)} %proj_ref.2) | copy-start | bytes 196612
  0.0 1.0 %copy-start = (bf16[16,32,128]{2,1,0:T(8,128)(2,1)S(1)}, bf16[16,32,128]{2,1,0:T(8,128)(2,1)}, u32[]{:S(2)}) copy-start(bf16[16,32,128]{2,1,0:T(8,128)(2,1)} %pair_ref.1) | copy-start | bytes 393220
  0.0 1.0 %copy-start.8 = (f32[128]{0:T(128)S(1)}, f32[128]{0:T(128)}, u32[]{:S(2)}) copy-start(f32[128]{0:T(128)} %param.16) | copy-start | bytes 1540
  0.0 1.0 %copy-start.9 = (f32[128]{0:T(128)S(1)}, f32[128]{0:T(128)}, u32[]{:S(2)}) copy-start(f32[128]{0:T(128)} %param.17) | copy-start | bytes 1540
  0.1 0.9 %copy-start.5 = (s32[8]{0:T(128)S(1)}, s32[8]{0:T(128)}, u32[]{:S(2)}) copy-start(s32[8]{0:T(128)} %param.11) | copy-start | bytes 100
  0.1 0.9 %copy-start.6 = (f32[128]{0:T(128)S(1)}, f32[128]{0:T(128)}, u32[]{:S(2)}) copy-start(f32[128]{0:T(128)} %param.12) | copy-start | bytes 1540
  0.1 0.9 %copy-start.7 = (f32[128]{0:T(128)S(1)}, f32[128]{0:T(128)}, u32[]{:S(2)}) copy-start(f32[128]{0:T(128)} %param.13) | copy-start | bytes 1540
  19.9 10.2 %copy-start.3 = (bf16[128,128]{1,0:T(8,128)(2,1)S(1)}, bf16[128,128]{1,0:T(8,128)(2,1)}, u32[]{:S(2)}) copy-start(bf16[128,128]{1,0:T(8,128)(2,1)} %proj_ref.3) | copy-start | bytes 98308
  19.9 10.2 %copy-start.4 = (bf16[128,128]{1,0:T(8,128)(2,1)S(1)}, bf16[128,128]{1,0:T(8,128)(2,1)}, u32[]{:S(2)}) copy-start(bf16[128,128]{1,0:T(8,128)(2,1)} %gate_ref.3) | copy-start | bytes 98308

commit v27 on v20

--- a/solution.py
+++ b/solution.py
@@ -393,7 +393,7 @@
         norm_out_gain.reshape(1, LANES),
         norm_out_bias.reshape(1, LANES),
     )
-    axes_in, axes_out = "ycxz", "ycxz"
+    axes_in, axes_out = "xycz", "xycz"
     ring_in = ring_of(axes_in, grid_rows, grid_cols)
     ring_out = ring_of(axes_out, grid_rows, grid_cols)
     got = lax.all_to_all(sent, tuple(axes_in), 0, 0, tiled=True)

time: 31.2 us -> 32.1 us (1.029)
  blocking collectives: 27.3 us -> 28.2 us
    all_to_all x1, blocking collectives: 9.46 us -> 10.9 us  [exchanged(): mine = lax.all_to_all(sums, tuple(axes_out), 0, 0, tiled=True)]
    all_to_all x1, blocking collectives: 17.9 us -> 17.3 us  [exchanged(): got = lax.all_to_all(sent, tuple(axes_in), 0, 0, tiled=True)]
where the time goes in v27:
time: 32.1 us; the launch traced here: 31.9 us
  blocking collectives  28.2 us (88%)
  Pallas kernels  2.61 us (8%)
  local copies, waits for them, and re-layouts  0.92 us (3%)
    all_to_all x1, blocking collectives, exchanged(): got = lax.all_to_all(sent, tuple(axes_in), 0, 0, tiled=True)  17.3 us
    all_to_all x1, blocking collectives, exchanged(): mine = lax.all_to_all(sums, tuple(axes_out), 0, 0, tiled=True)  10.9 us
    pallas_call x1, Pallas kernels, exchanged(): pl.pallas_call(functools.partial(update_kernel, places), out_shape=jax.Sh...  1.27 us
    pallas_call x1, Pallas kernels, exchanged(): pl.pallas_call(functools.partial(mix_kernel, slots), out_shape=(jax.Shape...  1 us
    unnamed x20, local copies, waits for them, and re-layouts  0.92 us

profile of v27, /device:TPU:0, one launch (start us, length us, event | category | flops | bytes accessed | tf_op | source)
XLA Modules:
  0.0 31.9 jit_solution(2793751793890195315)
XLA Ops:
  0.0 0.0 copy-start.2
  0.0 0.0 copy-start.1
  0.0 0.0 copy-start
  0.0 0.0 copy-start.8
  0.0 0.0 copy-start.9
  0.1 0.0 copy-start.5
  0.1 0.0 copy-start.6
  0.1 0.0 copy-start.7
  0.1 0.7 %copy-done.2 = bf16[128,256]{1,0:T(8,128)(2,1)S(1)} copy-done((bf16[128,256]{1,0:T(8,128)(2,1)S(1)}, bf16[128,256]{1,0:T(8,128)(2,1)}, u32[]{:S(2)}) %copy-start.2) | copy-done | bytes 65560
  0.8 0.0 copy-done.1
  0.9 0.1 copy-done
  1.0 0.0 copy-done.8
  1.0 0.0 copy-done.9
  1.0 0.0 copy-done.5
  1.0 0.0 copy-done.6
  1.0 0.0 copy-done.7
  1.0 1.0 %mix.1 = (bf16[32,32,128]{2,1,0:T(8,128)(2,1)S(1)}, bf16[512,128]{1,0:T(8,128)(2,1)S(1)}, f32[128,128]{1,0:T(8,128)S(1)}, f32[128,128]{1,0:T(8,128)S(1)}) custom-call(bf16[256,256]{1,0:T(8,128)(2,1)S(1)} %order.1.order_ref, s32[1,8]{1,0:T(1,128)S(1)} %bitcast.5, bf16[16,32,128]{2,1,0:T(8,128)(2,1)S(1)} %copy-done, f32[1,128]{1,0:T(1,128)S(1)} %bitcast.6, ...), custom_call_target="tpu_custom_call" | custom-call | tf_op jit(solution)/shard_map/mix/pallas_call | solution.py:373
  2.0 17.3 %all_to_all.10.got_ref = bf16[32,32,128]{2,1,0:T(8,128)(2,1)S(1)} all-to-all(bf16[32,32,128]{2,1,0:T(8,128)(2,1)S(1)} %get-tuple-element.9), channel_id=1, replica_groups=mesh['z'=4,'y'=2,'x'=2,'c'=2] {'x','y','c','z'}, dimensions={0} | all-to-all | bytes 524288 | tf_op jit(solution)/shard_map/all_to_all | solution.py:399
  19.3 0.3 triangle.1
  19.7 0.0 copy-start.3
  19.7 0.0 copy-start.4
  19.7 10.9 %all_to_all.11.got_ref = bf16[32,16,128]{2,1,0:T(8,128)(2,1)S(1)} all-to-all(bf16[32,16,128]{2,1,0:T(8,128)(2,1)S(1)} %triangle.1), channel_id=1, replica_groups=mesh['z'=4,'y'=2,'x'=2,'c'=2] {'x','y','c','z'}, dimensions={0} | all-to-all | bytes 262144 | tf_op jit(solution)/shard_map/all_to_all | solution.py:408
  30.6 0.0 copy-done.3
  30.6 0.0 copy-done.4
  30.6 1.3 %update.1 = bf16[16,32,128]{2,1,0:T(8,128)(2,1)} custom-call(bf16[32,16,128]{2,1,0:T(8,128)(2,1)S(1)} %all_to_all.11.got_ref, bf16[256,256]{1,0:T(8,128)(2,1)S(1)} %order.1.order_ref, bf16[512,128]{1,0:T(8,128)(2,1)S(1)} %get-tuple-element.10.normed_ref, f32[128,128]{1,0:T(8,128)S(1)} %get-tuple-element.11.gain_ref, ...), custom_call_target="tpu_custom_call" | custom-call | tf_op jit(solution)/shard_map/update/pallas_call | solution.py:410
  (1 shorter events, 0.0 us)
Async XLA Ops:
  0.0 0.8 %copy-start.2 = (bf16[128,256]{1,0:T(8,128)(2,1)S(1)}, bf16[128,256]{1,0:T(8,128)(2,1)}, u32[]{:S(2)}) copy-start(bf16[128,256]{1,0:T(8,128)(2,1)} %gate_ref.2) | copy-start | bytes 196612
  0.0 0.9 %copy-start.1 = (bf16[128,256]{1,0:T(8,128)(2,1)S(1)}, bf16[128,256]{1,0:T(8,128)(2,1)}, u32[]{:S(2)}) copy-start(bf16[128,256]{1,0:T(8,128)(2,1)} %proj_ref.2) | copy-start | bytes 196612
  0.0 1.0 %copy-start = (bf16[16,32,128]{2,1,0:T(8,128)(2,1)S(1)}, bf16[16,32,128]{2,1,0:T(8,128)(2,1)}, u32[]{:S(2)}) copy-start(bf16[16,32,128]{2,1,0:T(8,128)(2,1)} %pair_ref.1) | copy-start | bytes 393220
  0.0 1.0 %copy-start.8 = (f32[128]{0:T(128)S(1)}, f32[128]{0:T(128)}, u32[]{:S(2)}) copy-start(f32[128]{0:T(128)} %param.16) | copy-start | bytes 1540
  0.0 1.0 %copy-start.9 = (f32[128]{0:T(128)S(1)}, f32[128]{0:T(128)}, u32[]{:S(2)}) copy-start(f32[128]{0:T(128)} %param.17) | copy-start | bytes 1540
  0.1 0.9 %copy-start.5 = (s32[8]{0:T(128)S(1)}, s32[8]{0:T(128)}, u32[]{:S(2)}) copy-start(s32[8]{0:T(128)} %param.11) | copy-start | bytes 100
  0.1 0.9 %copy-start.6 = (f32[128]{0:T(128)S(1)}, f32[128]{0:T(128)}, u32[]{:S(2)}) copy-start(f32[128]{0:T(128)} %param.12) | copy-start | bytes 1540
  0.1 0.9 %copy-start.7 = (f32[128]{0:T(128)S(1)}, f32[128]{0:T(128)}, u32[]{:S(2)}) copy-start(f32[128]{0:T(128)} %param.13) | copy-start | bytes 1540
  19.7 10.9 %copy-start.3 = (bf16[128,128]{1,0:T(8,128)(2,1)S(1)}, bf16[128,128]{1,0:T(8,128)(2,1)}, u32[]{:S(2)}) copy-start(bf16[128,128]{1,0:T(8,128)(2,1)} %proj_ref.3) | copy-start | bytes 98308
  19.7 10.9 %copy-start.4 = (bf16[128,128]{1,0:T(8,128)(2,1)S(1)}, bf16[128,128]{1,0:T(8,128)(2,1)}, u32[]{:S(2)}) copy-start(bf16[128,128]{1,0:T(8,128)(2,1)} %gate_ref.3) | copy-start | bytes 98308

commit v28 on v27

--- a/solution.py
+++ b/solution.py
@@ -393,7 +393,7 @@
         norm_out_gain.reshape(1, LANES),
         norm_out_bias.reshape(1, LANES),
     )
-    axes_in, axes_out = "xycz", "xycz"
+    axes_in, axes_out = "cyxz", "cyxz"
     ring_in = ring_of(axes_in, grid_rows, grid_cols)
     ring_out = ring_of(axes_out, grid_rows, grid_cols)
     got = lax.all_to_all(sent, tuple(axes_in), 0, 0, tiled=True)

time: 32.1 us -> 31.6 us (0.984)
  blocking collectives: 28.2 us -> 27.7 us
    all_to_all x1, blocking collectives: 10.9 us -> 9.69 us  [exchanged(): mine = lax.all_to_all(sums, tuple(axes_out), 0, 0, tiled=True)]
    all_to_all x1, blocking collectives: 17.3 us -> 18.1 us  [exchanged(): got = lax.all_to_all(sent, tuple(axes_in), 0, 0, tiled=True)]
where the time goes in v28:
time: 31.6 us; the launch traced here: 31.4 us
  blocking collectives  27.7 us (88%)
  Pallas kernels  2.61 us (8%)
  local copies, waits for them, and re-layouts  0.92 us (3%)
    all_to_all x1, blocking collectives, exchanged(): got = lax.all_to_all(sent, tuple(axes_in), 0, 0, tiled=True)  18.1 us
    all_to_all x1, blocking collectives, exchanged(): mine = lax.all_to_all(sums, tuple(axes_out), 0, 0, tiled=True)  9.69 us
    pallas_call x1, Pallas kernels, exchanged(): pl.pallas_call(functools.partial(update_kernel, places), out_shape=jax.Sh...  1.27 us
    pallas_call x1, Pallas kernels, exchanged(): pl.pallas_call(functools.partial(mix_kernel, slots), out_shape=(jax.Shape...  1 us
    unnamed x20, local copies, waits for them, and re-layouts  0.92 us

profile of v28, /device:TPU:0, one launch (start us, length us, event | category | flops | bytes accessed | tf_op | source)
XLA Modules:
  0.0 31.4 jit_solution(14950626403042680095)
XLA Ops:
  0.0 0.0 copy-start.2
  0.0 0.0 copy-start.1
  0.0 0.0 copy-start
  0.0 0.0 copy-start.8
  0.0 0.0 copy-start.9
  0.1 0.0 copy-start.5
  0.1 0.0 copy-start.6
  0.1 0.0 copy-start.7
  0.1 0.7 %copy-done.2 = bf16[128,256]{1,0:T(8,128)(2,1)S(1)} copy-done((bf16[128,256]{1,0:T(8,128)(2,1)S(1)}, bf16[128,256]{1,0:T(8,128)(2,1)}, u32[]{:S(2)}) %copy-start.2) | copy-done | bytes 65560
  0.8 0.0 copy-done.1
  0.9 0.1 copy-done
  1.0 0.0 copy-done.8
  1.0 0.0 copy-done.9
  1.0 0.0 copy-done.5
  1.0 0.0 copy-done.6
  1.0 0.0 copy-done.7
  1.0 1.0 %mix.1 = (bf16[32,32,128]{2,1,0:T(8,128)(2,1)S(1)}, bf16[512,128]{1,0:T(8,128)(2,1)S(1)}, f32[128,128]{1,0:T(8,128)S(1)}, f32[128,128]{1,0:T(8,128)S(1)}) custom-call(bf16[256,256]{1,0:T(8,128)(2,1)S(1)} %order.1.order_ref, s32[1,8]{1,0:T(1,128)S(1)} %bitcast.5, bf16[16,32,128]{2,1,0:T(8,128)(2,1)S(1)} %copy-done, f32[1,128]{1,0:T(1,128)S(1)} %bitcast.6, ...), custom_call_target="tpu_custom_call" | custom-call | tf_op jit(solution)/shard_map/mix/pallas_call | solution.py:373
  2.0 18.1 %all_to_all.10.got_ref = bf16[32,32,128]{2,1,0:T(8,128)(2,1)S(1)} all-to-all(bf16[32,32,128]{2,1,0:T(8,128)(2,1)S(1)} %get-tuple-element.9), channel_id=1, replica_groups=mesh['z'=4,'y'=2,'x'=2,'c'=2] {'c','y','x','z'}, dimensions={0} | all-to-all | bytes 524288 | tf_op jit(solution)/shard_map/all_to_all | solution.py:399
  20.1 0.3 triangle.1
  20.4 0.0 copy-start.3
  20.4 0.0 copy-start.4
  20.4 9.7 %all_to_all.11.got_ref = bf16[32,16,128]{2,1,0:T(8,128)(2,1)S(1)} all-to-all(bf16[32,16,128]{2,1,0:T(8,128)(2,1)S(1)} %triangle.1), channel_id=1, replica_groups=mesh['z'=4,'y'=2,'x'=2,'c'=2] {'c','y','x','z'}, dimensions={0} | all-to-all | bytes 262144 | tf_op jit(solution)/shard_map/all_to_all | solution.py:408
  30.1 0.0 copy-done.3
  30.1 0.0 copy-done.4
  30.1 1.3 %update.1 = bf16[16,32,128]{2,1,0:T(8,128)(2,1)} custom-call(bf16[32,16,128]{2,1,0:T(8,128)(2,1)S(1)} %all_to_all.11.got_ref, bf16[256,256]{1,0:T(8,128)(2,1)S(1)} %order.1.order_ref, bf16[512,128]{1,0:T(8,128)(2,1)S(1)} %get-tuple-element.10.normed_ref, f32[128,128]{1,0:T(8,128)S(1)} %get-tuple-element.11.gain_ref, ...), custom_call_target="tpu_custom_call" | custom-call | tf_op jit(solution)/shard_map/update/pallas_call | solution.py:410
  (1 shorter events, 0.0 us)
Async XLA Ops:
  0.0 0.8 %copy-start.2 = (bf16[128,256]{1,0:T(8,128)(2,1)S(1)}, bf16[128,256]{1,0:T(8,128)(2,1)}, u32[]{:S(2)}) copy-start(bf16[128,256]{1,0:T(8,128)(2,1)} %gate_ref.2) | copy-start | bytes 196612
  0.0 0.9 %copy-start.1 = (bf16[128,256]{1,0:T(8,128)(2,1)S(1)}, bf16[128,256]{1,0:T(8,128)(2,1)}, u32[]{:S(2)}) copy-start(bf16[128,256]{1,0:T(8,128)(2,1)} %proj_ref.2) | copy-start | bytes 196612
  0.0 1.0 %copy-start = (bf16[16,32,128]{2,1,0:T(8,128)(2,1)S(1)}, bf16[16,32,128]{2,1,0:T(8,128)(2,1)}, u32[]{:S(2)}) copy-start(bf16[16,32,128]{2,1,0:T(8,128)(2,1)} %pair_ref.1) | copy-start | bytes 393220
  0.0 1.0 %copy-start.8 = (f32[128]{0:T(128)S(1)}, f32[128]{0:T(128)}, u32[]{:S(2)}) copy-start(f32[128]{0:T(128)} %param.16) | copy-start | bytes 1540
  0.0 1.0 %copy-start.9 = (f32[128]{0:T(128)S(1)}, f32[128]{0:T(128)}, u32[]{:S(2)}) copy-start(f32[128]{0:T(128)} %param.17) | copy-start | bytes 1540
  0.1 0.9 %copy-start.5 = (s32[8]{0:T(128)S(1)}, s32[8]{0:T(128)}, u32[]{:S(2)}) copy-start(s32[8]{0:T(128)} %param.11) | copy-start | bytes 100
  0.1 0.9 %copy-start.6 = (f32[128]{0:T(128)S(1)}, f32[128]{0:T(128)}, u32[]{:S(2)}) copy-start(f32[128]{0:T(128)} %param.12) | copy-start | bytes 1540
  0.1 0.9 %copy-start.7 = (f32[128]{0:T(128)S(1)}, f32[128]{0:T(128)}, u32[]{:S(2)}) copy-start(f32[128]{0:T(128)} %param.13) | copy-start | bytes 1540
  20.4 9.7 %copy-start.3 = (bf16[128,128]{1,0:T(8,128)(2,1)S(1)}, bf16[128,128]{1,0:T(8,128)(2,1)}, u32[]{:S(2)}) copy-start(bf16[128,128]{1,0:T(8,128)(2,1)} %proj_ref.3) | copy-start | bytes 98308
  20.4 9.7 %copy-start.4 = (bf16[128,128]{1,0:T(8,128)(2,1)S(1)}, bf16[128,128]{1,0:T(8,128)(2,1)}, u32[]{:S(2)}) copy-start(bf16[128,128]{1,0:T(8,128)(2,1)} %gate_ref.3) | copy-start | bytes 98308

commit v29 on v22

--- a/solution.py
+++ b/solution.py
@@ -184,13 +184,13 @@
     slots,
     order_ref,
     chain_ref,
-    pair_ref,
     gain_ref,
     bias_ref,
+    last_gain_ref,
+    last_bias_ref,
     proj_ref,
     gate_ref,
-    last_gain_ref,
-    last_bias_ref,
+    pair_ref,
     sent_ref,
     normed_ref,
     last_gain_out,
@@ -205,9 +205,8 @@
     flat = pair_ref[...].reshape(cells, channels).astype(F32)
     normed = layer_norm(flat, gain_ref[...], bias_ref[...]).astype(BF16)
     normed_ref[...] = normed
-    for source, target in ((last_gain_ref, last_gain_out), (last_bias_ref, last_bias_out)):
-        target[...] = jnp.broadcast_to(column(source[...]), target.shape)
-
+    last_gain_out[...] = last_gain_ref[...]
+    last_bias_out[...] = last_bias_ref[...]
     weights = jnp.concatenate([proj_ref[...], gate_ref[...] * 0.5], axis=1)
     products = dot(weights, normed, 0, 1)
     values, gates = products[: 2 * hidden], products[2 * hidden :]
@@ -304,7 +303,7 @@
         jnp.concatenate([part[row * SOME : (row + 1) * SOME] for part in parts], axis=0)
         for row in range(rows)
     ]
-    gain, bias = gain_ref[...], bias_ref[...]
+    gain, bias = column(gain_ref[...]), column(bias_ref[...])
     opened = sigmoid(dot(normed_ref[...], gate_ref[...] * 0.5))
     results = []
     for g in range(groups):
@@ -360,14 +359,14 @@
         cost_estimate=pl.CostEstimate(flops=10**9, bytes_accessed=10**6, transcendentals=0),
         name="order",
     )()
-    square = jax.ShapeDtypeStruct((LANES, LANES), F32)
+    row = jax.ShapeDtypeStruct((1, LANES), F32)
     sent, normed, last_gain, last_bias = pl.pallas_call(
         functools.partial(mix_kernel, slots),
         out_shape=(
             jax.ShapeDtypeStruct((devices, 2 * rows, LANES), BF16),
             jax.ShapeDtypeStruct((rows * cols, channels), BF16),
-            square,
-            square,
+            row,
+            row,
         ),
         in_specs=[VMEM] * 9,
         out_specs=[VMEM] * 4,
@@ -376,13 +375,13 @@
     )(
         order,
         chain_lengths.reshape(1, -1),
-        pair,
         norm_in_gain.reshape(1, LANES),
         norm_in_bias.reshape(1, LANES),
+        norm_out_gain.reshape(1, LANES),
+        norm_out_bias.reshape(1, LANES),
         proj_in,
         gate_in,
-        norm_out_gain.reshape(1, LANES),
-        norm_out_bias.reshape(1, LANES),
+        pair,
     )
     axes = ("col", "low", "high")
     got = lax.all_to_all(sent, axes, 0, 0, tiled=True)

time: 31.2 us -> 31.2 us (level)
  no operation moved by 1% of the time
where the time goes in v29:
time: 31.2 us; the launch traced here: 31 us
  blocking collectives  27.3 us (88%)
  Pallas kernels  2.64 us (8%)
  local copies, waits for them, and re-layouts  0.92 us (3%)
    all_to_all x1, blocking collectives, exchanged(): got = lax.all_to_all(sent, axes, 0, 0, tiled=True)  17.9 us
    all_to_all x1, blocking collectives, exchanged(): mine = lax.all_to_all(sums, axes, 0, 0, tiled=True)  9.45 us
    pallas_call x1, Pallas kernels, exchanged(): pl.pallas_call(update_kernel, out_shape=jax.ShapeDtypeStruct((rows, cols,...  1.29 us
    pallas_call x1, Pallas kernels, exchanged(): pl.pallas_call(functools.partial(mix_kernel, slots), out_shape=(jax.Shape...  1 us
    unnamed x20, local copies, waits for them, and re-layouts  0.92 us

profile of v29, /device:TPU:0, one launch (start us, length us, event | category | flops | bytes accessed | tf_op | source)
XLA Modules:
  0.0 31.0 jit_solution(8142961526917284656)
XLA Ops:
  0.0 0.0 copy-start.2
  0.0 0.0 copy-start.1
  0.0 0.0 copy-start
  0.0 0.0 copy-start.8
  0.0 0.0 copy-start.9
  0.1 0.0 copy-start.5
  0.1 0.0 copy-start.6
  0.1 0.0 copy-start.7
  0.1 0.7 %copy-done.2 = bf16[128,256]{1,0:T(8,128)(2,1)S(1)} copy-done((bf16[128,256]{1,0:T(8,128)(2,1)S(1)}, bf16[128,256]{1,0:T(8,128)(2,1)}, u32[]{:S(2)}) %copy-start.2) | copy-done | bytes 65560
  0.8 0.0 copy-done.1
  0.9 0.1 copy-done
  1.0 0.0 copy-done.8
  1.0 0.0 copy-done.9
  1.0 0.0 copy-done.5
  1.0 0.0 copy-done.6
  1.0 0.0 copy-done.7
  1.0 1.0 %mix.1 = (bf16[32,32,128]{2,1,0:T(8,128)(2,1)S(1)}, bf16[512,128]{1,0:T(8,128)(2,1)S(1)}, f32[1,128]{1,0:T(1,128)S(1)}, f32[1,128]{1,0:T(1,128)S(1)}) custom-call(bf16[256,256]{1,0:T(8,128)(2,1)S(1)} %order.1.order_ref, s32[1,8]{1,0:T(1,128)S(1)} %bitcast.5, f32[1,128]{1,0:T(1,128)S(1)} %bitcast.6, f32[1,128]{1,0:T(1,128)S(1)} %bitcast.7, ...), custom_call_target="tpu_custom_call" | custom-call | tf_op jit(solution)/shard_map/mix/pallas_call | solution.py:363
  2.0 17.9 %all_to_all.10.got_ref = bf16[32,32,128]{2,1,0:T(8,128)(2,1)S(1)} all-to-all(bf16[32,32,128]{2,1,0:T(8,128)(2,1)S(1)} %get-tuple-element.9), channel_id=1, replica_groups=mesh['high'=4,'low'=2,'col'=4] {'col','low','high'}, dimensions={0} | all-to-all | bytes 524288 | tf_op jit(solution)/shard_map/all_to_all | solution.py:387
  19.9 0.3 triangle.1
  20.2 0.0 copy-start.3
  20.2 0.0 copy-start.4
  20.2 9.5 %all_to_all.11.got_ref = bf16[32,16,128]{2,1,0:T(8,128)(2,1)S(1)} all-to-all(bf16[32,16,128]{2,1,0:T(8,128)(2,1)S(1)} %triangle.1), channel_id=1, replica_groups=mesh['high'=4,'low'=2,'col'=4] {'col','low','high'}, dimensions={0} | all-to-all | bytes 262144 | tf_op jit(solution)/shard_map/all_to_all | solution.py:396
  29.7 0.0 copy-done.3
  29.7 0.0 copy-done.4
  29.7 1.3 %update.1 = bf16[16,32,128]{2,1,0:T(8,128)(2,1)} custom-call(bf16[32,16,128]{2,1,0:T(8,128)(2,1)S(1)} %all_to_all.11.got_ref, bf16[256,256]{1,0:T(8,128)(2,1)S(1)} %order.1.order_ref, bf16[512,128]{1,0:T(8,128)(2,1)S(1)} %get-tuple-element.10.normed_ref, f32[1,128]{1,0:T(1,128)S(1)} %get-tuple-element.11.gain_ref, f32[1,128]{1,0:T(1,128)S(1)} %get-tuple-element.12.bias_ref, ...), custom_call_target="tpu_custom_call" | custom-call | tf_op jit(solution)/shard_map/update/pallas_call | solution.py:397
  (1 shorter events, 0.0 us)
Async XLA Ops:
  0.0 0.8 %copy-start.2 = (bf16[128,256]{1,0:T(8,128)(2,1)S(1)}, bf16[128,256]{1,0:T(8,128)(2,1)}, u32[]{:S(2)}) copy-start(bf16[128,256]{1,0:T(8,128)(2,1)} %gate_ref.2) | copy-start | bytes 196612
  0.0 0.9 %copy-start.1 = (bf16[128,256]{1,0:T(8,128)(2,1)S(1)}, bf16[128,256]{1,0:T(8,128)(2,1)}, u32[]{:S(2)}) copy-start(bf16[128,256]{1,0:T(8,128)(2,1)} %proj_ref.2) | copy-start | bytes 196612
  0.0 1.0 %copy-start = (bf16[16,32,128]{2,1,0:T(8,128)(2,1)S(1)}, bf16[16,32,128]{2,1,0:T(8,128)(2,1)}, u32[]{:S(2)}) copy-start(bf16[16,32,128]{2,1,0:T(8,128)(2,1)} %pair_ref.1) | copy-start | bytes 393220
  0.0 1.0 %copy-start.8 = (f32[128]{0:T(128)S(1)}, f32[128]{0:T(128)}, u32[]{:S(2)}) copy-start(f32[128]{0:T(128)} %param.16) | copy-start | bytes 1540
  0.0 1.0 %copy-start.9 = (f32[128]{0:T(128)S(1)}, f32[128]{0:T(128)}, u32[]{:S(2)}) copy-start(f32[128]{0:T(128)} %param.17) | copy-start | bytes 1540
  0.1 0.9 %copy-start.5 = (s32[8]{0:T(128)S(1)}, s32[8]{0:T(128)}, u32[]{:S(2)}) copy-start(s32[8]{0:T(128)} %param.11) | copy-start | bytes 100
  0.1 0.9 %copy-start.6 = (f32[128]{0:T(128)S(1)}, f32[128]{0:T(128)}, u32[]{:S(2)}) copy-start(f32[128]{0:T(128)} %param.12) | copy-start | bytes 1540
  0.1 0.9 %copy-start.7 = (f32[128]{0:T(128)S(1)}, f32[128]{0:T(128)}, u32[]{:S(2)}) copy-start(f32[128]{0:T(128)} %param.13) | copy-start | bytes 1540
  20.2 9.5 %copy-start.3 = (bf16[128,128]{1,0:T(8,128)(2,1)S(1)}, bf16[128,128]{1,0:T(8,128)(2,1)}, u32[]{:S(2)}) copy-start(bf16[128,128]{1,0:T(8,128)(2,1)} %proj_ref.3) | copy-start | bytes 98308
  20.2 9.5 %copy-start.4 = (bf16[128,128]{1,0:T(8,128)(2,1)S(1)}, bf16[128,128]{1,0:T(8,128)(2,1)}, u32[]{:S(2)}) copy-start(bf16[128,128]{1,0:T(8,128)(2,1)} %gate_ref.3) | copy-start | bytes 98308

commit v30 on v29

--- a/solution.py
+++ b/solution.py
@@ -207,32 +207,25 @@
     normed_ref[...] = normed
     last_gain_out[...] = last_gain_ref[...]
     last_bias_out[...] = last_bias_ref[...]
-    weights = jnp.concatenate([proj_ref[...], gate_ref[...] * 0.5], axis=1)
-    products = dot(weights, normed, 0, 1)
-    values, gates = products[: 2 * hidden], products[2 * hidden :]
     mask = cell_mask(chain_ref[...], slots, rows, cols)
-    mixed = (sigmoid(gates) * values * mask).astype(BF16)
-
-    by_row = []
+    order = order_ref[...]
     for side in range(2):
+        own = slice(side * hidden, (side + 1) * hidden)
+        values = dot(proj_ref[:, own], normed, 0, 1)
+        gates = dot(gate_ref[:, own] * 0.5, normed, 0, 1)
+        mixed = (sigmoid(gates) * values * mask).astype(BF16)
         lines = []
         for g in range(groups):
             lines += exchange_blocks(
                 [
-                    mixed[
-                        side * hidden + n * chunks : side * hidden + (n + 1) * chunks,
-                        g * LANES : (g + 1) * LANES,
-                    ]
+                    mixed[n * chunks : (n + 1) * chunks, g * LANES : (g + 1) * LANES]
                     for n in range(inner)
                 ],
                 cols,
             )
-        by_row.append(lines)
-    order = order_ref[...]
-    for part in range(chunks // SOME):
-        for side in range(2):
+        for part in range(chunks // SOME):
             stack = jnp.concatenate(
-                [line[part * SOME : (part + 1) * SOME] for line in by_row[side]], axis=0
+                [line[part * SOME : (part + 1) * SOME] for line in lines], axis=0
             )
             sent_ref[part * SOME : (part + 1) * SOME, side * rows : (side + 1) * rows] = (
                 dot(order, stack).astype(BF16).reshape(SOME, rows, LANES)

time: 31.2 us -> 31.5 us (level)
  no operation moved by 1% of the time
where the time goes in v30:
time: 31.5 us; the launch traced here: 31.3 us
  blocking collectives  27.3 us (87%)
  Pallas kernels  2.92 us (9%)
  local copies, waits for them, and re-layouts  0.92 us (3%)
    all_to_all x1, blocking collectives, exchanged(): got = lax.all_to_all(sent, axes, 0, 0, tiled=True)  17.9 us
    all_to_all x1, blocking collectives, exchanged(): mine = lax.all_to_all(sums, axes, 0, 0, tiled=True)  9.45 us
    pallas_call x1, Pallas kernels, exchanged(): pl.pallas_call(update_kernel, out_shape=jax.ShapeDtypeStruct((rows, cols,...  1.29 us
    pallas_call x1, Pallas kernels, exchanged(): pl.pallas_call(functools.partial(mix_kernel, slots), out_shape=(jax.Shape...  1.28 us
    unnamed x20, local copies, waits for them, and re-layouts  0.92 us

profile of v30, /device:TPU:0, one launch (start us, length us, event | category | flops | bytes accessed | tf_op | source)
XLA Modules:
  0.0 31.3 jit_solution(15094214576762117227)
XLA Ops:
  0.0 0.0 copy-start.2
  0.0 0.0 copy-start.1
  0.0 0.0 copy-start
  0.0 0.0 copy-start.8
  0.0 0.0 copy-start.9
  0.1 0.0 copy-start.5
  0.1 0.0 copy-start.6
  0.1 0.0 copy-start.7
  0.1 0.7 %copy-done.2 = bf16[128,256]{1,0:T(8,128)(2,1)S(1)} copy-done((bf16[128,256]{1,0:T(8,128)(2,1)S(1)}, bf16[128,256]{1,0:T(8,128)(2,1)}, u32[]{:S(2)}) %copy-start.2) | copy-done | bytes 65560
  0.8 0.0 copy-done.1
  0.9 0.1 copy-done
  1.0 0.0 copy-done.8
  1.0 0.0 copy-done.9
  1.0 0.0 copy-done.5
  1.0 0.0 copy-done.6
  1.0 0.0 copy-done.7
  1.0 1.3 %mix.1 = (bf16[32,32,128]{2,1,0:T(8,128)(2,1)S(1)}, bf16[512,128]{1,0:T(8,128)(2,1)S(1)}, f32[1,128]{1,0:T(1,128)S(1)}, f32[1,128]{1,0:T(1,128)S(1)}) custom-call(bf16[256,256]{1,0:T(8,128)(2,1)S(1)} %order.1.order_ref, s32[1,8]{1,0:T(1,128)S(1)} %bitcast.5, f32[1,128]{1,0:T(1,128)S(1)} %bitcast.6, f32[1,128]{1,0:T(1,128)S(1)} %bitcast.7, ...), custom_call_target="tpu_custom_call" | custom-call | tf_op jit(solution)/shard_map/mix/pallas_call | solution.py:356
  2.3 17.9 %all_to_all.10.got_ref = bf16[32,32,128]{2,1,0:T(8,128)(2,1)S(1)} all-to-all(bf16[32,32,128]{2,1,0:T(8,128)(2,1)S(1)} %get-tuple-element.9), channel_id=1, replica_groups=mesh['high'=4,'low'=2,'col'=4] {'col','low','high'}, dimensions={0} | all-to-all | bytes 524288 | tf_op jit(solution)/shard_map/all_to_all | solution.py:380
  20.2 0.3 triangle.1
  20.5 0.0 copy-start.3
  20.5 0.0 copy-start.4
  20.5 9.5 %all_to_all.11.got_ref = bf16[32,16,128]{2,1,0:T(8,128)(2,1)S(1)} all-to-all(bf16[32,16,128]{2,1,0:T(8,128)(2,1)S(1)} %triangle.1), channel_id=1, replica_groups=mesh['high'=4,'low'=2,'col'=4] {'col','low','high'}, dimensions={0} | all-to-all | bytes 262144 | tf_op jit(solution)/shard_map/all_to_all | solution.py:389
  30.0 0.0 copy-done.3
  30.0 0.0 copy-done.4
  30.0 1.3 %update.1 = bf16[16,32,128]{2,1,0:T(8,128)(2,1)} custom-call(bf16[32,16,128]{2,1,0:T(8,128)(2,1)S(1)} %all_to_all.11.got_ref, bf16[256,256]{1,0:T(8,128)(2,1)S(1)} %order.1.order_ref, bf16[512,128]{1,0:T(8,128)(2,1)S(1)} %get-tuple-element.10.normed_ref, f32[1,128]{1,0:T(1,128)S(1)} %get-tuple-element.11.gain_ref, f32[1,128]{1,0:T(1,128)S(1)} %get-tuple-element.12.bias_ref, ...), custom_call_target="tpu_custom_call" | custom-call | tf_op jit(solution)/shard_map/update/pallas_call | solution.py:390
  (1 shorter events, 0.0 us)
Async XLA Ops:
  0.0 0.8 %copy-start.2 = (bf16[128,256]{1,0:T(8,128)(2,1)S(1)}, bf16[128,256]{1,0:T(8,128)(2,1)}, u32[]{:S(2)}) copy-start(bf16[128,256]{1,0:T(8,128)(2,1)} %gate_ref.2) | copy-start | bytes 196612
  0.0 0.9 %copy-start.1 = (bf16[128,256]{1,0:T(8,128)(2,1)S(1)}, bf16[128,256]{1,0:T(8,128)(2,1)}, u32[]{:S(2)}) copy-start(bf16[128,256]{1,0:T(8,128)(2,1)} %proj_ref.2) | copy-start | bytes 196612
  0.0 1.0 %copy-start = (bf16[16,32,128]{2,1,0:T(8,128)(2,1)S(1)}, bf16[16,32,128]{2,1,0:T(8,128)(2,1)}, u32[]{:S(2)}) copy-start(bf16[16,32,128]{2,1,0:T(8,128)(2,1)} %pair_ref.1) | copy-start | bytes 393220
  0.0 1.0 %copy-start.8 = (f32[128]{0:T(128)S(1)}, f32[128]{0:T(128)}, u32[]{:S(2)}) copy-start(f32[128]{0:T(128)} %param.16) | copy-start | bytes 1540
  0.0 1.0 %copy-start.9 = (f32[128]{0:T(128)S(1)}, f32[128]{0:T(128)}, u32[]{:S(2)}) copy-start(f32[128]{0:T(128)} %param.17) | copy-start | bytes 1540
  0.1 0.9 %copy-start.5 = (s32[8]{0:T(128)S(1)}, s32[8]{0:T(128)}, u32[]{:S(2)}) copy-start(s32[8]{0:T(128)} %param.11) | copy-start | bytes 100
  0.1 0.9 %copy-start.6 = (f32[128]{0:T(128)S(1)}, f32[128]{0:T(128)}, u32[]{:S(2)}) copy-start(f32[128]{0:T(128)} %param.12) | copy-start | bytes 1540
  0.1 0.9 %copy-start.7 = (f32[128]{0:T(128)S(1)}, f32[128]{0:T(128)}, u32[]{:S(2)}) copy-start(f32[128]{0:T(128)} %param.13) | copy-start | bytes 1540
  20.5 9.5 %copy-start.3 = (bf16[128,128]{1,0:T(8,128)(2,1)S(1)}, bf16[128,128]{1,0:T(8,128)(2,1)}, u32[]{:S(2)}) copy-start(bf16[128,128]{1,0:T(8,128)(2,1)} %proj_ref.3) | copy-start | bytes 98308
  20.5 9.5 %copy-start.4 = (bf16[128,128]{1,0:T(8,128)(2,1)S(1)}, bf16[128,128]{1,0:T(8,128)(2,1)}, u32[]{:S(2)}) copy-start(bf16[128,128]{1,0:T(8,128)(2,1)} %gate_ref.3) | copy-start | bytes 98308

commit v31 on v29

--- a/solution.py
+++ b/solution.py
@@ -228,15 +228,18 @@
                 cols,
             )
         by_row.append(lines)
-    order = order_ref[...]
-    for part in range(chunks // SOME):
-        for side in range(2):
-            stack = jnp.concatenate(
-                [line[part * SOME : (part + 1) * SOME] for line in by_row[side]], axis=0
-            )
-            sent_ref[part * SOME : (part + 1) * SOME, side * rows : (side + 1) * rows] = (
-                dot(order, stack).astype(BF16).reshape(SOME, rows, LANES)
-            )
+    blocks = [(part, side) for part in range(chunks // SOME) for side in range(2)]
+    stacks = [
+        jnp.concatenate(
+            [line[part * SOME : (part + 1) * SOME] for line in by_row[side]], axis=0
+        )
+        for part, side in blocks
+    ]
+    moved = dot(order_ref[...], jnp.concatenate(stacks, axis=1)).astype(BF16)
+    for n, (part, side) in enumerate(blocks):
+        sent_ref[part * SOME : (part + 1) * SOME, side * rows : (side + 1) * rows] = moved[
+            :, n * LANES : (n + 1) * LANES
+        ].reshape(SOME, rows, LANES)
 
 
 def triangle_kernel(split, grid_cols, rows, cols, got_ref, sent_ref):
@@ -294,11 +297,15 @@
     chunks = got_ref.shape[0]
     inner = LANES // cols
     groups = rows // inner
-    order = order_ref[...]
-    parts = [
-        dot(order, got_ref[part * SOME : (part + 1) * SOME].reshape(SOME * rows, LANES)).astype(BF16)
-        for part in range(chunks // SOME)
-    ]
+    got = jnp.concatenate(
+        [
+            got_ref[part * SOME : (part + 1) * SOME].reshape(SOME * rows, LANES)
+            for part in range(chunks // SOME)
+        ],
+        axis=1,
+    )
+    moved = dot(order_ref[...], got).astype(BF16)
+    parts = [moved[:, part * LANES : (part + 1) * LANES] for part in range(chunks // SOME)]
     lines = [
         jnp.concatenate([part[row * SOME : (row + 1) * SOME] for part in parts], axis=0)
         for row in range(rows)

time: 31.2 us -> 31.1 us (level)
  no operation moved by 1% of the time
where the time goes in v31:
time: 31.1 us; the launch traced here: 30.9 us
  blocking collectives  27.3 us (88%)
  Pallas kernels  2.54 us (8%)
  local copies, waits for them, and re-layouts  0.92 us (3%)
    all_to_all x1, blocking collectives, exchanged(): got = lax.all_to_all(sent, axes, 0, 0, tiled=True)  17.9 us
    all_to_all x1, blocking collectives, exchanged(): mine = lax.all_to_all(sums, axes, 0, 0, tiled=True)  9.45 us
    pallas_call x1, Pallas kernels, exchanged(): pl.pallas_call(update_kernel, out_shape=jax.ShapeDtypeStruct((rows, cols,...  1.29 us
    unnamed x20, local copies, waits for them, and re-layouts  0.92 us
    pallas_call x1, Pallas kernels, exchanged(): pl.pallas_call(functools.partial(mix_kernel, slots), out_shape=(jax.Shape...  0.91 us

profile of v31, /device:TPU:0, one launch (start us, length us, event | category | flops | bytes accessed | tf_op | source)
XLA Modules:
  0.0 30.9 jit_solution(6949494460929472581)
XLA Ops:
  0.0 0.0 copy-start.2
  0.0 0.0 copy-start.1
  0.0 0.0 copy-start
  0.0 0.0 copy-start.8
  0.0 0.0 copy-start.9
  0.1 0.0 copy-start.5
  0.1 0.0 copy-start.6
  0.1 0.0 copy-start.7
  0.1 0.7 %copy-done.2 = bf16[128,256]{1,0:T(8,128)(2,1)S(1)} copy-done((bf16[128,256]{1,0:T(8,128)(2,1)S(1)}, bf16[128,256]{1,0:T(8,128)(2,1)}, u32[]{:S(2)}) %copy-start.2) | copy-done | bytes 65560
  0.8 0.0 copy-done.1
  0.9 0.1 copy-done
  1.0 0.0 copy-done.8
  1.0 0.0 copy-done.9
  1.0 0.0 copy-done.5
  1.0 0.0 copy-done.6
  1.0 0.0 copy-done.7
  1.0 0.9 %mix.1 = (bf16[32,32,128]{2,1,0:T(8,128)(2,1)S(1)}, bf16[512,128]{1,0:T(8,128)(2,1)S(1)}, f32[1,128]{1,0:T(1,128)S(1)}, f32[1,128]{1,0:T(1,128)S(1)}) custom-call(bf16[256,256]{1,0:T(8,128)(2,1)S(1)} %order.1.order_ref, s32[1,8]{1,0:T(1,128)S(1)} %bitcast.5, f32[1,128]{1,0:T(1,128)S(1)} %bitcast.6, f32[1,128]{1,0:T(1,128)S(1)} %bitcast.7, ...), custom_call_target="tpu_custom_call" | custom-call | tf_op jit(solution)/shard_map/mix/pallas_call | solution.py:370
  1.9 17.9 %all_to_all.10.got_ref = bf16[32,32,128]{2,1,0:T(8,128)(2,1)S(1)} all-to-all(bf16[32,32,128]{2,1,0:T(8,128)(2,1)S(1)} %get-tuple-element.9), channel_id=1, replica_groups=mesh['high'=4,'low'=2,'col'=4] {'col','low','high'}, dimensions={0} | all-to-all | bytes 524288 | tf_op jit(solution)/shard_map/all_to_all | solution.py:394
  19.8 0.3 triangle.1
  20.1 0.0 copy-start.3
  20.1 0.0 copy-start.4
  20.1 9.5 %all_to_all.11.got_ref = bf16[32,16,128]{2,1,0:T(8,128)(2,1)S(1)} all-to-all(bf16[32,16,128]{2,1,0:T(8,128)(2,1)S(1)} %triangle.1), channel_id=1, replica_groups=mesh['high'=4,'low'=2,'col'=4] {'col','low','high'}, dimensions={0} | all-to-all | bytes 262144 | tf_op jit(solution)/shard_map/all_to_all | solution.py:403
  29.6 0.0 copy-done.3
  29.6 0.0 copy-done.4
  29.6 1.3 %update.1 = bf16[16,32,128]{2,1,0:T(8,128)(2,1)} custom-call(bf16[32,16,128]{2,1,0:T(8,128)(2,1)S(1)} %all_to_all.11.got_ref, bf16[256,256]{1,0:T(8,128)(2,1)S(1)} %order.1.order_ref, bf16[512,128]{1,0:T(8,128)(2,1)S(1)} %get-tuple-element.10.normed_ref, f32[1,128]{1,0:T(1,128)S(1)} %get-tuple-element.11.gain_ref, f32[1,128]{1,0:T(1,128)S(1)} %get-tuple-element.12.bias_ref, ...), custom_call_target="tpu_custom_call" | custom-call | tf_op jit(solution)/shard_map/update/pallas_call | solution.py:404
  (1 shorter events, 0.0 us)
Async XLA Ops:
  0.0 0.8 %copy-start.2 = (bf16[128,256]{1,0:T(8,128)(2,1)S(1)}, bf16[128,256]{1,0:T(8,128)(2,1)}, u32[]{:S(2)}) copy-start(bf16[128,256]{1,0:T(8,128)(2,1)} %gate_ref.2) | copy-start | bytes 196612
  0.0 0.9 %copy-start.1 = (bf16[128,256]{1,0:T(8,128)(2,1)S(1)}, bf16[128,256]{1,0:T(8,128)(2,1)}, u32[]{:S(2)}) copy-start(bf16[128,256]{1,0:T(8,128)(2,1)} %proj_ref.2) | copy-start | bytes 196612
  0.0 1.0 %copy-start = (bf16[16,32,128]{2,1,0:T(8,128)(2,1)S(1)}, bf16[16,32,128]{2,1,0:T(8,128)(2,1)}, u32[]{:S(2)}) copy-start(bf16[16,32,128]{2,1,0:T(8,128)(2,1)} %pair_ref.1) | copy-start | bytes 393220
  0.0 1.0 %copy-start.8 = (f32[128]{0:T(128)S(1)}, f32[128]{0:T(128)}, u32[]{:S(2)}) copy-start(f32[128]{0:T(128)} %param.16) | copy-start | bytes 1540
  0.0 1.0 %copy-start.9 = (f32[128]{0:T(128)S(1)}, f32[128]{0:T(128)}, u32[]{:S(2)}) copy-start(f32[128]{0:T(128)} %param.17) | copy-start | bytes 1540
  0.1 0.9 %copy-start.5 = (s32[8]{0:T(128)S(1)}, s32[8]{0:T(128)}, u32[]{:S(2)}) copy-start(s32[8]{0:T(128)} %param.11) | copy-start | bytes 100
  0.1 0.9 %copy-start.6 = (f32[128]{0:T(128)S(1)}, f32[128]{0:T(128)}, u32[]{:S(2)}) copy-start(f32[128]{0:T(128)} %param.12) | copy-start | bytes 1540
  0.1 0.9 %copy-start.7 = (f32[128]{0:T(128)S(1)}, f32[128]{0:T(128)}, u32[]{:S(2)}) copy-start(f32[128]{0:T(128)} %param.13) | copy-start | bytes 1540
  20.1 9.5 %copy-start.3 = (bf16[128,128]{1,0:T(8,128)(2,1)S(1)}, bf16[128,128]{1,0:T(8,128)(2,1)}, u32[]{:S(2)}) copy-start(bf16[128,128]{1,0:T(8,128)(2,1)} %proj_ref.3) | copy-start | bytes 98308
  20.1 9.5 %copy-start.4 = (bf16[128,128]{1,0:T(8,128)(2,1)S(1)}, bf16[128,128]{1,0:T(8,128)(2,1)}, u32[]{:S(2)}) copy-start(bf16[128,128]{1,0:T(8,128)(2,1)} %gate_ref.3) | copy-start | bytes 98308

commit v32 on v31

--- a/solution.py
+++ b/solution.py
@@ -297,15 +297,11 @@
     chunks = got_ref.shape[0]
     inner = LANES // cols
     groups = rows // inner
-    got = jnp.concatenate(
-        [
-            got_ref[part * SOME : (part + 1) * SOME].reshape(SOME * rows, LANES)
-            for part in range(chunks // SOME)
-        ],
-        axis=1,
-    )
-    moved = dot(order_ref[...], got).astype(BF16)
-    parts = [moved[:, part * LANES : (part + 1) * LANES] for part in range(chunks // SOME)]
+    order = order_ref[...]
+    parts = [
+        dot(order, got_ref[part * SOME : (part + 1) * SOME].reshape(SOME * rows, LANES)).astype(BF16)
+        for part in range(chunks // SOME)
+    ]
     lines = [
         jnp.concatenate([part[row * SOME : (row + 1) * SOME] for part in parts], axis=0)
         for row in range(rows)

time: 31.1 us -> 31.1 us (level)
  no operation moved by 1% of the time
where the time goes in v32:
time: 31.1 us; the launch traced here: 30.9 us
  blocking collectives  27.3 us (88%)
  Pallas kernels  2.55 us (8%)
  local copies, waits for them, and re-layouts  0.92 us (3%)
    all_to_all x1, blocking collectives, exchanged(): got = lax.all_to_all(sent, axes, 0, 0, tiled=True)  17.9 us
    all_to_all x1, blocking collectives, exchanged(): mine = lax.all_to_all(sums, axes, 0, 0, tiled=True)  9.45 us
    pallas_call x1, Pallas kernels, exchanged(): pl.pallas_call(update_kernel, out_shape=jax.ShapeDtypeStruct((rows, cols,...  1.29 us
    unnamed x20, local copies, waits for them, and re-layouts  0.92 us
    pallas_call x1, Pallas kernels, exchanged(): pl.pallas_call(functools.partial(mix_kernel, slots), out_shape=(jax.Shape...  0.91 us

profile of v32, /device:TPU:0, one launch (start us, length us, event | category | flops | bytes accessed | tf_op | source)
XLA Modules:
  0.0 30.9 jit_solution(4269365171029809587)
XLA Ops:
  0.0 0.0 copy-start.2
  0.0 0.0 copy-start.1
  0.0 0.0 copy-start
  0.0 0.0 copy-start.8
  0.0 0.0 copy-start.9
  0.1 0.0 copy-start.5
  0.1 0.0 copy-start.6
  0.1 0.0 copy-start.7
  0.1 0.7 %copy-done.2 = bf16[128,256]{1,0:T(8,128)(2,1)S(1)} copy-done((bf16[128,256]{1,0:T(8,128)(2,1)S(1)}, bf16[128,256]{1,0:T(8,128)(2,1)}, u32[]{:S(2)}) %copy-start.2) | copy-done | bytes 65560
  0.8 0.0 copy-done.1
  0.9 0.1 copy-done
  1.0 0.0 copy-done.8
  1.0 0.0 copy-done.9
  1.0 0.0 copy-done.5
  1.0 0.0 copy-done.6
  1.0 0.0 copy-done.7
  1.0 0.9 %mix.1 = (bf16[32,32,128]{2,1,0:T(8,128)(2,1)S(1)}, bf16[512,128]{1,0:T(8,128)(2,1)S(1)}, f32[1,128]{1,0:T(1,128)S(1)}, f32[1,128]{1,0:T(1,128)S(1)}) custom-call(bf16[256,256]{1,0:T(8,128)(2,1)S(1)} %order.1.order_ref, s32[1,8]{1,0:T(1,128)S(1)} %bitcast.5, f32[1,128]{1,0:T(1,128)S(1)} %bitcast.6, f32[1,128]{1,0:T(1,128)S(1)} %bitcast.7, ...), custom_call_target="tpu_custom_call" | custom-call | tf_op jit(solution)/shard_map/mix/pallas_call | solution.py:366
  1.9 17.9 %all_to_all.10.got_ref = bf16[32,32,128]{2,1,0:T(8,128)(2,1)S(1)} all-to-all(bf16[32,32,128]{2,1,0:T(8,128)(2,1)S(1)} %get-tuple-element.9), channel_id=1, replica_groups=mesh['high'=4,'low'=2,'col'=4] {'col','low','high'}, dimensions={0} | all-to-all | bytes 524288 | tf_op jit(solution)/shard_map/all_to_all | solution.py:390
  19.8 0.3 triangle.1
  20.1 0.0 copy-start.3
  20.1 0.0 copy-start.4
  20.1 9.5 %all_to_all.11.got_ref = bf16[32,16,128]{2,1,0:T(8,128)(2,1)S(1)} all-to-all(bf16[32,16,128]{2,1,0:T(8,128)(2,1)S(1)} %triangle.1), channel_id=1, replica_groups=mesh['high'=4,'low'=2,'col'=4] {'col','low','high'}, dimensions={0} | all-to-all | bytes 262144 | tf_op jit(solution)/shard_map/all_to_all | solution.py:399
  29.6 0.0 copy-done.3
  29.6 0.0 copy-done.4
  29.6 1.3 %update.1 = bf16[16,32,128]{2,1,0:T(8,128)(2,1)} custom-call(bf16[32,16,128]{2,1,0:T(8,128)(2,1)S(1)} %all_to_all.11.got_ref, bf16[256,256]{1,0:T(8,128)(2,1)S(1)} %order.1.order_ref, bf16[512,128]{1,0:T(8,128)(2,1)S(1)} %get-tuple-element.10.normed_ref, f32[1,128]{1,0:T(1,128)S(1)} %get-tuple-element.11.gain_ref, f32[1,128]{1,0:T(1,128)S(1)} %get-tuple-element.12.bias_ref, ...), custom_call_target="tpu_custom_call" | custom-call | tf_op jit(solution)/shard_map/update/pallas_call | solution.py:400
  (1 shorter events, 0.0 us)
Async XLA Ops:
  0.0 0.8 %copy-start.2 = (bf16[128,256]{1,0:T(8,128)(2,1)S(1)}, bf16[128,256]{1,0:T(8,128)(2,1)}, u32[]{:S(2)}) copy-start(bf16[128,256]{1,0:T(8,128)(2,1)} %gate_ref.2) | copy-start | bytes 196612
  0.0 0.9 %copy-start.1 = (bf16[128,256]{1,0:T(8,128)(2,1)S(1)}, bf16[128,256]{1,0:T(8,128)(2,1)}, u32[]{:S(2)}) copy-start(bf16[128,256]{1,0:T(8,128)(2,1)} %proj_ref.2) | copy-start | bytes 196612
  0.0 1.0 %copy-start = (bf16[16,32,128]{2,1,0:T(8,128)(2,1)S(1)}, bf16[16,32,128]{2,1,0:T(8,128)(2,1)}, u32[]{:S(2)}) copy-start(bf16[16,32,128]{2,1,0:T(8,128)(2,1)} %pair_ref.1) | copy-start | bytes 393220
  0.0 1.0 %copy-start.8 = (f32[128]{0:T(128)S(1)}, f32[128]{0:T(128)}, u32[]{:S(2)}) copy-start(f32[128]{0:T(128)} %param.16) | copy-start | bytes 1540
  0.0 1.0 %copy-start.9 = (f32[128]{0:T(128)S(1)}, f32[128]{0:T(128)}, u32[]{:S(2)}) copy-start(f32[128]{0:T(128)} %param.17) | copy-start | bytes 1540
  0.1 0.9 %copy-start.5 = (s32[8]{0:T(128)S(1)}, s32[8]{0:T(128)}, u32[]{:S(2)}) copy-start(s32[8]{0:T(128)} %param.11) | copy-start | bytes 100
  0.1 0.9 %copy-start.6 = (f32[128]{0:T(128)S(1)}, f32[128]{0:T(128)}, u32[]{:S(2)}) copy-start(f32[128]{0:T(128)} %param.12) | copy-start | bytes 1540
  0.1 0.9 %copy-start.7 = (f32[128]{0:T(128)S(1)}, f32[128]{0:T(128)}, u32[]{:S(2)}) copy-start(f32[128]{0:T(128)} %param.13) | copy-start | bytes 1540
  20.1 9.5 %copy-start.3 = (bf16[128,128]{1,0:T(8,128)(2,1)S(1)}, bf16[128,128]{1,0:T(8,128)(2,1)}, u32[]{:S(2)}) copy-start(bf16[128,128]{1,0:T(8,128)(2,1)} %proj_ref.3) | copy-start | bytes 98308
  20.1 9.5 %copy-start.4 = (bf16[128,128]{1,0:T(8,128)(2,1)S(1)}, bf16[128,128]{1,0:T(8,128)(2,1)}, u32[]{:S(2)}) copy-start(bf16[128,128]{1,0:T(8,128)(2,1)} %gate_ref.3) | copy-start | bytes 98308

commit v33 on v22

--- a/solution.py
+++ b/solution.py
@@ -229,15 +229,18 @@
                 cols,
             )
         by_row.append(lines)
-    order = order_ref[...]
-    for part in range(chunks // SOME):
-        for side in range(2):
-            stack = jnp.concatenate(
-                [line[part * SOME : (part + 1) * SOME] for line in by_row[side]], axis=0
-            )
-            sent_ref[part * SOME : (part + 1) * SOME, side * rows : (side + 1) * rows] = (
-                dot(order, stack).astype(BF16).reshape(SOME, rows, LANES)
-            )
+    blocks = [(part, side) for part in range(chunks // SOME) for side in range(2)]
+    stacks = [
+        jnp.concatenate(
+            [line[part * SOME : (part + 1) * SOME] for line in by_row[side]], axis=0
+        )
+        for part, side in blocks
+    ]
+    moved = dot(order_ref[...], jnp.concatenate(stacks, axis=1)).astype(BF16)
+    for n, (part, side) in enumerate(blocks):
+        sent_ref[part * SOME : (part + 1) * SOME, side * rows : (side + 1) * rows] = moved[
+            :, n * LANES : (n + 1) * LANES
+        ].reshape(SOME, rows, LANES)
 
 
 def triangle_kernel(split, grid_cols, rows, cols, got_ref, sent_ref):

time: 31.2 us -> 31.1 us (level)
  no operation moved by 1% of the time
where the time goes in v33:
time: 31.1 us; the launch traced here: 30.9 us
  blocking collectives  27.3 us (88%)
  Pallas kernels  2.53 us (8%)
  local copies, waits for them, and re-layouts  0.92 us (3%)
    all_to_all x1, blocking collectives, exchanged(): got = lax.all_to_all(sent, axes, 0, 0, tiled=True)  17.9 us
    all_to_all x1, blocking collectives, exchanged(): mine = lax.all_to_all(sums, axes, 0, 0, tiled=True)  9.45 us
    pallas_call x1, Pallas kernels, exchanged(): pl.pallas_call(update_kernel, out_shape=jax.ShapeDtypeStruct((rows, cols,...  1.27 us
    unnamed x20, local copies, waits for them, and re-layouts  0.92 us
    pallas_call x1, Pallas kernels, exchanged(): pl.pallas_call(functools.partial(mix_kernel, slots), out_shape=(jax.Shape...  0.91 us

profile of v33, /device:TPU:0, one launch (start us, length us, event | category | flops | bytes accessed | tf_op | source)
XLA Modules:
  0.0 30.9 jit_solution(3479404765255168503)
XLA Ops:
  0.0 0.0 copy-start.2
  0.0 0.0 copy-start.1
  0.0 0.0 copy-start
  0.0 0.0 copy-start.8
  0.0 0.0 copy-start.9
  0.1 0.0 copy-start.5
  0.1 0.0 copy-start.6
  0.1 0.0 copy-start.7
  0.1 0.7 %copy-done.2 = bf16[128,256]{1,0:T(8,128)(2,1)S(1)} copy-done((bf16[128,256]{1,0:T(8,128)(2,1)S(1)}, bf16[128,256]{1,0:T(8,128)(2,1)}, u32[]{:S(2)}) %copy-start.2) | copy-done | bytes 65560
  0.8 0.0 copy-done.1
  0.9 0.1 copy-done
  1.0 0.0 copy-done.8
  1.0 0.0 copy-done.9
  1.0 0.0 copy-done.5
  1.0 0.0 copy-done.6
  1.0 0.0 copy-done.7
  1.0 0.9 %mix.1 = (bf16[32,32,128]{2,1,0:T(8,128)(2,1)S(1)}, bf16[512,128]{1,0:T(8,128)(2,1)S(1)}, f32[128,128]{1,0:T(8,128)S(1)}, f32[128,128]{1,0:T(8,128)S(1)}) custom-call(bf16[256,256]{1,0:T(8,128)(2,1)S(1)} %order.1.order_ref, s32[1,8]{1,0:T(1,128)S(1)} %bitcast.5, bf16[16,32,128]{2,1,0:T(8,128)(2,1)S(1)} %copy-done, f32[1,128]{1,0:T(1,128)S(1)} %bitcast.6, ...), custom_call_target="tpu_custom_call" | custom-call | tf_op jit(solution)/shard_map/mix/pallas_call | solution.py:367
  1.9 17.9 %all_to_all.10.got_ref = bf16[32,32,128]{2,1,0:T(8,128)(2,1)S(1)} all-to-all(bf16[32,32,128]{2,1,0:T(8,128)(2,1)S(1)} %get-tuple-element.9), channel_id=1, replica_groups=mesh['high'=4,'low'=2,'col'=4] {'col','low','high'}, dimensions={0} | all-to-all | bytes 524288 | tf_op jit(solution)/shard_map/all_to_all | solution.py:391
  19.8 0.3 %triangle.1 = bf16[32,16,128]{2,1,0:T(8,128)(2,1)S(1)} custom-call(bf16[32,32,128]{2,1,0:T(8,128)(2,1)S(1)} %all_to_all.10.got_ref), custom_call_target="tpu_custom_call" | custom-call | tf_op jit(solution)/shard_map/triangle/pallas_call | solution.py:392
  20.1 0.0 copy-start.3
  20.1 0.0 copy-start.4
  20.1 9.5 %all_to_all.11.got_ref = bf16[32,16,128]{2,1,0:T(8,128)(2,1)S(1)} all-to-all(bf16[32,16,128]{2,1,0:T(8,128)(2,1)S(1)} %triangle.1), channel_id=1, replica_groups=mesh['high'=4,'low'=2,'col'=4] {'col','low','high'}, dimensions={0} | all-to-all | bytes 262144 | tf_op jit(solution)/shard_map/all_to_all | solution.py:400
  29.6 0.0 copy-done.3
  29.6 0.0 copy-done.4
  29.6 1.3 %update.1 = bf16[16,32,128]{2,1,0:T(8,128)(2,1)} custom-call(bf16[32,16,128]{2,1,0:T(8,128)(2,1)S(1)} %all_to_all.11.got_ref, bf16[256,256]{1,0:T(8,128)(2,1)S(1)} %order.1.order_ref, bf16[512,128]{1,0:T(8,128)(2,1)S(1)} %get-tuple-element.10.normed_ref, f32[128,128]{1,0:T(8,128)S(1)} %get-tuple-element.11.gain_ref, ...), custom_call_target="tpu_custom_call" | custom-call | tf_op jit(solution)/shard_map/update/pallas_call | solution.py:401
  (1 shorter events, 0.0 us)
Async XLA Ops:
  0.0 0.8 %copy-start.2 = (bf16[128,256]{1,0:T(8,128)(2,1)S(1)}, bf16[128,256]{1,0:T(8,128)(2,1)}, u32[]{:S(2)}) copy-start(bf16[128,256]{1,0:T(8,128)(2,1)} %gate_ref.2) | copy-start | bytes 196612
  0.0 0.9 %copy-start.1 = (bf16[128,256]{1,0:T(8,128)(2,1)S(1)}, bf16[128,256]{1,0:T(8,128)(2,1)}, u32[]{:S(2)}) copy-start(bf16[128,256]{1,0:T(8,128)(2,1)} %proj_ref.2) | copy-start | bytes 196612
  0.0 1.0 %copy-start = (bf16[16,32,128]{2,1,0:T(8,128)(2,1)S(1)}, bf16[16,32,128]{2,1,0:T(8,128)(2,1)}, u32[]{:S(2)}) copy-start(bf16[16,32,128]{2,1,0:T(8,128)(2,1)} %pair_ref.1) | copy-start | bytes 393220
  0.0 1.0 %copy-start.8 = (f32[128]{0:T(128)S(1)}, f32[128]{0:T(128)}, u32[]{:S(2)}) copy-start(f32[128]{0:T(128)} %param.16) | copy-start | bytes 1540
  0.0 1.0 %copy-start.9 = (f32[128]{0:T(128)S(1)}, f32[128]{0:T(128)}, u32[]{:S(2)}) copy-start(f32[128]{0:T(128)} %param.17) | copy-start | bytes 1540
  0.1 0.9 %copy-start.5 = (s32[8]{0:T(128)S(1)}, s32[8]{0:T(128)}, u32[]{:S(2)}) copy-start(s32[8]{0:T(128)} %param.11) | copy-start | bytes 100
  0.1 0.9 %copy-start.6 = (f32[128]{0:T(128)S(1)}, f32[128]{0:T(128)}, u32[]{:S(2)}) copy-start(f32[128]{0:T(128)} %param.12) | copy-start | bytes 1540
  0.1 0.9 %copy-start.7 = (f32[128]{0:T(128)S(1)}, f32[128]{0:T(128)}, u32[]{:S(2)}) copy-start(f32[128]{0:T(128)} %param.13) | copy-start | bytes 1540
  20.1 9.5 %copy-start.3 = (bf16[128,128]{1,0:T(8,128)(2,1)S(1)}, bf16[128,128]{1,0:T(8,128)(2,1)}, u32[]{:S(2)}) copy-start(bf16[128,128]{1,0:T(8,128)(2,1)} %proj_ref.3) | copy-start | bytes 98308
  20.1 9.5 %copy-start.4 = (bf16[128,128]{1,0:T(8,128)(2,1)S(1)}, bf16[128,128]{1,0:T(8,128)(2,1)}, u32[]{:S(2)}) copy-start(bf16[128,128]{1,0:T(8,128)(2,1)} %gate_ref.3) | copy-start | bytes 98308
